TPU v7x, 32 devices: a whole 2x2x4 slice. The times are simulated.
32 devices in a mesh: tx: 8 (over z, x), ty: 4 (over y, core).
Axes of the slice: x: 2, y: 2, z: 4, core: 2. Of those that a mesh axis runs over, the one named last changes fastest.
Arguments:
- sar_image: bfloat16 [2, 2048, 512], P(None, ('tx', 'ty')), may hold values from -6 to 6
- kernel_first: bfloat16 [16, 2, 3, 3], replicated, may hold values from -2 to 2
- kernel_second: bfloat16 [16, 16, 3, 3], replicated, may hold values from -0.75 to 0.75
- kernel_third: bfloat16 [16, 16, 3, 3], replicated, may hold values from -0.75 to 0.75
- kernel_last: bfloat16 [1, 16, 3, 3], replicated, may hold values from -1 to 1
- geo_weight: float32 [2048, 512], P(('tx', 'ty')), may hold values from 0.25 to 1
- cell_index: int32 [2048, 512], P(('tx', 'ty')), may hold values from 0 to 511
- block_tile: int32 [2048, 1], P(('tx', 'ty')), may hold values from 0 to 31; in each aligned block of 64 rows (0 to 63, 64 to 127, ...) at most 4 rows name the same one
- block_row: int32 [2048, 1], P(('tx', 'ty')), may hold values from 0 to 254
- depth: float32 [2048, 1024], P('tx', 'ty'), may hold values from 0.1 to 1
- slope: float32 [2048, 1024], P('tx', 'ty'), may hold values from 0.01 to 1
- flow_dir: int32 [2048, 1024], P('tx', 'ty'), may hold values from 0 to 7
- rain: float32 [2048, 1024], P('tx', 'ty'), may hold values from 0 to 0.1
Outputs:
- water_fraction: bfloat16 [2048, 512], P(('tx', 'ty'))
- level: float32 [2048, 1024], P('tx', 'ty')
Inputs may be any that keep to these rules, and one draw needn't show every extreme that they name: `block_tile`: in the rows of one device no tile is named more than 4 times, a bound that some block reaches.
All inputs are finite; a program needn't handle non-finite values.
Results may differ from a plain program's by a relative error of at most 0.003.
The roundings to bfloat16 on the way count: a program that leaves them out, or rounds other values in their place, can miss the bound.
Values may be sent and summed in bfloat16 or wider, within the bound.
No kernel may reach another device: no remote copies, remote signals or barrier semaphores. Data moves between devices by JAX's collectives and lax.ppermute only.
A program may use at most 128 MiB of HBM per device.

v0:
```python
import functools

import jax
import jax.numpy as jnp
from jax import lax
from jax.experimental import pallas as pl
from jax.experimental.pallas import tpu as pltpu
from jax.sharding import PartitionSpec as P

WIN_ROWS = 2
SUBSTEPS = 8
CH = 16
OUT_LINES = 14
IN_LINES = OUT_LINES + 2
HALO_LINES = 4
LANES = 128
VMEM_LIMIT = 48 * 1024 * 1024

wet_depth = 0.5
runoff_coef = 0.25
bf16 = jnp.bfloat16
f32 = jnp.float32


def iota(shape, dim):
    return lax.broadcasted_iota(jnp.int32, shape, dim)


def dot(a, b):
    return lax.dot_general(a, b, (((1,), (0,)), ((), ())), preferred_element_type=f32)


def dot_t(a, b):
    return lax.dot_general(a, b, (((1,), (1,)), ((), ())), preferred_element_type=f32)


def pixel_shifts(x):
    width = x.shape[1]
    pix = iota(x.shape, 1)
    before = jnp.where(pix == 0, 0.0, pltpu.roll(x, 1, 1))
    after = jnp.where(pix == width - 1, 0.0, pltpu.roll(x, width - 1, 1))
    return before, after


def band_weights(tiled, rows, cols, per_row, line_of):
    out_line = iota((rows, cols), 0) // per_row
    off = line_of(iota((rows, cols), 1)) - out_line
    out = jnp.zeros((rows, cols), f32)
    for ky in range(3):
        out = jnp.where(off == ky, tiled[ky], out)
    return out.astype(bf16)


def stack_rows(x, times):
    return jnp.broadcast_to(x[None], (times,) + x.shape).reshape(times * x.shape[0], x.shape[1])


def swath_kernel(
    devices, capacity,
    sar_ref, top_ref, bot_ref, wk_ref, gw_ref, cell_ref, tile_ref, row_ref,
    frac_ref, send_ref,
    s_ref, xa_ref, xb_ref, x3_ref, obs_ref, wnd_ref,
):
    lines, px = gw_ref.shape
    blocks = (lines + 2 * HALO_LINES - 2) // OUT_LINES
    frame = lines + 2 * HALO_LINES
    total = frame + 2
    me = lax.axis_index("tx") * lax.axis_size("ty") + lax.axis_index("ty")
    first = me == 0
    last = me == devices - 1

    for ch in range(2):
        s_ref[ch, 0:HALO_LINES, :] = top_ref[ch].astype(f32)
        s_ref[ch, HALO_LINES : HALO_LINES + lines, :] = sar_ref[ch].astype(f32)
        s_ref[ch, HALO_LINES + lines : frame, :] = bot_ref[ch].astype(f32)

    rows = OUT_LINES * CH
    cols = IN_LINES * CH
    spread = (iota((CH, cols), 1) % CH == iota((CH, cols), 0)).astype(bf16)

    cols1 = 3 * 2 * IN_LINES
    spread1 = (iota((CH, cols1), 1) // IN_LINES == iota((CH, cols1), 0)).astype(bf16)
    wide1 = dot(wk_ref[0:48, :], spread1)
    w1 = band_weights(
        [stack_rows(wide1[ky * CH : (ky + 1) * CH], OUT_LINES) for ky in range(3)],
        rows, cols1, CH, lambda k: k % IN_LINES,
    )

    def mid_weights(base):
        wide = dot(wk_ref[base : base + 144, :], spread)
        return [
            band_weights(
                [stack_rows(wide[(ky * 3 + kx) * CH : (ky * 3 + kx + 1) * CH], OUT_LINES) for ky in range(3)],
                rows, cols, CH, lambda k: k // CH,
            )
            for kx in range(3)
        ]

    def put(ref, line, acc):
        feat = jnp.maximum(acc, 0.0)
        at = pl.ds(line * CH, rows)
        if len(ref.shape) == 2:
            ref[at, :] = feat.astype(bf16)
            return
        before, after = pixel_shifts(feat)
        ref[0, at, :] = before.astype(bf16)
        ref[1, at, :] = feat.astype(bf16)
        ref[2, at, :] = after.astype(bf16)

    def clear(ref, lo, hi):
        shape = ref.shape[:-2] + ((hi - lo) * CH, px)
        ref[..., lo * CH : hi * CH, :] = jnp.zeros(shape, bf16)

    def outside(ref):
        @pl.when(first)
        def _():
            clear(ref, 0, HALO_LINES)

        @pl.when(last)
        def _():
            clear(ref, HALO_LINES + lines, frame)

    for b in range(blocks):
        at = b * OUT_LINES
        x = jnp.concatenate([s_ref[0, at : at + IN_LINES, :], s_ref[1, at : at + IN_LINES, :]], 0)
        before, after = pixel_shifts(x)
        put(xa_ref, 1 + at, dot(w1, jnp.concatenate([before, x, after], 0).astype(bf16)))
    clear(xa_ref, frame - 1, total)
    outside(xa_ref)

    for base, src, dst, line in ((48, xa_ref, xb_ref, 2), (192, xb_ref, x3_ref, 3)):
        w = mid_weights(base)
        for b in range(blocks):
            at = pl.ds((line - 1 + b * OUT_LINES) * CH, cols)
            acc = dot(w[0], src[0, at, :]) + dot(w[1], src[1, at, :]) + dot(w[2], src[2, at, :])
            put(dst, line + b * OUT_LINES, acc)
        if len(dst.shape) == 3:
            clear(dst, frame, total)
        outside(dst)

    cols4 = (lines + 2) * CH
    spread4 = (iota((CH, cols4), 1) % CH == iota((CH, cols4), 0)).astype(bf16)
    wide4 = dot(wk_ref[336:352, :], spread4)
    w4 = [
        band_weights(
            [jnp.broadcast_to(wide4[ky * 3 + kx : ky * 3 + kx + 1], (lines, cols4)) for ky in range(3)],
            lines, cols4, 1, lambda k: k // CH,
        )
        for kx in range(3)
    ]
    parts = dot(jnp.concatenate(w4, 0), x3_ref[(HALO_LINES - 1) * CH : (HALO_LINES + lines + 1) * CH, :])
    from_before, _ = pixel_shifts(parts[0:lines])
    _, from_after = pixel_shifts(parts[2 * lines : 3 * lines])
    logit = from_before + parts[lines : 2 * lines] + from_after
    frac = (1.0 / (1.0 + jnp.exp(-logit))).astype(bf16)
    frac_ref[...] = frac
    obs_ref[...] = frac.astype(f32) * gw_ref[...]

    kind = iota((8, px), 0)
    lane_col = iota((LANES, px), 0)
    group = 8

    def window_group(g, carry):
        at = pl.ds(pl.multiple_of(g * group, group), group)
        cell = cell_ref[at, :]
        obs = obs_ref[at, :]
        cov = gw_ref[at, :]
        part = cell // LANES
        col = cell % LANES
        for i in range(group):
            value = jnp.where(kind < 4, obs[i : i + 1], cov[i : i + 1])
            value = jnp.where(kind % 4 == part[i : i + 1], value, 0.0)
            coarse = value.astype(bf16).astype(f32)
            left = jnp.concatenate([coarse, value - coarse], 0).astype(bf16)
            hot = jnp.where(lane_col == col[i : i + 1], 1.0, 0.0).astype(bf16)
            sums = dot_t(left, hot)
            wnd_ref[pl.ds(pl.multiple_of(g * (8 * group) + 8 * i, 8), 8), :] = sums[0:8] + sums[8:16]
        return carry

    lax.fori_loop(0, lines // group, window_group, 0)

    tile = tile_ref[...].astype(f32)
    same = iota((lines, lines), 0) == iota((lines, lines), 1)
    tile_sub = jnp.sum(jnp.where(same, jnp.broadcast_to(tile, (lines, lines)), 0.0), 1, keepdims=True)
    rival = (tile_sub == tile) & (iota((lines, lines), 0) < iota((lines, lines), 1))
    slot = tile * capacity + jnp.sum(jnp.where(rival, 1.0, 0.0), 0, keepdims=True)
    wnd_rows = 8 * lines
    widen = (iota((lines, wnd_rows), 1) // 8 == iota((lines, wnd_rows), 0)).astype(bf16)
    slot_wide = dot(jnp.broadcast_to(slot, (8, lines)).astype(bf16), widen)[0:1]
    place = slot_wide.astype(jnp.int32) * 4 + (iota((1, wnd_rows), 1) // 2) % 4
    slots = devices * capacity * 4
    perm = jnp.where(iota((slots, wnd_rows), 0) == place, 1.0, 0.0).astype(bf16)
    wnd = wnd_ref[...]
    half = iota((wnd_rows, LANES), 0) % 2
    own_line = iota((wnd_rows, lines), 0) // 8 == iota((wnd_rows, lines), 1)
    row_part = jnp.where(own_line, jnp.broadcast_to(row_ref[...].astype(f32), (wnd_rows, lines)), 0.0)
    row_wide = dot(row_part.astype(bf16), jnp.ones((lines, LANES), bf16))
    goods = jnp.concatenate(
        [jnp.where(half == 0, wnd, 0.0), jnp.where(half == 1, wnd, 0.0), jnp.where(half == 0, row_wide, 0.0)], 1
    ).astype(bf16)
    send_ref[...] = dot(perm, goods).astype(bf16)


def transposed(x):
    return jnp.transpose(x, (1, 0))


def level_kernel(got_ref, depth_ref, slope_ref, dir_ref, rain_ref, level_ref, top_ref, bot_ref, left_ref, right_ref):
    tile_rows, tile_cols = depth_ref.shape
    k = got_ref.shape[0]
    line = transposed(got_ref[:, tile_cols:].astype(f32))[0:1]
    lane = iota((1, k), 1)
    target = line.astype(jnp.int32) + lane % 2 + tile_rows * ((lane // 2) % 2)
    placer = jnp.where(iota((2 * tile_rows, k), 0) == target, 1.0, 0.0).astype(bf16)
    summed = dot(placer, got_ref[:, 0:tile_cols])
    observed = summed[0:tile_rows]
    covered = summed[tile_rows:]
    depth = depth_ref[...]
    wet = depth / (depth + wet_depth)
    innovation = (observed - covered * wet) / (covered + 1.0)
    level = depth * jnp.exp(innovation)
    level_ref[...] = level
    conveyance = runoff_coef * jnp.sqrt(slope_ref[...])
    fields = (level, rain_ref[...], conveyance, dir_ref[...].astype(f32))
    h = SUBSTEPS
    top_ref[...] = jnp.concatenate([x[0:h] for x in fields], 0).astype(bf16)
    bot_ref[...] = jnp.concatenate([x[tile_rows - h :] for x in fields], 0).astype(bf16)
    left_ref[...] = jnp.concatenate([transposed(x[:, 0:LANES])[0:h] for x in fields], 0).astype(bf16)
    right_ref[...] = jnp.concatenate(
        [transposed(x[:, tile_cols - LANES :])[LANES - h :] for x in fields], 0
    ).astype(bf16)


def flow_kernel(
    level_ref, slope_ref, dir_ref, rain_ref, above_ref, below_ref, left_ref, right_ref,
    out_ref,
    rain_s, conv_s, m_ref, part_ref, up_ref, down_ref,
):
    tile_rows, tile_cols = level_ref.shape
    h = SUBSTEPS
    wide_rows = tile_rows + 2 * h
    wide_cols = tile_cols + LANES

    gap = jnp.zeros((LANES - 2 * h, 2 * tile_cols), f32)

    def widened(field, own):
        at = slice(field * h, (field + 1) * h)
        rights = jnp.concatenate(
            [right_ref[...], below_ref[:, tile_cols : tile_cols + LANES], above_ref[:, tile_cols : tile_cols + LANES]], 1
        )
        lefts = jnp.concatenate(
            [left_ref[...], below_ref[:, tile_cols + LANES :], above_ref[:, tile_cols + LANES :]], 1
        )
        side = transposed(jnp.concatenate([rights.astype(f32)[at], gap, lefts.astype(f32)[at]], 0))
        above = jnp.concatenate([above_ref[:, 0:tile_cols].astype(f32)[at], side[tile_rows + 2 * LANES - h :]], 1)
        below = jnp.concatenate([below_ref[:, 0:tile_cols].astype(f32)[at], side[tile_rows : tile_rows + h]], 1)
        mid = jnp.concatenate([own, side[0:tile_rows]], 1)
        return jnp.concatenate([above, mid, below], 0)

    zeros = jnp.zeros((h, wide_cols), f32)
    for buf in range(2):
        for ref in (up_ref, down_ref):
            ref[buf, 0:h, :] = zeros
            ref[buf, h + wide_rows :, :] = zeros
    part_ref[0] = widened(0, level_ref[...])
    rain_s[...] = widened(1, rain_ref[...])
    conv = widened(2, runoff_coef * jnp.sqrt(slope_ref[...]))
    conv_s[...] = conv
    code = widened(3, dir_ref[...].astype(f32))
    sides = (-1, 0, 1, -1, 1, -1, 0, 1)
    for direction, side in enumerate(sides):
        share = jnp.where(code == direction, conv, 0.0)
        m_ref[direction] = pltpu.roll(share, side % wide_cols, 1) if side else share

    chunk = 16

    def level_at(buf, r, n, step):
        level = part_ref[buf, r : r + n, :]
        if step:
            level = level + up_ref[buf, h + r + 1 : h + r + 1 + n, :] + down_ref[buf, h + r - 1 : h + r - 1 + n, :]
        return level

    for step in range(SUBSTEPS):
        buf, new = step % 2, (step + 1) % 2
        for r in range(0, wide_rows, chunk):
            level = level_at(buf, r, chunk, step)
            power = level * jnp.exp((2.0 / 3.0) * jnp.log(jnp.maximum(jnp.abs(level), 1e-30)))
            from_right = pltpu.roll(power, wide_cols - 1, 1)
            from_left = pltpu.roll(power, 1, 1)
            m = [m_ref[d, r : r + chunk, :] for d in range(8)]
            up_ref[new, h + r : h + r + chunk, :] = m[0] * from_right + m[1] * power + m[2] * from_left
            down_ref[new, h + r : h + r + chunk, :] = m[5] * from_right + m[6] * power + m[7] * from_left
            part_ref[new, r : r + chunk, :] = (
                level + rain_s[r : r + chunk, :] - conv_s[r : r + chunk, :] * power
                + (m[3] * from_right + m[4] * from_left)
            )
    buf = SUBSTEPS % 2
    out_ref[...] = level_at(buf, h, tile_rows, SUBSTEPS)[:, 0:tile_cols]


def vmem_specs(n):
    return [pl.BlockSpec(memory_space=pltpu.VMEM)] * n


def kernel_rows(kernel_first, kernel_second, kernel_third, kernel_last):
    first = jnp.transpose(kernel_first, (2, 0, 3, 1)).reshape(3 * CH, 6)
    first = jnp.pad(first, ((0, 0), (0, CH - 6)))
    mids = [jnp.transpose(k, (2, 3, 0, 1)).reshape(9 * CH, CH) for k in (kernel_second, kernel_third)]
    last = jnp.transpose(kernel_last[0], (1, 2, 0)).reshape(9, CH)
    last = jnp.pad(last, ((0, CH - 9), (0, 0)))
    return jnp.concatenate([first, *mids, last], 0)


def per_device(
    sar_image, kernel_first, kernel_second, kernel_third, kernel_last,
    geo_weight, cell_index, block_tile, block_row, depth, slope, flow_dir, rain,
):
    both = ("tx", "ty")
    devices = lax.axis_size(both)
    az_lines, range_px = geo_weight.shape
    tile_rows, tile_cols = depth.shape
    capacity = max(2, 2 * az_lines // devices)

    def steps(axis):
        size = lax.axis_size(axis)
        up = [(i, i + 1) for i in range(size - 1)]
        return up, [(j, i) for i, j in up]

    up, down = steps(both)
    top = lax.ppermute(sar_image[:, az_lines - HALO_LINES :], both, up)
    bot = lax.ppermute(sar_image[:, :HALO_LINES], both, down)
    weights = kernel_rows(kernel_first, kernel_second, kernel_third, kernel_last)

    params = pltpu.CompilerParams(vmem_limit_bytes=VMEM_LIMIT)
    slots = devices * capacity * 4
    frame = az_lines + 2 * HALO_LINES
    feats = (frame + 2) * CH
    send_lanes = tile_cols + LANES
    fraction, send = pl.pallas_call(
        functools.partial(swath_kernel, devices, capacity),
        out_shape=(
            jax.ShapeDtypeStruct((az_lines, range_px), bf16),
            jax.ShapeDtypeStruct((slots, send_lanes), bf16),
        ),
        in_specs=vmem_specs(8),
        out_specs=tuple(vmem_specs(2)),
        scratch_shapes=[
            pltpu.VMEM((2, frame + 8, range_px), f32),
            pltpu.VMEM((3, feats, range_px), bf16),
            pltpu.VMEM((3, feats, range_px), bf16),
            pltpu.VMEM((feats, range_px), bf16),
            pltpu.VMEM((az_lines, range_px), f32),
            pltpu.VMEM((8 * az_lines, LANES), f32),
        ],
        compiler_params=params,
        name="swath",
    )(
        sar_image, top, bot, weights, geo_weight, cell_index,
        block_tile.reshape(1, az_lines), block_row.reshape(1, az_lines),
    )

    got = lax.all_to_all(
        send.reshape(devices, capacity * 4, send_lanes), both, split_axis=0, concat_axis=0, tiled=True
    ).reshape(slots, send_lanes)

    edge = jax.ShapeDtypeStruct((4 * SUBSTEPS, tile_cols), bf16)
    level, top_rows, bot_rows, left_cols, right_cols = pl.pallas_call(
        level_kernel,
        out_shape=(jax.ShapeDtypeStruct((tile_rows, tile_cols), f32), edge, edge, edge, edge),
        in_specs=vmem_specs(5),
        out_specs=tuple(vmem_specs(5)),
        compiler_params=params,
        name="level",
    )(got, depth, slope, flow_dir, rain)

    up, down = steps("ty")
    left = lax.ppermute(right_cols, "ty", up)
    right = lax.ppermute(left_cols, "ty", down)
    up, down = steps("tx")
    cut = tile_cols - LANES
    above = lax.ppermute(jnp.concatenate([bot_rows, right[:, cut:], left[:, cut:]], 1), "tx", up)
    below = lax.ppermute(jnp.concatenate([top_rows, right[:, :LANES], left[:, :LANES]], 1), "tx", down)

    wide_rows = tile_rows + 2 * SUBSTEPS
    wide_cols = tile_cols + LANES
    level = pl.pallas_call(
        flow_kernel,
        out_shape=jax.ShapeDtypeStruct((tile_rows, tile_cols), f32),
        in_specs=vmem_specs(8),
        out_specs=vmem_specs(1)[0],
        scratch_shapes=[
            pltpu.VMEM((wide_rows, wide_cols), f32),
            pltpu.VMEM((wide_rows, wide_cols), f32),
            pltpu.VMEM((8, wide_rows, wide_cols), f32),
            pltpu.VMEM((2, wide_rows, wide_cols), f32),
            pltpu.VMEM((2, wide_rows + 2 * SUBSTEPS, wide_cols), f32),
            pltpu.VMEM((2, wide_rows + 2 * SUBSTEPS, wide_cols), f32),
        ],
        compiler_params=params,
        name="flow",
    )(level, slope, flow_dir, rain, above, below, left, right)
    return (fraction, level)


def solution(mesh):
    placed = (
        P(None, ("tx", "ty"), None),
        P(),
        P(),
        P(),
        P(),
        P(("tx", "ty"), None),
        P(("tx", "ty"), None),
        P(("tx", "ty"), None),
        P(("tx", "ty"), None),
        P("tx", "ty"),
        P("tx", "ty"),
        P("tx", "ty"),
        P("tx", "ty"),
    )
    return jax.shard_map(
        per_device,
        mesh=mesh,
        in_specs=placed,
        out_specs=(P(("tx", "ty"), None), P("tx", "ty")),
        check_vma=False,
    )
```

profile of v0, /device:TPU:0, one launch (start us, length us, event | category | flops | bytes accessed | tf_op | source)
XLA Modules:
  0.0 60.3 jit_solution(5706649495452327622)
XLA Ops:
  0.6 0.0 copy-start.4
  0.6 0.0 copy-start.5
  0.6 0.8 %fusion.5 = (bf16[2,4,512]{2,1,0:T(4,128)(2,1)S(1)}, bf16[2,4,512]{2,1,0:T(4,128)(2,1)S(1)}) fusion(bf16[2,64,512]{2,1,0:T(8,128)(2,1)} %sar_ref.1), kind=kLoop, calls=%fused_computation.9 | loop fusion | bytes 32768 | tf_op jit(solution)/shard_map/slice | solution.py:331
  1.4 1.3 %collective-permute-start.1 = (bf16[2,4,512]{2,1,0:T(4,128)(2,1)S(1)}, bf16[2,4,512]{2,1,0:T(4,128)(2,1)S(1)}, u32[]{:S(2)}, u32[]{:S(2)}) collective-permute-start(bf16[2,4,512]{2,1,0:T(4,128)(2,1)S(1)} %get-tuple-element.16), channel_id=1, source_target_pairs={{1,0},{2,1},{3,2},{4,3},{5,4},{6,5},{7,6},{8,7},{9,8},{10,9},{11,1... | collective-permute-start | bytes 24584 | tf_op jit(solution)/shard_map/ppermute | solution.py:331
  2.7 3.0 %collective-permute-start = (bf16[2,4,512]{2,1,0:T(4,128)(2,1)S(1)}, bf16[2,4,512]{2,1,0:T(4,128)(2,1)S(1)}, u32[]{:S(2)}, u32[]{:S(2)}) collective-permute-start(bf16[2,4,512]{2,1,0:T(4,128)(2,1)S(1)} %get-tuple-element.17), channel_id=1, source_target_pairs={{0,1},{1,2},{2,3},{3,4},{4,5},{5,6},{6,7},{7,8},{8,9},{9,10},{10,1... | collective-permute-start | bytes 24584 | tf_op jit(solution)/shard_map/ppermute | solution.py:330
  5.8 0.7 %reshape.31 = bf16[9,16]{1,0:T(8,128)(2,1)S(1)} reshape(bf16[3,3,16]{2,1,0:T(4,128)(2,1)} %bitcast.23) | data formatting | bytes 576 | tf_op jit(solution)/shard_map/reshape | solution.py:309
  6.5 0.7 %copy.28 = bf16[3,16,3,2]{1,0,3,2:T(4,128)(2,1)S(1)} copy(bf16[3,16,3,2]{1,3,2,0:T(2,128)(2,1)} %bitcast.22) | data formatting | bytes 1152 | tf_op jit(solution)/shard_map/transpose | solution.py:306
  7.2 0.1 reshape.28
  7.3 0.1 copy.29
  7.4 0.8 %fusion.2.wk_ref = bf16[352,16]{1,0:T(8,128)(2,1)S(1)} fusion(bf16[9,16]{1,0:T(8,128)(2,1)S(1)} %reshape.31, bf16[48,6]{1,0:T(8,128)(2,1)S(1)} %copy.29, bf16[144,16]{1,0:T(8,128)(2,1)} %bitcast.20, bf16[144,16]{1,0:T(8,128)(2,1)} %bitcast.21), kind=kLoop, calls=%fused_computation.4 | loop fusion | flops 67584 | bytes 21344 | tf_op jit(solution)/shard_map/concatenate | solution.py:311
  8.2 0.0 collective-permute-done.1.bot_ref
  8.2 0.0 collective-permute-done.top_ref
  8.2 0.0 copy-start.7
  8.2 0.0 copy-start.8
  8.2 0.0 copy-done.4
  8.2 0.0 copy-done.5
  8.2 0.6 %copy-done.7 = s32[64,1]{0,1:T(1,128)S(1)} copy-done((s32[64,1]{0,1:T(1,128)S(1)}, s32[64,1]{0,1:T(1,128)}, u32[]{:S(2)}) %copy-start.7) | copy-done | bytes 280
  8.9 0.0 copy-done.8
  8.9 0.0 copy-start.6
  8.9 0.9 %copy-done.6 = s32[64,512]{1,0:T(8,128)S(1)} copy-done((s32[64,512]{1,0:T(8,128)S(1)}, s32[64,512]{1,0:T(8,128)}, u32[]{:S(2)}) %copy-start.6) | copy-done | bytes 131096
  9.8 0.0 copy-start.3
  9.8 8.6 %swath.1 = (bf16[64,512]{1,0:T(8,128)(2,1)}, bf16[512,384]{1,0:T(8,128)(2,1)S(1)}) custom-call(bf16[2,64,512]{2,1,0:T(8,128)(2,1)S(1)} %copy-done.4, bf16[2,4,512]{2,1,0:T(4,128)(2,1)S(1)} %collective-permute-done.top_ref, bf16[2,4,512]{2,1,0:T(4,128)(2,1)S(1)} %collective-permute-done.1.bot_ref, bf16[352,16]{1,0:T(8,128)(2,1)S(1)} %fusion.2.wk_ref, ...), custom_call_target="tpu_custom_call" | custom-call | tf_op jit(solution)/shard_map/swath/pallas_call | solution.py:339
  18.4 0.0 copy-start
  18.4 0.0 copy-start.1
  18.4 0.0 copy-start.2
  18.4 22.1 %all_to_all.5 = bf16[32,16,384]{2,1,0:T(8,128)(2,1)S(1)} all-to-all(bf16[32,16,384]{2,1,0:T(8,128)(2,1)S(1)} %bitcast.17), channel_id=1, replica_groups=mesh['tx'=8,'ty'=4] {'tx','ty'}, dimensions={0} | all-to-all | bytes 786432 | tf_op jit(solution)/shard_map/all_to_all | solution.py:362
  40.5 0.0 copy-done.3
  40.5 0.0 copy-done
  40.5 0.0 copy-done.1
  40.5 0.0 copy-done.2
  40.5 0.5 level.1
  41.1 1.3 %collective-permute-start.2 = (bf16[32,256]{1,0:T(8,128)(2,1)S(1)}, bf16[32,256]{1,0:T(8,128)(2,1)S(1)}, u32[]{:S(2)}, u32[]{:S(2)}) collective-permute-start(bf16[32,256]{1,0:T(8,128)(2,1)S(1)} %get-tuple-element.13), channel_id=1, source_target_pairs={{1,0},{2,1},{3,2},{5,4},{6,5},{7,6},{9,8},{10,9},{11,10},{13,12},{... | collective-permute-start | bytes 49160 | tf_op jit(solution)/shard_map/ppermute | solution.py:378
  42.4 3.0 %collective-permute-start.3 = (bf16[32,256]{1,0:T(8,128)(2,1)S(1)}, bf16[32,256]{1,0:T(8,128)(2,1)S(1)}, u32[]{:S(2)}, u32[]{:S(2)}) collective-permute-start(bf16[32,256]{1,0:T(8,128)(2,1)S(1)} %get-tuple-element.14), channel_id=1, source_target_pairs={{0,1},{1,2},{2,3},{4,5},{5,6},{6,7},{8,9},{9,10},{10,11},{12,13},{... | collective-permute-start | bytes 49160 | tf_op jit(solution)/shard_map/ppermute | solution.py:377
  45.4 0.0 collective-permute-done.2.right_ref
  45.4 0.8 %collective-permute-done.3.left_ref = bf16[32,256]{1,0:T(8,128)(2,1)S(1)} collective-permute-done((bf16[32,256]{1,0:T(8,128)(2,1)S(1)}, bf16[32,256]{1,0:T(8,128)(2,1)S(1)}, u32[]{:S(2)}, u32[]{:S(2)}) %collective-permute-start.3) | collective-permute-done | bytes 16416 | tf_op jit(solution)/shard_map/ppermute | solution.py:377
  46.3 2.9 %collective-permute-start.4 = (bf16[32,512]{1,0:T(8,128)(2,1)S(1)}, bf16[32,512]{1,0:T(8,128)(2,1)S(1)}, u32[]{:S(2)}, u32[]{:S(2)}) collective-permute-start(bf16[32,512]{1,0:T(8,128)(2,1)S(1)} %pad_maximum_fusion), channel_id=1, source_target_pairs={{0,4},{4,8},{8,12},{12,16},{16,20},{20,24},{24,28},{1,5},{5,9},{9,... | collective-permute-start | bytes 98312 | tf_op jit(solution)/shard_map/ppermute | solution.py:381
  49.2 1.3 %collective-permute-start.5 = (bf16[32,512]{1,0:T(8,128)(2,1)S(1)}, bf16[32,512]{1,0:T(8,128)(2,1)S(1)}, u32[]{:S(2)}, u32[]{:S(2)}) collective-permute-start(bf16[32,512]{1,0:T(8,128)(2,1)S(1)} %pad_maximum_fusion.1), channel_id=1, source_target_pairs={{4,0},{8,4},{12,8},{16,12},{20,16},{24,20},{28,24},{5,1},{9,5},{13... | collective-permute-start | bytes 98312 | tf_op jit(solution)/shard_map/ppermute | solution.py:382
  50.5 0.3 collective-permute-done.4.above_ref
  50.7 4.2 %collective-permute-done.5.below_ref = bf16[32,512]{1,0:T(8,128)(2,1)S(1)} collective-permute-done((bf16[32,512]{1,0:T(8,128)(2,1)S(1)}, bf16[32,512]{1,0:T(8,128)(2,1)S(1)}, u32[]{:S(2)}, u32[]{:S(2)}) %collective-permute-start.5) | collective-permute-done | bytes 32800 | tf_op jit(solution)/shard_map/ppermute | solution.py:382
  55.0 5.3 %flow.1 = f32[256,256]{1,0:T(8,128)} custom-call(f32[256,256]{1,0:T(8,128)S(1)} %get-tuple-element.11.level_ref, f32[256,256]{1,0:T(8,128)S(1)} %copy-done, s32[256,256]{1,0:T(8,128)S(1)} %copy-done.1, f32[256,256]{1,0:T(8,128)S(1)} %copy-done.2, bf16[32,512]{1,0:T(8,128)(2,1)S(1)} %collective-permute-done.4.above_ref, ...), custom_call_target="tpu_custom_call" | custom-call | tf_op jit(solution)/shard_map/flow/pallas_call | solution.py:386
  (4 shorter events, 0.0 us)
Async XLA Ops:
  0.6 7.6 %copy-start.4 = (bf16[2,64,512]{2,1,0:T(8,128)(2,1)S(1)}, bf16[2,64,512]{2,1,0:T(8,128)(2,1)}, u32[]{:S(2)}) copy-start(bf16[2,64,512]{2,1,0:T(8,128)(2,1)} %sar_ref.1) | copy-start | bytes 393220
  0.6 7.6 %copy-start.5 = (f32[64,512]{1,0:T(8,128)S(1)}, f32[64,512]{1,0:T(8,128)}, u32[]{:S(2)}) copy-start(f32[64,512]{1,0:T(8,128)} %gw_ref.1) | copy-start | bytes 393220
  1.4 6.7 %collective-permute-start.1 = (bf16[2,4,512]{2,1,0:T(4,128)(2,1)S(1)}, bf16[2,4,512]{2,1,0:T(4,128)(2,1)S(1)}, u32[]{:S(2)}, u32[]{:S(2)}) collective-permute-start(bf16[2,4,512]{2,1,0:T(4,128)(2,1)S(1)} %get-tuple-element.16), channel_id=1, source_target_pairs={{1,0},{2,1},{3,2},{4,3},{5,4},{6,5},{7,6},{8,7},{9,8},{10,9},{11,1... | collective-permute-start | bytes 24584 | tf_op jit(solution)/shard_map/ppermute | solution.py:331
  2.7 5.5 %collective-permute-start = (bf16[2,4,512]{2,1,0:T(4,128)(2,1)S(1)}, bf16[2,4,512]{2,1,0:T(4,128)(2,1)S(1)}, u32[]{:S(2)}, u32[]{:S(2)}) collective-permute-start(bf16[2,4,512]{2,1,0:T(4,128)(2,1)S(1)} %get-tuple-element.17), channel_id=1, source_target_pairs={{0,1},{1,2},{2,3},{3,4},{4,5},{5,6},{6,7},{7,8},{8,9},{9,10},{10,1... | collective-permute-start | bytes 24584 | tf_op jit(solution)/shard_map/ppermute | solution.py:330
  8.2 0.7 %copy-start.7 = (s32[64,1]{0,1:T(1,128)S(1)}, s32[64,1]{0,1:T(1,128)}, u32[]{:S(2)}) copy-start(s32[64,1]{0,1:T(1,128)} %param.20) | copy-start | bytes 772
  8.2 0.7 %copy-start.8 = (s32[64,1]{0,1:T(1,128)S(1)}, s32[64,1]{0,1:T(1,128)}, u32[]{:S(2)}) copy-start(s32[64,1]{0,1:T(1,128)} %param.21) | copy-start | bytes 772
  8.9 0.9 %copy-start.6 = (s32[64,512]{1,0:T(8,128)S(1)}, s32[64,512]{1,0:T(8,128)}, u32[]{:S(2)}) copy-start(s32[64,512]{1,0:T(8,128)} %cell_ref.1) | copy-start | bytes 393220
  9.8 30.7 %copy-start.3 = (f32[256,256]{1,0:T(8,128)S(1)}, f32[256,256]{1,0:T(8,128)}, u32[]{:S(2)}) copy-start(f32[256,256]{1,0:T(8,128)} %depth_ref.1) | copy-start | bytes 786436
  18.4 22.1 %copy-start = (f32[256,256]{1,0:T(8,128)S(1)}, f32[256,256]{1,0:T(8,128)}, u32[]{:S(2)}) copy-start(f32[256,256]{1,0:T(8,128)} %slope_ref.3) | copy-start | bytes 786436
  18.4 22.1 %copy-start.1 = (s32[256,256]{1,0:T(8,128)S(1)}, s32[256,256]{1,0:T(8,128)}, u32[]{:S(2)}) copy-start(s32[256,256]{1,0:T(8,128)} %dir_ref.3) | copy-start | bytes 786436
  18.4 22.1 %copy-start.2 = (f32[256,256]{1,0:T(8,128)S(1)}, f32[256,256]{1,0:T(8,128)}, u32[]{:S(2)}) copy-start(f32[256,256]{1,0:T(8,128)} %rain_ref.3) | copy-start | bytes 786436
  41.1 4.3 %collective-permute-start.2 = (bf16[32,256]{1,0:T(8,128)(2,1)S(1)}, bf16[32,256]{1,0:T(8,128)(2,1)S(1)}, u32[]{:S(2)}, u32[]{:S(2)}) collective-permute-start(bf16[32,256]{1,0:T(8,128)(2,1)S(1)} %get-tuple-element.13), channel_id=1, source_target_pairs={{1,0},{2,1},{3,2},{5,4},{6,5},{7,6},{9,8},{10,9},{11,10},{13,12},{... | collective-permute-start | bytes 49160 | tf_op jit(solution)/shard_map/ppermute | solution.py:378
  42.4 3.9 %collective-permute-start.3 = (bf16[32,256]{1,0:T(8,128)(2,1)S(1)}, bf16[32,256]{1,0:T(8,128)(2,1)S(1)}, u32[]{:S(2)}, u32[]{:S(2)}) collective-permute-start(bf16[32,256]{1,0:T(8,128)(2,1)S(1)} %get-tuple-element.14), channel_id=1, source_target_pairs={{0,1},{1,2},{2,3},{4,5},{5,6},{6,7},{8,9},{9,10},{10,11},{12,13},{... | collective-permute-start | bytes 49160 | tf_op jit(solution)/shard_map/ppermute | solution.py:377
  46.3 4.5 %collective-permute-start.4 = (bf16[32,512]{1,0:T(8,128)(2,1)S(1)}, bf16[32,512]{1,0:T(8,128)(2,1)S(1)}, u32[]{:S(2)}, u32[]{:S(2)}) collective-permute-start(bf16[32,512]{1,0:T(8,128)(2,1)S(1)} %pad_maximum_fusion), channel_id=1, source_target_pairs={{0,4},{4,8},{8,12},{12,16},{16,20},{20,24},{24,28},{1,5},{5,9},{9,... | collective-permute-start | bytes 98312 | tf_op jit(solution)/shard_map/ppermute | solution.py:381
  49.2 5.8 %collective-permute-start.5 = (bf16[32,512]{1,0:T(8,128)(2,1)S(1)}, bf16[32,512]{1,0:T(8,128)(2,1)S(1)}, u32[]{:S(2)}, u32[]{:S(2)}) collective-permute-start(bf16[32,512]{1,0:T(8,128)(2,1)S(1)} %pad_maximum_fusion.1), channel_id=1, source_target_pairs={{4,0},{8,4},{12,8},{16,12},{20,16},{24,20},{28,24},{5,1},{9,5},{13... | collective-permute-start | bytes 98312 | tf_op jit(solution)/shard_map/ppermute | solution.py:382
where the time goes:
time: 61.2 us; the launch traced here: 60.3 us
  blocking collectives  22.1 us (36%)
  Pallas kernels  14.4 us (24%)
  starting transfers between devices  12.8 us (21%)
  waiting for transfers between devices  5.31 us (9%)
  local copies, waits for them, and re-layouts  3.96 us (6%)
  other arithmetic  0.83 us (1%)
  between operations  0.82 us (1%)
    all_to_all x1, blocking collectives, per_device(): lax.all_to_all(send.reshape(devices, capacity * 4, send_lanes), both, spl...  22.1 us
    pallas_call x1, Pallas kernels, per_device(): pl.pallas_call(functools.partial(swath_kernel, devices, capacity), out_sh...  8.6 us
    pallas_call x1, Pallas kernels, per_device(): pl.pallas_call(flow_kernel, out_shape=jax.ShapeDtypeStruct((tile_rows, ti...  5.29 us
    ppermute x1, waiting for transfers between devices, per_device(): lax.ppermute(jnp.concatenate([top_rows, right[:, :LANES], left[:, :LANES]...  4.24 us
    ppermute x1, starting transfers between devices, per_device(): left = lax.ppermute(right_cols, 'ty', up)  3.03 us
    ppermute x1, starting transfers between devices, per_device(): top = lax.ppermute(sar_image[:, az_lines - HALO_LINES:], both, up)  3.03 us
    ppermute x1, starting transfers between devices, per_device(): lax.ppermute(jnp.concatenate([bot_rows, right[:, cut:], left[:, cut:]], 1...  2.89 us
    unnamed x18, local copies, waits for them, and re-layouts  1.57 us
  transfers between devices with their start and end apart: 6, of which 3 were waited for; matrix products, arithmetic and copies ran while one was open for 4% of the time, Pallas kernels for 0%

commit v1 on v0

--- a/solution.py
+++ b/solution.py
@@ -66,6 +66,7 @@
     frame = lines + 2 * HALO_LINES
     total = frame + 2
     me = lax.axis_index("tx") * lax.axis_size("ty") + lax.axis_index("ty")
+    n_ty = lax.axis_size("ty")
     first = me == 0
     last = me == devices - 1
 
@@ -183,7 +184,8 @@
     same = iota((lines, lines), 0) == iota((lines, lines), 1)
     tile_sub = jnp.sum(jnp.where(same, jnp.broadcast_to(tile, (lines, lines)), 0.0), 1, keepdims=True)
     rival = (tile_sub == tile) & (iota((lines, lines), 0) < iota((lines, lines), 1))
-    slot = tile * capacity + jnp.sum(jnp.where(rival, 1.0, 0.0), 0, keepdims=True)
+    by_column = (tile_ref[...] % n_ty) * (devices // n_ty) + tile_ref[...] // n_ty
+    slot = by_column.astype(f32) * capacity + jnp.sum(jnp.where(rival, 1.0, 0.0), 0, keepdims=True)
     wnd_rows = 8 * lines
     widen = (iota((lines, wnd_rows), 1) // 8 == iota((lines, wnd_rows), 0)).astype(bf16)
     slot_wide = dot(jnp.broadcast_to(slot, (8, lines)).astype(bf16), widen)[0:1]
@@ -359,9 +361,11 @@
         block_tile.reshape(1, az_lines), block_row.reshape(1, az_lines),
     )
 
+    n_tx, n_ty = lax.axis_size("tx"), lax.axis_size("ty")
     got = lax.all_to_all(
-        send.reshape(devices, capacity * 4, send_lanes), both, split_axis=0, concat_axis=0, tiled=True
-    ).reshape(slots, send_lanes)
+        send.reshape(n_ty, n_tx, capacity * 4, send_lanes), "ty", split_axis=0, concat_axis=0, tiled=True
+    )
+    got = lax.all_to_all(got, "tx", split_axis=1, concat_axis=1, tiled=True).reshape(slots, send_lanes)
 
     edge = jax.ShapeDtypeStruct((4 * SUBSTEPS, tile_cols), bf16)
     level, top_rows, bot_rows, left_cols, right_cols = pl.pallas_call(

time: 61.2 us -> 71.7 us (1.17)
  blocking collectives: 22.1 us -> 31.5 us
  local copies, waits for them, and re-layouts: 3.96 us -> 5.07 us
    all_to_all x1 -> x2, blocking collectives: 22.1 us -> 31.5 us  [the longest x1 18.5 us: per_device(): lax.all_to_all(got, 'tx', split_axis=1, concat_axis=1, tiled=True)]
    unnamed x18, local copies, waits for them, and re-layouts: 1.57 us -> 2.61 us
  transfers between devices with their start and end apart: 6 -> 6, of which waited for: 3 -> 3; matrix products, arithmetic and copies ran while one was open for 4% -> 3% of each run, Pallas kernels for 0% -> 0%
where the time goes in v1:
time: 71.7 us; the launch traced here: 70.9 us
  blocking collectives  31.5 us (44%)
  Pallas kernels  14.4 us (20%)
  starting transfers between devices  12.9 us (18%)
  waiting for transfers between devices  5.31 us (7%)
  local copies, waits for them, and re-layouts  5.07 us (7%)
  other arithmetic  0.83 us (1%)
  between operations  0.82 us (1%)
    all_to_all x1, blocking collectives, per_device(): lax.all_to_all(got, 'tx', split_axis=1, concat_axis=1, tiled=True)  18.5 us
    all_to_all x1, blocking collectives, per_device(): lax.all_to_all(send.reshape(n_ty, n_tx, capacity * 4, send_lanes), 'ty',...  13.1 us
    pallas_call x1, Pallas kernels, per_device(): pl.pallas_call(functools.partial(swath_kernel, devices, capacity), out_sh...  8.61 us
    pallas_call x1, Pallas kernels, per_device(): pl.pallas_call(flow_kernel, out_shape=jax.ShapeDtypeStruct((tile_rows, ti...  5.29 us
    ppermute x1, waiting for transfers between devices, per_device(): lax.ppermute(jnp.concatenate([top_rows, right[:, :LANES], left[:, :LANES]...  4.24 us
    ppermute x1, starting transfers between devices, per_device(): left = lax.ppermute(right_cols, 'ty', up)  3.03 us
    ppermute x1, starting transfers between devices, per_device(): top = lax.ppermute(sar_image[:, az_lines - HALO_LINES:], both, up)  3.03 us
    ppermute x1, starting transfers between devices, per_device(): lax.ppermute(jnp.concatenate([bot_rows, right[:, cut:], left[:, cut:]], 1...  3.01 us
  transfers between devices with their start and end apart: 6, of which 3 were waited for; matrix products, arithmetic and copies ran while one was open for 3% of the time, Pallas kernels for 0%

profile of v1, /device:TPU:0, one launch (start us, length us, event | category | flops | bytes accessed | tf_op | source)
XLA Modules:
  0.0 70.9 jit_solution(16982709775451506371)
XLA Ops:
  0.6 0.0 copy-start.4
  0.6 0.0 copy-start.5
  0.6 0.8 %fusion.5 = (bf16[2,4,512]{2,1,0:T(4,128)(2,1)S(1)}, bf16[2,4,512]{2,1,0:T(4,128)(2,1)S(1)}) fusion(bf16[2,64,512]{2,1,0:T(8,128)(2,1)} %sar_ref.1), kind=kLoop, calls=%fused_computation.9 | loop fusion | bytes 32768 | tf_op jit(solution)/shard_map/slice | solution.py:333
  1.4 1.3 %collective-permute-start.1 = (bf16[2,4,512]{2,1,0:T(4,128)(2,1)S(1)}, bf16[2,4,512]{2,1,0:T(4,128)(2,1)S(1)}, u32[]{:S(2)}, u32[]{:S(2)}) collective-permute-start(bf16[2,4,512]{2,1,0:T(4,128)(2,1)S(1)} %get-tuple-element.16), channel_id=1, source_target_pairs={{1,0},{2,1},{3,2},{4,3},{5,4},{6,5},{7,6},{8,7},{9,8},{10,9},{11,1... | collective-permute-start | bytes 24584 | tf_op jit(solution)/shard_map/ppermute | solution.py:333
  2.7 3.0 %collective-permute-start = (bf16[2,4,512]{2,1,0:T(4,128)(2,1)S(1)}, bf16[2,4,512]{2,1,0:T(4,128)(2,1)S(1)}, u32[]{:S(2)}, u32[]{:S(2)}) collective-permute-start(bf16[2,4,512]{2,1,0:T(4,128)(2,1)S(1)} %get-tuple-element.17), channel_id=1, source_target_pairs={{0,1},{1,2},{2,3},{3,4},{4,5},{5,6},{6,7},{7,8},{8,9},{9,10},{10,1... | collective-permute-start | bytes 24584 | tf_op jit(solution)/shard_map/ppermute | solution.py:332
  5.8 0.7 reshape.31
  6.5 0.7 copy.39
  7.2 0.1 reshape.28
  7.3 0.1 copy.40
  7.4 0.8 %fusion.2.wk_ref = bf16[352,16]{1,0:T(8,128)(2,1)S(1)} fusion(bf16[9,16]{1,0:T(8,128)(2,1)S(1)} %reshape.31, bf16[48,6]{1,0:T(8,128)(2,1)S(1)} %copy.40, bf16[144,16]{1,0:T(8,128)(2,1)} %bitcast.20, bf16[144,16]{1,0:T(8,128)(2,1)} %bitcast.21), kind=kLoop, calls=%fused_computation.4 | loop fusion | flops 67584 | bytes 21344 | tf_op jit(solution)/shard_map/concatenate | solution.py:313
  8.2 0.0 collective-permute-done.1.bot_ref
  8.2 0.0 collective-permute-done.top_ref
  8.2 0.0 copy-start.7
  8.2 0.0 copy-start.8
  8.2 0.0 copy-done.4
  8.2 0.0 copy-done.5
  8.2 0.6 copy-done.7
  8.9 0.0 copy-done.8
  8.9 0.0 copy-start.6
  8.9 0.9 %copy-done.6 = s32[64,512]{1,0:T(8,128)S(1)} copy-done((s32[64,512]{1,0:T(8,128)S(1)}, s32[64,512]{1,0:T(8,128)}, u32[]{:S(2)}) %copy-start.6) | copy-done | bytes 131096
  9.8 8.6 %swath.1 = (bf16[64,512]{1,0:T(8,128)(2,1)}, bf16[512,384]{1,0:T(8,128)(2,1)S(1)}) custom-call(bf16[2,64,512]{2,1,0:T(8,128)(2,1)S(1)} %copy-done.4, bf16[2,4,512]{2,1,0:T(4,128)(2,1)S(1)} %collective-permute-done.top_ref, bf16[2,4,512]{2,1,0:T(4,128)(2,1)S(1)} %collective-permute-done.1.bot_ref, bf16[352,16]{1,0:T(8,128)(2,1)S(1)} %fusion.2.wk_ref, ...), custom_call_target="tpu_custom_call" | custom-call | tf_op jit(solution)/shard_map/swath/pallas_call | solution.py:341
  18.4 13.1 %all_to_all.10 = bf16[4,8,16,384]{3,2,1,0:T(8,128)(2,1)S(1)} all-to-all(bf16[4,8,16,384]{3,2,1,0:T(8,128)(2,1)S(1)} %bitcast.17), channel_id=1, replica_groups=mesh['tx'=8,'ty'=4] {'ty'}, dimensions={0} | all-to-all | bytes 786432 | tf_op jit(solution)/shard_map/all_to_all | solution.py:365
  31.5 0.0 copy-start.3
  31.5 18.5 %all_to_all.11 = bf16[4,8,16,384]{3,2,0,1:T(8,128)(2,1)S(1)} all-to-all(bf16[4,8,16,384]{3,2,0,1:T(8,128)(2,1)S(1)} %copy.45), channel_id=1, replica_groups=mesh['tx'=8,'ty'=4] {'tx'}, dimensions={1} | all-to-all | bytes 786432 | tf_op jit(solution)/shard_map/all_to_all | solution.py:368
  50.0 0.0 copy-start
  50.0 0.0 copy-start.1
  50.0 0.0 copy-start.2
  50.0 0.0 copy-done.3
  50.0 0.9 %copy-done = f32[256,256]{1,0:T(8,128)S(1)} copy-done((f32[256,256]{1,0:T(8,128)S(1)}, f32[256,256]{1,0:T(8,128)}, u32[]{:S(2)}) %copy-start) | copy-done | bytes 262168
  50.9 0.1 copy-done.1
  51.0 0.1 copy-done.2
  51.1 0.5 level.1
  51.6 1.3 %collective-permute-start.2 = (bf16[32,256]{1,0:T(8,128)(2,1)S(1)}, bf16[32,256]{1,0:T(8,128)(2,1)S(1)}, u32[]{:S(2)}, u32[]{:S(2)}) collective-permute-start(bf16[32,256]{1,0:T(8,128)(2,1)S(1)} %get-tuple-element.13), channel_id=1, source_target_pairs={{1,0},{2,1},{3,2},{5,4},{6,5},{7,6},{9,8},{10,9},{11,10},{13,12},{... | collective-permute-start | bytes 49160 | tf_op jit(solution)/shard_map/ppermute | solution.py:382
  52.9 3.0 %collective-permute-start.3 = (bf16[32,256]{1,0:T(8,128)(2,1)S(1)}, bf16[32,256]{1,0:T(8,128)(2,1)S(1)}, u32[]{:S(2)}, u32[]{:S(2)}) collective-permute-start(bf16[32,256]{1,0:T(8,128)(2,1)S(1)} %get-tuple-element.14), channel_id=1, source_target_pairs={{0,1},{1,2},{2,3},{4,5},{5,6},{6,7},{8,9},{9,10},{10,11},{12,13},{... | collective-permute-start | bytes 49160 | tf_op jit(solution)/shard_map/ppermute | solution.py:381
  56.0 0.0 collective-permute-done.2.right_ref
  56.0 0.8 %collective-permute-done.3.left_ref = bf16[32,256]{1,0:T(8,128)(2,1)S(1)} collective-permute-done((bf16[32,256]{1,0:T(8,128)(2,1)S(1)}, bf16[32,256]{1,0:T(8,128)(2,1)S(1)}, u32[]{:S(2)}, u32[]{:S(2)}) %collective-permute-start.3) | collective-permute-done | bytes 16416 | tf_op jit(solution)/shard_map/ppermute | solution.py:381
  56.8 3.0 %collective-permute-start.4 = (bf16[32,512]{1,0:T(8,128)(2,1)S(1)}, bf16[32,512]{1,0:T(8,128)(2,1)S(1)}, u32[]{:S(2)}, u32[]{:S(2)}) collective-permute-start(bf16[32,512]{1,0:T(8,128)(2,1)S(1)} %pad_maximum_fusion), channel_id=1, source_target_pairs={{0,4},{4,8},{8,12},{12,16},{16,20},{20,24},{24,28},{1,5},{5,9},{9,... | collective-permute-start | bytes 98312 | tf_op jit(solution)/shard_map/ppermute | solution.py:385
  59.8 1.3 %collective-permute-start.5 = (bf16[32,512]{1,0:T(8,128)(2,1)S(1)}, bf16[32,512]{1,0:T(8,128)(2,1)S(1)}, u32[]{:S(2)}, u32[]{:S(2)}) collective-permute-start(bf16[32,512]{1,0:T(8,128)(2,1)S(1)} %pad_maximum_fusion.1), channel_id=1, source_target_pairs={{4,0},{8,4},{12,8},{16,12},{20,16},{24,20},{28,24},{5,1},{9,5},{13... | collective-permute-start | bytes 98312 | tf_op jit(solution)/shard_map/ppermute | solution.py:386
  61.1 0.3 collective-permute-done.4.above_ref
  61.4 4.2 %collective-permute-done.5.below_ref = bf16[32,512]{1,0:T(8,128)(2,1)S(1)} collective-permute-done((bf16[32,512]{1,0:T(8,128)(2,1)S(1)}, bf16[32,512]{1,0:T(8,128)(2,1)S(1)}, u32[]{:S(2)}, u32[]{:S(2)}) %collective-permute-start.5) | collective-permute-done | bytes 32800 | tf_op jit(solution)/shard_map/ppermute | solution.py:386
  65.6 5.3 %flow.1 = f32[256,256]{1,0:T(8,128)} custom-call(f32[256,256]{1,0:T(8,128)S(1)} %get-tuple-element.11.level_ref, f32[256,256]{1,0:T(8,128)S(1)} %copy-done, s32[256,256]{1,0:T(8,128)S(1)} %copy-done.1, f32[256,256]{1,0:T(8,128)S(1)} %copy-done.2, bf16[32,512]{1,0:T(8,128)(2,1)S(1)} %collective-permute-done.4.above_ref, ...), custom_call_target="tpu_custom_call" | custom-call | tf_op jit(solution)/shard_map/flow/pallas_call | solution.py:390
  (6 shorter events, 0.1 us)
Async XLA Ops:
  0.6 7.6 %copy-start.4 = (bf16[2,64,512]{2,1,0:T(8,128)(2,1)S(1)}, bf16[2,64,512]{2,1,0:T(8,128)(2,1)}, u32[]{:S(2)}) copy-start(bf16[2,64,512]{2,1,0:T(8,128)(2,1)} %sar_ref.1) | copy-start | bytes 393220
  0.6 7.6 %copy-start.5 = (f32[64,512]{1,0:T(8,128)S(1)}, f32[64,512]{1,0:T(8,128)}, u32[]{:S(2)}) copy-start(f32[64,512]{1,0:T(8,128)} %gw_ref.1) | copy-start | bytes 393220
  1.4 6.7 %collective-permute-start.1 = (bf16[2,4,512]{2,1,0:T(4,128)(2,1)S(1)}, bf16[2,4,512]{2,1,0:T(4,128)(2,1)S(1)}, u32[]{:S(2)}, u32[]{:S(2)}) collective-permute-start(bf16[2,4,512]{2,1,0:T(4,128)(2,1)S(1)} %get-tuple-element.16), channel_id=1, source_target_pairs={{1,0},{2,1},{3,2},{4,3},{5,4},{6,5},{7,6},{8,7},{9,8},{10,9},{11,1... | collective-permute-start | bytes 24584 | tf_op jit(solution)/shard_map/ppermute | solution.py:333
  2.7 5.5 %collective-permute-start = (bf16[2,4,512]{2,1,0:T(4,128)(2,1)S(1)}, bf16[2,4,512]{2,1,0:T(4,128)(2,1)S(1)}, u32[]{:S(2)}, u32[]{:S(2)}) collective-permute-start(bf16[2,4,512]{2,1,0:T(4,128)(2,1)S(1)} %get-tuple-element.17), channel_id=1, source_target_pairs={{0,1},{1,2},{2,3},{3,4},{4,5},{5,6},{6,7},{7,8},{8,9},{9,10},{10,1... | collective-permute-start | bytes 24584 | tf_op jit(solution)/shard_map/ppermute | solution.py:332
  8.2 0.7 copy-start.7
  8.2 0.7 copy-start.8
  8.9 0.9 %copy-start.6 = (s32[64,512]{1,0:T(8,128)S(1)}, s32[64,512]{1,0:T(8,128)}, u32[]{:S(2)}) copy-start(s32[64,512]{1,0:T(8,128)} %cell_ref.1) | copy-start | bytes 393220
  31.5 18.5 %copy-start.3 = (f32[256,256]{1,0:T(8,128)S(1)}, f32[256,256]{1,0:T(8,128)}, u32[]{:S(2)}) copy-start(f32[256,256]{1,0:T(8,128)} %depth_ref.1) | copy-start | bytes 786436
  50.0 1.0 %copy-start = (f32[256,256]{1,0:T(8,128)S(1)}, f32[256,256]{1,0:T(8,128)}, u32[]{:S(2)}) copy-start(f32[256,256]{1,0:T(8,128)} %slope_ref.3) | copy-start | bytes 786436
  50.0 1.0 %copy-start.1 = (s32[256,256]{1,0:T(8,128)S(1)}, s32[256,256]{1,0:T(8,128)}, u32[]{:S(2)}) copy-start(s32[256,256]{1,0:T(8,128)} %dir_ref.3) | copy-start | bytes 786436
  50.0 1.1 %copy-start.2 = (f32[256,256]{1,0:T(8,128)S(1)}, f32[256,256]{1,0:T(8,128)}, u32[]{:S(2)}) copy-start(f32[256,256]{1,0:T(8,128)} %rain_ref.3) | copy-start | bytes 786436
  51.6 4.3 %collective-permute-start.2 = (bf16[32,256]{1,0:T(8,128)(2,1)S(1)}, bf16[32,256]{1,0:T(8,128)(2,1)S(1)}, u32[]{:S(2)}, u32[]{:S(2)}) collective-permute-start(bf16[32,256]{1,0:T(8,128)(2,1)S(1)} %get-tuple-element.13), channel_id=1, source_target_pairs={{1,0},{2,1},{3,2},{5,4},{6,5},{7,6},{9,8},{10,9},{11,10},{13,12},{... | collective-permute-start | bytes 49160 | tf_op jit(solution)/shard_map/ppermute | solution.py:382
  52.9 3.9 %collective-permute-start.3 = (bf16[32,256]{1,0:T(8,128)(2,1)S(1)}, bf16[32,256]{1,0:T(8,128)(2,1)S(1)}, u32[]{:S(2)}, u32[]{:S(2)}) collective-permute-start(bf16[32,256]{1,0:T(8,128)(2,1)S(1)} %get-tuple-element.14), channel_id=1, source_target_pairs={{0,1},{1,2},{2,3},{4,5},{5,6},{6,7},{8,9},{9,10},{10,11},{12,13},{... | collective-permute-start | bytes 49160 | tf_op jit(solution)/shard_map/ppermute | solution.py:381
  56.8 4.6 %collective-permute-start.4 = (bf16[32,512]{1,0:T(8,128)(2,1)S(1)}, bf16[32,512]{1,0:T(8,128)(2,1)S(1)}, u32[]{:S(2)}, u32[]{:S(2)}) collective-permute-start(bf16[32,512]{1,0:T(8,128)(2,1)S(1)} %pad_maximum_fusion), channel_id=1, source_target_pairs={{0,4},{4,8},{8,12},{12,16},{16,20},{20,24},{24,28},{1,5},{5,9},{9,... | collective-permute-start | bytes 98312 | tf_op jit(solution)/shard_map/ppermute | solution.py:385
  59.8 5.8 %collective-permute-start.5 = (bf16[32,512]{1,0:T(8,128)(2,1)S(1)}, bf16[32,512]{1,0:T(8,128)(2,1)S(1)}, u32[]{:S(2)}, u32[]{:S(2)}) collective-permute-start(bf16[32,512]{1,0:T(8,128)(2,1)S(1)} %pad_maximum_fusion.1), channel_id=1, source_target_pairs={{4,0},{8,4},{12,8},{16,12},{20,16},{24,20},{28,24},{5,1},{9,5},{13... | collective-permute-start | bytes 98312 | tf_op jit(solution)/shard_map/ppermute | solution.py:386

commit v2 on v0

--- a/solution.py
+++ b/solution.py
@@ -30,6 +30,10 @@
     return lax.dot_general(a, b, (((1,), (0,)), ((), ())), preferred_element_type=f32)
 
 
+def dot_0(a, b):
+    return lax.dot_general(a, b, (((0,), (0,)), ((), ())), preferred_element_type=f32)
+
+
 def dot_t(a, b):
     return lax.dot_general(a, b, (((1,), (1,)), ((), ())), preferred_element_type=f32)
 
@@ -55,39 +59,83 @@
     return jnp.broadcast_to(x[None], (times,) + x.shape).reshape(times * x.shape[0], x.shape[1])
 
 
+def edge_kernel(sar_ref, depth_ref, slope_ref, rain_ref, dir_ref, up_ref, down_ref):
+    lines, px = sar_ref.shape[1:]
+    cols = depth_ref.shape[1]
+    h = SUBSTEPS
+    fields = (
+        depth_ref[...],
+        runoff_coef * jnp.sqrt(slope_ref[...]),
+        rain_ref[...],
+        dir_ref[...].astype(f32),
+    )
+    zeros = jnp.zeros((8, px), f32)
+    for ref, lo, strip in (
+        (up_ref, lines - HALO_LINES, lambda x: jnp.transpose(x[:, cols - LANES :], (1, 0))[LANES - h :]),
+        (down_ref, 0, lambda x: jnp.transpose(x[:, 0:LANES], (1, 0))[0:h]),
+    ):
+        image = [sar_ref[ch].astype(f32)[lo : lo + HALO_LINES] for ch in range(2)]
+        strips = [strip(x) for x in fields]
+        ref[...] = jnp.concatenate(
+            [jnp.concatenate(strips[0:2], 1), jnp.concatenate(strips[2:4], 1), *image, zeros], 0
+        ).astype(bf16)
+
+
+def strips_of(ref, keep):
+    both = jnp.where(keep, ref[0:16, :].astype(f32), 0.0)
+    cols = both.shape[1] // 2
+    return [both[0:8, 0:cols], both[0:8, cols:], both[8:16, 0:cols], both[8:16, cols:]]
+
+
 def swath_kernel(
     devices, capacity,
-    sar_ref, top_ref, bot_ref, wk_ref, gw_ref, cell_ref, tile_ref, row_ref,
+    sar_ref, above_ref, below_ref, k1_ref, k2_ref, k3_ref, k4_ref, gw_any, cell_any, tile_any, row_any,
     frac_ref, send_ref,
-    s_ref, xa_ref, xb_ref, x3_ref, obs_ref, wnd_ref,
+    s_ref, xa_ref, xb_ref, x3_ref, obs_ref, wnd_ref, t1_ref, t4_ref, gw_ref, cell_ref, tile_ref, row_ref, sems,
 ):
+    late = [
+        pltpu.make_async_copy(src, dst, sems.at[i])
+        for i, (src, dst) in enumerate(
+            ((gw_any, gw_ref), (cell_any, cell_ref), (tile_any, tile_ref), (row_any, row_ref))
+        )
+    ]
+    for copy in late:
+        copy.start()
     lines, px = gw_ref.shape
     blocks = (lines + 2 * HALO_LINES - 2) // OUT_LINES
     frame = lines + 2 * HALO_LINES
     total = frame + 2
-    me = lax.axis_index("tx") * lax.axis_size("ty") + lax.axis_index("ty")
+    n_ty = lax.axis_size("ty")
+    me = lax.axis_index("tx") * n_ty + lax.axis_index("ty")
     first = me == 0
     last = me == devices - 1
+    above = above_ref[16:32, :].astype(f32)
+    below = below_ref[16:32, :].astype(f32)
 
     for ch in range(2):
-        s_ref[ch, 0:HALO_LINES, :] = top_ref[ch].astype(f32)
+        s_ref[ch, 0:HALO_LINES, :] = above[ch * HALO_LINES : (ch + 1) * HALO_LINES]
         s_ref[ch, HALO_LINES : HALO_LINES + lines, :] = sar_ref[ch].astype(f32)
-        s_ref[ch, HALO_LINES + lines : frame, :] = bot_ref[ch].astype(f32)
+        s_ref[ch, HALO_LINES + lines : frame, :] = below[ch * HALO_LINES : (ch + 1) * HALO_LINES]
 
     rows = OUT_LINES * CH
     cols = IN_LINES * CH
     spread = (iota((CH, cols), 1) % CH == iota((CH, cols), 0)).astype(bf16)
 
     cols1 = 3 * 2 * IN_LINES
-    spread1 = (iota((CH, cols1), 1) // IN_LINES == iota((CH, cols1), 0)).astype(bf16)
-    wide1 = dot(wk_ref[0:48, :], spread1)
+    spread1 = (iota((8, cols1), 1) // IN_LINES == iota((8, cols1), 0)).astype(bf16)
+    t1_ref[...] = jnp.zeros(t1_ref.shape, f32)
+    t4_ref[...] = jnp.zeros(t4_ref.shape, f32)
+    for ky in range(3):
+        for kx in range(3):
+            t1_ref[ky * 8 + 2 * kx : ky * 8 + 2 * kx + 2, :] = k1_ref[ky, kx].astype(f32)
+        t4_ref[ky * 3 : ky * 3 + 3, :] = k4_ref[ky].astype(f32)
     w1 = band_weights(
-        [stack_rows(wide1[ky * CH : (ky + 1) * CH], OUT_LINES) for ky in range(3)],
+        [stack_rows(dot_0(t1_ref[ky * 8 : ky * 8 + 8, :].astype(bf16), spread1), OUT_LINES) for ky in range(3)],
         rows, cols1, CH, lambda k: k % IN_LINES,
     )
 
-    def mid_weights(base):
-        wide = dot(wk_ref[base : base + 144, :], spread)
+    def mid_weights(ref):
+        wide = dot(ref[...], spread)
         return [
             band_weights(
                 [stack_rows(wide[(ky * 3 + kx) * CH : (ky * 3 + kx + 1) * CH], OUT_LINES) for ky in range(3)],
@@ -128,8 +176,8 @@
     clear(xa_ref, frame - 1, total)
     outside(xa_ref)
 
-    for base, src, dst, line in ((48, xa_ref, xb_ref, 2), (192, xb_ref, x3_ref, 3)):
-        w = mid_weights(base)
+    for k_ref, src, dst, line in ((k2_ref, xa_ref, xb_ref, 2), (k3_ref, xb_ref, x3_ref, 3)):
+        w = mid_weights(k_ref)
         for b in range(blocks):
             at = pl.ds((line - 1 + b * OUT_LINES) * CH, cols)
             acc = dot(w[0], src[0, at, :]) + dot(w[1], src[1, at, :]) + dot(w[2], src[2, at, :])
@@ -140,7 +188,7 @@
 
     cols4 = (lines + 2) * CH
     spread4 = (iota((CH, cols4), 1) % CH == iota((CH, cols4), 0)).astype(bf16)
-    wide4 = dot(wk_ref[336:352, :], spread4)
+    wide4 = dot(t4_ref[...].astype(bf16), spread4)
     w4 = [
         band_weights(
             [jnp.broadcast_to(wide4[ky * 3 + kx : ky * 3 + kx + 1], (lines, cols4)) for ky in range(3)],
@@ -154,6 +202,8 @@
     logit = from_before + parts[lines : 2 * lines] + from_after
     frac = (1.0 / (1.0 + jnp.exp(-logit))).astype(bf16)
     frac_ref[...] = frac
+    for copy in late:
+        copy.wait()
     obs_ref[...] = frac.astype(f32) * gw_ref[...]
 
     kind = iota((8, px), 0)
@@ -198,41 +248,87 @@
     goods = jnp.concatenate(
         [jnp.where(half == 0, wnd, 0.0), jnp.where(half == 1, wnd, 0.0), jnp.where(half == 0, row_wide, 0.0)], 1
     ).astype(bf16)
-    send_ref[...] = dot(perm, goods).astype(bf16)
+    sorted_rows = dot(perm, goods)
+    per_tile = 4 * capacity
+    none = jnp.zeros((per_tile, LANES), f32)
+    cut = sorted_rows.shape[1] - LANES
+
+    def of_right(x):
+        return jnp.concatenate([x[per_tile:], none], 0)
+
+    def of_left(x):
+        return jnp.concatenate([none, x[: slots - per_tile]], 0)
+
+    spot = iota((slots, LANES), 1)
+    column = (iota((slots, LANES), 0) // per_tile) % n_ty
+    row_own = sorted_rows[:, cut:]
+    side = jnp.where((spot < SUBSTEPS) & (column < n_ty - 1), of_right(sorted_rows[:, 0:LANES]), 0.0)
+    side = jnp.where((spot >= LANES - SUBSTEPS) & (column > 0), of_left(sorted_rows[:, cut - LANES : cut]), side)
+    for turn, value in enumerate((row_own, of_right(row_own), of_left(row_own))):
+        side = jnp.where(spot == SUBSTEPS + turn, value, side)
+    send_ref[...] = jnp.concatenate([sorted_rows[:, 0:cut], side], 1).astype(bf16)
 
 
 def transposed(x):
     return jnp.transpose(x, (1, 0))
 
 
-def level_kernel(got_ref, depth_ref, slope_ref, dir_ref, rain_ref, level_ref, top_ref, bot_ref, left_ref, right_ref):
+def level_kernel(
+    got_ref, from_left_ref, from_right_ref, depth_ref, slope_ref, rain_ref, dir_ref,
+    level_ref, side_ref, top_ref, bot_ref,
+):
     tile_rows, tile_cols = depth_ref.shape
     k = got_ref.shape[0]
-    line = transposed(got_ref[:, tile_cols:].astype(f32))[0:1]
+    h = SUBSTEPS
+    extra = got_ref[:, tile_cols:].astype(f32)
+    lines = transposed(extra)
     lane = iota((1, k), 1)
-    target = line.astype(jnp.int32) + lane % 2 + tile_rows * ((lane // 2) % 2)
-    placer = jnp.where(iota((2 * tile_rows, k), 0) == target, 1.0, 0.0).astype(bf16)
-    summed = dot(placer, got_ref[:, 0:tile_cols])
-    observed = summed[0:tile_rows]
-    covered = summed[tile_rows:]
-    depth = depth_ref[...]
-    wet = depth / (depth + wet_depth)
-    innovation = (observed - covered * wet) / (covered + 1.0)
-    level = depth * jnp.exp(innovation)
+    offset = lane % 2 + tile_rows * ((lane // 2) % 2)
+
+    def placer(turn):
+        target = lines[h + turn : h + turn + 1].astype(jnp.int32) + offset
+        return jnp.where(iota((2 * tile_rows, k), 0) == target, 1.0, 0.0).astype(bf16)
+
+    spot = iota((k, LANES), 1)
+    rights = jnp.where(spot < h, extra, 0.0).astype(bf16)
+    lefts = jnp.where(spot >= LANES - h, extra, 0.0).astype(bf16)
+    summed = dot(placer(0), got_ref[:, 0:tile_cols])
+    summed_side = dot(placer(1), rights) + dot(placer(2), lefts)
+
+    ty = lax.axis_index("ty")
+    left = strips_of(from_left_ref, ty > 0)
+    right = strips_of(from_right_ref, ty < lax.axis_size("ty") - 1)
+    gap = jnp.zeros((LANES - 2 * h, tile_rows), f32)
+    depth_side, conv_side, rain_side, code_side = [
+        transposed(jnp.concatenate([r, gap, l], 0)) for r, l in zip(right, left)
+    ]
+
+    def analysed(sums, depth):
+        observed = sums[0:tile_rows]
+        covered = sums[tile_rows:]
+        wet = depth / (depth + wet_depth)
+        innovation = (observed - covered * wet) / (covered + 1.0)
+        return depth * jnp.exp(innovation)
+
+    level = analysed(summed, depth_ref[...])
     level_ref[...] = level
-    conveyance = runoff_coef * jnp.sqrt(slope_ref[...])
-    fields = (level, rain_ref[...], conveyance, dir_ref[...].astype(f32))
-    h = SUBSTEPS
-    top_ref[...] = jnp.concatenate([x[0:h] for x in fields], 0).astype(bf16)
-    bot_ref[...] = jnp.concatenate([x[tile_rows - h :] for x in fields], 0).astype(bf16)
-    left_ref[...] = jnp.concatenate([transposed(x[:, 0:LANES])[0:h] for x in fields], 0).astype(bf16)
-    right_ref[...] = jnp.concatenate(
-        [transposed(x[:, tile_cols - LANES :])[LANES - h :] for x in fields], 0
-    ).astype(bf16)
+    sides = (analysed(summed_side, depth_side), rain_side, conv_side, code_side)
+    owns = (level, rain_ref, slope_ref, dir_ref)
+
+    def end_rows(at):
+        own = [x[at, :] for x in owns]
+        own[2] = runoff_coef * jnp.sqrt(own[2])
+        own[3] = own[3].astype(f32)
+        return jnp.concatenate([jnp.concatenate([o, x[at]], 1) for o, x in zip(own, sides)], 0).astype(bf16)
+
+    for i, x in enumerate(sides):
+        side_ref[i] = x
+    top_ref[...] = end_rows(slice(0, h))
+    bot_ref[...] = end_rows(slice(tile_rows - h, tile_rows))
 
 
 def flow_kernel(
-    level_ref, slope_ref, dir_ref, rain_ref, above_ref, below_ref, left_ref, right_ref,
+    level_ref, side_ref, slope_ref, dir_ref, rain_ref, above_ref, below_ref,
     out_ref,
     rain_s, conv_s, m_ref, part_ref, up_ref, down_ref,
 ):
@@ -241,21 +337,10 @@
     wide_rows = tile_rows + 2 * h
     wide_cols = tile_cols + LANES
 
-    gap = jnp.zeros((LANES - 2 * h, 2 * tile_cols), f32)
-
     def widened(field, own):
         at = slice(field * h, (field + 1) * h)
-        rights = jnp.concatenate(
-            [right_ref[...], below_ref[:, tile_cols : tile_cols + LANES], above_ref[:, tile_cols : tile_cols + LANES]], 1
-        )
-        lefts = jnp.concatenate(
-            [left_ref[...], below_ref[:, tile_cols + LANES :], above_ref[:, tile_cols + LANES :]], 1
-        )
-        side = transposed(jnp.concatenate([rights.astype(f32)[at], gap, lefts.astype(f32)[at]], 0))
-        above = jnp.concatenate([above_ref[:, 0:tile_cols].astype(f32)[at], side[tile_rows + 2 * LANES - h :]], 1)
-        below = jnp.concatenate([below_ref[:, 0:tile_cols].astype(f32)[at], side[tile_rows : tile_rows + h]], 1)
-        mid = jnp.concatenate([own, side[0:tile_rows]], 1)
-        return jnp.concatenate([above, mid, below], 0)
+        mid = jnp.concatenate([own, side_ref[field]], 1)
+        return jnp.concatenate([above_ref[...].astype(f32)[at], mid, below_ref[...].astype(f32)[at]], 0)
 
     zeros = jnp.zeros((h, wide_cols), f32)
     for buf in range(2):
@@ -302,15 +387,6 @@
     return [pl.BlockSpec(memory_space=pltpu.VMEM)] * n
 
 
-def kernel_rows(kernel_first, kernel_second, kernel_third, kernel_last):
-    first = jnp.transpose(kernel_first, (2, 0, 3, 1)).reshape(3 * CH, 6)
-    first = jnp.pad(first, ((0, 0), (0, CH - 6)))
-    mids = [jnp.transpose(k, (2, 3, 0, 1)).reshape(9 * CH, CH) for k in (kernel_second, kernel_third)]
-    last = jnp.transpose(kernel_last[0], (1, 2, 0)).reshape(9, CH)
-    last = jnp.pad(last, ((0, CH - 9), (0, 0)))
-    return jnp.concatenate([first, *mids, last], 0)
-
-
 def per_device(
     sar_image, kernel_first, kernel_second, kernel_third, kernel_last,
     geo_weight, cell_index, block_tile, block_row, depth, slope, flow_dir, rain,
@@ -326,23 +402,34 @@
         up = [(i, i + 1) for i in range(size - 1)]
         return up, [(j, i) for i, j in up]
 
+    params = pltpu.CompilerParams(vmem_limit_bytes=VMEM_LIMIT)
     up, down = steps(both)
-    top = lax.ppermute(sar_image[:, az_lines - HALO_LINES :], both, up)
-    bot = lax.ppermute(sar_image[:, :HALO_LINES], both, down)
-    weights = kernel_rows(kernel_first, kernel_second, kernel_third, kernel_last)
-
-    params = pltpu.CompilerParams(vmem_limit_bytes=VMEM_LIMIT)
+    message = jax.ShapeDtypeStruct((32, range_px), bf16)
+    to_next, to_previous = pl.pallas_call(
+        edge_kernel,
+        out_shape=(message, message),
+        in_specs=vmem_specs(5),
+        out_specs=tuple(vmem_specs(2)),
+        compiler_params=params,
+        name="edges",
+    )(sar_image, depth, slope, rain, flow_dir)
+    from_previous = lax.ppermute(to_next, both, up)
+    from_next = lax.ppermute(to_previous, both, down)
+
     slots = devices * capacity * 4
     frame = az_lines + 2 * HALO_LINES
     feats = (frame + 2) * CH
     send_lanes = tile_cols + LANES
+    late = (
+        geo_weight, cell_index, block_tile.reshape(1, az_lines), block_row.reshape(1, az_lines),
+    )
     fraction, send = pl.pallas_call(
         functools.partial(swath_kernel, devices, capacity),
         out_shape=(
             jax.ShapeDtypeStruct((az_lines, range_px), bf16),
             jax.ShapeDtypeStruct((slots, send_lanes), bf16),
         ),
-        in_specs=vmem_specs(8),
+        in_specs=vmem_specs(7) + [pl.BlockSpec(memory_space=pl.ANY)] * 4,
         out_specs=tuple(vmem_specs(2)),
         scratch_shapes=[
             pltpu.VMEM((2, frame + 8, range_px), f32),
@@ -351,42 +438,51 @@
             pltpu.VMEM((feats, range_px), bf16),
             pltpu.VMEM((az_lines, range_px), f32),
             pltpu.VMEM((8 * az_lines, LANES), f32),
+            pltpu.VMEM((24, CH), f32),
+            pltpu.VMEM((16, CH), f32),
+            *[pltpu.VMEM(x.shape, x.dtype) for x in late],
+            pltpu.SemaphoreType.DMA((4,)),
         ],
         compiler_params=params,
         name="swath",
     )(
-        sar_image, top, bot, weights, geo_weight, cell_index,
-        block_tile.reshape(1, az_lines), block_row.reshape(1, az_lines),
+        sar_image, from_previous, from_next,
+        jnp.transpose(kernel_first, (2, 3, 1, 0)),
+        jnp.transpose(kernel_second, (2, 3, 0, 1)).reshape(9 * CH, CH),
+        jnp.transpose(kernel_third, (2, 3, 0, 1)).reshape(9 * CH, CH),
+        jnp.transpose(kernel_last[0], (1, 2, 0)),
+        *late,
     )
 
     got = lax.all_to_all(
         send.reshape(devices, capacity * 4, send_lanes), both, split_axis=0, concat_axis=0, tiled=True
     ).reshape(slots, send_lanes)
 
-    edge = jax.ShapeDtypeStruct((4 * SUBSTEPS, tile_cols), bf16)
-    level, top_rows, bot_rows, left_cols, right_cols = pl.pallas_call(
+    edge = jax.ShapeDtypeStruct((4 * SUBSTEPS, send_lanes), bf16)
+    level, side, top_rows, bot_rows = pl.pallas_call(
         level_kernel,
-        out_shape=(jax.ShapeDtypeStruct((tile_rows, tile_cols), f32), edge, edge, edge, edge),
-        in_specs=vmem_specs(5),
-        out_specs=tuple(vmem_specs(5)),
+        out_shape=(
+            jax.ShapeDtypeStruct((tile_rows, tile_cols), f32),
+            jax.ShapeDtypeStruct((4, tile_rows, LANES), f32),
+            edge,
+            edge,
+        ),
+        in_specs=vmem_specs(7),
+        out_specs=tuple(vmem_specs(4)),
         compiler_params=params,
         name="level",
-    )(got, depth, slope, flow_dir, rain)
-
-    up, down = steps("ty")
-    left = lax.ppermute(right_cols, "ty", up)
-    right = lax.ppermute(left_cols, "ty", down)
+    )(got, from_previous, from_next, depth, slope, rain, flow_dir)
+
     up, down = steps("tx")
-    cut = tile_cols - LANES
-    above = lax.ppermute(jnp.concatenate([bot_rows, right[:, cut:], left[:, cut:]], 1), "tx", up)
-    below = lax.ppermute(jnp.concatenate([top_rows, right[:, :LANES], left[:, :LANES]], 1), "tx", down)
+    above = lax.ppermute(bot_rows, "tx", up)
+    below = lax.ppermute(top_rows, "tx", down)
 
     wide_rows = tile_rows + 2 * SUBSTEPS
     wide_cols = tile_cols + LANES
     level = pl.pallas_call(
         flow_kernel,
         out_shape=jax.ShapeDtypeStruct((tile_rows, tile_cols), f32),
-        in_specs=vmem_specs(8),
+        in_specs=vmem_specs(7),
         out_specs=vmem_specs(1)[0],
         scratch_shapes=[
             pltpu.VMEM((wide_rows, wide_cols), f32),
@@ -398,7 +494,7 @@
         ],
         compiler_params=params,
         name="flow",
-    )(level, slope, flow_dir, rain, above, below, left, right)
+    )(level, side, slope, flow_dir, rain, above, below)
     return (fraction, level)
 
 

time: 61.2 us -> 59.6 us (0.974)
  starting transfers between devices: 12.8 us -> 7.85 us
  waiting for transfers between devices: 5.31 us -> 8.35 us
  local copies, waits for them, and re-layouts: 3.96 us -> 5.39 us
  other arithmetic: 0.83 us -> 0 us
    ppermute x6 -> x4, starting transfers between devices: 12.8 us -> 7.85 us  [the longest x1 2.9 us: per_device(): above = lax.ppermute(bot_rows, 'tx', up)]
    unnamed x18 -> x34, local copies, waits for them, and re-layouts: 1.57 us -> 5.39 us
    ppermute x6 -> x4, waiting for transfers between devices: 5.31 us -> 8.35 us  [the longest x1 4.22 us: per_device(): below = lax.ppermute(top_rows, 'tx', down)]
    reshape x3 -> x0, local copies, waits for them, and re-layouts: 0.9 us -> none  [the longest x1 0.7 us: kernel_rows(): last = jnp.transpose(kernel_last[0], (1, 2, 0)).reshape(9, CH)]
    concatenate x3 -> x0, other arithmetic: 0.83 us -> none  [the longest x1 0.81 us: kernel_rows(): return jnp.concatenate([first, *mids, last], 0)]
    slice x3 -> x0, local copies, waits for them, and re-layouts: 0.79 us -> none  [the longest x1 0.79 us: per_device(): bot = lax.ppermute(sar_image[:, :HALO_LINES], both, down)]
    transpose x1 -> x0, local copies, waits for them, and re-layouts: 0.69 us -> none  [kernel_rows(): first = jnp.transpose(kernel_first, (2, 0, 3, 1)).reshape(3 * CH, 6)]
  transfers between devices with their start and end apart: 6 -> 4, of which waited for: 3 -> 3; matrix products, arithmetic and copies ran while one was open for 4% -> 0% of each run, Pallas kernels for 0% -> 0%
where the time goes in v2:
time: 59.6 us; the launch traced here: 59.2 us
  blocking collectives  21.8 us (37%)
  Pallas kernels  15 us (25%)
  waiting for transfers between devices  8.35 us (14%)
  starting transfers between devices  7.85 us (13%)
  local copies, waits for them, and re-layouts  5.39 us (9%)
  between operations  0.78 us (1%)
    all_to_all x1, blocking collectives, per_device(): lax.all_to_all(send.reshape(devices, capacity * 4, send_lanes), both, spl...  21.8 us
    pallas_call x1, Pallas kernels, per_device(): pl.pallas_call(functools.partial(swath_kernel, devices, capacity), out_sh...  8.87 us
    unnamed x34, local copies, waits for them, and re-layouts  5.39 us
    pallas_call x1, Pallas kernels, per_device(): pl.pallas_call(flow_kernel, out_shape=jax.ShapeDtypeStruct((tile_rows, ti...  5.29 us
    ppermute x1, waiting for transfers between devices, per_device(): below = lax.ppermute(top_rows, 'tx', down)  4.22 us
    ppermute x1, waiting for transfers between devices, per_device(): from_next = lax.ppermute(to_previous, both, down)  3.93 us
    ppermute x1, starting transfers between devices, per_device(): above = lax.ppermute(bot_rows, 'tx', up)  2.9 us
    ppermute x1, starting transfers between devices, per_device(): from_previous = lax.ppermute(to_next, both, up)  2.36 us
  transfers between devices with their start and end apart: 4, of which 3 were waited for; matrix products, arithmetic and copies ran while one was open for 0% of the time, Pallas kernels for 0%

profile of v2, /device:TPU:0, one launch (start us, length us, event | category | flops | bytes accessed | tf_op | source)
XLA Modules:
  0.0 59.2 jit_solution(1781837825182765125)
XLA Ops:
  0.6 0.0 copy-start
  0.6 0.9 %copy-done = f32[256,256]{1,0:T(8,128)S(1)} copy-done((f32[256,256]{1,0:T(8,128)S(1)}, f32[256,256]{1,0:T(8,128)}, u32[]{:S(2)}) %copy-start) | copy-done | bytes 262168
  1.6 0.0 copy-start.2
  1.6 0.9 %copy-done.2 = f32[256,256]{1,0:T(8,128)S(1)} copy-done((f32[256,256]{1,0:T(8,128)S(1)}, f32[256,256]{1,0:T(8,128)}, u32[]{:S(2)}) %copy-start.2) | copy-done | bytes 262168
  2.5 0.0 copy-start.4
  2.5 0.9 %copy-done.4 = s32[256,256]{1,0:T(8,128)S(1)} copy-done((s32[256,256]{1,0:T(8,128)S(1)}, s32[256,256]{1,0:T(8,128)}, u32[]{:S(2)}) %copy-start.4) | copy-done | bytes 262168
  3.5 0.0 copy-start.6
  3.5 0.9 %copy-done.6 = f32[256,256]{1,0:T(8,128)S(1)} copy-done((f32[256,256]{1,0:T(8,128)S(1)}, f32[256,256]{1,0:T(8,128)}, u32[]{:S(2)}) %copy-start.6) | copy-done | bytes 262168
  4.4 0.0 copy-start.8
  4.4 0.9 %copy-done.8 = bf16[2,64,512]{2,1,0:T(8,128)(2,1)S(1)} copy-done((bf16[2,64,512]{2,1,0:T(8,128)(2,1)S(1)}, bf16[2,64,512]{2,1,0:T(8,128)(2,1)}, u32[]{:S(2)}) %copy-start.8) | copy-done | bytes 131096
  5.3 0.0 copy-start.9
  5.3 0.0 copy-start.10
  5.3 0.0 copy-start.11
  5.3 0.0 copy-start.12
  5.4 0.2 edges.1
  5.5 2.4 %collective-permute-start = (bf16[32,512]{1,0:T(8,128)(2,1)S(1)}, bf16[32,512]{1,0:T(8,128)(2,1)S(1)}, u32[]{:S(2)}, u32[]{:S(2)}) collective-permute-start(bf16[32,512]{1,0:T(8,128)(2,1)S(1)} %get-tuple-element.10), channel_id=1, source_target_pairs={{0,1},{1,2},{2,3},{3,4},{4,5},{5,6},{6,7},{7,8},{8,9},{9,10},{10,1... | collective-permute-start | bytes 98312 | tf_op jit(solution)/shard_map/ppermute | solution.py:416
  7.9 1.3 %collective-permute-start.1 = (bf16[32,512]{1,0:T(8,128)(2,1)S(1)}, bf16[32,512]{1,0:T(8,128)(2,1)S(1)}, u32[]{:S(2)}, u32[]{:S(2)}) collective-permute-start(bf16[32,512]{1,0:T(8,128)(2,1)S(1)} %get-tuple-element.11), channel_id=1, source_target_pairs={{1,0},{2,1},{3,2},{4,3},{5,4},{6,5},{7,6},{8,7},{9,8},{10,9},{11,1... | collective-permute-start | bytes 98312 | tf_op jit(solution)/shard_map/ppermute | solution.py:417
  9.2 0.0 collective-permute-done.above_ref.from_left_ref
  9.2 3.9 %collective-permute-done.1.below_ref.from_right_ref = bf16[32,512]{1,0:T(8,128)(2,1)S(1)} collective-permute-done((bf16[32,512]{1,0:T(8,128)(2,1)S(1)}, bf16[32,512]{1,0:T(8,128)(2,1)S(1)}, u32[]{:S(2)}, u32[]{:S(2)}) %collective-permute-start.1) | collective-permute-done | bytes 32800 | tf_op jit(solution)/shard_map/ppermute | solution.py:417
  13.1 0.0 copy-start.13
  13.1 0.0 copy-start.14
  13.1 0.0 copy-start.15
  13.1 0.0 copy-start.16
  13.1 0.0 copy-done.9
  13.2 0.0 copy-done.10
  13.2 0.0 copy-done.11
  13.2 0.0 copy-done.12
  13.2 0.6 %copy-done.13 = bf16[16,2,3,3]{0,1,3,2:T(2,128)(2,1)S(1)} copy-done((bf16[16,2,3,3]{0,1,3,2:T(2,128)(2,1)S(1)}, bf16[16,2,3,3]{0,1,3,2:T(2,128)(2,1)}, u32[]{:S(2)}) %copy-start.13) | copy-done | bytes 600
  13.8 0.0 copy-done.14
  13.8 0.0 copy-done.15
  13.8 0.0 copy-done.16
  13.8 0.0 copy-start.7
  13.8 8.9 %swath.1 = (bf16[64,512]{1,0:T(8,128)(2,1)}, bf16[512,384]{1,0:T(8,128)(2,1)S(1)}) custom-call(bf16[2,64,512]{2,1,0:T(8,128)(2,1)S(1)} %copy-done.8, bf16[32,512]{1,0:T(8,128)(2,1)S(1)} %collective-permute-done.above_ref.from_left_ref, bf16[32,512]{1,0:T(8,128)(2,1)S(1)} %collective-permute-done.1.below_ref.from_right_ref, ...), custom_call_target="tpu_custom_call" | custom-call | tf_op jit(solution)/shard_map/swath/pallas_call | solution.py:426
  22.7 0.0 copy-start.1
  22.7 0.0 copy-start.3
  22.7 0.0 copy-start.5
  22.8 21.8 %all_to_all.5 = bf16[32,16,384]{2,1,0:T(8,128)(2,1)S(1)} all-to-all(bf16[32,16,384]{2,1,0:T(8,128)(2,1)S(1)} %bitcast.15), channel_id=1, replica_groups=mesh['tx'=8,'ty'=4] {'tx','ty'}, dimensions={0} | all-to-all | bytes 786432 | tf_op jit(solution)/shard_map/all_to_all | solution.py:457
  44.6 0.0 copy-done.7
  44.6 0.0 copy-done.1
  44.6 0.0 copy-done.3
  44.6 0.0 copy-done.5
  44.6 0.7 %level.1 = (f32[256,256]{1,0:T(8,128)S(1)}, f32[4,256,128]{2,1,0:T(8,128)S(1)}, bf16[32,384]{1,0:T(8,128)(2,1)S(1)}, bf16[32,384]{1,0:T(8,128)(2,1)S(1)}) custom-call(bf16[512,384]{1,0:T(8,128)(2,1)S(1)} %bitcast.14, bf16[32,512]{1,0:T(8,128)(2,1)S(1)} %collective-permute-done.above_ref.from_left_ref, ...), custom_call_target="tpu_custom_call" | custom-call | tf_op jit(solution)/shard_map/level/pallas_call | solution.py:462
  45.3 2.9 %collective-permute-start.2 = (bf16[32,384]{1,0:T(8,128)(2,1)S(1)}, bf16[32,384]{1,0:T(8,128)(2,1)S(1)}, u32[]{:S(2)}, u32[]{:S(2)}) collective-permute-start(bf16[32,384]{1,0:T(8,128)(2,1)S(1)} %get-tuple-element.16), channel_id=1, source_target_pairs={{0,4},{4,8},{8,12},{12,16},{16,20},{20,24},{24,28},{1,5},{5,9},{9,... | collective-permute-start | bytes 73736 | tf_op jit(solution)/shard_map/ppermute | solution.py:477
  48.2 1.3 %collective-permute-start.3 = (bf16[32,384]{1,0:T(8,128)(2,1)S(1)}, bf16[32,384]{1,0:T(8,128)(2,1)S(1)}, u32[]{:S(2)}, u32[]{:S(2)}) collective-permute-start(bf16[32,384]{1,0:T(8,128)(2,1)S(1)} %get-tuple-element.17), channel_id=1, source_target_pairs={{4,0},{8,4},{12,8},{16,12},{20,16},{24,20},{28,24},{5,1},{9,5},{13... | collective-permute-start | bytes 73736 | tf_op jit(solution)/shard_map/ppermute | solution.py:478
  49.5 0.2 collective-permute-done.2.above_ref
  49.7 4.2 %collective-permute-done.3.below_ref = bf16[32,384]{1,0:T(8,128)(2,1)S(1)} collective-permute-done((bf16[32,384]{1,0:T(8,128)(2,1)S(1)}, bf16[32,384]{1,0:T(8,128)(2,1)S(1)}, u32[]{:S(2)}, u32[]{:S(2)}) %collective-permute-start.3) | collective-permute-done | bytes 24608 | tf_op jit(solution)/shard_map/ppermute | solution.py:478
  53.9 5.3 %flow.1 = f32[256,256]{1,0:T(8,128)} custom-call(f32[256,256]{1,0:T(8,128)S(1)} %get-tuple-element.14.level_ref, f32[4,256,128]{2,1,0:T(8,128)S(1)} %get-tuple-element.15.side_ref, f32[256,256]{1,0:T(8,128)S(1)} %copy-done.1, s32[256,256]{1,0:T(8,128)S(1)} %copy-done.5, f32[256,256]{1,0:T(8,128)S(1)} %copy-done.3, ...), custom_call_target="tpu_custom_call" | custom-call | tf_op jit(solution)/shard_map/flow/pallas_call | solution.py:482
Async XLA Ops:
  0.6 1.0 %copy-start = (f32[256,256]{1,0:T(8,128)S(1)}, f32[256,256]{1,0:T(8,128)}, u32[]{:S(2)}) copy-start(f32[256,256]{1,0:T(8,128)} %slope_ref.5) | copy-start | bytes 786436
  1.6 0.9 %copy-start.2 = (f32[256,256]{1,0:T(8,128)S(1)}, f32[256,256]{1,0:T(8,128)}, u32[]{:S(2)}) copy-start(f32[256,256]{1,0:T(8,128)} %rain_ref.5) | copy-start | bytes 786436
  2.5 0.9 %copy-start.4 = (s32[256,256]{1,0:T(8,128)S(1)}, s32[256,256]{1,0:T(8,128)}, u32[]{:S(2)}) copy-start(s32[256,256]{1,0:T(8,128)} %dir_ref.5) | copy-start | bytes 786436
  3.5 0.9 %copy-start.6 = (f32[256,256]{1,0:T(8,128)S(1)}, f32[256,256]{1,0:T(8,128)}, u32[]{:S(2)}) copy-start(f32[256,256]{1,0:T(8,128)} %depth_ref.3) | copy-start | bytes 786436
  4.4 0.9 %copy-start.8 = (bf16[2,64,512]{2,1,0:T(8,128)(2,1)S(1)}, bf16[2,64,512]{2,1,0:T(8,128)(2,1)}, u32[]{:S(2)}) copy-start(bf16[2,64,512]{2,1,0:T(8,128)(2,1)} %sar_ref.3) | copy-start | bytes 393220
  5.3 7.8 %copy-start.9 = (f32[64,512]{1,0:T(8,128)S(1)}, f32[64,512]{1,0:T(8,128)}, u32[]{:S(2)}) copy-start(f32[64,512]{1,0:T(8,128)} %gw_any.1) | copy-start | bytes 393220
  5.3 7.8 %copy-start.10 = (s32[64,512]{1,0:T(8,128)S(1)}, s32[64,512]{1,0:T(8,128)}, u32[]{:S(2)}) copy-start(s32[64,512]{1,0:T(8,128)} %cell_any.1) | copy-start | bytes 393220
  5.3 7.8 %copy-start.11 = (bf16[16,16,3,3]{1,0,3,2:T(8,128)(2,1)S(1)}, bf16[16,16,3,3]{1,0,3,2:T(8,128)(2,1)}, u32[]{:S(2)}) copy-start(bf16[16,16,3,3]{1,0,3,2:T(8,128)(2,1)} %param.15) | copy-start | bytes 13828
  5.3 7.8 %copy-start.12 = (bf16[16,16,3,3]{1,0,3,2:T(8,128)(2,1)S(1)}, bf16[16,16,3,3]{1,0,3,2:T(8,128)(2,1)}, u32[]{:S(2)}) copy-start(bf16[16,16,3,3]{1,0,3,2:T(8,128)(2,1)} %param.16) | copy-start | bytes 13828
  5.5 3.7 %collective-permute-start = (bf16[32,512]{1,0:T(8,128)(2,1)S(1)}, bf16[32,512]{1,0:T(8,128)(2,1)S(1)}, u32[]{:S(2)}, u32[]{:S(2)}) collective-permute-start(bf16[32,512]{1,0:T(8,128)(2,1)S(1)} %get-tuple-element.10), channel_id=1, source_target_pairs={{0,1},{1,2},{2,3},{3,4},{4,5},{5,6},{6,7},{7,8},{8,9},{9,10},{10,1... | collective-permute-start | bytes 98312 | tf_op jit(solution)/shard_map/ppermute | solution.py:416
  7.9 5.2 %collective-permute-start.1 = (bf16[32,512]{1,0:T(8,128)(2,1)S(1)}, bf16[32,512]{1,0:T(8,128)(2,1)S(1)}, u32[]{:S(2)}, u32[]{:S(2)}) collective-permute-start(bf16[32,512]{1,0:T(8,128)(2,1)S(1)} %get-tuple-element.11), channel_id=1, source_target_pairs={{1,0},{2,1},{3,2},{4,3},{5,4},{6,5},{7,6},{8,7},{9,8},{10,9},{11,1... | collective-permute-start | bytes 98312 | tf_op jit(solution)/shard_map/ppermute | solution.py:417
  13.1 0.7 %copy-start.13 = (bf16[16,2,3,3]{0,1,3,2:T(2,128)(2,1)S(1)}, bf16[16,2,3,3]{0,1,3,2:T(2,128)(2,1)}, u32[]{:S(2)}) copy-start(bf16[16,2,3,3]{0,1,3,2:T(2,128)(2,1)} %param.14) | copy-start | bytes 1732
  13.1 0.7 %copy-start.14 = (bf16[1,16,3,3]{1,3,2,0:T(4,128)(2,1)S(1)}, bf16[1,16,3,3]{1,3,2,0:T(4,128)(2,1)}, u32[]{:S(2)}) copy-start(bf16[1,16,3,3]{1,3,2,0:T(4,128)(2,1)} %param.17) | copy-start | bytes 868
  13.1 0.7 %copy-start.15 = (s32[64,1]{0,1:T(1,128)S(1)}, s32[64,1]{0,1:T(1,128)}, u32[]{:S(2)}) copy-start(s32[64,1]{0,1:T(1,128)} %param.20) | copy-start | bytes 772
  13.1 0.7 %copy-start.16 = (s32[64,1]{0,1:T(1,128)S(1)}, s32[64,1]{0,1:T(1,128)}, u32[]{:S(2)}) copy-start(s32[64,1]{0,1:T(1,128)} %param.21) | copy-start | bytes 772
  13.8 30.7 %copy-start.7 = (f32[256,256]{1,0:T(8,128)S(1)}, f32[256,256]{1,0:T(8,128)}, u32[]{:S(2)}) copy-start(f32[256,256]{1,0:T(8,128)} %depth_ref.3) | copy-start | bytes 786436
  22.7 21.9 %copy-start.1 = (f32[256,256]{1,0:T(8,128)S(1)}, f32[256,256]{1,0:T(8,128)}, u32[]{:S(2)}) copy-start(f32[256,256]{1,0:T(8,128)} %slope_ref.5) | copy-start | bytes 786436
  22.7 21.8 %copy-start.3 = (f32[256,256]{1,0:T(8,128)S(1)}, f32[256,256]{1,0:T(8,128)}, u32[]{:S(2)}) copy-start(f32[256,256]{1,0:T(8,128)} %rain_ref.5) | copy-start | bytes 786436
  22.7 21.8 %copy-start.5 = (s32[256,256]{1,0:T(8,128)S(1)}, s32[256,256]{1,0:T(8,128)}, u32[]{:S(2)}) copy-start(s32[256,256]{1,0:T(8,128)} %dir_ref.5) | copy-start | bytes 786436
  45.3 4.4 %collective-permute-start.2 = (bf16[32,384]{1,0:T(8,128)(2,1)S(1)}, bf16[32,384]{1,0:T(8,128)(2,1)S(1)}, u32[]{:S(2)}, u32[]{:S(2)}) collective-permute-start(bf16[32,384]{1,0:T(8,128)(2,1)S(1)} %get-tuple-element.16), channel_id=1, source_target_pairs={{0,4},{4,8},{8,12},{12,16},{16,20},{20,24},{24,28},{1,5},{5,9},{9,... | collective-permute-start | bytes 73736 | tf_op jit(solution)/shard_map/ppermute | solution.py:477
  48.2 5.7 %collective-permute-start.3 = (bf16[32,384]{1,0:T(8,128)(2,1)S(1)}, bf16[32,384]{1,0:T(8,128)(2,1)S(1)}, u32[]{:S(2)}, u32[]{:S(2)}) collective-permute-start(bf16[32,384]{1,0:T(8,128)(2,1)S(1)} %get-tuple-element.17), channel_id=1, source_target_pairs={{4,0},{8,4},{12,8},{16,12},{20,16},{24,20},{28,24},{5,1},{9,5},{13... | collective-permute-start | bytes 73736 | tf_op jit(solution)/shard_map/ppermute | solution.py:478

commit v3 on v2

v3 whole, which is shorter than its diff:
```python
import functools

import jax
import jax.numpy as jnp
from jax import lax
from jax.experimental import pallas as pl
from jax.experimental.pallas import tpu as pltpu
from jax.sharding import PartitionSpec as P

WIN_ROWS = 2
SUBSTEPS = 8
CH = 16
OUT_LINES = 14
IN_LINES = OUT_LINES + 2
HALO_LINES = 4
LANES = 128
VMEM_LIMIT = 48 * 1024 * 1024

wet_depth = 0.5
runoff_coef = 0.25
bf16 = jnp.bfloat16
f32 = jnp.float32


def iota(shape, dim):
    return lax.broadcasted_iota(jnp.int32, shape, dim)


def dot(a, b):
    return lax.dot_general(a, b, (((1,), (0,)), ((), ())), preferred_element_type=f32)


def dot_0(a, b):
    return lax.dot_general(a, b, (((0,), (0,)), ((), ())), preferred_element_type=f32)


def dot_t(a, b):
    return lax.dot_general(a, b, (((1,), (1,)), ((), ())), preferred_element_type=f32)


def pixel_shifts(x):
    width = x.shape[1]
    pix = iota(x.shape, 1)
    before = jnp.where(pix == 0, 0.0, pltpu.roll(x, 1, 1))
    after = jnp.where(pix == width - 1, 0.0, pltpu.roll(x, width - 1, 1))
    return before, after


def band_weights(tiled, rows, cols, per_row, line_of):
    out_line = iota((rows, cols), 0) // per_row
    off = line_of(iota((rows, cols), 1)) - out_line
    out = jnp.zeros((rows, cols), f32)
    for ky in range(3):
        out = jnp.where(off == ky, tiled[ky], out)
    return out.astype(bf16)


def edge_kernel(
    sar_hbm, depth_hbm, slope_hbm, rain_hbm, dir_hbm, up_ref, down_ref,
    last_ref, first_ref, depth_ref, slope_ref, rain_ref, dir_ref, sems,
):
    lines, px = sar_hbm.shape[1:]
    cols = depth_hbm.shape[1]
    h = SUBSTEPS
    copies = [
        pltpu.make_async_copy(src, dst, sems.at[i])
        for i, (src, dst) in enumerate(
            (
                (depth_hbm, depth_ref), (slope_hbm, slope_ref), (rain_hbm, rain_ref), (dir_hbm, dir_ref),
                (sar_hbm.at[:, lines - 16 : lines, :], last_ref), (sar_hbm.at[:, 0:16, :], first_ref),
            )
        )
    ]
    for copy in copies:
        copy.start()
    for copy in copies:
        copy.wait()
    fields = (
        depth_ref[...],
        runoff_coef * jnp.sqrt(slope_ref[...]),
        rain_ref[...],
        dir_ref[...].astype(f32),
    )
    zeros = jnp.zeros((8, px), f32)
    for ref, image_ref, lo, strip in (
        (up_ref, last_ref, 16 - HALO_LINES, lambda x: jnp.transpose(x[:, cols - LANES :], (1, 0))[LANES - h :]),
        (down_ref, first_ref, 0, lambda x: jnp.transpose(x[:, 0:LANES], (1, 0))[0:h]),
    ):
        image = [image_ref[ch].astype(f32)[lo : lo + HALO_LINES] for ch in range(2)]
        strips = [strip(x) for x in fields]
        ref[...] = jnp.concatenate(
            [jnp.concatenate(strips[0:2], 1), jnp.concatenate(strips[2:4], 1), *image, zeros], 0
        ).astype(bf16)


def strips_of(ref, keep):
    both = jnp.where(keep, ref[0:16, :].astype(f32), 0.0)
    cols = both.shape[1] // 2
    return [both[0:8, 0:cols], both[0:8, cols:], both[8:16, 0:cols], both[8:16, cols:]]


def swath_kernel(
    devices, capacity,
    above_ref, below_ref,
    sar_hbm, k1_hbm, k2_hbm, k3_hbm, k4_hbm, gw_hbm, cell_hbm, tile_hbm, row_hbm,
    frac_ref, send_ref,
    sar_ref, k1_ref, k2_ref, k3_ref, k4_ref, gw_ref, cell_ref, tile_ref, row_ref, sems,
    s_ref, xa_ref, xb_ref, x3_ref, w2_ref, w3_ref, w1_ref, t1_ref, t4_ref, logit_ref, obs_ref, wnd_ref,
):
    pairs = (
        (k1_hbm, k1_ref), (k2_hbm, k2_ref), (k3_hbm, k3_ref), (k4_hbm, k4_ref), (sar_hbm, sar_ref),
        (gw_hbm, gw_ref), (cell_hbm, cell_ref), (tile_hbm, tile_ref), (row_hbm, row_ref),
    )
    copies = [pltpu.make_async_copy(src, dst, sems.at[i]) for i, (src, dst) in enumerate(pairs)]
    for copy in copies:
        copy.start()
    lines, px = gw_ref.shape
    blocks = (lines + 2 * HALO_LINES - 2) // OUT_LINES
    frame = lines + 2 * HALO_LINES
    total = xa_ref.shape[0] // CH
    n_ty = lax.axis_size("ty")
    me = lax.axis_index("tx") * n_ty + lax.axis_index("ty")
    first = me == 0
    last = me == devices - 1
    rows = OUT_LINES * CH
    cols = IN_LINES * CH

    out_of = iota((CH, OUT_LINES * cols), 1) // cols
    in_of = iota((CH, OUT_LINES * cols), 1) % cols - iota((CH, OUT_LINES * cols), 0)
    spread = [(in_of == CH * (out_of + ky)).astype(bf16) for ky in range(3)]
    n1 = OUT_LINES * LANES
    group1 = iota((8, n1), 1) % LANES // IN_LINES == iota((8, n1), 0)
    line1 = iota((8, n1), 1) % IN_LINES - iota((8, n1), 1) // LANES
    spread1 = [(group1 & (line1 == ky)).astype(bf16) for ky in range(3)]
    tile4 = (iota((CH, cols), 1) % CH == iota((CH, cols), 0)).astype(bf16)
    t1_ref[...] = jnp.zeros(t1_ref.shape, f32)
    t4_ref[...] = jnp.zeros(t4_ref.shape, f32)

    for copy in copies[0:4]:
        copy.wait()
    for ky in range(3):
        for kx in range(3):
            t1_ref[ky * 8 + 2 * kx : ky * 8 + 2 * kx + 2, :] = k1_ref[ky, kx].astype(f32)
        t4_ref[ky * 3 : ky * 3 + 3, :] = k4_ref[ky].astype(f32)
    wide1 = sum(dot_0(t1_ref[ky * 8 : ky * 8 + 8, :].astype(bf16), spread1[ky]) for ky in range(3))
    for i in range(OUT_LINES):
        w1_ref[i * CH : (i + 1) * CH, :] = wide1[:, i * LANES : (i + 1) * LANES].astype(bf16)
    for k_ref, w_ref in ((k2_ref, w2_ref), (k3_ref, w3_ref)):
        wide = sum(dot(k_ref[ky * 3 * CH : (ky + 1) * 3 * CH, :], spread[ky]) for ky in range(3))
        for kx in range(3):
            for i in range(OUT_LINES):
                w_ref[kx * rows + i * CH : kx * rows + (i + 1) * CH, :] = wide[
                    kx * CH : (kx + 1) * CH, i * cols : (i + 1) * cols
                ].astype(bf16)
    wide4 = dot(t4_ref[...].astype(bf16), tile4)
    w4 = jnp.concatenate(
        [
            band_weights(
                [jnp.broadcast_to(wide4[ky * 3 + kx : ky * 3 + kx + 1], (CH, cols)) for ky in range(3)],
                CH, cols, 1, lambda k: k // CH,
            )
            for kx in range(3)
        ],
        0,
    )

    def clear(ref, lo, hi):
        ref[lo * CH : hi * CH, :] = jnp.zeros(((hi - lo) * CH, px), bf16)

    def outside(ref):
        @pl.when(first)
        def _():
            clear(ref, 0, HALO_LINES)

        @pl.when(last)
        def _():
            clear(ref, HALO_LINES + lines, frame)

    def merged(sums, n):
        before, _ = pixel_shifts(sums[0:n])
        _, after = pixel_shifts(sums[2 * n : 3 * n])
        return before + sums[n : 2 * n] + after

    for ref, line in ((xa_ref, 1), (xb_ref, 2), (x3_ref, 3)):
        clear(ref, line + blocks * OUT_LINES, total)
    above = above_ref[16:32, :].astype(f32)
    below = below_ref[16:32, :].astype(f32)
    copies[4].wait()
    for ch in range(2):
        s_ref[ch, 0:HALO_LINES, :] = above[ch * HALO_LINES : (ch + 1) * HALO_LINES]
        s_ref[ch, HALO_LINES : HALO_LINES + lines, :] = sar_ref[ch].astype(f32)
        s_ref[ch, HALO_LINES + lines : frame, :] = below[ch * HALO_LINES : (ch + 1) * HALO_LINES]
    pad = jnp.zeros((LANES - 6 * IN_LINES, px), f32)
    for b in range(blocks):
        at = b * OUT_LINES
        x = jnp.concatenate([s_ref[0, at : at + IN_LINES, :], s_ref[1, at : at + IN_LINES, :]], 0)
        before, after = pixel_shifts(x)
        acc = dot(w1_ref[...], jnp.concatenate([before, x, after, pad], 0).astype(bf16))
        xa_ref[(1 + at) * CH : (1 + at) * CH + rows, :] = jnp.maximum(acc, 0.0).astype(bf16)
    outside(xa_ref)

    for w_ref, src, dst, line in ((w2_ref, xa_ref, xb_ref, 2), (w3_ref, xb_ref, x3_ref, 3)):
        for b in range(blocks):
            at = line + b * OUT_LINES
            sums = dot(w_ref[...], src[(at - 1) * CH : (at - 1) * CH + cols, :])
            dst[at * CH : at * CH + rows, :] = jnp.maximum(merged(sums, rows), 0.0).astype(bf16)
        outside(dst)

    for b in range(blocks):
        at = HALO_LINES - 1 + b * OUT_LINES
        sums = dot(w4, x3_ref[at * CH : at * CH + cols, :])
        logit_ref[b * OUT_LINES : b * OUT_LINES + CH, :] = merged(sums, CH)
    frac = (1.0 / (1.0 + jnp.exp(-logit_ref[0:lines, :]))).astype(bf16)
    frac_ref[...] = frac
    for copy in copies[5:]:
        copy.wait()
    obs_ref[...] = frac.astype(f32) * gw_ref[...]

    quarter = wnd_ref.shape[1]
    parts = wnd_ref.shape[0] // lines // 2
    kind = iota((CH, px), 0)
    is_obs = kind < parts
    kind_part = (kind % parts).astype(f32).astype(bf16)
    sub = kind.astype(f32).astype(bf16)
    one = jnp.ones((CH, px), bf16)
    nil = jnp.zeros((CH, px), bf16)
    spots = [sub + g * CH for g in range(quarter // CH)]
    group = 8

    def window_group(g, carry):
        at = pl.ds(pl.multiple_of(g * group, group), group)
        cell = cell_ref[at, :]
        obs = obs_ref[at, :]
        cov = gw_ref[at, :]
        part = (cell // quarter).astype(f32)
        col = (cell % quarter).astype(f32)

        def spread_row(x, i):
            return jnp.broadcast_to(x[i : i + 1], (CH, px)).astype(bf16)

        for i in range(group):
            value = jnp.where(is_obs, obs[i : i + 1], cov[i : i + 1]).astype(bf16)
            left = jnp.where(kind_part == spread_row(part, i), value, nil)
            where_col = spread_row(col, i)
            hot = jnp.concatenate([jnp.where(spot == where_col, one, nil) for spot in spots], 0)
            wnd_ref[pl.ds(pl.multiple_of(g * (CH * group) + CH * i, CH), CH), :] = dot_t(left, hot)
        return carry

    lax.fori_loop(0, lines // group, window_group, 0)

    tile = tile_ref[...].astype(f32)
    same = iota((lines, lines), 0) == iota((lines, lines), 1)
    tile_sub = jnp.sum(jnp.where(same, jnp.broadcast_to(tile, (lines, lines)), 0.0), 1, keepdims=True)
    rival = (tile_sub == tile) & (iota((lines, lines), 0) < iota((lines, lines), 1))
    slot = tile * capacity + jnp.sum(jnp.where(rival, 1.0, 0.0), 0, keepdims=True)
    wnd_rows = wnd_ref.shape[0]
    per_line = wnd_rows // lines
    widen = (iota((lines, wnd_rows), 1) // per_line == iota((lines, wnd_rows), 0)).astype(bf16)
    slot_wide = dot(jnp.broadcast_to(slot, (8, lines)).astype(bf16), widen)[0:1]
    place = slot_wide.astype(jnp.int32) * 4 + (iota((1, wnd_rows), 1) // 4) % 4
    per_tile = 4 * capacity
    slots = devices * per_tile
    perm = jnp.where(iota((slots, wnd_rows), 0) == place, 1.0, 0.0).astype(bf16)
    tile_cols = 4 * quarter
    repeat = (iota((quarter, tile_cols), 1) % quarter == iota((quarter, tile_cols), 0)).astype(bf16)
    tiled = dot(wnd_ref[...].astype(bf16), repeat)
    mine = iota((wnd_rows, tile_cols), 0) % 4 == iota((wnd_rows, tile_cols), 1) // quarter
    by_slot = dot(perm, jnp.where(mine, tiled, 0.0).astype(bf16))
    row_of = dot(
        jnp.where(same, jnp.broadcast_to(row_ref[...].astype(f32), (lines, lines)), 0.0).astype(bf16),
        jnp.ones((lines, LANES), bf16),
    )
    perm_line = jnp.where(iota((slots, lines), 0) // 4 == slot.astype(jnp.int32), 1.0, 0.0).astype(bf16)
    row_own = dot(perm_line, row_of.astype(bf16))

    none = jnp.zeros((per_tile, LANES), f32)

    def of_right(x):
        return jnp.concatenate([x[per_tile:], none], 0)

    def of_left(x):
        return jnp.concatenate([none, x[: slots - per_tile]], 0)

    h = SUBSTEPS
    lane = iota((slots, LANES), 1)
    entry = iota((slots, LANES), 0) % per_tile
    column = iota((slots, LANES), 0) // per_tile % n_ty
    source = iota((LANES, LANES), 0)
    target = iota((LANES, LANES), 1)
    take_first = ((source < h) & (target % h == source)).astype(bf16)
    take_last = ((source >= LANES - h) & (target % h == source - (LANES - h))).astype(bf16)
    right_strip = dot(of_right(by_slot[:, 0:LANES]).astype(bf16), take_first)
    left_strip = dot(of_left(by_slot[:, tile_cols - LANES :]).astype(bf16), take_last)
    right_strip = jnp.where((lane // h == entry) & (column < n_ty - 1), right_strip, 0.0)
    left_strip = jnp.where((lane // h == entry) & (column > 0), left_strip, 0.0)
    info = jnp.zeros((slots, LANES), f32)
    for turn, value in enumerate((row_own, of_right(row_own), of_left(row_own))):
        info = jnp.where(lane == turn * per_tile + entry, value, info)
    extra_row = iota((8 * devices, slots), 0)
    extra_tile = iota((8 * devices, slots), 1) // per_tile
    extra = sum(
        dot((extra_row == 8 * extra_tile + r).astype(bf16), x.astype(bf16))
        for r, x in enumerate((right_strip, left_strip, info))
    )
    halves = [by_slot[:, at : at + LANES].reshape(devices, per_tile, LANES) for at in range(0, tile_cols, LANES)]
    packed = jnp.concatenate([*halves, extra.reshape(devices, 8, LANES)], 1)
    send_ref[...] = packed.reshape(send_ref.shape).astype(bf16)


def transposed(x):
    return jnp.transpose(x, (1, 0))


def level_kernel(
    devices,
    got_ref, from_left_ref, from_right_ref, depth_ref, slope_ref, rain_ref, dir_ref,
    level_ref, side_ref, top_ref, bot_ref,
):
    tile_rows, tile_cols = depth_ref.shape
    h = SUBSTEPS
    halves = tile_cols // LANES
    n = (got_ref.shape[0] // devices - 8) // halves
    k = devices * n
    packed = got_ref[...].astype(f32).reshape(devices, halves * n + 8, LANES)
    main = jnp.concatenate([packed[:, i * n : (i + 1) * n].reshape(k, LANES) for i in range(halves)], 1)
    extra = packed[:, halves * n :]

    entry = iota((k, LANES), 0) % n
    spread = iota((k, LANES), 1) // h == entry

    def strip(r, first):
        rows = jnp.broadcast_to(extra[:, r : r + 1], (devices, n, LANES)).reshape(k, LANES)
        take = iota((LANES, LANES), 0) % h + first == iota((LANES, LANES), 1)
        return dot(jnp.where(spread, rows, 0.0).astype(bf16), take.astype(bf16)).astype(bf16)

    lane = iota((1, k), 1)
    offset = lane % 2 + tile_rows * ((lane // 2) % 2)
    own_source = iota((8 * devices, k), 0) == 8 * (iota((8 * devices, k), 1) // n) + 2
    info = extra.reshape(8 * devices, LANES).astype(bf16)

    def placer(turn):
        pick = (iota((LANES, k), 0) == turn * n + iota((LANES, k), 1) % n).astype(bf16)
        line = jnp.sum(jnp.where(own_source, dot(info, pick), 0.0), 0, keepdims=True)
        target = line.astype(jnp.int32) + offset
        return jnp.where(iota((2 * tile_rows, k), 0) == target, 1.0, 0.0).astype(bf16)

    summed = dot(placer(0), main.astype(bf16))
    summed_side = dot(placer(1), strip(0, 0)) + dot(placer(2), strip(1, LANES - h))

    ty = lax.axis_index("ty")
    left = strips_of(from_left_ref, ty > 0)
    right = strips_of(from_right_ref, ty < lax.axis_size("ty") - 1)
    gap = jnp.zeros((LANES - 2 * h, tile_rows), f32)
    depth_side, conv_side, rain_side, code_side = [
        transposed(jnp.concatenate([r, gap, l], 0)) for r, l in zip(right, left)
    ]

    def analysed(sums, depth):
        observed = sums[0:tile_rows]
        covered = sums[tile_rows:]
        wet = depth / (depth + wet_depth)
        innovation = (observed - covered * wet) / (covered + 1.0)
        return depth * jnp.exp(innovation)

    level = analysed(summed, depth_ref[...])
    level_ref[...] = level
    sides = (analysed(summed_side, depth_side), rain_side, conv_side, code_side)
    owns = (level, rain_ref, slope_ref, dir_ref)

    def end_rows(at):
        own = [x[at, :] for x in owns]
        own[2] = runoff_coef * jnp.sqrt(own[2])
        own[3] = own[3].astype(f32)
        return jnp.concatenate([jnp.concatenate([o, x[at]], 1) for o, x in zip(own, sides)], 0).astype(bf16)

    for i, x in enumerate(sides):
        side_ref[i] = x
    top_ref[...] = end_rows(slice(0, h))
    bot_ref[...] = end_rows(slice(tile_rows - h, tile_rows))


def flow_kernel(
    level_ref, side_ref, slope_ref, dir_ref, rain_ref, above_ref, below_ref,
    out_ref,
    rain_s, conv_s, m_ref, part_ref, up_ref, down_ref,
):
    tile_rows, tile_cols = level_ref.shape
    h = SUBSTEPS
    wide_rows = tile_rows + 2 * h
    wide_cols = tile_cols + LANES

    def widened(field, own):
        at = slice(field * h, (field + 1) * h)
        mid = jnp.concatenate([own, side_ref[field]], 1)
        return jnp.concatenate([above_ref[...].astype(f32)[at], mid, below_ref[...].astype(f32)[at]], 0)

    zeros = jnp.zeros((h, wide_cols), f32)
    for buf in range(2):
        for ref in (up_ref, down_ref):
            ref[buf, 0:h, :] = zeros
            ref[buf, h + wide_rows :, :] = zeros
    part_ref[0] = widened(0, level_ref[...])
    rain_s[...] = widened(1, rain_ref[...])
    conv = widened(2, runoff_coef * jnp.sqrt(slope_ref[...]))
    conv_s[...] = conv
    code = widened(3, dir_ref[...].astype(f32))
    sides = (-1, 0, 1, -1, 1, -1, 0, 1)
    for direction, side in enumerate(sides):
        share = jnp.where(code == direction, conv, 0.0)
        m_ref[direction] = pltpu.roll(share, side % wide_cols, 1) if side else share

    chunk = 16

    def level_at(buf, r, n, step):
        level = part_ref[buf, r : r + n, :]
        if step:
            level = level + up_ref[buf, h + r + 1 : h + r + 1 + n, :] + down_ref[buf, h + r - 1 : h + r - 1 + n, :]
        return level

    for step in range(SUBSTEPS):
        buf, new = step % 2, (step + 1) % 2
        for r in range(0, wide_rows, chunk):
            level = level_at(buf, r, chunk, step)
            power = level * jnp.exp((2.0 / 3.0) * jnp.log(jnp.maximum(jnp.abs(level), 1e-30)))
            from_right = pltpu.roll(power, wide_cols - 1, 1)
            from_left = pltpu.roll(power, 1, 1)
            m = [m_ref[d, r : r + chunk, :] for d in range(8)]
            up_ref[new, h + r : h + r + chunk, :] = m[0] * from_right + m[1] * power + m[2] * from_left
            down_ref[new, h + r : h + r + chunk, :] = m[5] * from_right + m[6] * power + m[7] * from_left
            part_ref[new, r : r + chunk, :] = (
                level + rain_s[r : r + chunk, :] - conv_s[r : r + chunk, :] * power
                + (m[3] * from_right + m[4] * from_left)
            )
    buf = SUBSTEPS % 2
    out_ref[...] = level_at(buf, h, tile_rows, SUBSTEPS)[:, 0:tile_cols]


def hbm_specs(n):
    return [pl.BlockSpec(memory_space=pltpu.HBM)] * n


def vmem_specs(n):
    return [pl.BlockSpec(memory_space=pltpu.VMEM)] * n


def per_device(
    sar_image, kernel_first, kernel_second, kernel_third, kernel_last,
    geo_weight, cell_index, block_tile, block_row, depth, slope, flow_dir, rain,
):
    both = ("tx", "ty")
    devices = lax.axis_size(both)
    az_lines, range_px = geo_weight.shape
    tile_rows, tile_cols = depth.shape
    capacity = max(2, 2 * az_lines // devices)

    def steps(axis):
        size = lax.axis_size(axis)
        up = [(i, i + 1) for i in range(size - 1)]
        return up, [(j, i) for i, j in up]

    params = pltpu.CompilerParams(vmem_limit_bytes=VMEM_LIMIT)
    up, down = steps(both)
    message = jax.ShapeDtypeStruct((32, range_px), bf16)
    to_next, to_previous = pl.pallas_call(
        edge_kernel,
        out_shape=(message, message),
        in_specs=hbm_specs(5),
        out_specs=tuple(vmem_specs(2)),
        scratch_shapes=[
            pltpu.VMEM((2, 16, range_px), bf16),
            pltpu.VMEM((2, 16, range_px), bf16),
            *[pltpu.VMEM(x.shape, x.dtype) for x in (depth, slope, rain, flow_dir)],
            pltpu.SemaphoreType.DMA((6,)),
        ],
        compiler_params=params,
        name="edges",
    )(sar_image, depth, slope, rain, flow_dir)
    from_previous = lax.ppermute(to_next, both, up)
    from_next = lax.ppermute(to_previous, both, down)

    feats = (az_lines + 2 * HALO_LINES + 4) * CH
    rows, cols = OUT_LINES * CH, IN_LINES * CH
    send_rows = tile_cols // LANES * 4 * capacity + 8
    inputs = (
        sar_image,
        jnp.transpose(kernel_first, (2, 3, 1, 0)),
        jnp.transpose(kernel_second, (2, 3, 0, 1)).reshape(9 * CH, CH),
        jnp.transpose(kernel_third, (2, 3, 0, 1)).reshape(9 * CH, CH),
        jnp.transpose(kernel_last[0], (1, 2, 0)),
        geo_weight, cell_index, block_tile.reshape(1, az_lines), block_row.reshape(1, az_lines),
    )
    fraction, send = pl.pallas_call(
        functools.partial(swath_kernel, devices, capacity),
        out_shape=(
            jax.ShapeDtypeStruct((az_lines, range_px), bf16),
            jax.ShapeDtypeStruct((devices * send_rows, LANES), bf16),
        ),
        in_specs=vmem_specs(2) + hbm_specs(9),
        out_specs=tuple(vmem_specs(2)),
        scratch_shapes=[
            *[pltpu.VMEM(x.shape, x.dtype) for x in inputs],
            pltpu.SemaphoreType.DMA((9,)),
            pltpu.VMEM((2, az_lines + 2 * HALO_LINES + 8, range_px), f32),
            pltpu.VMEM((feats, range_px), bf16),
            pltpu.VMEM((feats, range_px), bf16),
            pltpu.VMEM((feats, range_px), bf16),
            pltpu.VMEM((3 * rows, cols), bf16),
            pltpu.VMEM((3 * rows, cols), bf16),
            pltpu.VMEM((rows, LANES), bf16),
            pltpu.VMEM((24, CH), f32),
            pltpu.VMEM((16, CH), f32),
            pltpu.VMEM((az_lines + 2 * CH, range_px), f32),
            pltpu.VMEM((az_lines, range_px), f32),
            pltpu.VMEM((CH * az_lines, tile_cols // 4), f32),
        ],
        compiler_params=params,
        name="swath",
    )(from_previous, from_next, *inputs)

    got = lax.all_to_all(
        send.reshape(devices, send_rows, LANES), both, split_axis=0, concat_axis=0, tiled=True
    ).reshape(devices * send_rows, LANES)

    wide_rows = tile_rows + 2 * SUBSTEPS
    wide_cols = tile_cols + LANES
    edge = jax.ShapeDtypeStruct((4 * SUBSTEPS, wide_cols), bf16)
    level, side, top_rows, bot_rows = pl.pallas_call(
        functools.partial(level_kernel, devices),
        out_shape=(
            jax.ShapeDtypeStruct((tile_rows, tile_cols), f32),
            jax.ShapeDtypeStruct((4, tile_rows, LANES), f32),
            edge,
            edge,
        ),
        in_specs=vmem_specs(7),
        out_specs=tuple(vmem_specs(4)),
        compiler_params=params,
        name="level",
    )(got, from_previous, from_next, depth, slope, rain, flow_dir)

    up, down = steps("tx")
    above = lax.ppermute(bot_rows, "tx", up)
    below = lax.ppermute(top_rows, "tx", down)

    level = pl.pallas_call(
        flow_kernel,
        out_shape=jax.ShapeDtypeStruct((tile_rows, tile_cols), f32),
        in_specs=vmem_specs(7),
        out_specs=vmem_specs(1)[0],
        scratch_shapes=[
            pltpu.VMEM((wide_rows, wide_cols), f32),
            pltpu.VMEM((wide_rows, wide_cols), f32),
            pltpu.VMEM((8, wide_rows, wide_cols), f32),
            pltpu.VMEM((2, wide_rows, wide_cols), f32),
            pltpu.VMEM((2, wide_rows + 2 * SUBSTEPS, wide_cols), f32),
            pltpu.VMEM((2, wide_rows + 2 * SUBSTEPS, wide_cols), f32),
        ],
        compiler_params=params,
        name="flow",
    )(level, side, slope, flow_dir, rain, above, below)
    return (fraction, level)


def solution(mesh):
    placed = (
        P(None, ("tx", "ty"), None),
        P(),
        P(),
        P(),
        P(),
        P(("tx", "ty"), None),
        P(("tx", "ty"), None),
        P(("tx", "ty"), None),
        P(("tx", "ty"), None),
        P("tx", "ty"),
        P("tx", "ty"),
        P("tx", "ty"),
        P("tx", "ty"),
    )
    return jax.shard_map(
        per_device,
        mesh=mesh,
        in_specs=placed,
        out_specs=(P(("tx", "ty"), None), P("tx", "ty")),
        check_vma=False,
    )
```

time: 59.6 us -> 59.7 us (level)
  Pallas kernels: 15 us -> 16.5 us
  blocking collectives: 21.8 us -> 20.6 us
    all_to_all x1, blocking collectives: 21.8 us -> 20.6 us  [per_device(): lax.all_to_all(send.reshape(devices, send_rows, LANES), both, split_axis=...]
    pallas_call x2, Pallas kernels: 0.86 us -> 1.99 us  [the longest x1 1.63 us: per_device(): pl.pallas_call(functools.partial(level_kernel, devices), out_shape=(jax.S...]
  transfers between devices with their start and end apart: 4 -> 4, of which waited for: 3 -> 2; matrix products, arithmetic and copies ran while one was open for 0% -> 0% of each run, Pallas kernels for 0% -> 0%
where the time goes in v3:
time: 59.7 us; the launch traced here: 59.3 us
  blocking collectives  20.6 us (35%)
  Pallas kernels  16.5 us (28%)
  waiting for transfers between devices  8.17 us (14%)
  starting transfers between devices  7.87 us (13%)
  local copies, waits for them, and re-layouts  5.39 us (9%)
  between operations  0.79 us (1%)
    all_to_all x1, blocking collectives, per_device(): lax.all_to_all(send.reshape(devices, send_rows, LANES), both, split_axis=...  20.6 us
    pallas_call x1, Pallas kernels, per_device(): pl.pallas_call(functools.partial(swath_kernel, devices, capacity), out_sh...  9.17 us
    unnamed x34, local copies, waits for them, and re-layouts  5.39 us
    pallas_call x1, Pallas kernels, per_device(): pl.pallas_call(flow_kernel, out_shape=jax.ShapeDtypeStruct((tile_rows, ti...  5.29 us
    ppermute x1, waiting for transfers between devices, per_device(): below = lax.ppermute(top_rows, 'tx', down)  4.22 us
    ppermute x1, waiting for transfers between devices, per_device(): from_next = lax.ppermute(to_previous, both, down)  3.93 us
    ppermute x1, starting transfers between devices, per_device(): above = lax.ppermute(bot_rows, 'tx', up)  2.75 us
    ppermute x1, starting transfers between devices, per_device(): from_previous = lax.ppermute(to_next, both, up)  2.36 us
  transfers between devices with their start and end apart: 4, of which 2 were waited for; matrix products, arithmetic and copies ran while one was open for 0% of the time, Pallas kernels for 0%

profile of v3, /device:TPU:0, one launch (start us, length us, event | category | flops | bytes accessed | tf_op | source)
XLA Modules:
  0.0 59.3 jit_solution(4265369447241092600)
XLA Ops:
  0.6 0.0 copy-start
  0.6 0.9 %copy-done = f32[256,256]{1,0:T(8,128)S(1)} copy-done((f32[256,256]{1,0:T(8,128)S(1)}, f32[256,256]{1,0:T(8,128)}, u32[]{:S(2)}) %copy-start) | copy-done | bytes 262168
  1.6 0.0 copy-start.2
  1.6 0.9 %copy-done.2 = f32[256,256]{1,0:T(8,128)S(1)} copy-done((f32[256,256]{1,0:T(8,128)S(1)}, f32[256,256]{1,0:T(8,128)}, u32[]{:S(2)}) %copy-start.2) | copy-done | bytes 262168
  2.5 0.0 copy-start.4
  2.5 0.9 %copy-done.4 = s32[256,256]{1,0:T(8,128)S(1)} copy-done((s32[256,256]{1,0:T(8,128)S(1)}, s32[256,256]{1,0:T(8,128)}, u32[]{:S(2)}) %copy-start.4) | copy-done | bytes 262168
  3.5 0.0 copy-start.6
  3.5 0.9 %copy-done.6 = f32[256,256]{1,0:T(8,128)S(1)} copy-done((f32[256,256]{1,0:T(8,128)S(1)}, f32[256,256]{1,0:T(8,128)}, u32[]{:S(2)}) %copy-start.6) | copy-done | bytes 262168
  4.4 0.0 copy-start.8
  4.4 0.9 %copy-done.8 = bf16[2,64,512]{2,1,0:T(8,128)(2,1)S(1)} copy-done((bf16[2,64,512]{2,1,0:T(8,128)(2,1)S(1)}, bf16[2,64,512]{2,1,0:T(8,128)(2,1)}, u32[]{:S(2)}) %copy-start.8) | copy-done | bytes 131096
  5.3 0.0 copy-start.9
  5.3 0.0 copy-start.10
  5.3 0.0 copy-start.11
  5.3 0.0 copy-start.12
  5.4 0.4 edges.1
  5.7 2.4 %collective-permute-start = (bf16[32,512]{1,0:T(8,128)(2,1)S(1)}, bf16[32,512]{1,0:T(8,128)(2,1)S(1)}, u32[]{:S(2)}, u32[]{:S(2)}) collective-permute-start(bf16[32,512]{1,0:T(8,128)(2,1)S(1)} %get-tuple-element.10), channel_id=1, source_target_pairs={{0,1},{1,2},{2,3},{3,4},{4,5},{5,6},{6,7},{7,8},{8,9},{9,10},{10,1... | collective-permute-start | bytes 98312 | tf_op jit(solution)/shard_map/ppermute | solution.py:478
  8.1 1.3 %collective-permute-start.1 = (bf16[32,512]{1,0:T(8,128)(2,1)S(1)}, bf16[32,512]{1,0:T(8,128)(2,1)S(1)}, u32[]{:S(2)}, u32[]{:S(2)}) collective-permute-start(bf16[32,512]{1,0:T(8,128)(2,1)S(1)} %get-tuple-element.11), channel_id=1, source_target_pairs={{1,0},{2,1},{3,2},{4,3},{5,4},{6,5},{7,6},{8,7},{9,8},{10,9},{11,1... | collective-permute-start | bytes 98312 | tf_op jit(solution)/shard_map/ppermute | solution.py:479
  9.4 0.0 collective-permute-done.above_ref.from_left_ref
  9.4 3.9 %collective-permute-done.1.below_ref.from_right_ref = bf16[32,512]{1,0:T(8,128)(2,1)S(1)} collective-permute-done((bf16[32,512]{1,0:T(8,128)(2,1)S(1)}, bf16[32,512]{1,0:T(8,128)(2,1)S(1)}, u32[]{:S(2)}, u32[]{:S(2)}) %collective-permute-start.1) | collective-permute-done | bytes 32800 | tf_op jit(solution)/shard_map/ppermute | solution.py:479
  13.3 0.0 copy-start.13
  13.3 0.0 copy-start.14
  13.3 0.0 copy-start.15
  13.3 0.0 copy-start.16
  13.3 0.0 copy-done.9
  13.4 0.0 copy-done.10
  13.4 0.0 copy-done.11
  13.4 0.0 copy-done.12
  13.4 0.6 %copy-done.13 = bf16[16,2,3,3]{0,1,3,2:T(2,128)(2,1)S(1)} copy-done((bf16[16,2,3,3]{0,1,3,2:T(2,128)(2,1)S(1)}, bf16[16,2,3,3]{0,1,3,2:T(2,128)(2,1)}, u32[]{:S(2)}) %copy-start.13) | copy-done | bytes 600
  14.0 0.0 copy-done.14
  14.0 0.0 copy-done.15
  14.0 0.0 copy-done.16
  14.0 0.0 copy-start.5
  14.0 0.0 copy-start.7
  14.0 9.2 %swath.1 = (bf16[64,512]{1,0:T(8,128)(2,1)}, bf16[1280,128]{1,0:T(8,128)(2,1)S(1)}) custom-call(bf16[32,512]{1,0:T(8,128)(2,1)S(1)} %collective-permute-done.above_ref.from_left_ref, bf16[32,512]{1,0:T(8,128)(2,1)S(1)} %collective-permute-done.1.below_ref.from_right_ref, bf16[2,64,512]{2,1,0:T(8,128)(2,1)S(1)} %copy-done.8, ...), custom_call_target="tpu_custom_call" | custom-call | tf_op jit(solution)/shard_map/swath/pallas_call | solution.py:492
  23.2 0.0 copy-start.1
  23.2 0.0 copy-start.3
  23.2 20.6 %all_to_all.5 = bf16[32,40,128]{2,1,0:T(8,128)(2,1)S(1)} all-to-all(bf16[32,40,128]{2,1,0:T(8,128)(2,1)S(1)} %bitcast.15), channel_id=1, replica_groups=mesh['tx'=8,'ty'=4] {'tx','ty'}, dimensions={0} | all-to-all | bytes 655360 | tf_op jit(solution)/shard_map/all_to_all | solution.py:520
  43.9 0.0 copy-done.5
  43.9 0.0 copy-done.7
  43.9 0.0 copy-done.1
  43.9 0.0 copy-done.3
  43.9 1.6 %level.1 = (f32[256,256]{1,0:T(8,128)S(1)}, f32[4,256,128]{2,1,0:T(8,128)S(1)}, bf16[32,384]{1,0:T(8,128)(2,1)S(1)}, bf16[32,384]{1,0:T(8,128)(2,1)S(1)}) custom-call(bf16[1280,128]{1,0:T(8,128)(2,1)S(1)} %bitcast.14, bf16[32,512]{1,0:T(8,128)(2,1)S(1)} %collective-permute-done.above_ref.from_left_ref, ...), custom_call_target="tpu_custom_call" | custom-call | tf_op jit(solution)/shard_map/level/pallas_call | solution.py:527
  45.5 2.7 %collective-permute-start.2 = (bf16[32,384]{1,0:T(8,128)(2,1)S(1)}, bf16[32,384]{1,0:T(8,128)(2,1)S(1)}, u32[]{:S(2)}, u32[]{:S(2)}) collective-permute-start(bf16[32,384]{1,0:T(8,128)(2,1)S(1)} %get-tuple-element.16), channel_id=1, source_target_pairs={{0,4},{4,8},{8,12},{12,16},{16,20},{20,24},{24,28},{1,5},{5,9},{9,... | collective-permute-start | bytes 73736 | tf_op jit(solution)/shard_map/ppermute | solution.py:542
  48.3 1.5 %collective-permute-start.3 = (bf16[32,384]{1,0:T(8,128)(2,1)S(1)}, bf16[32,384]{1,0:T(8,128)(2,1)S(1)}, u32[]{:S(2)}, u32[]{:S(2)}) collective-permute-start(bf16[32,384]{1,0:T(8,128)(2,1)S(1)} %get-tuple-element.17), channel_id=1, source_target_pairs={{4,0},{8,4},{12,8},{16,12},{20,16},{24,20},{28,24},{5,1},{9,5},{13... | collective-permute-start | bytes 73736 | tf_op jit(solution)/shard_map/ppermute | solution.py:543
  49.8 0.0 collective-permute-done.2.above_ref
  49.8 4.2 %collective-permute-done.3.below_ref = bf16[32,384]{1,0:T(8,128)(2,1)S(1)} collective-permute-done((bf16[32,384]{1,0:T(8,128)(2,1)S(1)}, bf16[32,384]{1,0:T(8,128)(2,1)S(1)}, u32[]{:S(2)}, u32[]{:S(2)}) %collective-permute-start.3) | collective-permute-done | bytes 24608 | tf_op jit(solution)/shard_map/ppermute | solution.py:543
  54.0 5.3 %flow.1 = f32[256,256]{1,0:T(8,128)} custom-call(f32[256,256]{1,0:T(8,128)S(1)} %get-tuple-element.14.level_ref, f32[4,256,128]{2,1,0:T(8,128)S(1)} %get-tuple-element.15.side_ref, f32[256,256]{1,0:T(8,128)S(1)} %copy-done.1, s32[256,256]{1,0:T(8,128)S(1)} %copy-done.5, f32[256,256]{1,0:T(8,128)S(1)} %copy-done.3, ...), custom_call_target="tpu_custom_call" | custom-call | tf_op jit(solution)/shard_map/flow/pallas_call | solution.py:545
Async XLA Ops:
  0.6 1.0 %copy-start = (f32[256,256]{1,0:T(8,128)S(1)}, f32[256,256]{1,0:T(8,128)}, u32[]{:S(2)}) copy-start(f32[256,256]{1,0:T(8,128)} %slope_ref.3) | copy-start | bytes 786436
  1.6 0.9 %copy-start.2 = (f32[256,256]{1,0:T(8,128)S(1)}, f32[256,256]{1,0:T(8,128)}, u32[]{:S(2)}) copy-start(f32[256,256]{1,0:T(8,128)} %rain_ref.3) | copy-start | bytes 786436
  2.5 0.9 %copy-start.4 = (s32[256,256]{1,0:T(8,128)S(1)}, s32[256,256]{1,0:T(8,128)}, u32[]{:S(2)}) copy-start(s32[256,256]{1,0:T(8,128)} %dir_ref.3) | copy-start | bytes 786436
  3.5 0.9 %copy-start.6 = (f32[256,256]{1,0:T(8,128)S(1)}, f32[256,256]{1,0:T(8,128)}, u32[]{:S(2)}) copy-start(f32[256,256]{1,0:T(8,128)} %depth_ref.1) | copy-start | bytes 786436
  4.4 0.9 %copy-start.8 = (bf16[2,64,512]{2,1,0:T(8,128)(2,1)S(1)}, bf16[2,64,512]{2,1,0:T(8,128)(2,1)}, u32[]{:S(2)}) copy-start(bf16[2,64,512]{2,1,0:T(8,128)(2,1)} %sar_hbm.3) | copy-start | bytes 393220
  5.3 8.0 %copy-start.9 = (f32[64,512]{1,0:T(8,128)S(1)}, f32[64,512]{1,0:T(8,128)}, u32[]{:S(2)}) copy-start(f32[64,512]{1,0:T(8,128)} %gw_hbm.1) | copy-start | bytes 393220
  5.3 8.0 %copy-start.10 = (s32[64,512]{1,0:T(8,128)S(1)}, s32[64,512]{1,0:T(8,128)}, u32[]{:S(2)}) copy-start(s32[64,512]{1,0:T(8,128)} %cell_hbm.1) | copy-start | bytes 393220
  5.3 8.0 %copy-start.11 = (bf16[16,16,3,3]{1,0,3,2:T(8,128)(2,1)S(1)}, bf16[16,16,3,3]{1,0,3,2:T(8,128)(2,1)}, u32[]{:S(2)}) copy-start(bf16[16,16,3,3]{1,0,3,2:T(8,128)(2,1)} %param.15) | copy-start | bytes 13828
  5.3 8.0 %copy-start.12 = (bf16[16,16,3,3]{1,0,3,2:T(8,128)(2,1)S(1)}, bf16[16,16,3,3]{1,0,3,2:T(8,128)(2,1)}, u32[]{:S(2)}) copy-start(bf16[16,16,3,3]{1,0,3,2:T(8,128)(2,1)} %param.16) | copy-start | bytes 13828
  5.7 3.7 %collective-permute-start = (bf16[32,512]{1,0:T(8,128)(2,1)S(1)}, bf16[32,512]{1,0:T(8,128)(2,1)S(1)}, u32[]{:S(2)}, u32[]{:S(2)}) collective-permute-start(bf16[32,512]{1,0:T(8,128)(2,1)S(1)} %get-tuple-element.10), channel_id=1, source_target_pairs={{0,1},{1,2},{2,3},{3,4},{4,5},{5,6},{6,7},{7,8},{8,9},{9,10},{10,1... | collective-permute-start | bytes 98312 | tf_op jit(solution)/shard_map/ppermute | solution.py:478
  8.1 5.2 %collective-permute-start.1 = (bf16[32,512]{1,0:T(8,128)(2,1)S(1)}, bf16[32,512]{1,0:T(8,128)(2,1)S(1)}, u32[]{:S(2)}, u32[]{:S(2)}) collective-permute-start(bf16[32,512]{1,0:T(8,128)(2,1)S(1)} %get-tuple-element.11), channel_id=1, source_target_pairs={{1,0},{2,1},{3,2},{4,3},{5,4},{6,5},{7,6},{8,7},{9,8},{10,9},{11,1... | collective-permute-start | bytes 98312 | tf_op jit(solution)/shard_map/ppermute | solution.py:479
  13.3 0.7 %copy-start.13 = (bf16[16,2,3,3]{0,1,3,2:T(2,128)(2,1)S(1)}, bf16[16,2,3,3]{0,1,3,2:T(2,128)(2,1)}, u32[]{:S(2)}) copy-start(bf16[16,2,3,3]{0,1,3,2:T(2,128)(2,1)} %param.14) | copy-start | bytes 1732
  13.3 0.7 %copy-start.14 = (bf16[1,16,3,3]{1,3,2,0:T(4,128)(2,1)S(1)}, bf16[1,16,3,3]{1,3,2,0:T(4,128)(2,1)}, u32[]{:S(2)}) copy-start(bf16[1,16,3,3]{1,3,2,0:T(4,128)(2,1)} %param.17) | copy-start | bytes 868
  13.3 0.7 %copy-start.15 = (s32[64,1]{0,1:T(1,128)S(1)}, s32[64,1]{0,1:T(1,128)}, u32[]{:S(2)}) copy-start(s32[64,1]{0,1:T(1,128)} %param.20) | copy-start | bytes 772
  13.3 0.7 %copy-start.16 = (s32[64,1]{0,1:T(1,128)S(1)}, s32[64,1]{0,1:T(1,128)}, u32[]{:S(2)}) copy-start(s32[64,1]{0,1:T(1,128)} %param.21) | copy-start | bytes 772
  14.0 29.8 %copy-start.5 = (s32[256,256]{1,0:T(8,128)S(1)}, s32[256,256]{1,0:T(8,128)}, u32[]{:S(2)}) copy-start(s32[256,256]{1,0:T(8,128)} %dir_ref.3) | copy-start | bytes 786436
  14.0 29.8 %copy-start.7 = (f32[256,256]{1,0:T(8,128)S(1)}, f32[256,256]{1,0:T(8,128)}, u32[]{:S(2)}) copy-start(f32[256,256]{1,0:T(8,128)} %depth_ref.1) | copy-start | bytes 786436
  23.2 20.7 %copy-start.1 = (f32[256,256]{1,0:T(8,128)S(1)}, f32[256,256]{1,0:T(8,128)}, u32[]{:S(2)}) copy-start(f32[256,256]{1,0:T(8,128)} %slope_ref.3) | copy-start | bytes 786436
  23.2 20.7 %copy-start.3 = (f32[256,256]{1,0:T(8,128)S(1)}, f32[256,256]{1,0:T(8,128)}, u32[]{:S(2)}) copy-start(f32[256,256]{1,0:T(8,128)} %rain_ref.3) | copy-start | bytes 786436
  45.5 4.3 %collective-permute-start.2 = (bf16[32,384]{1,0:T(8,128)(2,1)S(1)}, bf16[32,384]{1,0:T(8,128)(2,1)S(1)}, u32[]{:S(2)}, u32[]{:S(2)}) collective-permute-start(bf16[32,384]{1,0:T(8,128)(2,1)S(1)} %get-tuple-element.16), channel_id=1, source_target_pairs={{0,4},{4,8},{8,12},{12,16},{16,20},{20,24},{24,28},{1,5},{5,9},{9,... | collective-permute-start | bytes 73736 | tf_op jit(solution)/shard_map/ppermute | solution.py:542
  48.3 5.7 %collective-permute-start.3 = (bf16[32,384]{1,0:T(8,128)(2,1)S(1)}, bf16[32,384]{1,0:T(8,128)(2,1)S(1)}, u32[]{:S(2)}, u32[]{:S(2)}) collective-permute-start(bf16[32,384]{1,0:T(8,128)(2,1)S(1)} %get-tuple-element.17), channel_id=1, source_target_pairs={{4,0},{8,4},{12,8},{16,12},{20,16},{24,20},{28,24},{5,1},{9,5},{13... | collective-permute-start | bytes 73736 | tf_op jit(solution)/shard_map/ppermute | solution.py:543

commit v4 on v3

--- a/solution.py
+++ b/solution.py
@@ -15,6 +15,7 @@
 HALO_LINES = 4
 LANES = 128
 VMEM_LIMIT = 48 * 1024 * 1024
+VMEM_MOST = 61920 * 1024
 
 wet_depth = 0.5
 runoff_coef = 0.25
@@ -24,6 +25,16 @@
 
 def iota(shape, dim):
     return lax.broadcasted_iota(jnp.int32, shape, dim)
+
+
+def quo(x, n):
+    assert n & (n - 1) == 0
+    return lax.shift_right_logical(x, jnp.int32(n.bit_length() - 1)) if n > 1 else x
+
+
+def rem(x, n):
+    assert n & (n - 1) == 0
+    return x & (n - 1)
 
 
 def dot(a, b):
@@ -47,7 +58,7 @@
 
 
 def band_weights(tiled, rows, cols, per_row, line_of):
-    out_line = iota((rows, cols), 0) // per_row
+    out_line = quo(iota((rows, cols), 0), per_row)
     off = line_of(iota((rows, cols), 1)) - out_line
     out = jnp.zeros((rows, cols), f32)
     for ky in range(3):
@@ -125,14 +136,14 @@
     rows = OUT_LINES * CH
     cols = IN_LINES * CH
 
-    out_of = iota((CH, OUT_LINES * cols), 1) // cols
-    in_of = iota((CH, OUT_LINES * cols), 1) % cols - iota((CH, OUT_LINES * cols), 0)
+    out_of = quo(iota((CH, OUT_LINES * cols), 1), cols)
+    in_of = rem(iota((CH, OUT_LINES * cols), 1), cols) - iota((CH, OUT_LINES * cols), 0)
     spread = [(in_of == CH * (out_of + ky)).astype(bf16) for ky in range(3)]
     n1 = OUT_LINES * LANES
-    group1 = iota((8, n1), 1) % LANES // IN_LINES == iota((8, n1), 0)
-    line1 = iota((8, n1), 1) % IN_LINES - iota((8, n1), 1) // LANES
+    group1 = quo(rem(iota((8, n1), 1), LANES), IN_LINES) == iota((8, n1), 0)
+    line1 = rem(iota((8, n1), 1), IN_LINES) - quo(iota((8, n1), 1), LANES)
     spread1 = [(group1 & (line1 == ky)).astype(bf16) for ky in range(3)]
-    tile4 = (iota((CH, cols), 1) % CH == iota((CH, cols), 0)).astype(bf16)
+    tile4 = (rem(iota((CH, cols), 1), CH) == iota((CH, cols), 0)).astype(bf16)
     t1_ref[...] = jnp.zeros(t1_ref.shape, f32)
     t4_ref[...] = jnp.zeros(t4_ref.shape, f32)
 
@@ -157,7 +168,7 @@
         [
             band_weights(
                 [jnp.broadcast_to(wide4[ky * 3 + kx : ky * 3 + kx + 1], (CH, cols)) for ky in range(3)],
-                CH, cols, 1, lambda k: k // CH,
+                CH, cols, 1, lambda k: quo(k, CH),
             )
             for kx in range(3)
         ],
@@ -220,7 +231,7 @@
     parts = wnd_ref.shape[0] // lines // 2
     kind = iota((CH, px), 0)
     is_obs = kind < parts
-    kind_part = (kind % parts).astype(f32).astype(bf16)
+    kind_part = rem(kind, parts).astype(f32).astype(bf16)
     sub = kind.astype(f32).astype(bf16)
     one = jnp.ones((CH, px), bf16)
     nil = jnp.zeros((CH, px), bf16)
@@ -232,8 +243,8 @@
         cell = cell_ref[at, :]
         obs = obs_ref[at, :]
         cov = gw_ref[at, :]
-        part = (cell // quarter).astype(f32)
-        col = (cell % quarter).astype(f32)
+        part = quo(cell, quarter).astype(f32)
+        col = rem(cell, quarter).astype(f32)
 
         def spread_row(x, i):
             return jnp.broadcast_to(x[i : i + 1], (CH, px)).astype(bf16)
@@ -255,22 +266,22 @@
     slot = tile * capacity + jnp.sum(jnp.where(rival, 1.0, 0.0), 0, keepdims=True)
     wnd_rows = wnd_ref.shape[0]
     per_line = wnd_rows // lines
-    widen = (iota((lines, wnd_rows), 1) // per_line == iota((lines, wnd_rows), 0)).astype(bf16)
+    widen = (quo(iota((lines, wnd_rows), 1), per_line) == iota((lines, wnd_rows), 0)).astype(bf16)
     slot_wide = dot(jnp.broadcast_to(slot, (8, lines)).astype(bf16), widen)[0:1]
-    place = slot_wide.astype(jnp.int32) * 4 + (iota((1, wnd_rows), 1) // 4) % 4
+    place = slot_wide.astype(jnp.int32) * 4 + rem(quo(iota((1, wnd_rows), 1), 4), 4)
     per_tile = 4 * capacity
     slots = devices * per_tile
     perm = jnp.where(iota((slots, wnd_rows), 0) == place, 1.0, 0.0).astype(bf16)
     tile_cols = 4 * quarter
-    repeat = (iota((quarter, tile_cols), 1) % quarter == iota((quarter, tile_cols), 0)).astype(bf16)
+    repeat = (rem(iota((quarter, tile_cols), 1), quarter) == iota((quarter, tile_cols), 0)).astype(bf16)
     tiled = dot(wnd_ref[...].astype(bf16), repeat)
-    mine = iota((wnd_rows, tile_cols), 0) % 4 == iota((wnd_rows, tile_cols), 1) // quarter
+    mine = rem(iota((wnd_rows, tile_cols), 0), 4) == quo(iota((wnd_rows, tile_cols), 1), quarter)
     by_slot = dot(perm, jnp.where(mine, tiled, 0.0).astype(bf16))
     row_of = dot(
         jnp.where(same, jnp.broadcast_to(row_ref[...].astype(f32), (lines, lines)), 0.0).astype(bf16),
         jnp.ones((lines, LANES), bf16),
     )
-    perm_line = jnp.where(iota((slots, lines), 0) // 4 == slot.astype(jnp.int32), 1.0, 0.0).astype(bf16)
+    perm_line = jnp.where(quo(iota((slots, lines), 0), 4) == slot.astype(jnp.int32), 1.0, 0.0).astype(bf16)
     row_own = dot(perm_line, row_of.astype(bf16))
 
     none = jnp.zeros((per_tile, LANES), f32)
@@ -283,21 +294,21 @@
 
     h = SUBSTEPS
     lane = iota((slots, LANES), 1)
-    entry = iota((slots, LANES), 0) % per_tile
-    column = iota((slots, LANES), 0) // per_tile % n_ty
+    entry = rem(iota((slots, LANES), 0), per_tile)
+    column = rem(quo(iota((slots, LANES), 0), per_tile), n_ty)
     source = iota((LANES, LANES), 0)
     target = iota((LANES, LANES), 1)
-    take_first = ((source < h) & (target % h == source)).astype(bf16)
-    take_last = ((source >= LANES - h) & (target % h == source - (LANES - h))).astype(bf16)
+    take_first = ((source < h) & (rem(target, h) == source)).astype(bf16)
+    take_last = ((source >= LANES - h) & (rem(target, h) == source - (LANES - h))).astype(bf16)
     right_strip = dot(of_right(by_slot[:, 0:LANES]).astype(bf16), take_first)
     left_strip = dot(of_left(by_slot[:, tile_cols - LANES :]).astype(bf16), take_last)
-    right_strip = jnp.where((lane // h == entry) & (column < n_ty - 1), right_strip, 0.0)
-    left_strip = jnp.where((lane // h == entry) & (column > 0), left_strip, 0.0)
+    right_strip = jnp.where((quo(lane, h) == entry) & (column < n_ty - 1), right_strip, 0.0)
+    left_strip = jnp.where((quo(lane, h) == entry) & (column > 0), left_strip, 0.0)
     info = jnp.zeros((slots, LANES), f32)
     for turn, value in enumerate((row_own, of_right(row_own), of_left(row_own))):
         info = jnp.where(lane == turn * per_tile + entry, value, info)
     extra_row = iota((8 * devices, slots), 0)
-    extra_tile = iota((8 * devices, slots), 1) // per_tile
+    extra_tile = quo(iota((8 * devices, slots), 1), per_tile)
     extra = sum(
         dot((extra_row == 8 * extra_tile + r).astype(bf16), x.astype(bf16))
         for r, x in enumerate((right_strip, left_strip, info))
@@ -325,21 +336,21 @@
     main = jnp.concatenate([packed[:, i * n : (i + 1) * n].reshape(k, LANES) for i in range(halves)], 1)
     extra = packed[:, halves * n :]
 
-    entry = iota((k, LANES), 0) % n
-    spread = iota((k, LANES), 1) // h == entry
+    entry = rem(iota((k, LANES), 0), n)
+    spread = quo(iota((k, LANES), 1), h) == entry
 
     def strip(r, first):
         rows = jnp.broadcast_to(extra[:, r : r + 1], (devices, n, LANES)).reshape(k, LANES)
-        take = iota((LANES, LANES), 0) % h + first == iota((LANES, LANES), 1)
+        take = rem(iota((LANES, LANES), 0), h) + first == iota((LANES, LANES), 1)
         return dot(jnp.where(spread, rows, 0.0).astype(bf16), take.astype(bf16)).astype(bf16)
 
     lane = iota((1, k), 1)
-    offset = lane % 2 + tile_rows * ((lane // 2) % 2)
-    own_source = iota((8 * devices, k), 0) == 8 * (iota((8 * devices, k), 1) // n) + 2
+    offset = rem(lane, 2) + tile_rows * rem(quo(lane, 2), 2)
+    own_source = iota((8 * devices, k), 0) == 8 * quo(iota((8 * devices, k), 1), n) + 2
     info = extra.reshape(8 * devices, LANES).astype(bf16)
 
     def placer(turn):
-        pick = (iota((LANES, k), 0) == turn * n + iota((LANES, k), 1) % n).astype(bf16)
+        pick = (iota((LANES, k), 0) == turn * n + rem(iota((LANES, k), 1), n)).astype(bf16)
         line = jnp.sum(jnp.where(own_source, dot(info, pick), 0.0), 0, keepdims=True)
         target = line.astype(jnp.int32) + offset
         return jnp.where(iota((2 * tile_rows, k), 0) == target, 1.0, 0.0).astype(bf16)
@@ -472,7 +483,7 @@
             *[pltpu.VMEM(x.shape, x.dtype) for x in (depth, slope, rain, flow_dir)],
             pltpu.SemaphoreType.DMA((6,)),
         ],
-        compiler_params=params,
+        compiler_params=pltpu.CompilerParams(vmem_limit_bytes=VMEM_MOST),
         name="edges",
     )(sar_image, depth, slope, rain, flow_dir)
     from_previous = lax.ppermute(to_next, both, up)

time: 59.7 us -> 56.8 us (0.951)
  local copies, waits for them, and re-layouts: 5.39 us -> 0.69 us
  Pallas kernels: 16.5 us -> 18.2 us
    unnamed x34 -> x26, local copies, waits for them, and re-layouts: 5.39 us -> 0.69 us
    pallas_call x1, Pallas kernels: 0.37 us -> 2.12 us  [per_device(): pl.pallas_call(edge_kernel, out_shape=(message, message), in_specs=hbm_sp...]
where the time goes in v4:
time: 56.8 us; the launch traced here: 56.6 us
  blocking collectives  20.6 us (36%)
  Pallas kernels  18.2 us (32%)
  waiting for transfers between devices  8.38 us (15%)
  starting transfers between devices  7.87 us (14%)
  between operations  0.82 us (1%)
  local copies, waits for them, and re-layouts  0.69 us (1%)
    all_to_all x1, blocking collectives, per_device(): lax.all_to_all(send.reshape(devices, send_rows, LANES), both, split_axis=...  20.6 us
    pallas_call x1, Pallas kernels, per_device(): pl.pallas_call(functools.partial(swath_kernel, devices, capacity), out_sh...  9.14 us
    pallas_call x1, Pallas kernels, per_device(): pl.pallas_call(flow_kernel, out_shape=jax.ShapeDtypeStruct((tile_rows, ti...  5.29 us
    ppermute x1, waiting for transfers between devices, per_device(): below = lax.ppermute(top_rows, 'tx', down)  4.22 us
    ppermute x1, waiting for transfers between devices, per_device(): from_next = lax.ppermute(to_previous, both, down)  4.14 us
    ppermute x1, starting transfers between devices, per_device(): above = lax.ppermute(bot_rows, 'tx', up)  2.75 us
    ppermute x1, starting transfers between devices, per_device(): from_previous = lax.ppermute(to_next, both, up)  2.36 us
    pallas_call x1, Pallas kernels, per_device(): pl.pallas_call(edge_kernel, out_shape=(message, message), in_specs=hbm_sp...  2.12 us
  transfers between devices with their start and end apart: 4, of which 2 were waited for; matrix products, arithmetic and copies ran while one was open for 0% of the time, Pallas kernels for 0%

profile of v4, /device:TPU:0, one launch (start us, length us, event | category | flops | bytes accessed | tf_op | source)
XLA Modules:
  0.0 56.6 jit_solution(17839824915885907459)
XLA Ops:
  0.6 0.0 copy-start.4
  0.6 0.0 copy-start.6
  0.7 0.0 copy-start.5
  0.7 0.0 copy-start.7
  0.7 0.0 copy-start.8
  0.7 2.1 %edges.1 = (bf16[32,512]{1,0:T(8,128)(2,1)}, bf16[32,512]{1,0:T(8,128)(2,1)}) custom-call(bf16[2,64,512]{2,1,0:T(8,128)(2,1)} %sar_hbm.3, f32[256,256]{1,0:T(8,128)} %depth_ref.1, f32[256,256]{1,0:T(8,128)} %slope_ref.3, f32[256,256]{1,0:T(8,128)} %rain_ref.3, s32[256,256]{1,0:T(8,128)} %dir_ref.3), custom_call_target="tpu_custom_call" | custom-call | tf_op jit(solution)/shard_map/edges/pallas_call | solution.py:475
  2.8 2.4 %collective-permute-start = (bf16[32,512]{1,0:T(8,128)(2,1)}, bf16[32,512]{1,0:T(8,128)(2,1)S(1)}, u32[]{:S(2)}, u32[]{:S(2)}) collective-permute-start(bf16[32,512]{1,0:T(8,128)(2,1)} %get-tuple-element.10), channel_id=1, source_target_pairs={{0,1},{1,2},{2,3},{3,4},{4,5},{5,6},{6,7},{7,8},{8,9},{9,10},{10,1... | collective-permute-start | bytes 98312 | tf_op jit(solution)/shard_map/ppermute | solution.py:489
  5.2 1.3 %collective-permute-start.1 = (bf16[32,512]{1,0:T(8,128)(2,1)}, bf16[32,512]{1,0:T(8,128)(2,1)S(1)}, u32[]{:S(2)}, u32[]{:S(2)}) collective-permute-start(bf16[32,512]{1,0:T(8,128)(2,1)} %get-tuple-element.11), channel_id=1, source_target_pairs={{1,0},{2,1},{3,2},{4,3},{5,4},{6,5},{7,6},{8,7},{9,8},{10,9},{11,1... | collective-permute-start | bytes 98312 | tf_op jit(solution)/shard_map/ppermute | solution.py:490
  6.5 0.0 collective-permute-done.above_ref.from_left_ref
  6.5 4.1 %collective-permute-done.1.below_ref.from_right_ref = bf16[32,512]{1,0:T(8,128)(2,1)S(1)} collective-permute-done((bf16[32,512]{1,0:T(8,128)(2,1)}, bf16[32,512]{1,0:T(8,128)(2,1)S(1)}, u32[]{:S(2)}, u32[]{:S(2)}) %collective-permute-start.1) | collective-permute-done | bytes 32800 | tf_op jit(solution)/shard_map/ppermute | solution.py:490
  10.6 0.0 copy-start.9
  10.6 0.0 copy-start.10
  10.6 0.0 copy-start.11
  10.6 0.0 copy-start.12
  10.6 0.0 copy-done.4
  10.6 0.0 copy-done.6
  10.7 0.0 copy-done.5
  10.7 0.0 copy-done.7
  10.7 0.0 copy-done.8
  10.7 0.6 %copy-done.9 = bf16[16,2,3,3]{0,1,3,2:T(2,128)(2,1)S(1)} copy-done((bf16[16,2,3,3]{0,1,3,2:T(2,128)(2,1)S(1)}, bf16[16,2,3,3]{0,1,3,2:T(2,128)(2,1)}, u32[]{:S(2)}) %copy-start.9) | copy-done | bytes 600
  11.3 0.0 copy-done.10
  11.3 0.0 copy-done.11
  11.3 0.0 copy-done.12
  11.3 0.0 copy-start.2
  11.3 0.0 copy-start.3
  11.3 9.1 %swath.1 = (bf16[64,512]{1,0:T(8,128)(2,1)}, bf16[1280,128]{1,0:T(8,128)(2,1)S(1)}) custom-call(bf16[32,512]{1,0:T(8,128)(2,1)S(1)} %collective-permute-done.above_ref.from_left_ref, bf16[32,512]{1,0:T(8,128)(2,1)S(1)} %collective-permute-done.1.below_ref.from_right_ref, bf16[2,64,512]{2,1,0:T(8,128)(2,1)S(1)} %copy-done.4, ...), custom_call_target="tpu_custom_call" | custom-call | tf_op jit(solution)/shard_map/swath/pallas_call | solution.py:503
  20.5 0.0 copy-start
  20.5 0.0 copy-start.1
  20.5 20.6 %all_to_all.5 = bf16[32,40,128]{2,1,0:T(8,128)(2,1)S(1)} all-to-all(bf16[32,40,128]{2,1,0:T(8,128)(2,1)S(1)} %bitcast.15), channel_id=1, replica_groups=mesh['tx'=8,'ty'=4] {'tx','ty'}, dimensions={0} | all-to-all | bytes 655360 | tf_op jit(solution)/shard_map/all_to_all | solution.py:531
  41.1 0.0 copy-done.2
  41.1 0.0 copy-done.3
  41.1 0.0 copy-done
  41.1 0.0 copy-done.1
  41.2 1.6 %level.1 = (f32[256,256]{1,0:T(8,128)S(1)}, f32[4,256,128]{2,1,0:T(8,128)S(1)}, bf16[32,384]{1,0:T(8,128)(2,1)S(1)}, bf16[32,384]{1,0:T(8,128)(2,1)S(1)}) custom-call(bf16[1280,128]{1,0:T(8,128)(2,1)S(1)} %bitcast.14, bf16[32,512]{1,0:T(8,128)(2,1)S(1)} %collective-permute-done.above_ref.from_left_ref, ...), custom_call_target="tpu_custom_call" | custom-call | tf_op jit(solution)/shard_map/level/pallas_call | solution.py:538
  42.8 2.7 %collective-permute-start.2 = (bf16[32,384]{1,0:T(8,128)(2,1)S(1)}, bf16[32,384]{1,0:T(8,128)(2,1)S(1)}, u32[]{:S(2)}, u32[]{:S(2)}) collective-permute-start(bf16[32,384]{1,0:T(8,128)(2,1)S(1)} %get-tuple-element.16), channel_id=1, source_target_pairs={{0,4},{4,8},{8,12},{12,16},{16,20},{20,24},{24,28},{1,5},{5,9},{9,... | collective-permute-start | bytes 73736 | tf_op jit(solution)/shard_map/ppermute | solution.py:553
  45.5 1.5 %collective-permute-start.3 = (bf16[32,384]{1,0:T(8,128)(2,1)S(1)}, bf16[32,384]{1,0:T(8,128)(2,1)S(1)}, u32[]{:S(2)}, u32[]{:S(2)}) collective-permute-start(bf16[32,384]{1,0:T(8,128)(2,1)S(1)} %get-tuple-element.17), channel_id=1, source_target_pairs={{4,0},{8,4},{12,8},{16,12},{20,16},{24,20},{28,24},{5,1},{9,5},{13... | collective-permute-start | bytes 73736 | tf_op jit(solution)/shard_map/ppermute | solution.py:554
  47.0 0.0 collective-permute-done.2.above_ref
  47.0 4.2 %collective-permute-done.3.below_ref = bf16[32,384]{1,0:T(8,128)(2,1)S(1)} collective-permute-done((bf16[32,384]{1,0:T(8,128)(2,1)S(1)}, bf16[32,384]{1,0:T(8,128)(2,1)S(1)}, u32[]{:S(2)}, u32[]{:S(2)}) %collective-permute-start.3) | collective-permute-done | bytes 24608 | tf_op jit(solution)/shard_map/ppermute | solution.py:554
  51.3 5.3 %flow.1 = f32[256,256]{1,0:T(8,128)} custom-call(f32[256,256]{1,0:T(8,128)S(1)} %get-tuple-element.14.level_ref, f32[4,256,128]{2,1,0:T(8,128)S(1)} %get-tuple-element.15.side_ref, f32[256,256]{1,0:T(8,128)S(1)} %copy-done, s32[256,256]{1,0:T(8,128)S(1)} %copy-done.2, f32[256,256]{1,0:T(8,128)S(1)} %copy-done.1, ...), custom_call_target="tpu_custom_call" | custom-call | tf_op jit(solution)/shard_map/flow/pallas_call | solution.py:556
Async XLA Ops:
  0.6 10.0 %copy-start.4 = (bf16[2,64,512]{2,1,0:T(8,128)(2,1)S(1)}, bf16[2,64,512]{2,1,0:T(8,128)(2,1)}, u32[]{:S(2)}) copy-start(bf16[2,64,512]{2,1,0:T(8,128)(2,1)} %sar_hbm.3) | copy-start | bytes 393220
  0.6 10.0 %copy-start.6 = (s32[64,512]{1,0:T(8,128)S(1)}, s32[64,512]{1,0:T(8,128)}, u32[]{:S(2)}) copy-start(s32[64,512]{1,0:T(8,128)} %cell_hbm.1) | copy-start | bytes 393220
  0.7 10.0 %copy-start.5 = (f32[64,512]{1,0:T(8,128)S(1)}, f32[64,512]{1,0:T(8,128)}, u32[]{:S(2)}) copy-start(f32[64,512]{1,0:T(8,128)} %gw_hbm.1) | copy-start | bytes 393220
  0.7 10.0 %copy-start.7 = (bf16[16,16,3,3]{1,0,3,2:T(8,128)(2,1)S(1)}, bf16[16,16,3,3]{1,0,3,2:T(8,128)(2,1)}, u32[]{:S(2)}) copy-start(bf16[16,16,3,3]{1,0,3,2:T(8,128)(2,1)} %param.15) | copy-start | bytes 13828
  0.7 10.0 %copy-start.8 = (bf16[16,16,3,3]{1,0,3,2:T(8,128)(2,1)S(1)}, bf16[16,16,3,3]{1,0,3,2:T(8,128)(2,1)}, u32[]{:S(2)}) copy-start(bf16[16,16,3,3]{1,0,3,2:T(8,128)(2,1)} %param.16) | copy-start | bytes 13828
  2.8 3.7 %collective-permute-start = (bf16[32,512]{1,0:T(8,128)(2,1)}, bf16[32,512]{1,0:T(8,128)(2,1)S(1)}, u32[]{:S(2)}, u32[]{:S(2)}) collective-permute-start(bf16[32,512]{1,0:T(8,128)(2,1)} %get-tuple-element.10), channel_id=1, source_target_pairs={{0,1},{1,2},{2,3},{3,4},{4,5},{5,6},{6,7},{7,8},{8,9},{9,10},{10,1... | collective-permute-start | bytes 98312 | tf_op jit(solution)/shard_map/ppermute | solution.py:489
  5.2 5.4 %collective-permute-start.1 = (bf16[32,512]{1,0:T(8,128)(2,1)}, bf16[32,512]{1,0:T(8,128)(2,1)S(1)}, u32[]{:S(2)}, u32[]{:S(2)}) collective-permute-start(bf16[32,512]{1,0:T(8,128)(2,1)} %get-tuple-element.11), channel_id=1, source_target_pairs={{1,0},{2,1},{3,2},{4,3},{5,4},{6,5},{7,6},{8,7},{9,8},{10,9},{11,1... | collective-permute-start | bytes 98312 | tf_op jit(solution)/shard_map/ppermute | solution.py:490
  10.6 0.7 %copy-start.9 = (bf16[16,2,3,3]{0,1,3,2:T(2,128)(2,1)S(1)}, bf16[16,2,3,3]{0,1,3,2:T(2,128)(2,1)}, u32[]{:S(2)}) copy-start(bf16[16,2,3,3]{0,1,3,2:T(2,128)(2,1)} %param.14) | copy-start | bytes 1732
  10.6 0.7 %copy-start.10 = (bf16[1,16,3,3]{1,3,2,0:T(4,128)(2,1)S(1)}, bf16[1,16,3,3]{1,3,2,0:T(4,128)(2,1)}, u32[]{:S(2)}) copy-start(bf16[1,16,3,3]{1,3,2,0:T(4,128)(2,1)} %param.17) | copy-start | bytes 868
  10.6 0.7 %copy-start.11 = (s32[64,1]{0,1:T(1,128)S(1)}, s32[64,1]{0,1:T(1,128)}, u32[]{:S(2)}) copy-start(s32[64,1]{0,1:T(1,128)} %param.20) | copy-start | bytes 772
  10.6 0.7 %copy-start.12 = (s32[64,1]{0,1:T(1,128)S(1)}, s32[64,1]{0,1:T(1,128)}, u32[]{:S(2)}) copy-start(s32[64,1]{0,1:T(1,128)} %param.21) | copy-start | bytes 772
  11.3 29.8 %copy-start.2 = (s32[256,256]{1,0:T(8,128)S(1)}, s32[256,256]{1,0:T(8,128)}, u32[]{:S(2)}) copy-start(s32[256,256]{1,0:T(8,128)} %dir_ref.3) | copy-start | bytes 786436
  11.3 29.8 %copy-start.3 = (f32[256,256]{1,0:T(8,128)S(1)}, f32[256,256]{1,0:T(8,128)}, u32[]{:S(2)}) copy-start(f32[256,256]{1,0:T(8,128)} %depth_ref.1) | copy-start | bytes 786436
  20.5 20.7 %copy-start = (f32[256,256]{1,0:T(8,128)S(1)}, f32[256,256]{1,0:T(8,128)}, u32[]{:S(2)}) copy-start(f32[256,256]{1,0:T(8,128)} %slope_ref.3) | copy-start | bytes 786436
  20.5 20.7 %copy-start.1 = (f32[256,256]{1,0:T(8,128)S(1)}, f32[256,256]{1,0:T(8,128)}, u32[]{:S(2)}) copy-start(f32[256,256]{1,0:T(8,128)} %rain_ref.3) | copy-start | bytes 786436
  42.8 4.3 %collective-permute-start.2 = (bf16[32,384]{1,0:T(8,128)(2,1)S(1)}, bf16[32,384]{1,0:T(8,128)(2,1)S(1)}, u32[]{:S(2)}, u32[]{:S(2)}) collective-permute-start(bf16[32,384]{1,0:T(8,128)(2,1)S(1)} %get-tuple-element.16), channel_id=1, source_target_pairs={{0,4},{4,8},{8,12},{12,16},{16,20},{20,24},{24,28},{1,5},{5,9},{9,... | collective-permute-start | bytes 73736 | tf_op jit(solution)/shard_map/ppermute | solution.py:553
  45.5 5.7 %collective-permute-start.3 = (bf16[32,384]{1,0:T(8,128)(2,1)S(1)}, bf16[32,384]{1,0:T(8,128)(2,1)S(1)}, u32[]{:S(2)}, u32[]{:S(2)}) collective-permute-start(bf16[32,384]{1,0:T(8,128)(2,1)S(1)} %get-tuple-element.17), channel_id=1, source_target_pairs={{4,0},{8,4},{12,8},{16,12},{20,16},{24,20},{28,24},{5,1},{9,5},{13... | collective-permute-start | bytes 73736 | tf_op jit(solution)/shard_map/ppermute | solution.py:554

commit v5 on v4

--- a/solution.py
+++ b/solution.py
@@ -110,29 +110,19 @@
     return [both[0:8, 0:cols], both[0:8, cols:], both[8:16, 0:cols], both[8:16, cols:]]
 
 
-def swath_kernel(
+def prep_kernel(
     devices, capacity,
-    above_ref, below_ref,
-    sar_hbm, k1_hbm, k2_hbm, k3_hbm, k4_hbm, gw_hbm, cell_hbm, tile_hbm, row_hbm,
-    frac_ref, send_ref,
-    sar_ref, k1_ref, k2_ref, k3_ref, k4_ref, gw_ref, cell_ref, tile_ref, row_ref, sems,
-    s_ref, xa_ref, xb_ref, x3_ref, w2_ref, w3_ref, w1_ref, t1_ref, t4_ref, logit_ref, obs_ref, wnd_ref,
+    k1_hbm, k2_hbm, k3_hbm, k4_hbm, tile_hbm, row_hbm,
+    w1_ref, w2_ref, w3_ref, w4_ref, perm_ref, extra_ref,
+    k1_ref, k2_ref, k3_ref, k4_ref, tile_ref, row_ref, sems, t1_ref, t4_ref,
 ):
     pairs = (
-        (k1_hbm, k1_ref), (k2_hbm, k2_ref), (k3_hbm, k3_ref), (k4_hbm, k4_ref), (sar_hbm, sar_ref),
-        (gw_hbm, gw_ref), (cell_hbm, cell_ref), (tile_hbm, tile_ref), (row_hbm, row_ref),
+        (k1_hbm, k1_ref), (k2_hbm, k2_ref), (k3_hbm, k3_ref), (k4_hbm, k4_ref),
+        (tile_hbm, tile_ref), (row_hbm, row_ref),
     )
     copies = [pltpu.make_async_copy(src, dst, sems.at[i]) for i, (src, dst) in enumerate(pairs)]
     for copy in copies:
         copy.start()
-    lines, px = gw_ref.shape
-    blocks = (lines + 2 * HALO_LINES - 2) // OUT_LINES
-    frame = lines + 2 * HALO_LINES
-    total = xa_ref.shape[0] // CH
-    n_ty = lax.axis_size("ty")
-    me = lax.axis_index("tx") * n_ty + lax.axis_index("ty")
-    first = me == 0
-    last = me == devices - 1
     rows = OUT_LINES * CH
     cols = IN_LINES * CH
 
@@ -146,8 +136,7 @@
     tile4 = (rem(iota((CH, cols), 1), CH) == iota((CH, cols), 0)).astype(bf16)
     t1_ref[...] = jnp.zeros(t1_ref.shape, f32)
     t4_ref[...] = jnp.zeros(t4_ref.shape, f32)
-
-    for copy in copies[0:4]:
+    for copy in copies:
         copy.wait()
     for ky in range(3):
         for kx in range(3):
@@ -164,7 +153,7 @@
                     kx * CH : (kx + 1) * CH, i * cols : (i + 1) * cols
                 ].astype(bf16)
     wide4 = dot(t4_ref[...].astype(bf16), tile4)
-    w4 = jnp.concatenate(
+    w4_ref[...] = jnp.concatenate(
         [
             band_weights(
                 [jnp.broadcast_to(wide4[ky * 3 + kx : ky * 3 + kx + 1], (CH, cols)) for ky in range(3)],
@@ -175,6 +164,67 @@
         0,
     )
 
+    lines = tile_ref.shape[1]
+    tile = tile_ref[...].astype(f32)
+    same = iota((lines, lines), 0) == iota((lines, lines), 1)
+    tile_sub = jnp.sum(jnp.where(same, jnp.broadcast_to(tile, (lines, lines)), 0.0), 1, keepdims=True)
+    rival = (tile_sub == tile) & (iota((lines, lines), 0) < iota((lines, lines), 1))
+    slot = tile * capacity + jnp.sum(jnp.where(rival, 1.0, 0.0), 0, keepdims=True)
+    slots, wnd_rows = perm_ref.shape
+    per_line = wnd_rows // lines
+    widen = (quo(iota((lines, wnd_rows), 1), per_line) == iota((lines, wnd_rows), 0)).astype(bf16)
+    slot_wide = dot(jnp.broadcast_to(slot, (8, lines)).astype(bf16), widen)[0:1]
+    place = slot_wide.astype(jnp.int32) * 4 + rem(quo(iota((1, wnd_rows), 1), 4), 4)
+    perm_ref[...] = jnp.where(iota((slots, wnd_rows), 0) == place, 1.0, 0.0).astype(bf16)
+
+    row_of = dot(
+        jnp.where(same, jnp.broadcast_to(row_ref[...].astype(f32), (lines, lines)), 0.0).astype(bf16),
+        jnp.ones((lines, LANES), bf16),
+    )
+    perm_line = jnp.where(quo(iota((slots, lines), 0), 4) == slot.astype(jnp.int32), 1.0, 0.0).astype(bf16)
+    row_own = dot(perm_line, row_of.astype(bf16))
+    per_tile = 4 * capacity
+    lane = iota((slots, LANES), 1)
+    entry = rem(iota((slots, LANES), 0), per_tile)
+    info = jnp.zeros((slots, LANES), f32)
+    for turn, value in enumerate((row_own, of_right(row_own, per_tile), of_left(row_own, per_tile))):
+        info = jnp.where(lane == turn * per_tile + entry, value, info)
+    info = jnp.sum(info.reshape(devices, per_tile, LANES), 1, keepdims=True)
+    at = iota((devices, 8, LANES), 1)
+    extra_ref[...] = jnp.where(at == 2, info, 0.0).reshape(8 * devices, LANES)
+
+
+def of_right(x, per_tile):
+    return jnp.concatenate([x[per_tile:], jnp.zeros((per_tile, x.shape[1]), x.dtype)], 0)
+
+
+def of_left(x, per_tile):
+    return jnp.concatenate([jnp.zeros((per_tile, x.shape[1]), x.dtype), x[: x.shape[0] - per_tile]], 0)
+
+
+def swath_kernel(
+    devices, capacity,
+    above_ref, below_ref, w1_ref, w2_ref, w3_ref, w4_ref, perm_ref, extra_ref,
+    sar_hbm, gw_hbm, cell_hbm,
+    frac_ref, send_ref,
+    sar_ref, gw_ref, cell_ref, sems,
+    s_ref, xa_ref, xb_ref, x3_ref, logit_ref, obs_ref, wnd_ref,
+):
+    pairs = ((sar_hbm, sar_ref), (gw_hbm, gw_ref), (cell_hbm, cell_ref))
+    copies = [pltpu.make_async_copy(src, dst, sems.at[i]) for i, (src, dst) in enumerate(pairs)]
+    for copy in copies:
+        copy.start()
+    lines, px = gw_ref.shape
+    blocks = (lines + 2 * HALO_LINES - 2) // OUT_LINES
+    frame = lines + 2 * HALO_LINES
+    total = xa_ref.shape[0] // CH
+    n_ty = lax.axis_size("ty")
+    me = lax.axis_index("tx") * n_ty + lax.axis_index("ty")
+    first = me == 0
+    last = me == devices - 1
+    rows = OUT_LINES * CH
+    cols = IN_LINES * CH
+
     def clear(ref, lo, hi):
         ref[lo * CH : hi * CH, :] = jnp.zeros(((hi - lo) * CH, px), bf16)
 
@@ -192,11 +242,21 @@
         _, after = pixel_shifts(sums[2 * n : 3 * n])
         return before + sums[n : 2 * n] + after
 
+    def by_block(body):
+        def step(b, carry):
+            body(b)
+            return carry
+
+        lax.fori_loop(0, blocks, step, 0)
+
+    def lines_at(b, line, count):
+        return pl.ds(pl.multiple_of(b * rows + line * CH, CH), count)
+
     for ref, line in ((xa_ref, 1), (xb_ref, 2), (x3_ref, 3)):
         clear(ref, line + blocks * OUT_LINES, total)
     above = above_ref[16:32, :].astype(f32)
     below = below_ref[16:32, :].astype(f32)
-    copies[4].wait()
+    copies[0].wait()
     for ch in range(2):
         s_ref[ch, 0:HALO_LINES, :] = above[ch * HALO_LINES : (ch + 1) * HALO_LINES]
         s_ref[ch, HALO_LINES : HALO_LINES + lines, :] = sar_ref[ch].astype(f32)
@@ -211,19 +271,21 @@
     outside(xa_ref)
 
     for w_ref, src, dst, line in ((w2_ref, xa_ref, xb_ref, 2), (w3_ref, xb_ref, x3_ref, 3)):
-        for b in range(blocks):
-            at = line + b * OUT_LINES
-            sums = dot(w_ref[...], src[(at - 1) * CH : (at - 1) * CH + cols, :])
-            dst[at * CH : at * CH + rows, :] = jnp.maximum(merged(sums, rows), 0.0).astype(bf16)
+
+        def conv(b):
+            sums = dot(w_ref[...], src[lines_at(b, line - 1, cols), :])
+            dst[lines_at(b, line, rows), :] = jnp.maximum(merged(sums, rows), 0.0).astype(bf16)
+
+        by_block(conv)
         outside(dst)
 
     for b in range(blocks):
         at = HALO_LINES - 1 + b * OUT_LINES
-        sums = dot(w4, x3_ref[at * CH : at * CH + cols, :])
+        sums = dot(w4_ref[...], x3_ref[at * CH : at * CH + cols, :])
         logit_ref[b * OUT_LINES : b * OUT_LINES + CH, :] = merged(sums, CH)
     frac = (1.0 / (1.0 + jnp.exp(-logit_ref[0:lines, :]))).astype(bf16)
     frac_ref[...] = frac
-    for copy in copies[5:]:
+    for copy in copies[1:]:
         copy.wait()
     obs_ref[...] = frac.astype(f32) * gw_ref[...]
 
@@ -259,62 +321,32 @@
 
     lax.fori_loop(0, lines // group, window_group, 0)
 
-    tile = tile_ref[...].astype(f32)
-    same = iota((lines, lines), 0) == iota((lines, lines), 1)
-    tile_sub = jnp.sum(jnp.where(same, jnp.broadcast_to(tile, (lines, lines)), 0.0), 1, keepdims=True)
-    rival = (tile_sub == tile) & (iota((lines, lines), 0) < iota((lines, lines), 1))
-    slot = tile * capacity + jnp.sum(jnp.where(rival, 1.0, 0.0), 0, keepdims=True)
-    wnd_rows = wnd_ref.shape[0]
-    per_line = wnd_rows // lines
-    widen = (quo(iota((lines, wnd_rows), 1), per_line) == iota((lines, wnd_rows), 0)).astype(bf16)
-    slot_wide = dot(jnp.broadcast_to(slot, (8, lines)).astype(bf16), widen)[0:1]
-    place = slot_wide.astype(jnp.int32) * 4 + rem(quo(iota((1, wnd_rows), 1), 4), 4)
     per_tile = 4 * capacity
-    slots = devices * per_tile
-    perm = jnp.where(iota((slots, wnd_rows), 0) == place, 1.0, 0.0).astype(bf16)
+    slots, wnd_rows = perm_ref.shape
     tile_cols = 4 * quarter
     repeat = (rem(iota((quarter, tile_cols), 1), quarter) == iota((quarter, tile_cols), 0)).astype(bf16)
     tiled = dot(wnd_ref[...].astype(bf16), repeat)
     mine = rem(iota((wnd_rows, tile_cols), 0), 4) == quo(iota((wnd_rows, tile_cols), 1), quarter)
-    by_slot = dot(perm, jnp.where(mine, tiled, 0.0).astype(bf16))
-    row_of = dot(
-        jnp.where(same, jnp.broadcast_to(row_ref[...].astype(f32), (lines, lines)), 0.0).astype(bf16),
-        jnp.ones((lines, LANES), bf16),
-    )
-    perm_line = jnp.where(quo(iota((slots, lines), 0), 4) == slot.astype(jnp.int32), 1.0, 0.0).astype(bf16)
-    row_own = dot(perm_line, row_of.astype(bf16))
-
-    none = jnp.zeros((per_tile, LANES), f32)
-
-    def of_right(x):
-        return jnp.concatenate([x[per_tile:], none], 0)
-
-    def of_left(x):
-        return jnp.concatenate([none, x[: slots - per_tile]], 0)
-
+    by_slot = dot(perm_ref[...], jnp.where(mine, tiled, 0.0).astype(bf16))
     h = SUBSTEPS
-    lane = iota((slots, LANES), 1)
     entry = rem(iota((slots, LANES), 0), per_tile)
+    here = quo(iota((slots, LANES), 1), h) == entry
     column = rem(quo(iota((slots, LANES), 0), per_tile), n_ty)
     source = iota((LANES, LANES), 0)
-    target = iota((LANES, LANES), 1)
-    take_first = ((source < h) & (rem(target, h) == source)).astype(bf16)
-    take_last = ((source >= LANES - h) & (rem(target, h) == source - (LANES - h))).astype(bf16)
-    right_strip = dot(of_right(by_slot[:, 0:LANES]).astype(bf16), take_first)
-    left_strip = dot(of_left(by_slot[:, tile_cols - LANES :]).astype(bf16), take_last)
-    right_strip = jnp.where((quo(lane, h) == entry) & (column < n_ty - 1), right_strip, 0.0)
-    left_strip = jnp.where((quo(lane, h) == entry) & (column > 0), left_strip, 0.0)
-    info = jnp.zeros((slots, LANES), f32)
-    for turn, value in enumerate((row_own, of_right(row_own), of_left(row_own))):
-        info = jnp.where(lane == turn * per_tile + entry, value, info)
-    extra_row = iota((8 * devices, slots), 0)
-    extra_tile = quo(iota((8 * devices, slots), 1), per_tile)
-    extra = sum(
-        dot((extra_row == 8 * extra_tile + r).astype(bf16), x.astype(bf16))
-        for r, x in enumerate((right_strip, left_strip, info))
-    )
+    spot = rem(iota((LANES, LANES), 1), h)
+
+    def strip(x, first_lane, keep):
+        take = ((spot + first_lane == source) & (source - first_lane < h)).astype(bf16)
+        x = jnp.where(here & keep, dot(x.astype(bf16), take), 0.0)
+        return jnp.sum(x.reshape(devices, per_tile, LANES), 1, keepdims=True)
+
+    right_strip = strip(of_right(by_slot[:, 0:LANES], per_tile), 0, column < n_ty - 1)
+    left_strip = strip(of_left(by_slot[:, tile_cols - LANES :], per_tile), LANES - h, column > 0)
+    at = iota((devices, 8, LANES), 1)
+    extra = extra_ref[...].reshape(devices, 8, LANES)
+    extra = jnp.where(at == 0, right_strip, jnp.where(at == 1, left_strip, extra))
     halves = [by_slot[:, at : at + LANES].reshape(devices, per_tile, LANES) for at in range(0, tile_cols, LANES)]
-    packed = jnp.concatenate([*halves, extra.reshape(devices, 8, LANES)], 1)
+    packed = jnp.concatenate([*halves, extra], 1)
     send_ref[...] = packed.reshape(send_ref.shape).astype(bf16)
 
 
@@ -346,13 +378,13 @@
 
     lane = iota((1, k), 1)
     offset = rem(lane, 2) + tile_rows * rem(quo(lane, 2), 2)
-    own_source = iota((8 * devices, k), 0) == 8 * quo(iota((8 * devices, k), 1), n) + 2
-    info = extra.reshape(8 * devices, LANES).astype(bf16)
+    info = jnp.broadcast_to(extra[:, 2:3], (devices, n, LANES)).reshape(k, LANES)
+    info = jnp.where(rem(iota((k, LANES), 1), n) == entry, info, 0.0).astype(bf16)
+    turns = (quo(iota((LANES, LANES), 0), n) == iota((LANES, LANES), 1)).astype(bf16)
+    lines = transposed(dot(info, turns))
 
     def placer(turn):
-        pick = (iota((LANES, k), 0) == turn * n + rem(iota((LANES, k), 1), n)).astype(bf16)
-        line = jnp.sum(jnp.where(own_source, dot(info, pick), 0.0), 0, keepdims=True)
-        target = line.astype(jnp.int32) + offset
+        target = lines[turn : turn + 1].astype(jnp.int32) + offset
         return jnp.where(iota((2 * tile_rows, k), 0) == target, 1.0, 0.0).astype(bf16)
 
     summed = dot(placer(0), main.astype(bf16))
@@ -406,10 +438,10 @@
         return jnp.concatenate([above_ref[...].astype(f32)[at], mid, below_ref[...].astype(f32)[at]], 0)
 
     zeros = jnp.zeros((h, wide_cols), f32)
-    for buf in range(2):
-        for ref in (up_ref, down_ref):
-            ref[buf, 0:h, :] = zeros
-            ref[buf, h + wide_rows :, :] = zeros
+    for ref in (up_ref, down_ref):
+        ref[0] = jnp.zeros(ref.shape[1:], f32)
+        ref[1, 0:h, :] = zeros
+        ref[1, h + wide_rows :, :] = zeros
     part_ref[0] = widened(0, level_ref[...])
     rain_s[...] = widened(1, rain_ref[...])
     conv = widened(2, runoff_coef * jnp.sqrt(slope_ref[...]))
@@ -422,16 +454,13 @@
 
     chunk = 16
 
-    def level_at(buf, r, n, step):
+    def level_at(buf, r, n):
         level = part_ref[buf, r : r + n, :]
-        if step:
-            level = level + up_ref[buf, h + r + 1 : h + r + 1 + n, :] + down_ref[buf, h + r - 1 : h + r - 1 + n, :]
-        return level
-
-    for step in range(SUBSTEPS):
-        buf, new = step % 2, (step + 1) % 2
+        return level + up_ref[buf, h + r + 1 : h + r + 1 + n, :] + down_ref[buf, h + r - 1 : h + r - 1 + n, :]
+
+    def substep(buf, new):
         for r in range(0, wide_rows, chunk):
-            level = level_at(buf, r, chunk, step)
+            level = level_at(buf, r, chunk)
             power = level * jnp.exp((2.0 / 3.0) * jnp.log(jnp.maximum(jnp.abs(level), 1e-30)))
             from_right = pltpu.roll(power, wide_cols - 1, 1)
             from_left = pltpu.roll(power, 1, 1)
@@ -442,8 +471,14 @@
                 level + rain_s[r : r + chunk, :] - conv_s[r : r + chunk, :] * power
                 + (m[3] * from_right + m[4] * from_left)
             )
-    buf = SUBSTEPS % 2
-    out_ref[...] = level_at(buf, h, tile_rows, SUBSTEPS)[:, 0:tile_cols]
+
+    def substep_pair(i, carry):
+        substep(0, 1)
+        substep(1, 0)
+        return carry
+
+    lax.fori_loop(0, SUBSTEPS // 2, substep_pair, 0)
+    out_ref[...] = level_at(0, h, tile_rows)[:, 0:tile_cols]
 
 
 def hbm_specs(n):
@@ -492,41 +527,60 @@
     feats = (az_lines + 2 * HALO_LINES + 4) * CH
     rows, cols = OUT_LINES * CH, IN_LINES * CH
     send_rows = tile_cols // LANES * 4 * capacity + 8
-    inputs = (
-        sar_image,
+    slots = devices * capacity * 4
+    wnd_rows = CH * az_lines
+    fixed = (
         jnp.transpose(kernel_first, (2, 3, 1, 0)),
         jnp.transpose(kernel_second, (2, 3, 0, 1)).reshape(9 * CH, CH),
         jnp.transpose(kernel_third, (2, 3, 0, 1)).reshape(9 * CH, CH),
         jnp.transpose(kernel_last[0], (1, 2, 0)),
-        geo_weight, cell_index, block_tile.reshape(1, az_lines), block_row.reshape(1, az_lines),
+        block_tile.reshape(1, az_lines), block_row.reshape(1, az_lines),
     )
+    prepared = pl.pallas_call(
+        functools.partial(prep_kernel, devices, capacity),
+        out_shape=(
+            jax.ShapeDtypeStruct((rows, LANES), bf16),
+            jax.ShapeDtypeStruct((3 * rows, cols), bf16),
+            jax.ShapeDtypeStruct((3 * rows, cols), bf16),
+            jax.ShapeDtypeStruct((3 * CH, cols), bf16),
+            jax.ShapeDtypeStruct((slots, wnd_rows), bf16),
+            jax.ShapeDtypeStruct((8 * devices, LANES), f32),
+        ),
+        in_specs=hbm_specs(6),
+        out_specs=tuple(vmem_specs(6)),
+        scratch_shapes=[
+            *[pltpu.VMEM(x.shape, x.dtype) for x in fixed],
+            pltpu.SemaphoreType.DMA((6,)),
+            pltpu.VMEM((24, CH), f32),
+            pltpu.VMEM((16, CH), f32),
+        ],
+        compiler_params=params,
+        cost_estimate=pl.CostEstimate(flops=2_000_000_000, bytes_accessed=4_000_000, transcendentals=0),
+        name="prep",
+    )(*fixed)
+    inputs = (sar_image, geo_weight, cell_index)
     fraction, send = pl.pallas_call(
         functools.partial(swath_kernel, devices, capacity),
         out_shape=(
             jax.ShapeDtypeStruct((az_lines, range_px), bf16),
             jax.ShapeDtypeStruct((devices * send_rows, LANES), bf16),
         ),
-        in_specs=vmem_specs(2) + hbm_specs(9),
+        in_specs=vmem_specs(8) + hbm_specs(3),
         out_specs=tuple(vmem_specs(2)),
         scratch_shapes=[
             *[pltpu.VMEM(x.shape, x.dtype) for x in inputs],
-            pltpu.SemaphoreType.DMA((9,)),
+            pltpu.SemaphoreType.DMA((3,)),
             pltpu.VMEM((2, az_lines + 2 * HALO_LINES + 8, range_px), f32),
             pltpu.VMEM((feats, range_px), bf16),
             pltpu.VMEM((feats, range_px), bf16),
             pltpu.VMEM((feats, range_px), bf16),
-            pltpu.VMEM((3 * rows, cols), bf16),
-            pltpu.VMEM((3 * rows, cols), bf16),
-            pltpu.VMEM((rows, LANES), bf16),
-            pltpu.VMEM((24, CH), f32),
-            pltpu.VMEM((16, CH), f32),
             pltpu.VMEM((az_lines + 2 * CH, range_px), f32),
             pltpu.VMEM((az_lines, range_px), f32),
-            pltpu.VMEM((CH * az_lines, tile_cols // 4), f32),
+            pltpu.VMEM((wnd_rows, tile_cols // 4), f32),
         ],
         compiler_params=params,
         name="swath",
-    )(from_previous, from_next, *inputs)
+    )(from_previous, from_next, *prepared, *inputs)
 
     got = lax.all_to_all(
         send.reshape(devices, send_rows, LANES), both, split_axis=0, concat_axis=0, tiled=True

time: 56.8 us -> 55.6 us (0.979)
  waiting for transfers between devices: 8.38 us -> 6.36 us
  Pallas kernels: 18.2 us -> 19.1 us
    ppermute x1, waiting for transfers between devices: 4.14 us -> 1.94 us  [per_device(): from_next = lax.ppermute(to_previous, both, down)]
    pallas_call x0 -> x1, Pallas kernels: none -> 1.46 us  [per_device(): pl.pallas_call(functools.partial(prep_kernel, devices, capacity), out_sha...]
    pallas_call x1, Pallas kernels: 1.63 us -> 0.91 us  [per_device(): pl.pallas_call(functools.partial(level_kernel, devices), out_shape=(jax.S...]
  transfers between devices with their start and end apart: 4 -> 4, of which waited for: 2 -> 3; matrix products, arithmetic and copies ran while one was open for 0% -> 0% of each run, Pallas kernels for 0% -> 3%
where the time goes in v5:
time: 55.6 us; the launch traced here: 55.3 us
  blocking collectives  20.6 us (37%)
  Pallas kernels  19.1 us (34%)
  starting transfers between devices  7.69 us (14%)
  waiting for transfers between devices  6.36 us (11%)
  between operations  0.83 us (1%)
  local copies, waits for them, and re-layouts  0.7 us (1%)
    all_to_all x1, blocking collectives, per_device(): lax.all_to_all(send.reshape(devices, send_rows, LANES), both, split_axis=...  20.6 us
    pallas_call x1, Pallas kernels, per_device(): pl.pallas_call(functools.partial(swath_kernel, devices, capacity), out_sh...  9.3 us
    pallas_call x1, Pallas kernels, per_device(): pl.pallas_call(flow_kernel, out_shape=jax.ShapeDtypeStruct((tile_rows, ti...  5.35 us
    ppermute x1, waiting for transfers between devices, per_device(): below = lax.ppermute(top_rows, 'tx', down)  4.22 us
    ppermute x1, starting transfers between devices, per_device(): above = lax.ppermute(bot_rows, 'tx', up)  2.75 us
    ppermute x1, starting transfers between devices, per_device(): from_previous = lax.ppermute(to_next, both, up)  2.36 us
    pallas_call x1, Pallas kernels, per_device(): pl.pallas_call(edge_kernel, out_shape=(message, message), in_specs=hbm_sp...  2.06 us
    ppermute x1, waiting for transfers between devices, per_device(): from_next = lax.ppermute(to_previous, both, down)  1.94 us
  transfers between devices with their start and end apart: 4, of which 3 were waited for; matrix products, arithmetic and copies ran while one was open for 0% of the time, Pallas kernels for 3%

profile of v5, /device:TPU:0, one launch (start us, length us, event | category | flops | bytes accessed | tf_op | source)
XLA Modules:
  0.0 55.3 jit_solution(15017378885686534939)
XLA Ops:
  0.6 0.0 copy-start.8
  0.6 0.0 copy-start.7
  0.6 2.1 %edges.1 = (bf16[32,512]{1,0:T(8,128)(2,1)}, bf16[32,512]{1,0:T(8,128)(2,1)}) custom-call(bf16[2,64,512]{2,1,0:T(8,128)(2,1)} %sar_hbm.3, f32[256,256]{1,0:T(8,128)} %depth_ref.1, f32[256,256]{1,0:T(8,128)} %slope_ref.3, f32[256,256]{1,0:T(8,128)} %rain_ref.3, s32[256,256]{1,0:T(8,128)} %dir_ref.3), custom_call_target="tpu_custom_call" | custom-call | tf_op jit(solution)/shard_map/edges/pallas_call | solution.py:510
  2.7 2.4 %collective-permute-start = (bf16[32,512]{1,0:T(8,128)(2,1)}, bf16[32,512]{1,0:T(8,128)(2,1)S(1)}, u32[]{:S(2)}, u32[]{:S(2)}) collective-permute-start(bf16[32,512]{1,0:T(8,128)(2,1)} %get-tuple-element.16), channel_id=1, source_target_pairs={{0,1},{1,2},{2,3},{3,4},{4,5},{5,6},{6,7},{7,8},{8,9},{9,10},{10,1... | collective-permute-start | bytes 98312 | tf_op jit(solution)/shard_map/ppermute | solution.py:524
  5.1 1.3 %collective-permute-start.1 = (bf16[32,512]{1,0:T(8,128)(2,1)}, bf16[32,512]{1,0:T(8,128)(2,1)S(1)}, u32[]{:S(2)}, u32[]{:S(2)}) collective-permute-start(bf16[32,512]{1,0:T(8,128)(2,1)} %get-tuple-element.17), channel_id=1, source_target_pairs={{1,0},{2,1},{3,2},{4,3},{5,4},{6,5},{7,6},{8,7},{9,8},{10,9},{11,1... | collective-permute-start | bytes 98312 | tf_op jit(solution)/shard_map/ppermute | solution.py:525
  6.4 0.0 copy-start.9
  6.4 0.0 copy-start.10
  6.4 0.0 copy-start.11
  6.4 0.0 copy-start.12
  6.4 0.0 copy-done.8
  6.4 0.0 copy-done.7
  6.4 0.6 %copy-done.9 = bf16[16,2,3,3]{0,1,3,2:T(2,128)(2,1)S(1)} copy-done((bf16[16,2,3,3]{0,1,3,2:T(2,128)(2,1)S(1)}, bf16[16,2,3,3]{0,1,3,2:T(2,128)(2,1)}, u32[]{:S(2)}) %copy-start.9) | copy-done | bytes 600
  7.1 0.0 copy-done.10
  7.1 0.0 copy-done.11
  7.1 0.0 copy-done.12
  7.1 0.0 copy-start.4
  7.1 0.0 copy-start.5
  7.1 0.0 copy-start.6
  7.1 1.5 %prep.1 = (bf16[224,128]{1,0:T(8,128)(2,1)S(1)}, bf16[672,256]{1,0:T(8,128)(2,1)S(1)}, bf16[672,256]{1,0:T(8,128)(2,1)S(1)}, bf16[48,256]{1,0:T(8,128)(2,1)S(1)}...) custom-call(bf16[3,3,2,16]{3,2,1,0:T(2,128)(2,1)S(1)} %bitcast.18, bf16[144,16]{1,0:T(8,128)(2,1)S(1)} %bitcast.16, ...), custom_call_target="tpu_custom_call" | custom-call | flops 2000000000 | bytes 4000000 | tf_op jit(solution)/shard_map/prep/pallas_call | solution.py:539
  8.6 0.0 collective-permute-done.above_ref.from_left_ref
  8.6 1.9 %collective-permute-done.1.below_ref.from_right_ref = bf16[32,512]{1,0:T(8,128)(2,1)S(1)} collective-permute-done((bf16[32,512]{1,0:T(8,128)(2,1)}, bf16[32,512]{1,0:T(8,128)(2,1)S(1)}, u32[]{:S(2)}, u32[]{:S(2)}) %collective-permute-start.1) | collective-permute-done | bytes 32800 | tf_op jit(solution)/shard_map/ppermute | solution.py:525
  10.5 0.0 copy-done.4
  10.5 0.0 copy-done.5
  10.5 0.0 copy-done.6
  10.5 0.0 copy-start.2
  10.5 0.0 copy-start.3
  10.6 9.3 %swath.1 = (bf16[64,512]{1,0:T(8,128)(2,1)}, bf16[1280,128]{1,0:T(8,128)(2,1)S(1)}) custom-call(bf16[32,512]{1,0:T(8,128)(2,1)S(1)} %collective-permute-done.above_ref.from_left_ref, bf16[32,512]{1,0:T(8,128)(2,1)S(1)} %collective-permute-done.1.below_ref.from_right_ref, bf16[224,128]{1,0:T(8,128)(2,1)S(1)} %get-tuple-element.18.w1_ref, ...), custom_call_target="tpu_custom_call" | custom-call | tf_op jit(solution)/shard_map/swath/pallas_call | solution.py:562
  19.9 0.0 copy-start
  19.9 0.0 copy-start.1
  19.9 20.6 %all_to_all.5 = bf16[32,40,128]{2,1,0:T(8,128)(2,1)S(1)} all-to-all(bf16[32,40,128]{2,1,0:T(8,128)(2,1)S(1)} %bitcast.15), channel_id=1, replica_groups=mesh['tx'=8,'ty'=4] {'tx','ty'}, dimensions={0} | all-to-all | bytes 655360 | tf_op jit(solution)/shard_map/all_to_all | solution.py:585
  40.5 0.0 copy-done.2
  40.5 0.0 copy-done.3
  40.5 0.0 copy-done
  40.5 0.0 copy-done.1
  40.5 0.9 %level.1 = (f32[256,256]{1,0:T(8,128)S(1)}, f32[4,256,128]{2,1,0:T(8,128)S(1)}, bf16[32,384]{1,0:T(8,128)(2,1)S(1)}, bf16[32,384]{1,0:T(8,128)(2,1)S(1)}) custom-call(bf16[1280,128]{1,0:T(8,128)(2,1)S(1)} %bitcast.14, bf16[32,512]{1,0:T(8,128)(2,1)S(1)} %collective-permute-done.above_ref.from_left_ref, ...), custom_call_target="tpu_custom_call" | custom-call | tf_op jit(solution)/shard_map/level/pallas_call | solution.py:592
  41.5 2.7 %collective-permute-start.2 = (bf16[32,384]{1,0:T(8,128)(2,1)S(1)}, bf16[32,384]{1,0:T(8,128)(2,1)S(1)}, u32[]{:S(2)}, u32[]{:S(2)}) collective-permute-start(bf16[32,384]{1,0:T(8,128)(2,1)S(1)} %get-tuple-element.28), channel_id=1, source_target_pairs={{0,4},{4,8},{8,12},{12,16},{16,20},{20,24},{24,28},{1,5},{5,9},{9,... | collective-permute-start | bytes 73736 | tf_op jit(solution)/shard_map/ppermute | solution.py:607
  44.2 1.3 %collective-permute-start.3 = (bf16[32,384]{1,0:T(8,128)(2,1)S(1)}, bf16[32,384]{1,0:T(8,128)(2,1)S(1)}, u32[]{:S(2)}, u32[]{:S(2)}) collective-permute-start(bf16[32,384]{1,0:T(8,128)(2,1)S(1)} %get-tuple-element.29), channel_id=1, source_target_pairs={{4,0},{8,4},{12,8},{16,12},{20,16},{24,20},{28,24},{5,1},{9,5},{13... | collective-permute-start | bytes 73736 | tf_op jit(solution)/shard_map/ppermute | solution.py:608
  45.5 0.2 collective-permute-done.2.above_ref
  45.7 4.2 %collective-permute-done.3.below_ref = bf16[32,384]{1,0:T(8,128)(2,1)S(1)} collective-permute-done((bf16[32,384]{1,0:T(8,128)(2,1)S(1)}, bf16[32,384]{1,0:T(8,128)(2,1)S(1)}, u32[]{:S(2)}, u32[]{:S(2)}) %collective-permute-start.3) | collective-permute-done | bytes 24608 | tf_op jit(solution)/shard_map/ppermute | solution.py:608
  49.9 5.3 %flow.1 = f32[256,256]{1,0:T(8,128)} custom-call(f32[256,256]{1,0:T(8,128)S(1)} %get-tuple-element.26.level_ref, f32[4,256,128]{2,1,0:T(8,128)S(1)} %get-tuple-element.27.side_ref, f32[256,256]{1,0:T(8,128)S(1)} %copy-done, s32[256,256]{1,0:T(8,128)S(1)} %copy-done.2, f32[256,256]{1,0:T(8,128)S(1)} %copy-done.1, ...), custom_call_target="tpu_custom_call" | custom-call | tf_op jit(solution)/shard_map/flow/pallas_call | solution.py:610
Async XLA Ops:
  0.6 5.8 %copy-start.8 = (bf16[16,16,3,3]{1,0,3,2:T(8,128)(2,1)S(1)}, bf16[16,16,3,3]{1,0,3,2:T(8,128)(2,1)}, u32[]{:S(2)}) copy-start(bf16[16,16,3,3]{1,0,3,2:T(8,128)(2,1)} %param.16) | copy-start | bytes 13828
  0.6 5.8 %copy-start.7 = (bf16[16,16,3,3]{1,0,3,2:T(8,128)(2,1)S(1)}, bf16[16,16,3,3]{1,0,3,2:T(8,128)(2,1)}, u32[]{:S(2)}) copy-start(bf16[16,16,3,3]{1,0,3,2:T(8,128)(2,1)} %param.15) | copy-start | bytes 13828
  2.7 5.9 %collective-permute-start = (bf16[32,512]{1,0:T(8,128)(2,1)}, bf16[32,512]{1,0:T(8,128)(2,1)S(1)}, u32[]{:S(2)}, u32[]{:S(2)}) collective-permute-start(bf16[32,512]{1,0:T(8,128)(2,1)} %get-tuple-element.16), channel_id=1, source_target_pairs={{0,1},{1,2},{2,3},{3,4},{4,5},{5,6},{6,7},{7,8},{8,9},{9,10},{10,1... | collective-permute-start | bytes 98312 | tf_op jit(solution)/shard_map/ppermute | solution.py:524
  5.1 5.4 %collective-permute-start.1 = (bf16[32,512]{1,0:T(8,128)(2,1)}, bf16[32,512]{1,0:T(8,128)(2,1)S(1)}, u32[]{:S(2)}, u32[]{:S(2)}) collective-permute-start(bf16[32,512]{1,0:T(8,128)(2,1)} %get-tuple-element.17), channel_id=1, source_target_pairs={{1,0},{2,1},{3,2},{4,3},{5,4},{6,5},{7,6},{8,7},{9,8},{10,9},{11,1... | collective-permute-start | bytes 98312 | tf_op jit(solution)/shard_map/ppermute | solution.py:525
  6.4 0.7 %copy-start.9 = (bf16[16,2,3,3]{0,1,3,2:T(2,128)(2,1)S(1)}, bf16[16,2,3,3]{0,1,3,2:T(2,128)(2,1)}, u32[]{:S(2)}) copy-start(bf16[16,2,3,3]{0,1,3,2:T(2,128)(2,1)} %param.14) | copy-start | bytes 1732
  6.4 0.7 %copy-start.10 = (bf16[1,16,3,3]{1,3,2,0:T(4,128)(2,1)S(1)}, bf16[1,16,3,3]{1,3,2,0:T(4,128)(2,1)}, u32[]{:S(2)}) copy-start(bf16[1,16,3,3]{1,3,2,0:T(4,128)(2,1)} %param.17) | copy-start | bytes 868
  6.4 0.7 %copy-start.11 = (s32[64,1]{0,1:T(1,128)S(1)}, s32[64,1]{0,1:T(1,128)}, u32[]{:S(2)}) copy-start(s32[64,1]{0,1:T(1,128)} %param.20) | copy-start | bytes 772
  6.4 0.7 %copy-start.12 = (s32[64,1]{0,1:T(1,128)S(1)}, s32[64,1]{0,1:T(1,128)}, u32[]{:S(2)}) copy-start(s32[64,1]{0,1:T(1,128)} %param.21) | copy-start | bytes 772
  7.1 3.4 %copy-start.4 = (bf16[2,64,512]{2,1,0:T(8,128)(2,1)S(1)}, bf16[2,64,512]{2,1,0:T(8,128)(2,1)}, u32[]{:S(2)}) copy-start(bf16[2,64,512]{2,1,0:T(8,128)(2,1)} %sar_hbm.3) | copy-start | bytes 393220
  7.1 3.4 %copy-start.5 = (f32[64,512]{1,0:T(8,128)S(1)}, f32[64,512]{1,0:T(8,128)}, u32[]{:S(2)}) copy-start(f32[64,512]{1,0:T(8,128)} %gw_hbm.1) | copy-start | bytes 393220
  7.1 3.4 %copy-start.6 = (s32[64,512]{1,0:T(8,128)S(1)}, s32[64,512]{1,0:T(8,128)}, u32[]{:S(2)}) copy-start(s32[64,512]{1,0:T(8,128)} %cell_hbm.1) | copy-start | bytes 393220
  10.5 30.0 %copy-start.2 = (s32[256,256]{1,0:T(8,128)S(1)}, s32[256,256]{1,0:T(8,128)}, u32[]{:S(2)}) copy-start(s32[256,256]{1,0:T(8,128)} %dir_ref.3) | copy-start | bytes 786436
  10.5 30.0 %copy-start.3 = (f32[256,256]{1,0:T(8,128)S(1)}, f32[256,256]{1,0:T(8,128)}, u32[]{:S(2)}) copy-start(f32[256,256]{1,0:T(8,128)} %depth_ref.1) | copy-start | bytes 786436
  19.9 20.7 %copy-start = (f32[256,256]{1,0:T(8,128)S(1)}, f32[256,256]{1,0:T(8,128)}, u32[]{:S(2)}) copy-start(f32[256,256]{1,0:T(8,128)} %slope_ref.3) | copy-start | bytes 786436
  19.9 20.7 %copy-start.1 = (f32[256,256]{1,0:T(8,128)S(1)}, f32[256,256]{1,0:T(8,128)}, u32[]{:S(2)}) copy-start(f32[256,256]{1,0:T(8,128)} %rain_ref.3) | copy-start | bytes 786436
  41.5 4.3 %collective-permute-start.2 = (bf16[32,384]{1,0:T(8,128)(2,1)S(1)}, bf16[32,384]{1,0:T(8,128)(2,1)S(1)}, u32[]{:S(2)}, u32[]{:S(2)}) collective-permute-start(bf16[32,384]{1,0:T(8,128)(2,1)S(1)} %get-tuple-element.28), channel_id=1, source_target_pairs={{0,4},{4,8},{8,12},{12,16},{16,20},{20,24},{24,28},{1,5},{5,9},{9,... | collective-permute-start | bytes 73736 | tf_op jit(solution)/shard_map/ppermute | solution.py:607
  44.2 5.7 %collective-permute-start.3 = (bf16[32,384]{1,0:T(8,128)(2,1)S(1)}, bf16[32,384]{1,0:T(8,128)(2,1)S(1)}, u32[]{:S(2)}, u32[]{:S(2)}) collective-permute-start(bf16[32,384]{1,0:T(8,128)(2,1)S(1)} %get-tuple-element.29), channel_id=1, source_target_pairs={{4,0},{8,4},{12,8},{16,12},{20,16},{24,20},{28,24},{5,1},{9,5},{13... | collective-permute-start | bytes 73736 | tf_op jit(solution)/shard_map/ppermute | solution.py:608

commit v6 on v5

--- a/solution.py
+++ b/solution.py
@@ -13,9 +13,10 @@
 OUT_LINES = 14
 IN_LINES = OUT_LINES + 2
 HALO_LINES = 4
+END_LINES = 8
 LANES = 128
 VMEM_LIMIT = 48 * 1024 * 1024
-VMEM_MOST = 61920 * 1024
+VMEM_MOST = 61880 * 1024
 
 wet_depth = 0.5
 runoff_coef = 0.25
@@ -51,10 +52,61 @@
 
 def pixel_shifts(x):
     width = x.shape[1]
-    pix = iota(x.shape, 1)
-    before = jnp.where(pix == 0, 0.0, pltpu.roll(x, 1, 1))
-    after = jnp.where(pix == width - 1, 0.0, pltpu.roll(x, width - 1, 1))
+    pix = iota(x.shape, 1).astype(f32).astype(x.dtype)
+    end = (width - 1 - iota(x.shape, 1)).astype(f32).astype(x.dtype)
+    zero = jnp.zeros(x.shape, x.dtype)
+    before = jnp.where(pix == 0, zero, pltpu.roll(x, 1, 1))
+    after = jnp.where(end == 0, zero, pltpu.roll(x, width - 1, 1))
     return before, after
+
+
+def merged(sums, n):
+    before, _ = pixel_shifts(sums[0:n])
+    _, after = pixel_shifts(sums[2 * n : 3 * n])
+    return before + sums[n : 2 * n] + after
+
+
+def image_columns(x):
+    before, after = pixel_shifts(x)
+    pad = jnp.zeros((LANES - 3 * x.shape[0], x.shape[1]), f32)
+    return jnp.concatenate([before, x, after, pad], 0).astype(bf16)
+
+
+def sigmoid(x):
+    return (1.0 / (1.0 + jnp.exp(-x))).astype(bf16)
+
+
+def line_windows(cell, obs, cov, quarter):
+    px = cell.shape[1]
+    kind = iota((CH, px), 0)
+    is_obs = kind < CH // 2
+    kind_part = rem(kind, CH // 2).astype(f32).astype(bf16)
+    sub = kind.astype(f32).astype(bf16)
+    one = jnp.ones((CH, px), bf16)
+    nil = jnp.zeros((CH, px), bf16)
+    part = quo(cell, quarter).astype(f32)
+    col = rem(cell, quarter).astype(f32)
+
+    def spread_row(x, i):
+        return jnp.broadcast_to(x[i : i + 1], (CH, px)).astype(bf16)
+
+    out = []
+    for i in range(cell.shape[0]):
+        value = jnp.where(is_obs, obs[i : i + 1], cov[i : i + 1]).astype(bf16)
+        left = jnp.where(kind_part == spread_row(part, i), value, nil)
+        where_col = spread_row(col, i)
+        hot = jnp.concatenate([jnp.where(sub + g * CH == where_col, one, nil) for g in range(quarter // CH)], 0)
+        out.append(dot_t(left, hot))
+    return out
+
+
+def window_goods(sums):
+    rows, quarter = sums.shape
+    cols = 4 * quarter
+    repeat = (rem(iota((quarter, cols), 1), quarter) == iota((quarter, cols), 0)).astype(bf16)
+    tiled = dot(sums.astype(bf16), repeat)
+    mine = rem(iota((rows, cols), 0), 4) == quo(iota((rows, cols), 1), quarter)
+    return jnp.where(mine, tiled, 0.0).astype(bf16)
 
 
 def band_weights(tiled, rows, cols, per_row, line_of):
@@ -110,19 +162,12 @@
     return [both[0:8, 0:cols], both[0:8, cols:], both[8:16, 0:cols], both[8:16, cols:]]
 
 
-def prep_kernel(
+def inner_kernel(
     devices, capacity,
-    k1_hbm, k2_hbm, k3_hbm, k4_hbm, tile_hbm, row_hbm,
-    w1_ref, w2_ref, w3_ref, w4_ref, perm_ref, extra_ref,
-    k1_ref, k2_ref, k3_ref, k4_ref, tile_ref, row_ref, sems, t1_ref, t4_ref,
+    k1_ref, k2_ref, k3_ref, k4_ref, tile_ref, row_ref, sar_ref, gw_ref, cell_ref,
+    w1_ref, w2_ref, w3_ref, w4_ref, perm_ref, extra_ref, frac_ref, slots_ref, e1_ref, e2_ref, e3_ref,
+    t1_ref, t4_ref, s_ref, xa_ref, xb_ref, x3_ref, logit_ref, wnd_ref,
 ):
-    pairs = (
-        (k1_hbm, k1_ref), (k2_hbm, k2_ref), (k3_hbm, k3_ref), (k4_hbm, k4_ref),
-        (tile_hbm, tile_ref), (row_hbm, row_ref),
-    )
-    copies = [pltpu.make_async_copy(src, dst, sems.at[i]) for i, (src, dst) in enumerate(pairs)]
-    for copy in copies:
-        copy.start()
     rows = OUT_LINES * CH
     cols = IN_LINES * CH
 
@@ -136,8 +181,6 @@
     tile4 = (rem(iota((CH, cols), 1), CH) == iota((CH, cols), 0)).astype(bf16)
     t1_ref[...] = jnp.zeros(t1_ref.shape, f32)
     t4_ref[...] = jnp.zeros(t4_ref.shape, f32)
-    for copy in copies:
-        copy.wait()
     for ky in range(3):
         for kx in range(3):
             t1_ref[ky * 8 + 2 * kx : ky * 8 + 2 * kx + 2, :] = k1_ref[ky, kx].astype(f32)
@@ -149,7 +192,7 @@
         wide = sum(dot(k_ref[ky * 3 * CH : (ky + 1) * 3 * CH, :], spread[ky]) for ky in range(3))
         for kx in range(3):
             for i in range(OUT_LINES):
-                w_ref[kx * rows + i * CH : kx * rows + (i + 1) * CH, :] = wide[
+                w_ref[i * CH : (i + 1) * CH, kx * cols : (kx + 1) * cols] = wide[
                     kx * CH : (kx + 1) * CH, i * cols : (i + 1) * cols
                 ].astype(bf16)
     wide4 = dot(t4_ref[...].astype(bf16), tile4)
@@ -170,12 +213,15 @@
     tile_sub = jnp.sum(jnp.where(same, jnp.broadcast_to(tile, (lines, lines)), 0.0), 1, keepdims=True)
     rival = (tile_sub == tile) & (iota((lines, lines), 0) < iota((lines, lines), 1))
     slot = tile * capacity + jnp.sum(jnp.where(rival, 1.0, 0.0), 0, keepdims=True)
-    slots, wnd_rows = perm_ref.shape
-    per_line = wnd_rows // lines
+    slots = slots_ref.shape[0]
+    wnd_rows = CH * lines
+    per_line = CH
     widen = (quo(iota((lines, wnd_rows), 1), per_line) == iota((lines, wnd_rows), 0)).astype(bf16)
     slot_wide = dot(jnp.broadcast_to(slot, (8, lines)).astype(bf16), widen)[0:1]
     place = slot_wide.astype(jnp.int32) * 4 + rem(quo(iota((1, wnd_rows), 1), 4), 4)
-    perm_ref[...] = jnp.where(iota((slots, wnd_rows), 0) == place, 1.0, 0.0).astype(bf16)
+    perm = jnp.where(iota((slots, wnd_rows), 0) == place, 1.0, 0.0).astype(bf16)
+    end = END_LINES * CH
+    perm_ref[...] = jnp.concatenate([perm[:, 0:end], perm[:, wnd_rows - end :]], 1)
 
     row_of = dot(
         jnp.where(same, jnp.broadcast_to(row_ref[...].astype(f32), (lines, lines)), 0.0).astype(bf16),
@@ -194,6 +240,63 @@
     extra_ref[...] = jnp.where(at == 2, info, 0.0).reshape(8 * devices, LANES)
 
 
+    px = sar_ref.shape[2]
+    for ch in range(2):
+        s_ref[ch, 0:lines, :] = sar_ref[ch].astype(f32)
+        s_ref[ch, lines:, :] = jnp.zeros((s_ref.shape[1] - lines, px), f32)
+    total = xa_ref.shape[1] // CH
+    xa_ref[:, (total - 2) * CH :, :] = jnp.zeros((3, 2 * CH, px), bf16)
+
+    def put(ref, line, acc):
+        feat = jnp.maximum(acc, 0.0).astype(bf16)
+        at = slice(line * CH, line * CH + rows)
+        if len(ref.shape) == 2:
+            ref[at, :] = feat
+            return
+        before, after = pixel_shifts(feat)
+        ref[0, at, :] = before
+        ref[1, at, :] = feat
+        ref[2, at, :] = after
+
+    full = (lines + 4) // OUT_LINES + 1
+    for b in range(full):
+        at = b * OUT_LINES
+        x = jnp.concatenate([s_ref[0, at : at + IN_LINES, :], s_ref[1, at : at + IN_LINES, :]], 0)
+        put(xa_ref, 1 + at, dot(w1_ref[...], image_columns(x)))
+    for w_ref, src, dst, line, blocks in ((w2_ref, xa_ref, xb_ref, 2, full), (w3_ref, xb_ref, x3_ref, 3, full - 1)):
+        for b in range(blocks):
+            at = line + b * OUT_LINES
+            x = src[:, (at - 1) * CH : (at - 1) * CH + cols, :].reshape(3 * cols, px)
+            put(dst, at, dot(w_ref[...], x))
+
+    def ends_of(lo, center):
+        hi = lines - lo - 2
+        return jnp.concatenate([center[at * CH : (at + 2) * CH, :] for at in (lo, hi)], 0)
+
+    e1_ref[...] = ends_of(3, xa_ref.at[1])
+    e2_ref[...] = ends_of(4, xb_ref.at[1])
+    e3_ref[...] = ends_of(5, x3_ref)
+    logit_ref[0:END_LINES, :] = jnp.zeros((END_LINES, px), f32)
+    starts = [3 + b * OUT_LINES for b in range(full - 2)] + [lines - 5 - IN_LINES]
+    for at in starts:
+        sums = dot(w4_ref[...], x3_ref[at * CH : at * CH + cols, :])
+        logit_ref[at + 1 : at + 1 + CH, :] = merged(sums, CH)
+    frac_ref[...] = sigmoid(logit_ref[0:lines, :])
+    quarter = wnd_ref.shape[1]
+    group = 16
+
+    def window_group(g, carry):
+        at = pl.ds(pl.multiple_of(g * group + END_LINES, END_LINES), group)
+        cov = gw_ref[at, :]
+        obs = sigmoid(logit_ref[at, :]).astype(f32) * cov
+        for i, sums in enumerate(line_windows(cell_ref[at, :], obs, cov, quarter)):
+            wnd_ref[pl.ds(pl.multiple_of(g * (CH * group) + CH * i, CH), CH), :] = sums
+        return carry
+
+    lax.fori_loop(0, (lines - 2 * END_LINES) // group, window_group, 0)
+    slots_ref[...] = dot(perm[:, end : wnd_rows - end], window_goods(wnd_ref[...]))
+
+
 def of_right(x, per_tile):
     return jnp.concatenate([x[per_tile:], jnp.zeros((per_tile, x.shape[1]), x.dtype)], 0)
 
@@ -202,132 +305,51 @@
     return jnp.concatenate([jnp.zeros((per_tile, x.shape[1]), x.dtype), x[: x.shape[0] - per_tile]], 0)
 
 
-def swath_kernel(
+def ends_kernel(
     devices, capacity,
-    above_ref, below_ref, w1_ref, w2_ref, w3_ref, w4_ref, perm_ref, extra_ref,
-    sar_hbm, gw_hbm, cell_hbm,
+    above_ref, below_ref, w1_ref, w2_ref, w3_ref, w4_ref, perm_ref, extra_ref, frac_in, slots_in, e1_ref, e2_ref, e3_ref,
+    sar_ref, gw_ref, cell_ref,
     frac_ref, send_ref,
-    sar_ref, gw_ref, cell_ref, sems,
-    s_ref, xa_ref, xb_ref, x3_ref, logit_ref, obs_ref, wnd_ref,
+    f_ref,
 ):
-    pairs = ((sar_hbm, sar_ref), (gw_hbm, gw_ref), (cell_hbm, cell_ref))
-    copies = [pltpu.make_async_copy(src, dst, sems.at[i]) for i, (src, dst) in enumerate(pairs)]
-    for copy in copies:
-        copy.start()
     lines, px = gw_ref.shape
-    blocks = (lines + 2 * HALO_LINES - 2) // OUT_LINES
-    frame = lines + 2 * HALO_LINES
-    total = xa_ref.shape[0] // CH
     n_ty = lax.axis_size("ty")
     me = lax.axis_index("tx") * n_ty + lax.axis_index("ty")
-    first = me == 0
-    last = me == devices - 1
     rows = OUT_LINES * CH
-    cols = IN_LINES * CH
-
-    def clear(ref, lo, hi):
-        ref[lo * CH : hi * CH, :] = jnp.zeros(((hi - lo) * CH, px), bf16)
-
-    def outside(ref):
-        @pl.when(first)
-        def _():
-            clear(ref, 0, HALO_LINES)
-
-        @pl.when(last)
-        def _():
-            clear(ref, HALO_LINES + lines, frame)
-
-    def merged(sums, n):
-        before, _ = pixel_shifts(sums[0:n])
-        _, after = pixel_shifts(sums[2 * n : 3 * n])
-        return before + sums[n : 2 * n] + after
-
-    def by_block(body):
-        def step(b, carry):
-            body(b)
-            return carry
-
-        lax.fori_loop(0, blocks, step, 0)
-
-    def lines_at(b, line, count):
-        return pl.ds(pl.multiple_of(b * rows + line * CH, CH), count)
-
-    for ref, line in ((xa_ref, 1), (xb_ref, 2), (x3_ref, 3)):
-        clear(ref, line + blocks * OUT_LINES, total)
     above = above_ref[16:32, :].astype(f32)
     below = below_ref[16:32, :].astype(f32)
-    copies[0].wait()
+    n = HALO_LINES
+
+    pieces = []
     for ch in range(2):
-        s_ref[ch, 0:HALO_LINES, :] = above[ch * HALO_LINES : (ch + 1) * HALO_LINES]
-        s_ref[ch, HALO_LINES : HALO_LINES + lines, :] = sar_ref[ch].astype(f32)
-        s_ref[ch, HALO_LINES + lines : frame, :] = below[ch * HALO_LINES : (ch + 1) * HALO_LINES]
-    pad = jnp.zeros((LANES - 6 * IN_LINES, px), f32)
-    for b in range(blocks):
-        at = b * OUT_LINES
-        x = jnp.concatenate([s_ref[0, at : at + IN_LINES, :], s_ref[1, at : at + IN_LINES, :]], 0)
-        before, after = pixel_shifts(x)
-        acc = dot(w1_ref[...], jnp.concatenate([before, x, after, pad], 0).astype(bf16))
-        xa_ref[(1 + at) * CH : (1 + at) * CH + rows, :] = jnp.maximum(acc, 0.0).astype(bf16)
-    outside(xa_ref)
-
-    for w_ref, src, dst, line in ((w2_ref, xa_ref, xb_ref, 2), (w3_ref, xb_ref, x3_ref, 3)):
-
-        def conv(b):
-            sums = dot(w_ref[...], src[lines_at(b, line - 1, cols), :])
-            dst[lines_at(b, line, rows), :] = jnp.maximum(merged(sums, rows), 0.0).astype(bf16)
-
-        by_block(conv)
-        outside(dst)
-
-    for b in range(blocks):
-        at = HALO_LINES - 1 + b * OUT_LINES
-        sums = dot(w4_ref[...], x3_ref[at * CH : at * CH + cols, :])
-        logit_ref[b * OUT_LINES : b * OUT_LINES + CH, :] = merged(sums, CH)
-    frac = (1.0 / (1.0 + jnp.exp(-logit_ref[0:lines, :]))).astype(bf16)
-    frac_ref[...] = frac
-    for copy in copies[1:]:
-        copy.wait()
-    obs_ref[...] = frac.astype(f32) * gw_ref[...]
-
-    quarter = wnd_ref.shape[1]
-    parts = wnd_ref.shape[0] // lines // 2
-    kind = iota((CH, px), 0)
-    is_obs = kind < parts
-    kind_part = rem(kind, parts).astype(f32).astype(bf16)
-    sub = kind.astype(f32).astype(bf16)
-    one = jnp.ones((CH, px), bf16)
-    nil = jnp.zeros((CH, px), bf16)
-    spots = [sub + g * CH for g in range(quarter // CH)]
-    group = 8
-
-    def window_group(g, carry):
-        at = pl.ds(pl.multiple_of(g * group, group), group)
-        cell = cell_ref[at, :]
-        obs = obs_ref[at, :]
+        own = sar_ref[ch].astype(f32)
+        pieces += [above[ch * n : (ch + 1) * n], own[0:n], own[lines - n :], below[ch * n : (ch + 1) * n]]
+    x = image_columns(jnp.concatenate(pieces, 0))
+    out_line = quo(iota((rows, px), 0), CH)
+    low = jnp.where(me == 0, n, 0)
+    high = jnp.where(me == devices - 1, OUT_LINES - n, 2 * OUT_LINES)
+    for layer, (w_ref, e_ref) in enumerate(((w1_ref, e1_ref), (w2_ref, e2_ref), (w3_ref, e3_ref)), 1):
+        acc = jnp.maximum(dot(w_ref[...], x), 0.0)
+        inside = (out_line >= low - layer) & (out_line < high + layer)
+        feat = jnp.where(inside, acc, 0.0).astype(bf16)
+        block = jnp.concatenate([feat[0 : 6 * CH], e_ref[...], feat[8 * CH :]], 0)
+        if layer < 3:
+            before, after = pixel_shifts(block)
+            x = jnp.concatenate([before, block, after], 0)
+    frac = sigmoid(merged(dot(w4_ref[...], block), CH)).astype(f32)
+    f_ref[...] = frac_in[...].astype(f32)
+    f_ref[0:6, :] = frac[0:6]
+    f_ref[lines - 6 :, :] = frac[8:14]
+    frac_ref[...] = f_ref[...].astype(bf16)
+    quarter = slots_in.shape[1] // 4
+    sums = []
+    for at in (slice(0, END_LINES), slice(lines - END_LINES, lines)):
         cov = gw_ref[at, :]
-        part = quo(cell, quarter).astype(f32)
-        col = rem(cell, quarter).astype(f32)
-
-        def spread_row(x, i):
-            return jnp.broadcast_to(x[i : i + 1], (CH, px)).astype(bf16)
-
-        for i in range(group):
-            value = jnp.where(is_obs, obs[i : i + 1], cov[i : i + 1]).astype(bf16)
-            left = jnp.where(kind_part == spread_row(part, i), value, nil)
-            where_col = spread_row(col, i)
-            hot = jnp.concatenate([jnp.where(spot == where_col, one, nil) for spot in spots], 0)
-            wnd_ref[pl.ds(pl.multiple_of(g * (CH * group) + CH * i, CH), CH), :] = dot_t(left, hot)
-        return carry
-
-    lax.fori_loop(0, lines // group, window_group, 0)
+        sums += line_windows(cell_ref[at, :], f_ref[at, :] * cov, cov, quarter)
+    by_slot = slots_in[...] + dot(perm_ref[...], window_goods(jnp.concatenate(sums, 0)))
 
     per_tile = 4 * capacity
-    slots, wnd_rows = perm_ref.shape
-    tile_cols = 4 * quarter
-    repeat = (rem(iota((quarter, tile_cols), 1), quarter) == iota((quarter, tile_cols), 0)).astype(bf16)
-    tiled = dot(wnd_ref[...].astype(bf16), repeat)
-    mine = rem(iota((wnd_rows, tile_cols), 0), 4) == quo(iota((wnd_rows, tile_cols), 1), quarter)
-    by_slot = dot(perm_ref[...], jnp.where(mine, tiled, 0.0).astype(bf16))
+    slots, tile_cols = by_slot.shape
     h = SUBSTEPS
     entry = rem(iota((slots, LANES), 0), per_tile)
     here = quo(iota((slots, LANES), 1), h) == entry
@@ -422,47 +444,30 @@
     bot_ref[...] = end_rows(slice(tile_rows - h, tile_rows))
 
 
-def flow_kernel(
-    level_ref, side_ref, slope_ref, dir_ref, rain_ref, above_ref, below_ref,
-    out_ref,
-    rain_s, conv_s, m_ref, part_ref, up_ref, down_ref,
-):
-    tile_rows, tile_cols = level_ref.shape
+def substeps(level, rain, conv, code, rain_s, conv_s, m_ref, part_ref, up_ref, down_ref, chunk):
+    rows, cols = level.shape
     h = SUBSTEPS
-    wide_rows = tile_rows + 2 * h
-    wide_cols = tile_cols + LANES
-
-    def widened(field, own):
-        at = slice(field * h, (field + 1) * h)
-        mid = jnp.concatenate([own, side_ref[field]], 1)
-        return jnp.concatenate([above_ref[...].astype(f32)[at], mid, below_ref[...].astype(f32)[at]], 0)
-
-    zeros = jnp.zeros((h, wide_cols), f32)
     for ref in (up_ref, down_ref):
         ref[0] = jnp.zeros(ref.shape[1:], f32)
-        ref[1, 0:h, :] = zeros
-        ref[1, h + wide_rows :, :] = zeros
-    part_ref[0] = widened(0, level_ref[...])
-    rain_s[...] = widened(1, rain_ref[...])
-    conv = widened(2, runoff_coef * jnp.sqrt(slope_ref[...]))
+        ref[1, 0:h, :] = jnp.zeros((h, cols), f32)
+        ref[1, h + rows :, :] = jnp.zeros((h, cols), f32)
+    part_ref[0] = level
+    rain_s[...] = rain
     conv_s[...] = conv
-    code = widened(3, dir_ref[...].astype(f32))
     sides = (-1, 0, 1, -1, 1, -1, 0, 1)
     for direction, side in enumerate(sides):
         share = jnp.where(code == direction, conv, 0.0)
-        m_ref[direction] = pltpu.roll(share, side % wide_cols, 1) if side else share
-
-    chunk = 16
+        m_ref[direction] = pltpu.roll(share, side % cols, 1) if side else share
 
     def level_at(buf, r, n):
         level = part_ref[buf, r : r + n, :]
         return level + up_ref[buf, h + r + 1 : h + r + 1 + n, :] + down_ref[buf, h + r - 1 : h + r - 1 + n, :]
 
     def substep(buf, new):
-        for r in range(0, wide_rows, chunk):
+        for r in range(0, rows, chunk):
             level = level_at(buf, r, chunk)
             power = level * jnp.exp((2.0 / 3.0) * jnp.log(jnp.maximum(jnp.abs(level), 1e-30)))
-            from_right = pltpu.roll(power, wide_cols - 1, 1)
+            from_right = pltpu.roll(power, cols - 1, 1)
             from_left = pltpu.roll(power, 1, 1)
             m = [m_ref[d, r : r + chunk, :] for d in range(8)]
             up_ref[new, h + r : h + r + chunk, :] = m[0] * from_right + m[1] * power + m[2] * from_left
@@ -478,7 +483,45 @@
         return carry
 
     lax.fori_loop(0, SUBSTEPS // 2, substep_pair, 0)
-    out_ref[...] = level_at(0, h, tile_rows)[:, 0:tile_cols]
+    return level_at
+
+
+def flow_inner_kernel(level_ref, side_ref, slope_ref, dir_ref, rain_ref, out_ref, *scratch):
+    rows, cols = level_ref.shape
+    own = (level_ref[...], rain_ref[...], runoff_coef * jnp.sqrt(slope_ref[...]), dir_ref[...].astype(f32))
+    level_at = substeps(*[jnp.concatenate([x, side_ref[i]], 1) for i, x in enumerate(own)], *scratch, 16)
+    out_ref[...] = level_at(0, 0, rows)[:, 0:cols]
+
+
+def flow_ends_kernel(inner_ref, level_ref, side_ref, slope_ref, dir_ref, rain_ref, above_ref, below_ref, out_ref, *scratch):
+    rows, cols = level_ref.shape
+    h = SUBSTEPS
+    above = above_ref[...].astype(f32)
+    below = below_ref[...].astype(f32)
+    fields = []
+    for i, ref in enumerate((level_ref, rain_ref, slope_ref, dir_ref)):
+        ends = []
+        for at in (slice(0, 2 * h), slice(rows - 2 * h, rows)):
+            own = ref[at, :].astype(f32)
+            if i == 2:
+                own = runoff_coef * jnp.sqrt(own)
+            ends.append(jnp.concatenate([own, side_ref[i, at, :]], 1))
+        fields.append(jnp.concatenate([above[i * h : (i + 1) * h], *ends, below[i * h : (i + 1) * h]], 0))
+    level_at = substeps(*fields, *scratch, 16)
+    out_ref[h : rows - h, :] = inner_ref[h : rows - h, :]
+    out_ref[0:h, :] = level_at(0, h, h)[:, 0:cols]
+    out_ref[rows - h :, :] = level_at(0, 4 * h, h)[:, 0:cols]
+
+
+def flow_scratch(rows, cols):
+    return [
+        pltpu.VMEM((rows, cols), f32),
+        pltpu.VMEM((rows, cols), f32),
+        pltpu.VMEM((8, rows, cols), f32),
+        pltpu.VMEM((2, rows, cols), f32),
+        pltpu.VMEM((2, rows + 2 * SUBSTEPS, cols), f32),
+        pltpu.VMEM((2, rows + 2 * SUBSTEPS, cols), f32),
+    ]
 
 
 def hbm_specs(n):
@@ -524,69 +567,69 @@
     from_previous = lax.ppermute(to_next, both, up)
     from_next = lax.ppermute(to_previous, both, down)
 
-    feats = (az_lines + 2 * HALO_LINES + 4) * CH
     rows, cols = OUT_LINES * CH, IN_LINES * CH
+    slots = devices * capacity * 4
     send_rows = tile_cols // LANES * 4 * capacity + 8
-    slots = devices * capacity * 4
-    wnd_rows = CH * az_lines
-    fixed = (
+    full = (az_lines + 4) // OUT_LINES + 1
+    feats = (full * OUT_LINES + 3) * CH
+    blocks_in = (az_lines + IN_LINES, range_px)
+
+    def cost(flops):
+        return pl.CostEstimate(flops=flops, bytes_accessed=4_000_000, transcendentals=0)
+
+    prepared = pl.pallas_call(
+        functools.partial(inner_kernel, devices, capacity),
+        out_shape=(
+            jax.ShapeDtypeStruct((rows, LANES), bf16),
+            jax.ShapeDtypeStruct((rows, 3 * cols), bf16),
+            jax.ShapeDtypeStruct((rows, 3 * cols), bf16),
+            jax.ShapeDtypeStruct((3 * CH, cols), bf16),
+            jax.ShapeDtypeStruct((slots, 2 * END_LINES * CH), bf16),
+            jax.ShapeDtypeStruct((8 * devices, LANES), f32),
+            jax.ShapeDtypeStruct((az_lines, range_px), bf16),
+            jax.ShapeDtypeStruct((slots, tile_cols), f32),
+            *[jax.ShapeDtypeStruct((4 * CH, range_px), bf16)] * 3,
+        ),
+        in_specs=vmem_specs(9),
+        out_specs=tuple(vmem_specs(11)),
+        scratch_shapes=[
+            pltpu.VMEM((24, CH), f32),
+            pltpu.VMEM((16, CH), f32),
+            pltpu.VMEM((2, *blocks_in), f32),
+            pltpu.VMEM((3, feats, range_px), bf16),
+            pltpu.VMEM((3, feats, range_px), bf16),
+            pltpu.VMEM((feats, range_px), bf16),
+            pltpu.VMEM(blocks_in, f32),
+            pltpu.VMEM(((az_lines - 2 * END_LINES) * CH, tile_cols // 4), f32),
+        ],
+        compiler_params=params,
+        cost_estimate=cost(8_000_000_000),
+        name="inner",
+    )(
         jnp.transpose(kernel_first, (2, 3, 1, 0)),
         jnp.transpose(kernel_second, (2, 3, 0, 1)).reshape(9 * CH, CH),
         jnp.transpose(kernel_third, (2, 3, 0, 1)).reshape(9 * CH, CH),
         jnp.transpose(kernel_last[0], (1, 2, 0)),
         block_tile.reshape(1, az_lines), block_row.reshape(1, az_lines),
+        sar_image, geo_weight, cell_index,
     )
-    prepared = pl.pallas_call(
-        functools.partial(prep_kernel, devices, capacity),
-        out_shape=(
-            jax.ShapeDtypeStruct((rows, LANES), bf16),
-            jax.ShapeDtypeStruct((3 * rows, cols), bf16),
-            jax.ShapeDtypeStruct((3 * rows, cols), bf16),
-            jax.ShapeDtypeStruct((3 * CH, cols), bf16),
-            jax.ShapeDtypeStruct((slots, wnd_rows), bf16),
-            jax.ShapeDtypeStruct((8 * devices, LANES), f32),
-        ),
-        in_specs=hbm_specs(6),
-        out_specs=tuple(vmem_specs(6)),
-        scratch_shapes=[
-            *[pltpu.VMEM(x.shape, x.dtype) for x in fixed],
-            pltpu.SemaphoreType.DMA((6,)),
-            pltpu.VMEM((24, CH), f32),
-            pltpu.VMEM((16, CH), f32),
-        ],
-        compiler_params=params,
-        cost_estimate=pl.CostEstimate(flops=2_000_000_000, bytes_accessed=4_000_000, transcendentals=0),
-        name="prep",
-    )(*fixed)
-    inputs = (sar_image, geo_weight, cell_index)
     fraction, send = pl.pallas_call(
-        functools.partial(swath_kernel, devices, capacity),
+        functools.partial(ends_kernel, devices, capacity),
         out_shape=(
             jax.ShapeDtypeStruct((az_lines, range_px), bf16),
             jax.ShapeDtypeStruct((devices * send_rows, LANES), bf16),
         ),
-        in_specs=vmem_specs(8) + hbm_specs(3),
+        in_specs=vmem_specs(16),
         out_specs=tuple(vmem_specs(2)),
-        scratch_shapes=[
-            *[pltpu.VMEM(x.shape, x.dtype) for x in inputs],
-            pltpu.SemaphoreType.DMA((3,)),
-            pltpu.VMEM((2, az_lines + 2 * HALO_LINES + 8, range_px), f32),
-            pltpu.VMEM((feats, range_px), bf16),
-            pltpu.VMEM((feats, range_px), bf16),
-            pltpu.VMEM((feats, range_px), bf16),
-            pltpu.VMEM((az_lines + 2 * CH, range_px), f32),
-            pltpu.VMEM((az_lines, range_px), f32),
-            pltpu.VMEM((wnd_rows, tile_cols // 4), f32),
-        ],
+        scratch_shapes=[pltpu.VMEM((az_lines, range_px), f32)],
         compiler_params=params,
-        name="swath",
-    )(from_previous, from_next, *prepared, *inputs)
+        name="ends",
+    )(from_previous, from_next, *prepared, sar_image, geo_weight, cell_index)
 
     got = lax.all_to_all(
         send.reshape(devices, send_rows, LANES), both, split_axis=0, concat_axis=0, tiled=True
     ).reshape(devices * send_rows, LANES)
 
-    wide_rows = tile_rows + 2 * SUBSTEPS
     wide_cols = tile_cols + LANES
     edge = jax.ShapeDtypeStruct((4 * SUBSTEPS, wide_cols), bf16)
     level, side, top_rows, bot_rows = pl.pallas_call(
@@ -607,22 +650,25 @@
     above = lax.ppermute(bot_rows, "tx", up)
     below = lax.ppermute(top_rows, "tx", down)
 
+    inner = pl.pallas_call(
+        flow_inner_kernel,
+        out_shape=jax.ShapeDtypeStruct((tile_rows, tile_cols), f32),
+        in_specs=vmem_specs(5),
+        out_specs=vmem_specs(1)[0],
+        scratch_shapes=flow_scratch(tile_rows, wide_cols),
+        compiler_params=params,
+        cost_estimate=cost(5_000_000_000),
+        name="flow_inner",
+    )(level, side, slope, flow_dir, rain)
     level = pl.pallas_call(
-        flow_kernel,
+        flow_ends_kernel,
         out_shape=jax.ShapeDtypeStruct((tile_rows, tile_cols), f32),
-        in_specs=vmem_specs(7),
+        in_specs=vmem_specs(8),
         out_specs=vmem_specs(1)[0],
-        scratch_shapes=[
-            pltpu.VMEM((wide_rows, wide_cols), f32),
-            pltpu.VMEM((wide_rows, wide_cols), f32),
-            pltpu.VMEM((8, wide_rows, wide_cols), f32),
-            pltpu.VMEM((2, wide_rows, wide_cols), f32),
-            pltpu.VMEM((2, wide_rows + 2 * SUBSTEPS, wide_cols), f32),
-            pltpu.VMEM((2, wide_rows + 2 * SUBSTEPS, wide_cols), f32),
-        ],
+        scratch_shapes=flow_scratch(6 * SUBSTEPS, wide_cols),
         compiler_params=params,
-        name="flow",
-    )(level, side, slope, flow_dir, rain, above, below)
+        name="flow_ends",
+    )(inner, level, side, slope, flow_dir, rain, above, below)
     return (fraction, level)
 
 

time: 55.6 us -> 48.5 us (0.87)
  waiting for transfers between devices: 6.36 us -> 0.03 us
  Pallas kernels: 19.1 us -> 17.5 us
    ppermute x1, waiting for transfers between devices: 4.22 us -> 0.02 us  [per_device(): below = lax.ppermute(top_rows, 'tx', down)]
    ppermute x1, waiting for transfers between devices: 1.94 us -> 0.01 us  [per_device(): from_next = lax.ppermute(to_previous, both, down)]
    pallas_call x3 -> x4, Pallas kernels: 16.1 us -> 14.5 us  [the longest x1 5.23 us: per_device(): pl.pallas_call(functools.partial(inner_kernel, devices, capacity), out_sh...]
  transfers between devices with their start and end apart: 4 -> 4, of which waited for: 3 -> 0; matrix products, arithmetic and copies ran while one was open for 0% -> 0% of each run, Pallas kernels for 3% -> 20%
where the time goes in v6:
time: 48.5 us; the launch traced here: 47.7 us
  blocking collectives  21 us (43%)
  Pallas kernels  17.5 us (36%)
  starting transfers between devices  7.69 us (16%)
  between operations  0.85 us (2%)
  local copies, waits for them, and re-layouts  0.67 us (1%)
    all_to_all x1, blocking collectives, per_device(): lax.all_to_all(send.reshape(devices, send_rows, LANES), both, split_axis=...  21 us
    pallas_call x1, Pallas kernels, per_device(): pl.pallas_call(functools.partial(inner_kernel, devices, capacity), out_sh...  5.23 us
    pallas_call x1, Pallas kernels, per_device(): pl.pallas_call(flow_inner_kernel, out_shape=jax.ShapeDtypeStruct((tile_ro...  4.38 us
    pallas_call x1, Pallas kernels, per_device(): pl.pallas_call(functools.partial(ends_kernel, devices, capacity), out_sha...  2.81 us
    ppermute x1, starting transfers between devices, per_device(): above = lax.ppermute(bot_rows, 'tx', up)  2.75 us
    ppermute x1, starting transfers between devices, per_device(): from_previous = lax.ppermute(to_next, both, up)  2.36 us
    pallas_call x1, Pallas kernels, per_device(): pl.pallas_call(edge_kernel, out_shape=(message, message), in_specs=hbm_sp...  2.12 us
    pallas_call x1, Pallas kernels, per_device(): pl.pallas_call(flow_ends_kernel, out_shape=jax.ShapeDtypeStruct((tile_row...  2.03 us
  transfers between devices with their start and end apart: 4, of which 0 were waited for; matrix products, arithmetic and copies ran while one was open for 0% of the time, Pallas kernels for 20%

profile of v6, /device:TPU:0, one launch (start us, length us, event | category | flops | bytes accessed | tf_op | source)
XLA Modules:
  0.0 47.7 jit_solution(17770045726598206095)
XLA Ops:
  0.6 0.0 copy-start.4
  0.6 0.0 copy-start.6
  0.7 0.0 copy-start.5
  0.7 0.0 copy-start.8
  0.7 0.0 copy-start.7
  0.7 2.1 %edges.1 = (bf16[32,512]{1,0:T(8,128)(2,1)}, bf16[32,512]{1,0:T(8,128)(2,1)}) custom-call(bf16[2,64,512]{2,1,0:T(8,128)(2,1)} %sar_ref.3, f32[256,256]{1,0:T(8,128)} %depth_ref.1, f32[256,256]{1,0:T(8,128)} %slope_ref.5, f32[256,256]{1,0:T(8,128)} %rain_ref.5, s32[256,256]{1,0:T(8,128)} %dir_ref.5), custom_call_target="tpu_custom_call" | custom-call | tf_op jit(solution)/shard_map/edges/pallas_call | solution.py:553
  2.8 2.4 %collective-permute-start = (bf16[32,512]{1,0:T(8,128)(2,1)}, bf16[32,512]{1,0:T(8,128)(2,1)S(1)}, u32[]{:S(2)}, u32[]{:S(2)}) collective-permute-start(bf16[32,512]{1,0:T(8,128)(2,1)} %get-tuple-element.21), channel_id=1, source_target_pairs={{0,1},{1,2},{2,3},{3,4},{4,5},{5,6},{6,7},{7,8},{8,9},{9,10},{10,1... | collective-permute-start | bytes 98312 | tf_op jit(solution)/shard_map/ppermute | solution.py:567
  5.2 1.3 %collective-permute-start.1 = (bf16[32,512]{1,0:T(8,128)(2,1)}, bf16[32,512]{1,0:T(8,128)(2,1)S(1)}, u32[]{:S(2)}, u32[]{:S(2)}) collective-permute-start(bf16[32,512]{1,0:T(8,128)(2,1)} %get-tuple-element.22), channel_id=1, source_target_pairs={{1,0},{2,1},{3,2},{4,3},{5,4},{6,5},{7,6},{8,7},{9,8},{10,9},{11,1... | collective-permute-start | bytes 98312 | tf_op jit(solution)/shard_map/ppermute | solution.py:568
  6.5 0.0 copy-start.9
  6.5 0.0 copy-start.10
  6.5 0.0 copy-start.11
  6.5 0.0 copy-start.12
  6.5 0.0 copy-done.4
  6.5 0.0 copy-done.6
  6.5 0.0 copy-done.5
  6.6 0.0 copy-done.8
  6.6 0.0 copy-done.7
  6.6 0.6 %copy-done.9 = bf16[16,2,3,3]{0,1,3,2:T(2,128)(2,1)S(1)} copy-done((bf16[16,2,3,3]{0,1,3,2:T(2,128)(2,1)S(1)}, bf16[16,2,3,3]{0,1,3,2:T(2,128)(2,1)}, u32[]{:S(2)}) %copy-start.9) | copy-done | bytes 600
  7.2 0.0 copy-done.10
  7.2 0.0 copy-done.11
  7.2 0.0 copy-done.12
  7.2 5.2 %inner.1 = (bf16[224,128]{1,0:T(8,128)(2,1)S(1)}, bf16[224,768]{1,0:T(8,128)(2,1)S(1)}, bf16[224,768]{1,0:T(8,128)(2,1)S(1)}, bf16[48,256]{1,0:T(8,128)(2,1)S(1)...) custom-call(bf16[3,3,2,16]{3,2,1,0:T(2,128)(2,1)S(1)} %bitcast.18, ...), custom_call_target="tpu_custom_call" | custom-call | flops 8000000000 | bytes 4000000 | tf_op jit(solution)/shard_map/inner/pallas_call | solution.py:580
  12.4 0.0 collective-permute-done.above_ref.from_left_ref
  12.4 0.0 collective-permute-done.1.below_ref.from_right_ref
  12.4 0.0 copy-start.2
  12.4 0.0 copy-start.3
  12.5 2.8 %ends.1 = (bf16[64,512]{1,0:T(8,128)(2,1)}, bf16[1280,128]{1,0:T(8,128)(2,1)S(1)}) custom-call(bf16[32,512]{1,0:T(8,128)(2,1)S(1)} %collective-permute-done.above_ref.from_left_ref, bf16[32,512]{1,0:T(8,128)(2,1)S(1)} %collective-permute-done.1.below_ref.from_right_ref, bf16[224,128]{1,0:T(8,128)(2,1)S(1)} %get-tuple-element.23.w1_ref, ...), custom_call_target="tpu_custom_call" | custom-call | tf_op jit(solution)/shard_map/ends/pallas_call | solution.py:616
  15.3 0.0 copy-start
  15.3 0.0 copy-start.1
  15.3 21.0 %all_to_all.5 = bf16[32,40,128]{2,1,0:T(8,128)(2,1)S(1)} all-to-all(bf16[32,40,128]{2,1,0:T(8,128)(2,1)S(1)} %bitcast.15), channel_id=1, replica_groups=mesh['tx'=8,'ty'=4] {'tx','ty'}, dimensions={0} | all-to-all | bytes 655360 | tf_op jit(solution)/shard_map/all_to_all | solution.py:629
  36.3 0.0 copy-done.2
  36.3 0.0 copy-done.3
  36.3 0.0 copy-done
  36.3 0.0 copy-done.1
  36.3 0.9 %level.1 = (f32[256,256]{1,0:T(8,128)S(1)}, f32[4,256,128]{2,1,0:T(8,128)S(1)}, bf16[32,384]{1,0:T(8,128)(2,1)S(1)}, bf16[32,384]{1,0:T(8,128)(2,1)S(1)}) custom-call(bf16[1280,128]{1,0:T(8,128)(2,1)S(1)} %bitcast.14, bf16[32,512]{1,0:T(8,128)(2,1)S(1)} %collective-permute-done.above_ref.from_left_ref, ...), custom_call_target="tpu_custom_call" | custom-call | tf_op jit(solution)/shard_map/level/pallas_call | solution.py:635
  37.2 2.7 %collective-permute-start.2 = (bf16[32,384]{1,0:T(8,128)(2,1)S(1)}, bf16[32,384]{1,0:T(8,128)(2,1)S(1)}, u32[]{:S(2)}, u32[]{:S(2)}) collective-permute-start(bf16[32,384]{1,0:T(8,128)(2,1)S(1)} %get-tuple-element.38), channel_id=1, source_target_pairs={{0,4},{4,8},{8,12},{12,16},{16,20},{20,24},{24,28},{1,5},{5,9},{9,... | collective-permute-start | bytes 73736 | tf_op jit(solution)/shard_map/ppermute | solution.py:650
  39.9 1.3 %collective-permute-start.3 = (bf16[32,384]{1,0:T(8,128)(2,1)S(1)}, bf16[32,384]{1,0:T(8,128)(2,1)S(1)}, u32[]{:S(2)}, u32[]{:S(2)}) collective-permute-start(bf16[32,384]{1,0:T(8,128)(2,1)S(1)} %get-tuple-element.39), channel_id=1, source_target_pairs={{4,0},{8,4},{12,8},{16,12},{20,16},{24,20},{28,24},{5,1},{9,5},{13... | collective-permute-start | bytes 73736 | tf_op jit(solution)/shard_map/ppermute | solution.py:651
  41.2 4.4 %flow_inner.1.inner_ref = f32[256,256]{1,0:T(8,128)S(1)} custom-call(f32[256,256]{1,0:T(8,128)S(1)} %get-tuple-element.36.level_ref, f32[4,256,128]{2,1,0:T(8,128)S(1)} %get-tuple-element.37.side_ref, f32[256,256]{1,0:T(8,128)S(1)} %copy-done, s32[256,256]{1,0:T(8,128)S(1)} %copy-done.2, f32[256,256]{1,0:T(8,128)S(1)} %copy-done.1), custom_call_target="tpu_custom_call" | custom-call | flops 5000000000 | bytes 4000000 | tf_op jit(solution)/shard_map/flow_inner/pallas_call | solution.py:653
  45.6 0.0 collective-permute-done.2.above_ref
  45.6 0.0 collective-permute-done.3.below_ref
  45.7 2.0 %flow_ends.1 = f32[256,256]{1,0:T(8,128)} custom-call(f32[256,256]{1,0:T(8,128)S(1)} %flow_inner.1.inner_ref, f32[256,256]{1,0:T(8,128)S(1)} %get-tuple-element.36.level_ref, f32[4,256,128]{2,1,0:T(8,128)S(1)} %get-tuple-element.37.side_ref, f32[256,256]{1,0:T(8,128)S(1)} %copy-done, s32[256,256]{1,0:T(8,128)S(1)} %copy-done.2, f32[256,256]{1,0:T(8,128)S(1)} %copy-done.1, ...), custom_call_target="tpu_custom_call" | custom-call | tf_op jit(solution)/shard_map/flow_ends/pallas_call | solution.py:663
Async XLA Ops:
  0.6 5.9 %copy-start.4 = (bf16[2,64,512]{2,1,0:T(8,128)(2,1)S(1)}, bf16[2,64,512]{2,1,0:T(8,128)(2,1)}, u32[]{:S(2)}) copy-start(bf16[2,64,512]{2,1,0:T(8,128)(2,1)} %sar_ref.3) | copy-start | bytes 393220
  0.6 5.9 %copy-start.6 = (s32[64,512]{1,0:T(8,128)S(1)}, s32[64,512]{1,0:T(8,128)}, u32[]{:S(2)}) copy-start(s32[64,512]{1,0:T(8,128)} %cell_ref.3) | copy-start | bytes 393220
  0.7 5.9 %copy-start.5 = (f32[64,512]{1,0:T(8,128)S(1)}, f32[64,512]{1,0:T(8,128)}, u32[]{:S(2)}) copy-start(f32[64,512]{1,0:T(8,128)} %gw_ref.3) | copy-start | bytes 393220
  0.7 5.9 %copy-start.8 = (bf16[16,16,3,3]{1,0,3,2:T(8,128)(2,1)S(1)}, bf16[16,16,3,3]{1,0,3,2:T(8,128)(2,1)}, u32[]{:S(2)}) copy-start(bf16[16,16,3,3]{1,0,3,2:T(8,128)(2,1)} %param.16) | copy-start | bytes 13828
  0.7 5.9 %copy-start.7 = (bf16[16,16,3,3]{1,0,3,2:T(8,128)(2,1)S(1)}, bf16[16,16,3,3]{1,0,3,2:T(8,128)(2,1)}, u32[]{:S(2)}) copy-start(bf16[16,16,3,3]{1,0,3,2:T(8,128)(2,1)} %param.15) | copy-start | bytes 13828
  2.8 9.6 %collective-permute-start = (bf16[32,512]{1,0:T(8,128)(2,1)}, bf16[32,512]{1,0:T(8,128)(2,1)S(1)}, u32[]{:S(2)}, u32[]{:S(2)}) collective-permute-start(bf16[32,512]{1,0:T(8,128)(2,1)} %get-tuple-element.21), channel_id=1, source_target_pairs={{0,1},{1,2},{2,3},{3,4},{4,5},{5,6},{6,7},{7,8},{8,9},{9,10},{10,1... | collective-permute-start | bytes 98312 | tf_op jit(solution)/shard_map/ppermute | solution.py:567
  5.2 7.2 %collective-permute-start.1 = (bf16[32,512]{1,0:T(8,128)(2,1)}, bf16[32,512]{1,0:T(8,128)(2,1)S(1)}, u32[]{:S(2)}, u32[]{:S(2)}) collective-permute-start(bf16[32,512]{1,0:T(8,128)(2,1)} %get-tuple-element.22), channel_id=1, source_target_pairs={{1,0},{2,1},{3,2},{4,3},{5,4},{6,5},{7,6},{8,7},{9,8},{10,9},{11,1... | collective-permute-start | bytes 98312 | tf_op jit(solution)/shard_map/ppermute | solution.py:568
  6.5 0.7 %copy-start.9 = (bf16[16,2,3,3]{0,1,3,2:T(2,128)(2,1)S(1)}, bf16[16,2,3,3]{0,1,3,2:T(2,128)(2,1)}, u32[]{:S(2)}) copy-start(bf16[16,2,3,3]{0,1,3,2:T(2,128)(2,1)} %param.14) | copy-start | bytes 1732
  6.5 0.7 %copy-start.10 = (bf16[1,16,3,3]{1,3,2,0:T(4,128)(2,1)S(1)}, bf16[1,16,3,3]{1,3,2,0:T(4,128)(2,1)}, u32[]{:S(2)}) copy-start(bf16[1,16,3,3]{1,3,2,0:T(4,128)(2,1)} %param.17) | copy-start | bytes 868
  6.5 0.7 %copy-start.11 = (s32[64,1]{0,1:T(1,128)S(1)}, s32[64,1]{0,1:T(1,128)}, u32[]{:S(2)}) copy-start(s32[64,1]{0,1:T(1,128)} %param.20) | copy-start | bytes 772
  6.5 0.7 %copy-start.12 = (s32[64,1]{0,1:T(1,128)S(1)}, s32[64,1]{0,1:T(1,128)}, u32[]{:S(2)}) copy-start(s32[64,1]{0,1:T(1,128)} %param.21) | copy-start | bytes 772
  12.4 23.8 %copy-start.2 = (s32[256,256]{1,0:T(8,128)S(1)}, s32[256,256]{1,0:T(8,128)}, u32[]{:S(2)}) copy-start(s32[256,256]{1,0:T(8,128)} %dir_ref.5) | copy-start | bytes 786436
  12.4 23.8 %copy-start.3 = (f32[256,256]{1,0:T(8,128)S(1)}, f32[256,256]{1,0:T(8,128)}, u32[]{:S(2)}) copy-start(f32[256,256]{1,0:T(8,128)} %depth_ref.1) | copy-start | bytes 786436
  15.3 21.0 %copy-start = (f32[256,256]{1,0:T(8,128)S(1)}, f32[256,256]{1,0:T(8,128)}, u32[]{:S(2)}) copy-start(f32[256,256]{1,0:T(8,128)} %slope_ref.5) | copy-start | bytes 786436
  15.3 21.0 %copy-start.1 = (f32[256,256]{1,0:T(8,128)S(1)}, f32[256,256]{1,0:T(8,128)}, u32[]{:S(2)}) copy-start(f32[256,256]{1,0:T(8,128)} %rain_ref.5) | copy-start | bytes 786436
  37.2 8.4 %collective-permute-start.2 = (bf16[32,384]{1,0:T(8,128)(2,1)S(1)}, bf16[32,384]{1,0:T(8,128)(2,1)S(1)}, u32[]{:S(2)}, u32[]{:S(2)}) collective-permute-start(bf16[32,384]{1,0:T(8,128)(2,1)S(1)} %get-tuple-element.38), channel_id=1, source_target_pairs={{0,4},{4,8},{8,12},{12,16},{16,20},{20,24},{24,28},{1,5},{5,9},{9,... | collective-permute-start | bytes 73736 | tf_op jit(solution)/shard_map/ppermute | solution.py:650
  39.9 5.7 %collective-permute-start.3 = (bf16[32,384]{1,0:T(8,128)(2,1)S(1)}, bf16[32,384]{1,0:T(8,128)(2,1)S(1)}, u32[]{:S(2)}, u32[]{:S(2)}) collective-permute-start(bf16[32,384]{1,0:T(8,128)(2,1)S(1)} %get-tuple-element.39), channel_id=1, source_target_pairs={{4,0},{8,4},{12,8},{16,12},{20,16},{24,20},{28,24},{5,1},{9,5},{13... | collective-permute-start | bytes 73736 | tf_op jit(solution)/shard_map/ppermute | solution.py:651

commit v7 on v6

--- a/solution.py
+++ b/solution.py
@@ -119,9 +119,11 @@
 
 
 def edge_kernel(
-    sar_hbm, depth_hbm, slope_hbm, rain_hbm, dir_hbm, up_ref, down_ref,
+    sar_hbm, depth_hbm, slope_hbm, rain_hbm, dir_hbm, k1_hbm, k4_hbm, tile_hbm, row_hbm,
+    first_swap_ref, second_swap_ref, k1_ref, k4_ref, tile_ref, row_ref,
     last_ref, first_ref, depth_ref, slope_ref, rain_ref, dir_ref, sems,
 ):
+    even = rem(lax.axis_index("tx") * lax.axis_size("ty") + lax.axis_index("ty"), 2) == 0
     lines, px = sar_hbm.shape[1:]
     cols = depth_hbm.shape[1]
     h = SUBSTEPS
@@ -131,6 +133,7 @@
             (
                 (depth_hbm, depth_ref), (slope_hbm, slope_ref), (rain_hbm, rain_ref), (dir_hbm, dir_ref),
                 (sar_hbm.at[:, lines - 16 : lines, :], last_ref), (sar_hbm.at[:, 0:16, :], first_ref),
+                (k1_hbm, k1_ref), (k4_hbm, k4_ref), (tile_hbm, tile_ref), (row_hbm, row_ref),
             )
         )
     ]
@@ -145,19 +148,31 @@
         dir_ref[...].astype(f32),
     )
     zeros = jnp.zeros((8, px), f32)
-    for ref, image_ref, lo, strip in (
-        (up_ref, last_ref, 16 - HALO_LINES, lambda x: jnp.transpose(x[:, cols - LANES :], (1, 0))[LANES - h :]),
-        (down_ref, first_ref, 0, lambda x: jnp.transpose(x[:, 0:LANES], (1, 0))[0:h]),
+    messages = []
+    for image_ref, lo, strip in (
+        (last_ref, 16 - HALO_LINES, lambda x: jnp.transpose(x[:, cols - LANES :], (1, 0))[LANES - h :]),
+        (first_ref, 0, lambda x: jnp.transpose(x[:, 0:LANES], (1, 0))[0:h]),
     ):
         image = [image_ref[ch].astype(f32)[lo : lo + HALO_LINES] for ch in range(2)]
         strips = [strip(x) for x in fields]
-        ref[...] = jnp.concatenate(
-            [jnp.concatenate(strips[0:2], 1), jnp.concatenate(strips[2:4], 1), *image, zeros], 0
-        ).astype(bf16)
-
-
-def strips_of(ref, keep):
-    both = jnp.where(keep, ref[0:16, :].astype(f32), 0.0)
+        messages.append(
+            jnp.concatenate([jnp.concatenate(strips[0:2], 1), jnp.concatenate(strips[2:4], 1), *image, zeros], 0)
+        )
+    first, second = in_turn(even, *messages)
+    first_swap_ref[...] = first.astype(bf16)
+    second_swap_ref[...] = second.astype(bf16)
+
+
+def in_turn(even, to_next, to_previous):
+    return jnp.where(even, to_next, to_previous), jnp.where(even, to_previous, to_next)
+
+
+def from_turns(even, first, second):
+    return jnp.where(even, second, first), jnp.where(even, first, second)
+
+
+def strips_of(message, keep):
+    both = jnp.where(keep, message, 0.0)
     cols = both.shape[1] // 2
     return [both[0:8, 0:cols], both[0:8, cols:], both[8:16, 0:cols], both[8:16, cols:]]
 
@@ -307,7 +322,7 @@
 
 def ends_kernel(
     devices, capacity,
-    above_ref, below_ref, w1_ref, w2_ref, w3_ref, w4_ref, perm_ref, extra_ref, frac_in, slots_in, e1_ref, e2_ref, e3_ref,
+    first_swap_ref, second_swap_ref, w1_ref, w2_ref, w3_ref, w4_ref, perm_ref, extra_ref, frac_in, slots_in, e1_ref, e2_ref, e3_ref,
     sar_ref, gw_ref, cell_ref,
     frac_ref, send_ref,
     f_ref,
@@ -316,8 +331,9 @@
     n_ty = lax.axis_size("ty")
     me = lax.axis_index("tx") * n_ty + lax.axis_index("ty")
     rows = OUT_LINES * CH
-    above = above_ref[16:32, :].astype(f32)
-    below = below_ref[16:32, :].astype(f32)
+    above, below = from_turns(
+        rem(me, 2) == 0, first_swap_ref[16:32, :].astype(f32), second_swap_ref[16:32, :].astype(f32)
+    )
     n = HALO_LINES
 
     pieces = []
@@ -378,8 +394,8 @@
 
 def level_kernel(
     devices,
-    got_ref, from_left_ref, from_right_ref, depth_ref, slope_ref, rain_ref, dir_ref,
-    level_ref, side_ref, top_ref, bot_ref,
+    got_ref, first_swap_ref, second_swap_ref, depth_ref, slope_ref, rain_ref, dir_ref,
+    level_ref, side_ref, first_ref, second_ref,
 ):
     tile_rows, tile_cols = depth_ref.shape
     h = SUBSTEPS
@@ -413,8 +429,13 @@
     summed_side = dot(placer(1), strip(0, 0)) + dot(placer(2), strip(1, LANES - h))
 
     ty = lax.axis_index("ty")
-    left = strips_of(from_left_ref, ty > 0)
-    right = strips_of(from_right_ref, ty < lax.axis_size("ty") - 1)
+    tx = lax.axis_index("tx")
+    previous, following = from_turns(
+        rem(tx * lax.axis_size("ty") + ty, 2) == 0,
+        first_swap_ref[0:16, :].astype(f32), second_swap_ref[0:16, :].astype(f32),
+    )
+    left = strips_of(previous, ty > 0)
+    right = strips_of(following, ty < lax.axis_size("ty") - 1)
     gap = jnp.zeros((LANES - 2 * h, tile_rows), f32)
     depth_side, conv_side, rain_side, code_side = [
         transposed(jnp.concatenate([r, gap, l], 0)) for r, l in zip(right, left)
@@ -436,12 +457,13 @@
         own = [x[at, :] for x in owns]
         own[2] = runoff_coef * jnp.sqrt(own[2])
         own[3] = own[3].astype(f32)
-        return jnp.concatenate([jnp.concatenate([o, x[at]], 1) for o, x in zip(own, sides)], 0).astype(bf16)
+        return jnp.concatenate([jnp.concatenate([o, x[at]], 1) for o, x in zip(own, sides)], 0)
 
     for i, x in enumerate(sides):
         side_ref[i] = x
-    top_ref[...] = end_rows(slice(0, h))
-    bot_ref[...] = end_rows(slice(tile_rows - h, tile_rows))
+    first, second = in_turn(rem(tx, 2) == 0, end_rows(slice(tile_rows - h, tile_rows)), end_rows(slice(0, h)))
+    first_ref[...] = first.astype(bf16)
+    second_ref[...] = second.astype(bf16)
 
 
 def substeps(level, rain, conv, code, rain_s, conv_s, m_ref, part_ref, up_ref, down_ref, chunk):
@@ -493,11 +515,12 @@
     out_ref[...] = level_at(0, 0, rows)[:, 0:cols]
 
 
-def flow_ends_kernel(inner_ref, level_ref, side_ref, slope_ref, dir_ref, rain_ref, above_ref, below_ref, out_ref, *scratch):
+def flow_ends_kernel(inner_ref, level_ref, side_ref, slope_ref, dir_ref, rain_ref, first_swap_ref, second_swap_ref, out_ref, *scratch):
     rows, cols = level_ref.shape
     h = SUBSTEPS
-    above = above_ref[...].astype(f32)
-    below = below_ref[...].astype(f32)
+    above, below = from_turns(
+        rem(lax.axis_index("tx"), 2) == 0, first_swap_ref[...].astype(f32), second_swap_ref[...].astype(f32)
+    )
     fields = []
     for i, ref in enumerate((level_ref, rain_ref, slope_ref, dir_ref)):
         ends = []
@@ -542,30 +565,36 @@
     tile_rows, tile_cols = depth.shape
     capacity = max(2, 2 * az_lines // devices)
 
-    def steps(axis):
-        size = lax.axis_size(axis)
-        up = [(i, i + 1) for i in range(size - 1)]
-        return up, [(j, i) for i, j in up]
+    def swaps(axis, first, second):
+        out = []
+        for start, x in enumerate((first, second)):
+            pairs = [(i, i + 1) for i in range(start, lax.axis_size(axis) - 1, 2)]
+            out.append(lax.ppermute(x, axis, pairs + [(j, i) for i, j in pairs]))
+        return out
 
     params = pltpu.CompilerParams(vmem_limit_bytes=VMEM_LIMIT)
-    up, down = steps(both)
-    message = jax.ShapeDtypeStruct((32, range_px), bf16)
-    to_next, to_previous = pl.pallas_call(
+    message = pltpu.VMEM((32, range_px), bf16)
+    small = (
+        jnp.transpose(kernel_first, (2, 3, 1, 0)),
+        jnp.transpose(kernel_last[0], (1, 2, 0)),
+        block_tile.reshape(1, az_lines),
+        block_row.reshape(1, az_lines),
+    )
+    first, second, *small = pl.pallas_call(
         edge_kernel,
-        out_shape=(message, message),
-        in_specs=hbm_specs(5),
-        out_specs=tuple(vmem_specs(2)),
+        out_shape=(message, message, *[pltpu.VMEM(x.shape, x.dtype) for x in small]),
+        in_specs=hbm_specs(9),
+        out_specs=tuple(vmem_specs(6)),
         scratch_shapes=[
             pltpu.VMEM((2, 16, range_px), bf16),
             pltpu.VMEM((2, 16, range_px), bf16),
             *[pltpu.VMEM(x.shape, x.dtype) for x in (depth, slope, rain, flow_dir)],
-            pltpu.SemaphoreType.DMA((6,)),
+            pltpu.SemaphoreType.DMA((10,)),
         ],
         compiler_params=pltpu.CompilerParams(vmem_limit_bytes=VMEM_MOST),
         name="edges",
-    )(sar_image, depth, slope, rain, flow_dir)
-    from_previous = lax.ppermute(to_next, both, up)
-    from_next = lax.ppermute(to_previous, both, down)
+    )(sar_image, depth, slope, rain, flow_dir, *small)
+    halo = swaps(both, first, second)
 
     rows, cols = OUT_LINES * CH, IN_LINES * CH
     slots = devices * capacity * 4
@@ -606,11 +635,10 @@
         cost_estimate=cost(8_000_000_000),
         name="inner",
     )(
-        jnp.transpose(kernel_first, (2, 3, 1, 0)),
+        small[0],
         jnp.transpose(kernel_second, (2, 3, 0, 1)).reshape(9 * CH, CH),
         jnp.transpose(kernel_third, (2, 3, 0, 1)).reshape(9 * CH, CH),
-        jnp.transpose(kernel_last[0], (1, 2, 0)),
-        block_tile.reshape(1, az_lines), block_row.reshape(1, az_lines),
+        *small[1:],
         sar_image, geo_weight, cell_index,
     )
     fraction, send = pl.pallas_call(
@@ -624,7 +652,7 @@
         scratch_shapes=[pltpu.VMEM((az_lines, range_px), f32)],
         compiler_params=params,
         name="ends",
-    )(from_previous, from_next, *prepared, sar_image, geo_weight, cell_index)
+    )(*halo, *prepared, sar_image, geo_weight, cell_index)
 
     got = lax.all_to_all(
         send.reshape(devices, send_rows, LANES), both, split_axis=0, concat_axis=0, tiled=True
@@ -632,7 +660,7 @@
 
     wide_cols = tile_cols + LANES
     edge = jax.ShapeDtypeStruct((4 * SUBSTEPS, wide_cols), bf16)
-    level, side, top_rows, bot_rows = pl.pallas_call(
+    level, side, first, second = pl.pallas_call(
         functools.partial(level_kernel, devices),
         out_shape=(
             jax.ShapeDtypeStruct((tile_rows, tile_cols), f32),
@@ -644,11 +672,9 @@
         out_specs=tuple(vmem_specs(4)),
         compiler_params=params,
         name="level",
-    )(got, from_previous, from_next, depth, slope, rain, flow_dir)
-
-    up, down = steps("tx")
-    above = lax.ppermute(bot_rows, "tx", up)
-    below = lax.ppermute(top_rows, "tx", down)
+    )(got, *halo, depth, slope, rain, flow_dir)
+
+    row_halo = swaps("tx", first, second)
 
     inner = pl.pallas_call(
         flow_inner_kernel,
@@ -668,7 +694,7 @@
         scratch_shapes=flow_scratch(6 * SUBSTEPS, wide_cols),
         compiler_params=params,
         name="flow_ends",
-    )(inner, level, side, slope, flow_dir, rain, above, below)
+    )(inner, level, side, slope, flow_dir, rain, *row_halo)
     return (fraction, level)
 
 

time: 48.5 us -> 42.1 us (0.87)
  the two profiles are of different devices: /device:TPU:0 before, /device:TPU:8 now
where the time goes in v7:
time: 42.1 us; the launch traced here: 41.9 us
  Pallas kernels  17 us (40%)
  blocking collectives  15.1 us (36%)
  starting transfers between devices  8.99 us (21%)
  between operations  0.82 us (2%)
    all_to_all x1, blocking collectives, per_device(): lax.all_to_all(send.reshape(devices, send_rows, LANES), both, split_axis=...  15.1 us
    ppermute x4, starting transfers between devices, swaps(): out.append(lax.ppermute(x, axis, pairs + [(j, i) for i, j in pairs]))  8.99 us
    pallas_call x1, Pallas kernels, per_device(): pl.pallas_call(functools.partial(inner_kernel, devices, capacity), out_sh...  5.23 us
    pallas_call x1, Pallas kernels, per_device(): pl.pallas_call(flow_inner_kernel, out_shape=jax.ShapeDtypeStruct((tile_ro...  4.38 us
    pallas_call x1, Pallas kernels, per_device(): pl.pallas_call(functools.partial(ends_kernel, devices, capacity), out_sha...  2.82 us
    pallas_call x1, Pallas kernels, per_device(): pl.pallas_call(flow_ends_kernel, out_shape=jax.ShapeDtypeStruct((tile_row...  2.04 us
    pallas_call x1, Pallas kernels, per_device(): pl.pallas_call(edge_kernel, out_shape=(message, message, *[pltpu.VMEM(x.s...  1.55 us
    pallas_call x1, Pallas kernels, per_device(): pl.pallas_call(functools.partial(level_kernel, devices), out_shape=(jax.S...  0.93 us
  transfers between devices with their start and end apart: 4, of which 0 were waited for; matrix products, arithmetic and copies ran while one was open for 0% of the time, Pallas kernels for 23%

profile of v7, /device:TPU:8, one launch (start us, length us, event | category | flops | bytes accessed | tf_op | source)
XLA Modules:
  0.0 41.9 jit_solution(18089059321986932011)
XLA Ops:
  0.6 0.0 copy-start.4
  0.6 0.0 copy-start.5
  0.7 0.0 copy-start.6
  0.7 0.0 copy-start.7
  0.7 0.0 copy-start.8
  0.7 1.6 %edges.1 = (bf16[32,512]{1,0:T(8,128)(2,1)S(1)}, bf16[32,512]{1,0:T(8,128)(2,1)S(1)}, bf16[3,3,2,16]{3,2,1,0:T(2,128)(2,1)S(1)}, bf16[3,3,16]{2,1,0:T(4,128)(2,1...) custom-call(bf16[2,64,512]{2,1,0:T(8,128)(2,1)} %sar_ref.3, f32[256,256]{1,0:T(8,128)} %depth_ref.1, ...), custom_call_target="tpu_custom_call" | custom-call | tf_op jit(solution)/shard_map/edges/pallas_call | solution.py:583
  2.2 0.1 collective-permute-start
  2.3 4.3 %collective-permute-start.1 = (bf16[32,512]{1,0:T(8,128)(2,1)S(1)}, bf16[32,512]{1,0:T(8,128)(2,1)S(1)}, u32[]{:S(2)}, u32[]{:S(2)}) collective-permute-start(bf16[32,512]{1,0:T(8,128)(2,1)S(1)} %get-tuple-element.26), channel_id=1, source_target_pairs={{1,2},{3,4},{5,6},{7,8},{9,10},{11,12},{13,14},{15,16},{17,18},{19... | collective-permute-start | bytes 98312 | tf_op jit(solution)/shard_map/ppermute | solution.py:572
  6.7 0.0 copy-done.4
  6.7 0.0 copy-done.5
  6.7 0.0 copy-done.6
  6.7 0.0 copy-done.7
  6.7 0.0 copy-done.8
  6.7 5.2 %inner.1 = (bf16[224,128]{1,0:T(8,128)(2,1)S(1)}, bf16[224,768]{1,0:T(8,128)(2,1)S(1)}, bf16[224,768]{1,0:T(8,128)(2,1)S(1)}, bf16[48,256]{1,0:T(8,128)(2,1)S(1)...) custom-call(bf16[3,3,2,16]{3,2,1,0:T(2,128)(2,1)S(1)} %get-tuple-ele, ...), custom_call_target="tpu_custom_call" | custom-call | flops 8000000000 | bytes 4000000 | tf_op jit(solution)/shard_map/inner/pallas_call | solution.py:609
  11.9 0.0 collective-permute-done.first_swap_ref
  12.0 0.0 collective-permute-done.1.second_swap_ref
  12.0 0.0 copy-start.2
  12.0 0.0 copy-start.3
  12.0 2.8 %ends.1 = (bf16[64,512]{1,0:T(8,128)(2,1)}, bf16[1280,128]{1,0:T(8,128)(2,1)S(1)}) custom-call(bf16[32,512]{1,0:T(8,128)(2,1)S(1)} %collective-permute-done.first_swap_ref, bf16[32,512]{1,0:T(8,128)(2,1)S(1)} %collective-permute-done.1.second_swap_ref, bf16[224,128]{1,0:T(8,128)(2,1)S(1)} %get-tuple-element.31.w1_ref, ...), custom_call_target="tpu_custom_call" | custom-call | tf_op jit(solution)/shard_map/ends/pallas_call | solution.py:644
  14.8 0.0 copy-start
  14.8 0.0 copy-start.1
  14.8 15.1 %all_to_all.5 = bf16[32,40,128]{2,1,0:T(8,128)(2,1)S(1)} all-to-all(bf16[32,40,128]{2,1,0:T(8,128)(2,1)S(1)} %bitcast.15), channel_id=1, replica_groups=mesh['tx'=8,'ty'=4] {'tx','ty'}, dimensions={0} | all-to-all | bytes 655360 | tf_op jit(solution)/shard_map/all_to_all | solution.py:657
  29.9 0.0 copy-done.2
  29.9 0.0 copy-done.3
  29.9 0.0 copy-done
  29.9 0.0 copy-done.1
  30.0 0.9 %level.1 = (f32[256,256]{1,0:T(8,128)S(1)}, f32[4,256,128]{2,1,0:T(8,128)S(1)}, bf16[32,384]{1,0:T(8,128)(2,1)S(1)}, bf16[32,384]{1,0:T(8,128)(2,1)S(1)}) custom-call(bf16[1280,128]{1,0:T(8,128)(2,1)S(1)} %bitcast.14, bf16[32,512]{1,0:T(8,128)(2,1)S(1)} %collective-permute-done.first_swap_ref, bf16[32,512]{1,0:T(8,128)(2,1)S(1)} %collective-permute-done.1.second_swap_ref, ...), custom_call_target="tpu_custom_call" | custom-call | tf_op jit(solution)/shard_map/level/pallas_call | solution.py:663
  30.9 0.7 %collective-permute-start.2 = (bf16[32,384]{1,0:T(8,128)(2,1)S(1)}, bf16[32,384]{1,0:T(8,128)(2,1)S(1)}, u32[]{:S(2)}, u32[]{:S(2)}) collective-permute-start(bf16[32,384]{1,0:T(8,128)(2,1)S(1)} %get-tuple-element.46), channel_id=1, source_target_pairs={{0,4},{8,12},{16,20},{24,28},{4,0},{12,8},{20,16},{28,24},{1,5},{9... | collective-permute-start | bytes 73736 | tf_op jit(solution)/shard_map/ppermute | solution.py:572
  31.6 3.9 %collective-permute-start.3 = (bf16[32,384]{1,0:T(8,128)(2,1)S(1)}, bf16[32,384]{1,0:T(8,128)(2,1)S(1)}, u32[]{:S(2)}, u32[]{:S(2)}) collective-permute-start(bf16[32,384]{1,0:T(8,128)(2,1)S(1)} %get-tuple-element.47), channel_id=1, source_target_pairs={{4,8},{12,16},{20,24},{8,4},{16,12},{24,20},{5,9},{13,17},{21,25},... | collective-permute-start | bytes 73736 | tf_op jit(solution)/shard_map/ppermute | solution.py:572
  35.5 4.4 %flow_inner.1.inner_ref = f32[256,256]{1,0:T(8,128)S(1)} custom-call(f32[256,256]{1,0:T(8,128)S(1)} %get-tuple-element.44.level_ref, f32[4,256,128]{2,1,0:T(8,128)S(1)} %get-tuple-element.45.side_ref, f32[256,256]{1,0:T(8,128)S(1)} %copy-done, s32[256,256]{1,0:T(8,128)S(1)} %copy-done.2, f32[256,256]{1,0:T(8,128)S(1)} %copy-done.1), custom_call_target="tpu_custom_call" | custom-call | flops 5000000000 | bytes 4000000 | tf_op jit(solution)/shard_map/flow_inner/pallas_call | solution.py:679
  39.9 0.0 collective-permute-done.2.first_swap_ref
  39.9 0.0 collective-permute-done.3.second_swap_ref
  39.9 2.0 %flow_ends.1 = f32[256,256]{1,0:T(8,128)} custom-call(f32[256,256]{1,0:T(8,128)S(1)} %flow_inner.1.inner_ref, f32[256,256]{1,0:T(8,128)S(1)} %get-tuple-element.44.level_ref, f32[4,256,128]{2,1,0:T(8,128)S(1)} %get-tuple-element.45.side_ref, f32[256,256]{1,0:T(8,128)S(1)} %copy-done, s32[256,256]{1,0:T(8,128)S(1)} %copy-done.2, f32[256,256]{1,0:T(8,128)S(1)} %copy-done.1, ...), custom_call_target="tpu_custom_call" | custom-call | tf_op jit(solution)/shard_map/flow_ends/pallas_call | solution.py:689
Async XLA Ops:
  0.6 6.0 %copy-start.4 = (bf16[2,64,512]{2,1,0:T(8,128)(2,1)S(1)}, bf16[2,64,512]{2,1,0:T(8,128)(2,1)}, u32[]{:S(2)}) copy-start(bf16[2,64,512]{2,1,0:T(8,128)(2,1)} %sar_ref.3) | copy-start | bytes 393220
  0.6 6.0 %copy-start.5 = (f32[64,512]{1,0:T(8,128)S(1)}, f32[64,512]{1,0:T(8,128)}, u32[]{:S(2)}) copy-start(f32[64,512]{1,0:T(8,128)} %gw_ref.3) | copy-start | bytes 393220
  0.7 6.0 %copy-start.6 = (s32[64,512]{1,0:T(8,128)S(1)}, s32[64,512]{1,0:T(8,128)}, u32[]{:S(2)}) copy-start(s32[64,512]{1,0:T(8,128)} %cell_ref.3) | copy-start | bytes 393220
  0.7 6.0 %copy-start.7 = (bf16[16,16,3,3]{1,0,3,2:T(8,128)(2,1)S(1)}, bf16[16,16,3,3]{1,0,3,2:T(8,128)(2,1)}, u32[]{:S(2)}) copy-start(bf16[16,16,3,3]{1,0,3,2:T(8,128)(2,1)} %param.15) | copy-start | bytes 13828
  0.7 6.0 %copy-start.8 = (bf16[16,16,3,3]{1,0,3,2:T(8,128)(2,1)S(1)}, bf16[16,16,3,3]{1,0,3,2:T(8,128)(2,1)}, u32[]{:S(2)}) copy-start(bf16[16,16,3,3]{1,0,3,2:T(8,128)(2,1)} %param.16) | copy-start | bytes 13828
  2.2 9.7 %collective-permute-start = (bf16[32,512]{1,0:T(8,128)(2,1)S(1)}, bf16[32,512]{1,0:T(8,128)(2,1)S(1)}, u32[]{:S(2)}, u32[]{:S(2)}) collective-permute-start(bf16[32,512]{1,0:T(8,128)(2,1)S(1)} %get-tuple-element.25), channel_id=1, source_target_pairs={{0,1},{2,3},{4,5},{6,7},{8,9},{10,11},{12,13},{14,15},{16,17},{18,... | collective-permute-start | bytes 98312 | tf_op jit(solution)/shard_map/ppermute | solution.py:572
  2.3 9.6 %collective-permute-start.1 = (bf16[32,512]{1,0:T(8,128)(2,1)S(1)}, bf16[32,512]{1,0:T(8,128)(2,1)S(1)}, u32[]{:S(2)}, u32[]{:S(2)}) collective-permute-start(bf16[32,512]{1,0:T(8,128)(2,1)S(1)} %get-tuple-element.26), channel_id=1, source_target_pairs={{1,2},{3,4},{5,6},{7,8},{9,10},{11,12},{13,14},{15,16},{17,18},{19... | collective-permute-start | bytes 98312 | tf_op jit(solution)/shard_map/ppermute | solution.py:572
  12.0 18.0 %copy-start.2 = (s32[256,256]{1,0:T(8,128)S(1)}, s32[256,256]{1,0:T(8,128)}, u32[]{:S(2)}) copy-start(s32[256,256]{1,0:T(8,128)} %dir_ref.5) | copy-start | bytes 786436
  12.0 18.0 %copy-start.3 = (f32[256,256]{1,0:T(8,128)S(1)}, f32[256,256]{1,0:T(8,128)}, u32[]{:S(2)}) copy-start(f32[256,256]{1,0:T(8,128)} %depth_ref.1) | copy-start | bytes 786436
  14.8 15.1 %copy-start = (f32[256,256]{1,0:T(8,128)S(1)}, f32[256,256]{1,0:T(8,128)}, u32[]{:S(2)}) copy-start(f32[256,256]{1,0:T(8,128)} %slope_ref.5) | copy-start | bytes 786436
  14.8 15.1 %copy-start.1 = (f32[256,256]{1,0:T(8,128)S(1)}, f32[256,256]{1,0:T(8,128)}, u32[]{:S(2)}) copy-start(f32[256,256]{1,0:T(8,128)} %rain_ref.5) | copy-start | bytes 786436
  30.9 9.0 %collective-permute-start.2 = (bf16[32,384]{1,0:T(8,128)(2,1)S(1)}, bf16[32,384]{1,0:T(8,128)(2,1)S(1)}, u32[]{:S(2)}, u32[]{:S(2)}) collective-permute-start(bf16[32,384]{1,0:T(8,128)(2,1)S(1)} %get-tuple-element.46), channel_id=1, source_target_pairs={{0,4},{8,12},{16,20},{24,28},{4,0},{12,8},{20,16},{28,24},{1,5},{9... | collective-permute-start | bytes 73736 | tf_op jit(solution)/shard_map/ppermute | solution.py:572
  31.6 8.3 %collective-permute-start.3 = (bf16[32,384]{1,0:T(8,128)(2,1)S(1)}, bf16[32,384]{1,0:T(8,128)(2,1)S(1)}, u32[]{:S(2)}, u32[]{:S(2)}) collective-permute-start(bf16[32,384]{1,0:T(8,128)(2,1)S(1)} %get-tuple-element.47), channel_id=1, source_target_pairs={{4,8},{12,16},{20,24},{8,4},{16,12},{24,20},{5,9},{13,17},{21,25},... | collective-permute-start | bytes 73736 | tf_op jit(solution)/shard_map/ppermute | solution.py:572

commit v8 on v7

--- a/solution.py
+++ b/solution.py
@@ -1,4 +1,5 @@
 import functools
+import math
 
 import jax
 import jax.numpy as jnp
@@ -324,8 +325,8 @@
     devices, capacity,
     first_swap_ref, second_swap_ref, w1_ref, w2_ref, w3_ref, w4_ref, perm_ref, extra_ref, frac_in, slots_in, e1_ref, e2_ref, e3_ref,
     sar_ref, gw_ref, cell_ref,
-    frac_ref, send_ref,
-    f_ref,
+    frac_hbm, send_ref,
+    f_ref, frac_ref, sem,
 ):
     lines, px = gw_ref.shape
     n_ty = lax.axis_size("ty")
@@ -357,6 +358,8 @@
     f_ref[0:6, :] = frac[0:6]
     f_ref[lines - 6 :, :] = frac[8:14]
     frac_ref[...] = f_ref[...].astype(bf16)
+    copy = pltpu.make_async_copy(frac_ref, frac_hbm, sem)
+    copy.start()
     quarter = slots_in.shape[1] // 4
     sums = []
     for at in (slice(0, END_LINES), slice(lines - END_LINES, lines)):
@@ -386,6 +389,7 @@
     halves = [by_slot[:, at : at + LANES].reshape(devices, per_tile, LANES) for at in range(0, tile_cols, LANES)]
     packed = jnp.concatenate([*halves, extra], 1)
     send_ref[...] = packed.reshape(send_ref.shape).astype(bf16)
+    copy.wait()
 
 
 def transposed(x):
@@ -466,38 +470,40 @@
     second_ref[...] = second.astype(bf16)
 
 
-def substeps(level, rain, conv, code, rain_s, conv_s, m_ref, part_ref, up_ref, down_ref, chunk):
-    rows, cols = level.shape
-    h = SUBSTEPS
-    for ref in (up_ref, down_ref):
-        ref[0] = jnp.zeros(ref.shape[1:], f32)
-        ref[1, 0:h, :] = jnp.zeros((h, cols), f32)
-        ref[1, h + rows :, :] = jnp.zeros((h, cols), f32)
-    part_ref[0] = level
-    rain_s[...] = rain
-    conv_s[...] = conv
+def substeps(field, n, conv_s, rain_s, m_ref, part_ref, up_ref, down_ref):
+    cols = conv_s.shape[2]
     sides = (-1, 0, 1, -1, 1, -1, 0, 1)
-    for direction, side in enumerate(sides):
-        share = jnp.where(code == direction, conv, 0.0)
-        m_ref[direction] = pltpu.roll(share, side % cols, 1) if side else share
-
-    def level_at(buf, r, n):
-        level = part_ref[buf, r : r + n, :]
-        return level + up_ref[buf, h + r + 1 : h + r + 1 + n, :] + down_ref[buf, h + r - 1 : h + r - 1 + n, :]
+    up_ref[0] = jnp.zeros(up_ref.shape[1:], f32)
+    down_ref[0] = jnp.zeros(down_ref.shape[1:], f32)
+    for i in range(n):
+        conv = field(2, i)
+        code = field(3, i)
+        part_ref[0, i] = field(0, i)
+        rain_s[i] = field(1, i)
+        conv_s[i] = conv
+        for direction, side in enumerate(sides):
+            share = jnp.where(code == direction, conv, 0.0)
+            m_ref[direction, i] = pltpu.roll(share, side % cols, 1) if side else share
+
+    def level_at(buf, i):
+        return part_ref[buf, i] + up_ref[buf, i + 1] + down_ref[buf, i]
 
     def substep(buf, new):
-        for r in range(0, rows, chunk):
-            level = level_at(buf, r, chunk)
-            power = level * jnp.exp((2.0 / 3.0) * jnp.log(jnp.maximum(jnp.abs(level), 1e-30)))
+        for i in range(n):
+            level = level_at(buf, i)
+            power = level * jnp.exp2((2.0 / 3.0 / math.log(2.0)) * jnp.log(jnp.maximum(jnp.abs(level), 1e-30)))
             from_right = pltpu.roll(power, cols - 1, 1)
             from_left = pltpu.roll(power, 1, 1)
-            m = [m_ref[d, r : r + chunk, :] for d in range(8)]
-            up_ref[new, h + r : h + r + chunk, :] = m[0] * from_right + m[1] * power + m[2] * from_left
-            down_ref[new, h + r : h + r + chunk, :] = m[5] * from_right + m[6] * power + m[7] * from_left
-            part_ref[new, r : r + chunk, :] = (
-                level + rain_s[r : r + chunk, :] - conv_s[r : r + chunk, :] * power
-                + (m[3] * from_right + m[4] * from_left)
-            )
+            m = [m_ref[d, i] for d in range(8)]
+            up = m[0] * from_right + m[1] * power + m[2] * from_left
+            down = m[5] * from_right + m[6] * power + m[7] * from_left
+            up_ref[new, i] = up
+            down_ref[new, i + 1] = down
+            if i == 0:
+                up_ref[new, n] = pltpu.roll(up, 7, 0)
+            if i == n - 1:
+                down_ref[new, 0] = pltpu.roll(down, 1, 0)
+            part_ref[new, i] = level + rain_s[i] - conv_s[i] * power + (m[3] * from_right + m[4] * from_left)
 
     def substep_pair(i, carry):
         substep(0, 1)
@@ -505,45 +511,89 @@
         return carry
 
     lax.fori_loop(0, SUBSTEPS // 2, substep_pair, 0)
-    return level_at
-
-
-def flow_inner_kernel(level_ref, side_ref, slope_ref, dir_ref, rain_ref, out_ref, *scratch):
+    return functools.partial(level_at, 0)
+
+
+def staged(ref, n):
+    def field(f, i):
+        return jnp.concatenate([ref[f, t, pl.ds(i, 8, stride=n), :] for t in range(ref.shape[1])], 1)
+
+    return field
+
+
+def flow_inner_kernel(level_ref, side_ref, slope_ref, dir_ref, rain_ref, out_ref, wide_ref, *scratch):
     rows, cols = level_ref.shape
-    own = (level_ref[...], rain_ref[...], runoff_coef * jnp.sqrt(slope_ref[...]), dir_ref[...].astype(f32))
-    level_at = substeps(*[jnp.concatenate([x, side_ref[i]], 1) for i, x in enumerate(own)], *scratch, 16)
-    out_ref[...] = level_at(0, 0, rows)[:, 0:cols]
-
-
-def flow_ends_kernel(inner_ref, level_ref, side_ref, slope_ref, dir_ref, rain_ref, first_swap_ref, second_swap_ref, out_ref, *scratch):
+    n = rows // 8
+    tiles = cols // LANES
+    for f, ref in enumerate((level_ref, rain_ref, slope_ref, dir_ref)):
+        for t in range(tiles):
+            own = ref[:, t * LANES : (t + 1) * LANES].astype(f32)
+            wide_ref[f, t] = runoff_coef * jnp.sqrt(own) if f == 2 else own
+        wide_ref[f, tiles] = side_ref[f]
+    level = substeps(staged(wide_ref, n), n, *scratch)
+    for i in range(n):
+        x = level(i)
+        for t in range(tiles):
+            out_ref[t, pl.ds(i, 8, stride=n), :] = x[:, t * LANES : (t + 1) * LANES]
+
+
+def flow_ends_kernel(
+    inner_ref, level_ref, side_ref, slope_ref, dir_ref, rain_ref, first_swap_ref, second_swap_ref,
+    out_hbm, wide_ref, sems, *scratch,
+):
     rows, cols = level_ref.shape
     h = SUBSTEPS
+    tiles = cols // LANES
+
+    def copy_out(src, to, sem):
+        return pltpu.make_async_copy(src, out_hbm.at[to[0], to[1]], sem)
+
+    copies = []
+    for t in range(tiles):
+        lanes = slice(t * LANES, (t + 1) * LANES)
+        copies.append(copy_out(inner_ref.at[t, h : rows - h, :], (slice(h, rows - h), lanes), sems.at[t]))
+        copies[-1].start()
     above, below = from_turns(
         rem(lax.axis_index("tx"), 2) == 0, first_swap_ref[...].astype(f32), second_swap_ref[...].astype(f32)
     )
-    fields = []
-    for i, ref in enumerate((level_ref, rain_ref, slope_ref, dir_ref)):
-        ends = []
-        for at in (slice(0, 2 * h), slice(rows - 2 * h, rows)):
-            own = ref[at, :].astype(f32)
-            if i == 2:
-                own = runoff_coef * jnp.sqrt(own)
-            ends.append(jnp.concatenate([own, side_ref[i, at, :]], 1))
-        fields.append(jnp.concatenate([above[i * h : (i + 1) * h], *ends, below[i * h : (i + 1) * h]], 0))
-    level_at = substeps(*fields, *scratch, 16)
-    out_ref[h : rows - h, :] = inner_ref[h : rows - h, :]
-    out_ref[0:h, :] = level_at(0, h, h)[:, 0:cols]
-    out_ref[rows - h :, :] = level_at(0, 4 * h, h)[:, 0:cols]
+    for f, ref in enumerate((level_ref, rain_ref, slope_ref, dir_ref)):
+        for t in range(tiles + 1):
+            lanes = slice(t * LANES, (t + 1) * LANES)
+            wide_ref[f, t, 0:h, :] = above[f * h : (f + 1) * h, lanes]
+            wide_ref[f, t, 5 * h :, :] = below[f * h : (f + 1) * h, lanes]
+            for to, at in ((h, slice(0, 2 * h)), (3 * h, slice(rows - 2 * h, rows))):
+                if t < tiles:
+                    own = ref[at, lanes].astype(f32)
+                    own = runoff_coef * jnp.sqrt(own) if f == 2 else own
+                else:
+                    own = side_ref[f, at, :]
+                wide_ref[f, t, to : to + 2 * h, :] = own
+    n = 6 * h // 8
+    level = substeps(staged(wide_ref, n), n, *scratch)
+    for i in range(n):
+        x = level(i)
+        for t in range(tiles):
+            wide_ref[0, t, pl.ds(i, 8, stride=n), :] = x[:, t * LANES : (t + 1) * LANES]
+    for t in range(tiles):
+        lanes = slice(t * LANES, (t + 1) * LANES)
+        for k, (at, to) in enumerate(((h, 0), (4 * h, rows - h))):
+            copies.append(
+                copy_out(wide_ref.at[0, t, at : at + h, :], (slice(to, to + h), lanes), sems.at[tiles + 2 * t + k])
+            )
+            copies[-1].start()
+    for copy in copies:
+        copy.wait()
 
 
 def flow_scratch(rows, cols):
+    n = rows // 8
     return [
-        pltpu.VMEM((rows, cols), f32),
-        pltpu.VMEM((rows, cols), f32),
-        pltpu.VMEM((8, rows, cols), f32),
-        pltpu.VMEM((2, rows, cols), f32),
-        pltpu.VMEM((2, rows + 2 * SUBSTEPS, cols), f32),
-        pltpu.VMEM((2, rows + 2 * SUBSTEPS, cols), f32),
+        pltpu.VMEM((n, 8, cols), f32),
+        pltpu.VMEM((n, 8, cols), f32),
+        pltpu.VMEM((8, n, 8, cols), f32),
+        pltpu.VMEM((2, n, 8, cols), f32),
+        pltpu.VMEM((2, n + 1, 8, cols), f32),
+        pltpu.VMEM((2, n + 1, 8, cols), f32),
     ]
 
 
@@ -648,8 +698,12 @@
             jax.ShapeDtypeStruct((devices * send_rows, LANES), bf16),
         ),
         in_specs=vmem_specs(16),
-        out_specs=tuple(vmem_specs(2)),
-        scratch_shapes=[pltpu.VMEM((az_lines, range_px), f32)],
+        out_specs=(hbm_specs(1)[0], vmem_specs(1)[0]),
+        scratch_shapes=[
+            pltpu.VMEM((az_lines, range_px), f32),
+            pltpu.VMEM((az_lines, range_px), bf16),
+            pltpu.SemaphoreType.DMA(()),
+        ],
         compiler_params=params,
         name="ends",
     )(*halo, *prepared, sar_image, geo_weight, cell_index)
@@ -676,12 +730,16 @@
 
     row_halo = swaps("tx", first, second)
 
+    tiles = tile_cols // LANES
     inner = pl.pallas_call(
         flow_inner_kernel,
-        out_shape=jax.ShapeDtypeStruct((tile_rows, tile_cols), f32),
+        out_shape=jax.ShapeDtypeStruct((tiles, tile_rows, LANES), f32),
         in_specs=vmem_specs(5),
         out_specs=vmem_specs(1)[0],
-        scratch_shapes=flow_scratch(tile_rows, wide_cols),
+        scratch_shapes=[
+            pltpu.VMEM((4, tiles + 1, tile_rows, LANES), f32),
+            *flow_scratch(tile_rows, wide_cols),
+        ],
         compiler_params=params,
         cost_estimate=cost(5_000_000_000),
         name="flow_inner",
@@ -690,8 +748,12 @@
         flow_ends_kernel,
         out_shape=jax.ShapeDtypeStruct((tile_rows, tile_cols), f32),
         in_specs=vmem_specs(8),
-        out_specs=vmem_specs(1)[0],
-        scratch_shapes=flow_scratch(6 * SUBSTEPS, wide_cols),
+        out_specs=hbm_specs(1)[0],
+        scratch_shapes=[
+            pltpu.VMEM((4, tiles + 1, 6 * SUBSTEPS, LANES), f32),
+            pltpu.SemaphoreType.DMA((3 * tiles,)),
+            *flow_scratch(6 * SUBSTEPS, wide_cols),
+        ],
         compiler_params=params,
         name="flow_ends",
     )(inner, level, side, slope, flow_dir, rain, *row_halo)

time: 42.1 us -> 42.3 us (level)
  no operation moved by 1% of the time
where the time goes in v8:
time: 42.3 us; the launch traced here: 42.1 us
  Pallas kernels  17.1 us (40%)
  blocking collectives  15.1 us (36%)
  starting transfers between devices  8.99 us (21%)
  between operations  0.84 us (2%)
    all_to_all x1, blocking collectives, per_device(): lax.all_to_all(send.reshape(devices, send_rows, LANES), both, split_axis=...  15.1 us
    ppermute x4, starting transfers between devices, swaps(): out.append(lax.ppermute(x, axis, pairs + [(j, i) for i, j in pairs]))  8.99 us
    pallas_call x1, Pallas kernels, per_device(): pl.pallas_call(functools.partial(inner_kernel, devices, capacity), out_sh...  5.23 us
    pallas_call x1, Pallas kernels, per_device(): pl.pallas_call(flow_inner_kernel, out_shape=jax.ShapeDtypeStruct((tiles,...  4.6 us
    pallas_call x1, Pallas kernels, per_device(): pl.pallas_call(functools.partial(ends_kernel, devices, capacity), out_sha...  2.83 us
    pallas_call x1, Pallas kernels, per_device(): pl.pallas_call(flow_ends_kernel, out_shape=jax.ShapeDtypeStruct((tile_row...  1.93 us
    pallas_call x1, Pallas kernels, per_device(): pl.pallas_call(edge_kernel, out_shape=(message, message, *[pltpu.VMEM(x.s...  1.55 us
    pallas_call x1, Pallas kernels, per_device(): pl.pallas_call(functools.partial(level_kernel, devices), out_shape=(jax.S...  0.93 us
  transfers between devices with their start and end apart: 4, of which 0 were waited for; matrix products, arithmetic and copies ran while one was open for 0% of the time, Pallas kernels for 23%

profile of v8, /device:TPU:8, one launch (start us, length us, event | category | flops | bytes accessed | tf_op | source)
XLA Modules:
  0.0 42.1 jit_solution(12661932701472792352)
XLA Ops:
  0.6 0.0 copy-start.4
  0.6 0.0 copy-start.5
  0.7 0.0 copy-start.6
  0.7 0.0 copy-start.7
  0.7 0.0 copy-start.8
  0.7 1.6 %edges.1 = (bf16[32,512]{1,0:T(8,128)(2,1)S(1)}, bf16[32,512]{1,0:T(8,128)(2,1)S(1)}, bf16[3,3,2,16]{3,2,1,0:T(2,128)(2,1)S(1)}, bf16[3,3,16]{2,1,0:T(4,128)(2,1...) custom-call(bf16[2,64,512]{2,1,0:T(8,128)(2,1)} %sar_ref.3, f32[256,256]{1,0:T(8,128)} %depth_ref.1, ...), custom_call_target="tpu_custom_call" | custom-call | tf_op jit(solution)/shard_map/edges/pallas_call | solution.py:633
  2.2 0.1 collective-permute-start
  2.3 4.3 %collective-permute-start.1 = (bf16[32,512]{1,0:T(8,128)(2,1)S(1)}, bf16[32,512]{1,0:T(8,128)(2,1)S(1)}, u32[]{:S(2)}, u32[]{:S(2)}) collective-permute-start(bf16[32,512]{1,0:T(8,128)(2,1)S(1)} %get-tuple-element.26), channel_id=1, source_target_pairs={{1,2},{3,4},{5,6},{7,8},{9,10},{11,12},{13,14},{15,16},{17,18},{19... | collective-permute-start | bytes 98312 | tf_op jit(solution)/shard_map/ppermute | solution.py:622
  6.7 0.0 copy-done.4
  6.7 0.0 copy-done.5
  6.7 0.0 copy-done.6
  6.7 0.0 copy-done.7
  6.7 0.0 copy-done.8
  6.7 5.2 %inner.1 = (bf16[224,128]{1,0:T(8,128)(2,1)S(1)}, bf16[224,768]{1,0:T(8,128)(2,1)S(1)}, bf16[224,768]{1,0:T(8,128)(2,1)S(1)}, bf16[48,256]{1,0:T(8,128)(2,1)S(1)...) custom-call(bf16[3,3,2,16]{3,2,1,0:T(2,128)(2,1)S(1)} %get-tuple-ele, ...), custom_call_target="tpu_custom_call" | custom-call | flops 8000000000 | bytes 4000000 | tf_op jit(solution)/shard_map/inner/pallas_call | solution.py:659
  11.9 0.0 collective-permute-done.first_swap_ref
  12.0 0.0 collective-permute-done.1.second_swap_ref
  12.0 0.0 copy-start.2
  12.0 0.0 copy-start.3
  12.0 2.8 %ends.1 = (bf16[64,512]{1,0:T(8,128)(2,1)}, bf16[1280,128]{1,0:T(8,128)(2,1)S(1)}) custom-call(bf16[32,512]{1,0:T(8,128)(2,1)S(1)} %collective-permute-done.first_swap_ref, bf16[32,512]{1,0:T(8,128)(2,1)S(1)} %collective-permute-done.1.second_swap_ref, bf16[224,128]{1,0:T(8,128)(2,1)S(1)} %get-tuple-element.31.w1_ref, ...), custom_call_target="tpu_custom_call" | custom-call | tf_op jit(solution)/shard_map/ends/pallas_call | solution.py:694
  14.8 0.0 copy-start
  14.8 0.0 copy-start.1
  14.8 15.1 %all_to_all.5 = bf16[32,40,128]{2,1,0:T(8,128)(2,1)S(1)} all-to-all(bf16[32,40,128]{2,1,0:T(8,128)(2,1)S(1)} %bitcast.15), channel_id=1, replica_groups=mesh['tx'=8,'ty'=4] {'tx','ty'}, dimensions={0} | all-to-all | bytes 655360 | tf_op jit(solution)/shard_map/all_to_all | solution.py:711
  30.0 0.0 copy-done.2
  30.0 0.0 copy-done.3
  30.0 0.0 copy-done
  30.0 0.0 copy-done.1
  30.0 0.9 %level.1 = (f32[256,256]{1,0:T(8,128)S(1)}, f32[4,256,128]{2,1,0:T(8,128)S(1)}, bf16[32,384]{1,0:T(8,128)(2,1)S(1)}, bf16[32,384]{1,0:T(8,128)(2,1)S(1)}) custom-call(bf16[1280,128]{1,0:T(8,128)(2,1)S(1)} %bitcast.14, bf16[32,512]{1,0:T(8,128)(2,1)S(1)} %collective-permute-done.first_swap_ref, bf16[32,512]{1,0:T(8,128)(2,1)S(1)} %collective-permute-done.1.second_swap_ref, ...), custom_call_target="tpu_custom_call" | custom-call | tf_op jit(solution)/shard_map/level/pallas_call | solution.py:717
  30.9 0.7 %collective-permute-start.2 = (bf16[32,384]{1,0:T(8,128)(2,1)S(1)}, bf16[32,384]{1,0:T(8,128)(2,1)S(1)}, u32[]{:S(2)}, u32[]{:S(2)}) collective-permute-start(bf16[32,384]{1,0:T(8,128)(2,1)S(1)} %get-tuple-element.46), channel_id=1, source_target_pairs={{0,4},{8,12},{16,20},{24,28},{4,0},{12,8},{20,16},{28,24},{1,5},{9... | collective-permute-start | bytes 73736 | tf_op jit(solution)/shard_map/ppermute | solution.py:622
  31.7 3.9 %collective-permute-start.3 = (bf16[32,384]{1,0:T(8,128)(2,1)S(1)}, bf16[32,384]{1,0:T(8,128)(2,1)S(1)}, u32[]{:S(2)}, u32[]{:S(2)}) collective-permute-start(bf16[32,384]{1,0:T(8,128)(2,1)S(1)} %get-tuple-element.47), channel_id=1, source_target_pairs={{4,8},{12,16},{20,24},{8,4},{16,12},{24,20},{5,9},{13,17},{21,25},... | collective-permute-start | bytes 73736 | tf_op jit(solution)/shard_map/ppermute | solution.py:622
  35.5 4.6 %flow_inner.1.inner_ref = f32[2,256,128]{2,1,0:T(8,128)S(1)} custom-call(f32[256,256]{1,0:T(8,128)S(1)} %get-tuple-element.44.level_ref, f32[4,256,128]{2,1,0:T(8,128)S(1)} %get-tuple-element.45.side_ref, f32[256,256]{1,0:T(8,128)S(1)} %copy-done, s32[256,256]{1,0:T(8,128)S(1)} %copy-done.2, f32[256,256]{1,0:T(8,128)S(1)} %copy-done.1), custom_call_target="tpu_custom_call" | custom-call | flops 5000000000 | bytes 4000000 | tf_op jit(solution)/shard_map/flow_inner/pallas_call | solution.py:734
  40.1 0.0 collective-permute-done.2.first_swap_ref
  40.1 0.0 collective-permute-done.3.second_swap_ref
  40.2 1.9 %flow_ends.1 = f32[256,256]{1,0:T(8,128)} custom-call(f32[2,256,128]{2,1,0:T(8,128)S(1)} %flow_inner.1.inner_ref, f32[256,256]{1,0:T(8,128)S(1)} %get-tuple-element.44.level_ref, f32[4,256,128]{2,1,0:T(8,128)S(1)} %get-tuple-element.45.side_ref, f32[256,256]{1,0:T(8,128)S(1)} %copy-done, s32[256,256]{1,0:T(8,128)S(1)} %copy-done.2, ...), custom_call_target="tpu_custom_call" | custom-call | tf_op jit(solution)/shard_map/flow_ends/pallas_call | solution.py:747
Async XLA Ops:
  0.6 6.0 %copy-start.4 = (bf16[2,64,512]{2,1,0:T(8,128)(2,1)S(1)}, bf16[2,64,512]{2,1,0:T(8,128)(2,1)}, u32[]{:S(2)}) copy-start(bf16[2,64,512]{2,1,0:T(8,128)(2,1)} %sar_ref.3) | copy-start | bytes 393220
  0.6 6.0 %copy-start.5 = (f32[64,512]{1,0:T(8,128)S(1)}, f32[64,512]{1,0:T(8,128)}, u32[]{:S(2)}) copy-start(f32[64,512]{1,0:T(8,128)} %gw_ref.3) | copy-start | bytes 393220
  0.7 6.0 %copy-start.6 = (s32[64,512]{1,0:T(8,128)S(1)}, s32[64,512]{1,0:T(8,128)}, u32[]{:S(2)}) copy-start(s32[64,512]{1,0:T(8,128)} %cell_ref.3) | copy-start | bytes 393220
  0.7 6.0 %copy-start.7 = (bf16[16,16,3,3]{1,0,3,2:T(8,128)(2,1)S(1)}, bf16[16,16,3,3]{1,0,3,2:T(8,128)(2,1)}, u32[]{:S(2)}) copy-start(bf16[16,16,3,3]{1,0,3,2:T(8,128)(2,1)} %param.15) | copy-start | bytes 13828
  0.7 6.0 %copy-start.8 = (bf16[16,16,3,3]{1,0,3,2:T(8,128)(2,1)S(1)}, bf16[16,16,3,3]{1,0,3,2:T(8,128)(2,1)}, u32[]{:S(2)}) copy-start(bf16[16,16,3,3]{1,0,3,2:T(8,128)(2,1)} %param.16) | copy-start | bytes 13828
  2.2 9.7 %collective-permute-start = (bf16[32,512]{1,0:T(8,128)(2,1)S(1)}, bf16[32,512]{1,0:T(8,128)(2,1)S(1)}, u32[]{:S(2)}, u32[]{:S(2)}) collective-permute-start(bf16[32,512]{1,0:T(8,128)(2,1)S(1)} %get-tuple-element.25), channel_id=1, source_target_pairs={{0,1},{2,3},{4,5},{6,7},{8,9},{10,11},{12,13},{14,15},{16,17},{18,... | collective-permute-start | bytes 98312 | tf_op jit(solution)/shard_map/ppermute | solution.py:622
  2.3 9.6 %collective-permute-start.1 = (bf16[32,512]{1,0:T(8,128)(2,1)S(1)}, bf16[32,512]{1,0:T(8,128)(2,1)S(1)}, u32[]{:S(2)}, u32[]{:S(2)}) collective-permute-start(bf16[32,512]{1,0:T(8,128)(2,1)S(1)} %get-tuple-element.26), channel_id=1, source_target_pairs={{1,2},{3,4},{5,6},{7,8},{9,10},{11,12},{13,14},{15,16},{17,18},{19... | collective-permute-start | bytes 98312 | tf_op jit(solution)/shard_map/ppermute | solution.py:622
  12.0 18.0 %copy-start.2 = (s32[256,256]{1,0:T(8,128)S(1)}, s32[256,256]{1,0:T(8,128)}, u32[]{:S(2)}) copy-start(s32[256,256]{1,0:T(8,128)} %dir_ref.5) | copy-start | bytes 786436
  12.0 18.0 %copy-start.3 = (f32[256,256]{1,0:T(8,128)S(1)}, f32[256,256]{1,0:T(8,128)}, u32[]{:S(2)}) copy-start(f32[256,256]{1,0:T(8,128)} %depth_ref.1) | copy-start | bytes 786436
  14.8 15.2 %copy-start = (f32[256,256]{1,0:T(8,128)S(1)}, f32[256,256]{1,0:T(8,128)}, u32[]{:S(2)}) copy-start(f32[256,256]{1,0:T(8,128)} %slope_ref.5) | copy-start | bytes 786436
  14.8 15.2 %copy-start.1 = (f32[256,256]{1,0:T(8,128)S(1)}, f32[256,256]{1,0:T(8,128)}, u32[]{:S(2)}) copy-start(f32[256,256]{1,0:T(8,128)} %rain_ref.5) | copy-start | bytes 786436
  30.9 9.2 %collective-permute-start.2 = (bf16[32,384]{1,0:T(8,128)(2,1)S(1)}, bf16[32,384]{1,0:T(8,128)(2,1)S(1)}, u32[]{:S(2)}, u32[]{:S(2)}) collective-permute-start(bf16[32,384]{1,0:T(8,128)(2,1)S(1)} %get-tuple-element.46), channel_id=1, source_target_pairs={{0,4},{8,12},{16,20},{24,28},{4,0},{12,8},{20,16},{28,24},{1,5},{9... | collective-permute-start | bytes 73736 | tf_op jit(solution)/shard_map/ppermute | solution.py:622
  31.7 8.5 %collective-permute-start.3 = (bf16[32,384]{1,0:T(8,128)(2,1)S(1)}, bf16[32,384]{1,0:T(8,128)(2,1)S(1)}, u32[]{:S(2)}, u32[]{:S(2)}) collective-permute-start(bf16[32,384]{1,0:T(8,128)(2,1)S(1)} %get-tuple-element.47), channel_id=1, source_target_pairs={{4,8},{12,16},{20,24},{8,4},{16,12},{24,20},{5,9},{13,17},{21,25},... | collective-permute-start | bytes 73736 | tf_op jit(solution)/shard_map/ppermute | solution.py:622

commit v9 on v7

--- a/solution.py
+++ b/solution.py
@@ -167,8 +167,11 @@
     return jnp.where(even, to_next, to_previous), jnp.where(even, to_previous, to_next)
 
 
-def from_turns(even, first, second):
-    return jnp.where(even, second, first), jnp.where(even, first, second)
+def from_turns(place, size, first, second):
+    even = rem(place, 2) == 0
+    previous = jnp.where(even, second, first)
+    following = jnp.where(even, first, second)
+    return jnp.where(place > 0, previous, 0.0), jnp.where(place < size - 1, following, 0.0)
 
 
 def strips_of(message, keep):
@@ -332,7 +335,7 @@
     me = lax.axis_index("tx") * n_ty + lax.axis_index("ty")
     rows = OUT_LINES * CH
     above, below = from_turns(
-        rem(me, 2) == 0, first_swap_ref[16:32, :].astype(f32), second_swap_ref[16:32, :].astype(f32)
+        me, devices, first_swap_ref[16:32, :].astype(f32), second_swap_ref[16:32, :].astype(f32)
     )
     n = HALO_LINES
 
@@ -431,7 +434,7 @@
     ty = lax.axis_index("ty")
     tx = lax.axis_index("tx")
     previous, following = from_turns(
-        rem(tx * lax.axis_size("ty") + ty, 2) == 0,
+        tx * lax.axis_size("ty") + ty, devices,
         first_swap_ref[0:16, :].astype(f32), second_swap_ref[0:16, :].astype(f32),
     )
     left = strips_of(previous, ty > 0)
@@ -519,7 +522,8 @@
     rows, cols = level_ref.shape
     h = SUBSTEPS
     above, below = from_turns(
-        rem(lax.axis_index("tx"), 2) == 0, first_swap_ref[...].astype(f32), second_swap_ref[...].astype(f32)
+        lax.axis_index("tx"), lax.axis_size("tx"),
+        first_swap_ref[...].astype(f32), second_swap_ref[...].astype(f32),
     )
     fields = []
     for i, ref in enumerate((level_ref, rain_ref, slope_ref, dir_ref)):
@@ -566,9 +570,10 @@
     capacity = max(2, 2 * az_lines // devices)
 
     def swaps(axis, first, second):
+        size = lax.axis_size(axis)
         out = []
         for start, x in enumerate((first, second)):
-            pairs = [(i, i + 1) for i in range(start, lax.axis_size(axis) - 1, 2)]
+            pairs = [(i, (i + 1) % size) for i in range(start, size, 2)]
             out.append(lax.ppermute(x, axis, pairs + [(j, i) for i, j in pairs]))
         return out
 

time: 42.1 us -> 41.9 us (level)
  the two profiles are of different devices: /device:TPU:8 before, /device:TPU:0 now
where the time goes in v9:
time: 41.9 us; the launch traced here: 41.7 us
  Pallas kernels  17 us (41%)
  blocking collectives  13.8 us (33%)
  starting transfers between devices  9.76 us (23%)
  between operations  0.76 us (2%)
    all_to_all x1, blocking collectives, per_device(): lax.all_to_all(send.reshape(devices, send_rows, LANES), both, split_axis=...  13.8 us
    ppermute x4, starting transfers between devices, swaps(): out.append(lax.ppermute(x, axis, pairs + [(j, i) for i, j in pairs]))  9.76 us
    pallas_call x1, Pallas kernels, per_device(): pl.pallas_call(functools.partial(inner_kernel, devices, capacity), out_sh...  5.23 us
    pallas_call x1, Pallas kernels, per_device(): pl.pallas_call(flow_inner_kernel, out_shape=jax.ShapeDtypeStruct((tile_ro...  4.38 us
    pallas_call x1, Pallas kernels, per_device(): pl.pallas_call(functools.partial(ends_kernel, devices, capacity), out_sha...  2.83 us
    pallas_call x1, Pallas kernels, per_device(): pl.pallas_call(flow_ends_kernel, out_shape=jax.ShapeDtypeStruct((tile_row...  2.04 us
    pallas_call x1, Pallas kernels, per_device(): pl.pallas_call(edge_kernel, out_shape=(message, message, *[pltpu.VMEM(x.s...  1.55 us
    pallas_call x1, Pallas kernels, per_device(): pl.pallas_call(functools.partial(level_kernel, devices), out_shape=(jax.S...  0.92 us
  transfers between devices with their start and end apart: 4, of which 1 were waited for; matrix products, arithmetic and copies ran while one was open for 0% of the time, Pallas kernels for 23%

profile of v9, /device:TPU:0, one launch (start us, length us, event | category | flops | bytes accessed | tf_op | source)
XLA Modules:
  0.0 41.7 jit_solution(14988577769121628207)
XLA Ops:
  0.6 0.0 copy-start.4
  0.6 0.0 copy-start.5
  0.7 0.0 copy-start.6
  0.7 0.0 copy-start.7
  0.7 0.0 copy-start.8
  0.7 1.6 %edges.1 = (bf16[32,512]{1,0:T(8,128)(2,1)S(1)}, bf16[32,512]{1,0:T(8,128)(2,1)S(1)}, bf16[3,3,2,16]{3,2,1,0:T(2,128)(2,1)S(1)}, bf16[3,3,16]{2,1,0:T(4,128)(2,1...) custom-call(bf16[2,64,512]{2,1,0:T(8,128)(2,1)} %sar_ref.3, f32[256,256]{1,0:T(8,128)} %depth_ref.1, ...), custom_call_target="tpu_custom_call" | custom-call | tf_op jit(solution)/shard_map/edges/pallas_call | solution.py:588
  2.2 0.5 %collective-permute-start = (bf16[32,512]{1,0:T(8,128)(2,1)S(1)}, bf16[32,512]{1,0:T(8,128)(2,1)S(1)}, u32[]{:S(2)}, u32[]{:S(2)}) collective-permute-start(bf16[32,512]{1,0:T(8,128)(2,1)S(1)} %get-tuple-element.25), channel_id=1, source_target_pairs={{0,1},{2,3},{4,5},{6,7},{8,9},{10,11},{12,13},{14,15},{16,17},{18,... | collective-permute-start | bytes 98312 | tf_op jit(solution)/shard_map/ppermute | solution.py:577
  2.8 6.6 %collective-permute-start.1 = (bf16[32,512]{1,0:T(8,128)(2,1)S(1)}, bf16[32,512]{1,0:T(8,128)(2,1)S(1)}, u32[]{:S(2)}, u32[]{:S(2)}) collective-permute-start(bf16[32,512]{1,0:T(8,128)(2,1)S(1)} %get-tuple-element.26), channel_id=1, source_target_pairs={{1,2},{3,4},{5,6},{7,8},{9,10},{11,12},{13,14},{15,16},{17,18},{19... | collective-permute-start | bytes 98312 | tf_op jit(solution)/shard_map/ppermute | solution.py:577
  9.4 0.0 copy-done.4
  9.4 0.0 copy-done.5
  9.4 0.0 copy-done.6
  9.4 0.0 copy-done.7
  9.4 0.0 copy-done.8
  9.4 5.2 %inner.1 = (bf16[224,128]{1,0:T(8,128)(2,1)S(1)}, bf16[224,768]{1,0:T(8,128)(2,1)S(1)}, bf16[224,768]{1,0:T(8,128)(2,1)S(1)}, bf16[48,256]{1,0:T(8,128)(2,1)S(1)...) custom-call(bf16[3,3,2,16]{3,2,1,0:T(2,128)(2,1)S(1)} %get-tuple-ele, ...), custom_call_target="tpu_custom_call" | custom-call | flops 8000000000 | bytes 4000000 | tf_op jit(solution)/shard_map/inner/pallas_call | solution.py:614
  14.6 0.0 collective-permute-done.first_swap_ref
  14.6 0.0 collective-permute-done.1.second_swap_ref
  14.6 0.0 copy-start.2
  14.6 0.0 copy-start.3
  14.7 2.8 %ends.1 = (bf16[64,512]{1,0:T(8,128)(2,1)}, bf16[1280,128]{1,0:T(8,128)(2,1)S(1)}) custom-call(bf16[32,512]{1,0:T(8,128)(2,1)S(1)} %collective-permute-done.first_swap_ref, bf16[32,512]{1,0:T(8,128)(2,1)S(1)} %collective-permute-done.1.second_swap_ref, bf16[224,128]{1,0:T(8,128)(2,1)S(1)} %get-tuple-element.31.w1_ref, ...), custom_call_target="tpu_custom_call" | custom-call | tf_op jit(solution)/shard_map/ends/pallas_call | solution.py:649
  17.5 0.0 copy-start
  17.5 0.0 copy-start.1
  17.5 13.8 %all_to_all.5 = bf16[32,40,128]{2,1,0:T(8,128)(2,1)S(1)} all-to-all(bf16[32,40,128]{2,1,0:T(8,128)(2,1)S(1)} %bitcast.15), channel_id=1, replica_groups=mesh['tx'=8,'ty'=4] {'tx','ty'}, dimensions={0} | all-to-all | bytes 655360 | tf_op jit(solution)/shard_map/all_to_all | solution.py:662
  31.3 0.0 copy-done.2
  31.3 0.0 copy-done.3
  31.3 0.0 copy-done
  31.3 0.0 copy-done.1
  31.3 0.9 %level.1 = (f32[256,256]{1,0:T(8,128)S(1)}, f32[4,256,128]{2,1,0:T(8,128)S(1)}, bf16[32,384]{1,0:T(8,128)(2,1)S(1)}, bf16[32,384]{1,0:T(8,128)(2,1)S(1)}) custom-call(bf16[1280,128]{1,0:T(8,128)(2,1)S(1)} %bitcast.14, bf16[32,512]{1,0:T(8,128)(2,1)S(1)} %collective-permute-done.first_swap_ref, bf16[32,512]{1,0:T(8,128)(2,1)S(1)} %collective-permute-done.1.second_swap_ref, ...), custom_call_target="tpu_custom_call" | custom-call | tf_op jit(solution)/shard_map/level/pallas_call | solution.py:668
  32.3 0.9 %collective-permute-start.2 = (bf16[32,384]{1,0:T(8,128)(2,1)S(1)}, bf16[32,384]{1,0:T(8,128)(2,1)S(1)}, u32[]{:S(2)}, u32[]{:S(2)}) collective-permute-start(bf16[32,384]{1,0:T(8,128)(2,1)S(1)} %get-tuple-element.46), channel_id=1, source_target_pairs={{0,4},{8,12},{16,20},{24,28},{4,0},{12,8},{20,16},{28,24},{1,5},{9... | collective-permute-start | bytes 73736 | tf_op jit(solution)/shard_map/ppermute | solution.py:577
  33.2 1.7 %collective-permute-start.3 = (bf16[32,384]{1,0:T(8,128)(2,1)S(1)}, bf16[32,384]{1,0:T(8,128)(2,1)S(1)}, u32[]{:S(2)}, u32[]{:S(2)}) collective-permute-start(bf16[32,384]{1,0:T(8,128)(2,1)S(1)} %get-tuple-element.47), channel_id=1, source_target_pairs={{4,8},{12,16},{20,24},{28,0},{8,4},{16,12},{24,20},{0,28},{5,9},{1... | collective-permute-start | bytes 73736 | tf_op jit(solution)/shard_map/ppermute | solution.py:577
  34.9 4.4 %flow_inner.1.inner_ref = f32[256,256]{1,0:T(8,128)S(1)} custom-call(f32[256,256]{1,0:T(8,128)S(1)} %get-tuple-element.44.level_ref, f32[4,256,128]{2,1,0:T(8,128)S(1)} %get-tuple-element.45.side_ref, f32[256,256]{1,0:T(8,128)S(1)} %copy-done, s32[256,256]{1,0:T(8,128)S(1)} %copy-done.2, f32[256,256]{1,0:T(8,128)S(1)} %copy-done.1), custom_call_target="tpu_custom_call" | custom-call | flops 5000000000 | bytes 4000000 | tf_op jit(solution)/shard_map/flow_inner/pallas_call | solution.py:684
  39.3 0.0 collective-permute-done.2.first_swap_ref
  39.3 0.4 collective-permute-done.3.second_swap_ref
  39.7 2.0 %flow_ends.1 = f32[256,256]{1,0:T(8,128)} custom-call(f32[256,256]{1,0:T(8,128)S(1)} %flow_inner.1.inner_ref, f32[256,256]{1,0:T(8,128)S(1)} %get-tuple-element.44.level_ref, f32[4,256,128]{2,1,0:T(8,128)S(1)} %get-tuple-element.45.side_ref, f32[256,256]{1,0:T(8,128)S(1)} %copy-done, s32[256,256]{1,0:T(8,128)S(1)} %copy-done.2, f32[256,256]{1,0:T(8,128)S(1)} %copy-done.1, ...), custom_call_target="tpu_custom_call" | custom-call | tf_op jit(solution)/shard_map/flow_ends/pallas_call | solution.py:694
Async XLA Ops:
  0.6 8.7 %copy-start.4 = (bf16[2,64,512]{2,1,0:T(8,128)(2,1)S(1)}, bf16[2,64,512]{2,1,0:T(8,128)(2,1)}, u32[]{:S(2)}) copy-start(bf16[2,64,512]{2,1,0:T(8,128)(2,1)} %sar_ref.3) | copy-start | bytes 393220
  0.6 8.7 %copy-start.5 = (f32[64,512]{1,0:T(8,128)S(1)}, f32[64,512]{1,0:T(8,128)}, u32[]{:S(2)}) copy-start(f32[64,512]{1,0:T(8,128)} %gw_ref.3) | copy-start | bytes 393220
  0.7 8.7 %copy-start.6 = (s32[64,512]{1,0:T(8,128)S(1)}, s32[64,512]{1,0:T(8,128)}, u32[]{:S(2)}) copy-start(s32[64,512]{1,0:T(8,128)} %cell_ref.3) | copy-start | bytes 393220
  0.7 8.7 %copy-start.7 = (bf16[16,16,3,3]{1,0,3,2:T(8,128)(2,1)S(1)}, bf16[16,16,3,3]{1,0,3,2:T(8,128)(2,1)}, u32[]{:S(2)}) copy-start(bf16[16,16,3,3]{1,0,3,2:T(8,128)(2,1)} %param.15) | copy-start | bytes 13828
  0.7 8.7 %copy-start.8 = (bf16[16,16,3,3]{1,0,3,2:T(8,128)(2,1)S(1)}, bf16[16,16,3,3]{1,0,3,2:T(8,128)(2,1)}, u32[]{:S(2)}) copy-start(bf16[16,16,3,3]{1,0,3,2:T(8,128)(2,1)} %param.16) | copy-start | bytes 13828
  2.2 12.4 %collective-permute-start = (bf16[32,512]{1,0:T(8,128)(2,1)S(1)}, bf16[32,512]{1,0:T(8,128)(2,1)S(1)}, u32[]{:S(2)}, u32[]{:S(2)}) collective-permute-start(bf16[32,512]{1,0:T(8,128)(2,1)S(1)} %get-tuple-element.25), channel_id=1, source_target_pairs={{0,1},{2,3},{4,5},{6,7},{8,9},{10,11},{12,13},{14,15},{16,17},{18,... | collective-permute-start | bytes 98312 | tf_op jit(solution)/shard_map/ppermute | solution.py:577
  2.8 11.9 %collective-permute-start.1 = (bf16[32,512]{1,0:T(8,128)(2,1)S(1)}, bf16[32,512]{1,0:T(8,128)(2,1)S(1)}, u32[]{:S(2)}, u32[]{:S(2)}) collective-permute-start(bf16[32,512]{1,0:T(8,128)(2,1)S(1)} %get-tuple-element.26), channel_id=1, source_target_pairs={{1,2},{3,4},{5,6},{7,8},{9,10},{11,12},{13,14},{15,16},{17,18},{19... | collective-permute-start | bytes 98312 | tf_op jit(solution)/shard_map/ppermute | solution.py:577
  14.6 16.7 %copy-start.2 = (s32[256,256]{1,0:T(8,128)S(1)}, s32[256,256]{1,0:T(8,128)}, u32[]{:S(2)}) copy-start(s32[256,256]{1,0:T(8,128)} %dir_ref.5) | copy-start | bytes 786436
  14.6 16.7 %copy-start.3 = (f32[256,256]{1,0:T(8,128)S(1)}, f32[256,256]{1,0:T(8,128)}, u32[]{:S(2)}) copy-start(f32[256,256]{1,0:T(8,128)} %depth_ref.1) | copy-start | bytes 786436
  17.5 13.8 %copy-start = (f32[256,256]{1,0:T(8,128)S(1)}, f32[256,256]{1,0:T(8,128)}, u32[]{:S(2)}) copy-start(f32[256,256]{1,0:T(8,128)} %slope_ref.5) | copy-start | bytes 786436
  17.5 13.8 %copy-start.1 = (f32[256,256]{1,0:T(8,128)S(1)}, f32[256,256]{1,0:T(8,128)}, u32[]{:S(2)}) copy-start(f32[256,256]{1,0:T(8,128)} %rain_ref.5) | copy-start | bytes 786436
  32.3 7.0 %collective-permute-start.2 = (bf16[32,384]{1,0:T(8,128)(2,1)S(1)}, bf16[32,384]{1,0:T(8,128)(2,1)S(1)}, u32[]{:S(2)}, u32[]{:S(2)}) collective-permute-start(bf16[32,384]{1,0:T(8,128)(2,1)S(1)} %get-tuple-element.46), channel_id=1, source_target_pairs={{0,4},{8,12},{16,20},{24,28},{4,0},{12,8},{20,16},{28,24},{1,5},{9... | collective-permute-start | bytes 73736 | tf_op jit(solution)/shard_map/ppermute | solution.py:577
  33.2 6.5 %collective-permute-start.3 = (bf16[32,384]{1,0:T(8,128)(2,1)S(1)}, bf16[32,384]{1,0:T(8,128)(2,1)S(1)}, u32[]{:S(2)}, u32[]{:S(2)}) collective-permute-start(bf16[32,384]{1,0:T(8,128)(2,1)S(1)} %get-tuple-element.47), channel_id=1, source_target_pairs={{4,8},{12,16},{20,24},{28,0},{8,4},{16,12},{24,20},{0,28},{5,9},{1... | collective-permute-start | bytes 73736 | tf_op jit(solution)/shard_map/ppermute | solution.py:577

commit v10 on v9

--- a/solution.py
+++ b/solution.py
@@ -573,8 +573,10 @@
         size = lax.axis_size(axis)
         out = []
         for start, x in enumerate((first, second)):
-            pairs = [(i, (i + 1) % size) for i in range(start, size, 2)]
-            out.append(lax.ppermute(x, axis, pairs + [(j, i) for i, j in pairs]))
+            to = list(range(size))
+            for i in range(start, size - 1, 2):
+                to[i], to[i + 1] = i + 1, i
+            out.append(lax.ppermute(x, axis, list(enumerate(to))))
         return out
 
     params = pltpu.CompilerParams(vmem_limit_bytes=VMEM_LIMIT)

time: 41.9 us -> 42.1 us (level)
  the two profiles are of different devices: /device:TPU:0 before, /device:TPU:8 now
where the time goes in v10:
time: 42.1 us; the launch traced here: 41.9 us
  Pallas kernels  17 us (40%)
  blocking collectives  15.1 us (36%)
  starting transfers between devices  8.99 us (21%)
  between operations  0.82 us (2%)
    all_to_all x1, blocking collectives, per_device(): lax.all_to_all(send.reshape(devices, send_rows, LANES), both, split_axis=...  15.1 us
    ppermute x4, starting transfers between devices, swaps(): out.append(lax.ppermute(x, axis, list(enumerate(to))))  8.99 us
    pallas_call x1, Pallas kernels, per_device(): pl.pallas_call(functools.partial(inner_kernel, devices, capacity), out_sh...  5.23 us
    pallas_call x1, Pallas kernels, per_device(): pl.pallas_call(flow_inner_kernel, out_shape=jax.ShapeDtypeStruct((tile_ro...  4.38 us
    pallas_call x1, Pallas kernels, per_device(): pl.pallas_call(functools.partial(ends_kernel, devices, capacity), out_sha...  2.82 us
    pallas_call x1, Pallas kernels, per_device(): pl.pallas_call(flow_ends_kernel, out_shape=jax.ShapeDtypeStruct((tile_row...  2.04 us
    pallas_call x1, Pallas kernels, per_device(): pl.pallas_call(edge_kernel, out_shape=(message, message, *[pltpu.VMEM(x.s...  1.55 us
    pallas_call x1, Pallas kernels, per_device(): pl.pallas_call(functools.partial(level_kernel, devices), out_shape=(jax.S...  0.92 us
  transfers between devices with their start and end apart: 4, of which 0 were waited for; matrix products, arithmetic and copies ran while one was open for 0% of the time, Pallas kernels for 23%

profile of v10, /device:TPU:8, one launch (start us, length us, event | category | flops | bytes accessed | tf_op | source)
XLA Modules:
  0.0 41.9 jit_solution(14658392672742915579)
XLA Ops:
  0.6 0.0 copy-start.4
  0.6 0.0 copy-start.5
  0.7 0.0 copy-start.6
  0.7 0.0 copy-start.7
  0.7 0.0 copy-start.8
  0.7 1.6 %edges.1 = (bf16[32,512]{1,0:T(8,128)(2,1)S(1)}, bf16[32,512]{1,0:T(8,128)(2,1)S(1)}, bf16[3,3,2,16]{3,2,1,0:T(2,128)(2,1)S(1)}, bf16[3,3,16]{2,1,0:T(4,128)(2,1...) custom-call(bf16[2,64,512]{2,1,0:T(8,128)(2,1)} %sar_ref.3, f32[256,256]{1,0:T(8,128)} %depth_ref.1, ...), custom_call_target="tpu_custom_call" | custom-call | tf_op jit(solution)/shard_map/edges/pallas_call | solution.py:590
  2.2 0.1 collective-permute-start
  2.3 4.3 %collective-permute-start.1 = (bf16[32,512]{1,0:T(8,128)(2,1)S(1)}, bf16[32,512]{1,0:T(8,128)(2,1)S(1)}, u32[]{:S(2)}, u32[]{:S(2)}) collective-permute-start(bf16[32,512]{1,0:T(8,128)(2,1)S(1)} %get-tuple-element.26), channel_id=1, source_target_pairs={{0,0},{1,2},{2,1},{3,4},{4,3},{5,6},{6,5},{7,8},{8,7},{9,10},{10,9... | collective-permute-start | bytes 98312 | tf_op jit(solution)/shard_map/ppermute | solution.py:579
  6.7 0.0 copy-done.4
  6.7 0.0 copy-done.5
  6.7 0.0 copy-done.6
  6.7 0.0 copy-done.7
  6.7 0.0 copy-done.8
  6.7 5.2 %inner.1 = (bf16[224,128]{1,0:T(8,128)(2,1)S(1)}, bf16[224,768]{1,0:T(8,128)(2,1)S(1)}, bf16[224,768]{1,0:T(8,128)(2,1)S(1)}, bf16[48,256]{1,0:T(8,128)(2,1)S(1)...) custom-call(bf16[3,3,2,16]{3,2,1,0:T(2,128)(2,1)S(1)} %get-tuple-ele, ...), custom_call_target="tpu_custom_call" | custom-call | flops 8000000000 | bytes 4000000 | tf_op jit(solution)/shard_map/inner/pallas_call | solution.py:616
  11.9 0.0 collective-permute-done.first_swap_ref
  12.0 0.0 collective-permute-done.1.second_swap_ref
  12.0 0.0 copy-start.2
  12.0 0.0 copy-start.3
  12.0 2.8 %ends.1 = (bf16[64,512]{1,0:T(8,128)(2,1)}, bf16[1280,128]{1,0:T(8,128)(2,1)S(1)}) custom-call(bf16[32,512]{1,0:T(8,128)(2,1)S(1)} %collective-permute-done.first_swap_ref, bf16[32,512]{1,0:T(8,128)(2,1)S(1)} %collective-permute-done.1.second_swap_ref, bf16[224,128]{1,0:T(8,128)(2,1)S(1)} %get-tuple-element.31.w1_ref, ...), custom_call_target="tpu_custom_call" | custom-call | tf_op jit(solution)/shard_map/ends/pallas_call | solution.py:651
  14.8 0.0 copy-start
  14.8 0.0 copy-start.1
  14.8 15.1 %all_to_all.5 = bf16[32,40,128]{2,1,0:T(8,128)(2,1)S(1)} all-to-all(bf16[32,40,128]{2,1,0:T(8,128)(2,1)S(1)} %bitcast.15), channel_id=1, replica_groups=mesh['tx'=8,'ty'=4] {'tx','ty'}, dimensions={0} | all-to-all | bytes 655360 | tf_op jit(solution)/shard_map/all_to_all | solution.py:664
  29.9 0.0 copy-done.2
  29.9 0.0 copy-done.3
  29.9 0.0 copy-done
  29.9 0.0 copy-done.1
  30.0 0.9 %level.1 = (f32[256,256]{1,0:T(8,128)S(1)}, f32[4,256,128]{2,1,0:T(8,128)S(1)}, bf16[32,384]{1,0:T(8,128)(2,1)S(1)}, bf16[32,384]{1,0:T(8,128)(2,1)S(1)}) custom-call(bf16[1280,128]{1,0:T(8,128)(2,1)S(1)} %bitcast.14, bf16[32,512]{1,0:T(8,128)(2,1)S(1)} %collective-permute-done.first_swap_ref, bf16[32,512]{1,0:T(8,128)(2,1)S(1)} %collective-permute-done.1.second_swap_ref, ...), custom_call_target="tpu_custom_call" | custom-call | tf_op jit(solution)/shard_map/level/pallas_call | solution.py:670
  30.9 0.7 %collective-permute-start.2 = (bf16[32,384]{1,0:T(8,128)(2,1)S(1)}, bf16[32,384]{1,0:T(8,128)(2,1)S(1)}, u32[]{:S(2)}, u32[]{:S(2)}) collective-permute-start(bf16[32,384]{1,0:T(8,128)(2,1)S(1)} %get-tuple-element.46), channel_id=1, source_target_pairs={{0,4},{4,0},{8,12},{12,8},{16,20},{20,16},{24,28},{28,24},{1,5},{5... | collective-permute-start | bytes 73736 | tf_op jit(solution)/shard_map/ppermute | solution.py:579
  31.6 3.9 %collective-permute-start.3 = (bf16[32,384]{1,0:T(8,128)(2,1)S(1)}, bf16[32,384]{1,0:T(8,128)(2,1)S(1)}, u32[]{:S(2)}, u32[]{:S(2)}) collective-permute-start(bf16[32,384]{1,0:T(8,128)(2,1)S(1)} %get-tuple-element.47), channel_id=1, source_target_pairs={{0,0},{4,8},{8,4},{12,16},{16,12},{20,24},{24,20},{28,28},{1,1},{5... | collective-permute-start | bytes 73736 | tf_op jit(solution)/shard_map/ppermute | solution.py:579
  35.5 4.4 %flow_inner.1.inner_ref = f32[256,256]{1,0:T(8,128)S(1)} custom-call(f32[256,256]{1,0:T(8,128)S(1)} %get-tuple-element.44.level_ref, f32[4,256,128]{2,1,0:T(8,128)S(1)} %get-tuple-element.45.side_ref, f32[256,256]{1,0:T(8,128)S(1)} %copy-done, s32[256,256]{1,0:T(8,128)S(1)} %copy-done.2, f32[256,256]{1,0:T(8,128)S(1)} %copy-done.1), custom_call_target="tpu_custom_call" | custom-call | flops 5000000000 | bytes 4000000 | tf_op jit(solution)/shard_map/flow_inner/pallas_call | solution.py:686
  39.9 0.0 collective-permute-done.2.first_swap_ref
  39.9 0.0 collective-permute-done.3.second_swap_ref
  39.9 2.0 %flow_ends.1 = f32[256,256]{1,0:T(8,128)} custom-call(f32[256,256]{1,0:T(8,128)S(1)} %flow_inner.1.inner_ref, f32[256,256]{1,0:T(8,128)S(1)} %get-tuple-element.44.level_ref, f32[4,256,128]{2,1,0:T(8,128)S(1)} %get-tuple-element.45.side_ref, f32[256,256]{1,0:T(8,128)S(1)} %copy-done, s32[256,256]{1,0:T(8,128)S(1)} %copy-done.2, f32[256,256]{1,0:T(8,128)S(1)} %copy-done.1, ...), custom_call_target="tpu_custom_call" | custom-call | tf_op jit(solution)/shard_map/flow_ends/pallas_call | solution.py:696
Async XLA Ops:
  0.6 6.0 %copy-start.4 = (bf16[2,64,512]{2,1,0:T(8,128)(2,1)S(1)}, bf16[2,64,512]{2,1,0:T(8,128)(2,1)}, u32[]{:S(2)}) copy-start(bf16[2,64,512]{2,1,0:T(8,128)(2,1)} %sar_ref.3) | copy-start | bytes 393220
  0.6 6.0 %copy-start.5 = (f32[64,512]{1,0:T(8,128)S(1)}, f32[64,512]{1,0:T(8,128)}, u32[]{:S(2)}) copy-start(f32[64,512]{1,0:T(8,128)} %gw_ref.3) | copy-start | bytes 393220
  0.7 6.0 %copy-start.6 = (s32[64,512]{1,0:T(8,128)S(1)}, s32[64,512]{1,0:T(8,128)}, u32[]{:S(2)}) copy-start(s32[64,512]{1,0:T(8,128)} %cell_ref.3) | copy-start | bytes 393220
  0.7 6.0 %copy-start.7 = (bf16[16,16,3,3]{1,0,3,2:T(8,128)(2,1)S(1)}, bf16[16,16,3,3]{1,0,3,2:T(8,128)(2,1)}, u32[]{:S(2)}) copy-start(bf16[16,16,3,3]{1,0,3,2:T(8,128)(2,1)} %param.15) | copy-start | bytes 13828
  0.7 6.0 %copy-start.8 = (bf16[16,16,3,3]{1,0,3,2:T(8,128)(2,1)S(1)}, bf16[16,16,3,3]{1,0,3,2:T(8,128)(2,1)}, u32[]{:S(2)}) copy-start(bf16[16,16,3,3]{1,0,3,2:T(8,128)(2,1)} %param.16) | copy-start | bytes 13828
  2.2 9.7 %collective-permute-start = (bf16[32,512]{1,0:T(8,128)(2,1)S(1)}, bf16[32,512]{1,0:T(8,128)(2,1)S(1)}, u32[]{:S(2)}, u32[]{:S(2)}) collective-permute-start(bf16[32,512]{1,0:T(8,128)(2,1)S(1)} %get-tuple-element.25), channel_id=1, source_target_pairs={{0,1},{1,0},{2,3},{3,2},{4,5},{5,4},{6,7},{7,6},{8,9},{9,8},{10,11... | collective-permute-start | bytes 98312 | tf_op jit(solution)/shard_map/ppermute | solution.py:579
  2.3 9.6 %collective-permute-start.1 = (bf16[32,512]{1,0:T(8,128)(2,1)S(1)}, bf16[32,512]{1,0:T(8,128)(2,1)S(1)}, u32[]{:S(2)}, u32[]{:S(2)}) collective-permute-start(bf16[32,512]{1,0:T(8,128)(2,1)S(1)} %get-tuple-element.26), channel_id=1, source_target_pairs={{0,0},{1,2},{2,1},{3,4},{4,3},{5,6},{6,5},{7,8},{8,7},{9,10},{10,9... | collective-permute-start | bytes 98312 | tf_op jit(solution)/shard_map/ppermute | solution.py:579
  12.0 18.0 %copy-start.2 = (s32[256,256]{1,0:T(8,128)S(1)}, s32[256,256]{1,0:T(8,128)}, u32[]{:S(2)}) copy-start(s32[256,256]{1,0:T(8,128)} %dir_ref.5) | copy-start | bytes 786436
  12.0 18.0 %copy-start.3 = (f32[256,256]{1,0:T(8,128)S(1)}, f32[256,256]{1,0:T(8,128)}, u32[]{:S(2)}) copy-start(f32[256,256]{1,0:T(8,128)} %depth_ref.1) | copy-start | bytes 786436
  14.8 15.1 %copy-start = (f32[256,256]{1,0:T(8,128)S(1)}, f32[256,256]{1,0:T(8,128)}, u32[]{:S(2)}) copy-start(f32[256,256]{1,0:T(8,128)} %slope_ref.5) | copy-start | bytes 786436
  14.8 15.1 %copy-start.1 = (f32[256,256]{1,0:T(8,128)S(1)}, f32[256,256]{1,0:T(8,128)}, u32[]{:S(2)}) copy-start(f32[256,256]{1,0:T(8,128)} %rain_ref.5) | copy-start | bytes 786436
  30.9 9.0 %collective-permute-start.2 = (bf16[32,384]{1,0:T(8,128)(2,1)S(1)}, bf16[32,384]{1,0:T(8,128)(2,1)S(1)}, u32[]{:S(2)}, u32[]{:S(2)}) collective-permute-start(bf16[32,384]{1,0:T(8,128)(2,1)S(1)} %get-tuple-element.46), channel_id=1, source_target_pairs={{0,4},{4,0},{8,12},{12,8},{16,20},{20,16},{24,28},{28,24},{1,5},{5... | collective-permute-start | bytes 73736 | tf_op jit(solution)/shard_map/ppermute | solution.py:579
  31.6 8.3 %collective-permute-start.3 = (bf16[32,384]{1,0:T(8,128)(2,1)S(1)}, bf16[32,384]{1,0:T(8,128)(2,1)S(1)}, u32[]{:S(2)}, u32[]{:S(2)}) collective-permute-start(bf16[32,384]{1,0:T(8,128)(2,1)S(1)} %get-tuple-element.47), channel_id=1, source_target_pairs={{0,0},{4,8},{8,4},{12,16},{16,12},{20,24},{24,20},{28,28},{1,1},{5... | collective-permute-start | bytes 73736 | tf_op jit(solution)/shard_map/ppermute | solution.py:579

commit v11 on v9

--- a/solution.py
+++ b/solution.py
@@ -16,7 +16,7 @@
 END_LINES = 8
 LANES = 128
 VMEM_LIMIT = 48 * 1024 * 1024
-VMEM_MOST = 61880 * 1024
+VMEM_MOST = 60160 * 1024
 
 wet_depth = 0.5
 runoff_coef = 0.25
@@ -119,27 +119,24 @@
 
 
 def edge_kernel(
-    sar_hbm, depth_hbm, slope_hbm, rain_hbm, dir_hbm, k1_hbm, k4_hbm, tile_hbm, row_hbm,
-    first_swap_ref, second_swap_ref, k1_ref, k4_ref, tile_ref, row_ref,
-    last_ref, first_ref, depth_ref, slope_ref, rain_ref, dir_ref, sems,
+    depth_hbm, slope_hbm, rain_hbm, dir_hbm, sar_hbm, *refs
 ):
+    n_on = (len(refs) - 8) // 2
+    on_hbm = refs[:n_on]
+    first_swap_ref, second_swap_ref, sar_ref, *on_refs = refs[n_on : 2 * n_on + 3]
+    depth_ref, slope_ref, rain_ref, dir_ref, sems = refs[2 * n_on + 3 :]
     even = rem(lax.axis_index("tx") * lax.axis_size("ty") + lax.axis_index("ty"), 2) == 0
     lines, px = sar_hbm.shape[1:]
     cols = depth_hbm.shape[1]
     h = SUBSTEPS
-    copies = [
-        pltpu.make_async_copy(src, dst, sems.at[i])
-        for i, (src, dst) in enumerate(
-            (
-                (depth_hbm, depth_ref), (slope_hbm, slope_ref), (rain_hbm, rain_ref), (dir_hbm, dir_ref),
-                (sar_hbm.at[:, lines - 16 : lines, :], last_ref), (sar_hbm.at[:, 0:16, :], first_ref),
-                (k1_hbm, k1_ref), (k4_hbm, k4_ref), (tile_hbm, tile_ref), (row_hbm, row_ref),
-            )
-        )
-    ]
+    pairs = (
+        (depth_hbm, depth_ref), (slope_hbm, slope_ref), (rain_hbm, rain_ref), (dir_hbm, dir_ref),
+        (sar_hbm, sar_ref), *zip(on_hbm, on_refs),
+    )
+    copies = [pltpu.make_async_copy(src, dst, sems.at[i]) for i, (src, dst) in enumerate(pairs)]
     for copy in copies:
         copy.start()
-    for copy in copies:
+    for copy in copies[0:5]:
         copy.wait()
     fields = (
         depth_ref[...],
@@ -149,11 +146,11 @@
     )
     zeros = jnp.zeros((8, px), f32)
     messages = []
-    for image_ref, lo, strip in (
-        (last_ref, 16 - HALO_LINES, lambda x: jnp.transpose(x[:, cols - LANES :], (1, 0))[LANES - h :]),
-        (first_ref, 0, lambda x: jnp.transpose(x[:, 0:LANES], (1, 0))[0:h]),
+    for at, lo, strip in (
+        (lines - 16, 16 - HALO_LINES, lambda x: jnp.transpose(x[:, cols - LANES :], (1, 0))[LANES - h :]),
+        (0, 0, lambda x: jnp.transpose(x[:, 0:LANES], (1, 0))[0:h]),
     ):
-        image = [image_ref[ch].astype(f32)[lo : lo + HALO_LINES] for ch in range(2)]
+        image = [sar_ref[ch, at : at + 16, :].astype(f32)[lo : lo + HALO_LINES] for ch in range(2)]
         strips = [strip(x) for x in fields]
         messages.append(
             jnp.concatenate([jnp.concatenate(strips[0:2], 1), jnp.concatenate(strips[2:4], 1), *image, zeros], 0)
@@ -161,6 +158,8 @@
     first, second = in_turn(even, *messages)
     first_swap_ref[...] = first.astype(bf16)
     second_swap_ref[...] = second.astype(bf16)
+    for copy in copies[5:]:
+        copy.wait()
 
 
 def in_turn(even, to_next, to_previous):
@@ -395,6 +394,22 @@
     return jnp.transpose(x, (1, 0))
 
 
+def shares_by_direction(code, conv):
+    cols = conv.shape[1]
+    for direction, side in enumerate((-1, 0, 1, -1, 1, -1, 0, 1)):
+        share = jnp.where(code == direction, conv, 0.0)
+        yield direction, pltpu.roll(share, side % cols, 1) if side else share
+
+
+def static_kernel(side_ref, slope_ref, rain_ref, dir_ref, rain_wide_ref, conv_wide_ref, m_ref):
+    conv = jnp.concatenate([runoff_coef * jnp.sqrt(slope_ref[...]), side_ref[1]], 1)
+    code = jnp.concatenate([dir_ref[...].astype(f32), side_ref[2]], 1)
+    conv_wide_ref[...] = conv
+    rain_wide_ref[...] = jnp.concatenate([rain_ref[...], side_ref[0]], 1)
+    for direction, share in shares_by_direction(code, conv):
+        m_ref[direction] = share
+
+
 def level_kernel(
     devices,
     got_ref, first_swap_ref, second_swap_ref, depth_ref, slope_ref, rain_ref, dir_ref,
@@ -431,8 +446,7 @@
     summed = dot(placer(0), main.astype(bf16))
     summed_side = dot(placer(1), strip(0, 0)) + dot(placer(2), strip(1, LANES - h))
 
-    ty = lax.axis_index("ty")
-    tx = lax.axis_index("tx")
+    tx, ty = lax.axis_index("tx"), lax.axis_index("ty")
     previous, following = from_turns(
         tx * lax.axis_size("ty") + ty, devices,
         first_swap_ref[0:16, :].astype(f32), second_swap_ref[0:16, :].astype(f32),
@@ -451,55 +465,65 @@
         innovation = (observed - covered * wet) / (covered + 1.0)
         return depth * jnp.exp(innovation)
 
-    level = analysed(summed, depth_ref[...])
+    level = jnp.concatenate([analysed(summed, depth_ref[...]), analysed(summed_side, depth_side)], 1)
     level_ref[...] = level
-    sides = (analysed(summed_side, depth_side), rain_side, conv_side, code_side)
-    owns = (level, rain_ref, slope_ref, dir_ref)
-
-    def end_rows(at):
-        own = [x[at, :] for x in owns]
-        own[2] = runoff_coef * jnp.sqrt(own[2])
-        own[3] = own[3].astype(f32)
-        return jnp.concatenate([jnp.concatenate([o, x[at]], 1) for o, x in zip(own, sides)], 0)
-
+    sides = (rain_side, conv_side, code_side)
     for i, x in enumerate(sides):
         side_ref[i] = x
+
+    def end_rows(at):
+        own = (rain_ref[at, :], runoff_coef * jnp.sqrt(slope_ref[at, :]), dir_ref[at, :].astype(f32))
+        return jnp.concatenate([level[at], *[jnp.concatenate([o, x[at]], 1) for o, x in zip(own, sides)]], 0)
+
     first, second = in_turn(rem(tx, 2) == 0, end_rows(slice(tile_rows - h, tile_rows)), end_rows(slice(0, h)))
     first_ref[...] = first.astype(bf16)
     second_ref[...] = second.astype(bf16)
 
 
-def substeps(level, rain, conv, code, rain_s, conv_s, m_ref, part_ref, up_ref, down_ref, chunk):
-    rows, cols = level.shape
+def flow_kernel(
+    level_ref, rain_ref, conv_ref, m_ref, first_swap_ref, second_swap_ref,
+    out_ref,
+    end_ref, end_m_ref, part_ref, up_ref, down_ref,
+):
+    rows, cols = level_ref.shape
     h = SUBSTEPS
     for ref in (up_ref, down_ref):
         ref[0] = jnp.zeros(ref.shape[1:], f32)
         ref[1, 0:h, :] = jnp.zeros((h, cols), f32)
-        ref[1, h + rows :, :] = jnp.zeros((h, cols), f32)
-    part_ref[0] = level
-    rain_s[...] = rain
-    conv_s[...] = conv
-    sides = (-1, 0, 1, -1, 1, -1, 0, 1)
-    for direction, side in enumerate(sides):
-        share = jnp.where(code == direction, conv, 0.0)
-        m_ref[direction] = pltpu.roll(share, side % cols, 1) if side else share
+        ref[1, h + rows + 2 * h :, :] = jnp.zeros((h, cols), f32)
+    part_ref[0, h : h + rows, :] = level_ref[...]
+    ends = from_turns(
+        lax.axis_index("tx"), lax.axis_size("tx"),
+        first_swap_ref[...].astype(f32), second_swap_ref[...].astype(f32),
+    )
+    for k, (end, at) in enumerate(zip(ends, (0, h + rows))):
+        part_ref[0, at : at + h, :] = end[0:h]
+        end_ref[0, k * h : (k + 1) * h, :] = end[h : 2 * h]
+        end_ref[1, k * h : (k + 1) * h, :] = end[2 * h : 3 * h]
+        for direction, share in shares_by_direction(end[3 * h : 4 * h], end[2 * h : 3 * h]):
+            end_m_ref[direction, k * h : (k + 1) * h, :] = share
 
     def level_at(buf, r, n):
         level = part_ref[buf, r : r + n, :]
         return level + up_ref[buf, h + r + 1 : h + r + 1 + n, :] + down_ref[buf, h + r - 1 : h + r - 1 + n, :]
 
+    chunk = 16
+    chunks = [(0, h, end_ref.at[0], end_ref.at[1], end_m_ref, 0)]
+    chunks += [(h + r, chunk, rain_ref, conv_ref, m_ref, r) for r in range(0, rows, chunk)]
+    chunks += [(h + rows, h, end_ref.at[0], end_ref.at[1], end_m_ref, h)]
+
     def substep(buf, new):
-        for r in range(0, rows, chunk):
-            level = level_at(buf, r, chunk)
+        for r, n, rain, conv, shares, at in chunks:
+            level = level_at(buf, r, n)
             power = level * jnp.exp((2.0 / 3.0) * jnp.log(jnp.maximum(jnp.abs(level), 1e-30)))
             from_right = pltpu.roll(power, cols - 1, 1)
             from_left = pltpu.roll(power, 1, 1)
-            m = [m_ref[d, r : r + chunk, :] for d in range(8)]
-            up_ref[new, h + r : h + r + chunk, :] = m[0] * from_right + m[1] * power + m[2] * from_left
-            down_ref[new, h + r : h + r + chunk, :] = m[5] * from_right + m[6] * power + m[7] * from_left
-            part_ref[new, r : r + chunk, :] = (
-                level + rain_s[r : r + chunk, :] - conv_s[r : r + chunk, :] * power
-                + (m[3] * from_right + m[4] * from_left)
+            at = slice(at, at + n)
+            m = [shares[d, at, :] for d in range(8)]
+            up_ref[new, h + r : h + r + n, :] = m[0] * from_right + m[1] * power + m[2] * from_left
+            down_ref[new, h + r : h + r + n, :] = m[5] * from_right + m[6] * power + m[7] * from_left
+            part_ref[new, r : r + n, :] = (
+                level + rain[at, :] - conv[at, :] * power + (m[3] * from_right + m[4] * from_left)
             )
 
     def substep_pair(i, carry):
@@ -508,47 +532,7 @@
         return carry
 
     lax.fori_loop(0, SUBSTEPS // 2, substep_pair, 0)
-    return level_at
-
-
-def flow_inner_kernel(level_ref, side_ref, slope_ref, dir_ref, rain_ref, out_ref, *scratch):
-    rows, cols = level_ref.shape
-    own = (level_ref[...], rain_ref[...], runoff_coef * jnp.sqrt(slope_ref[...]), dir_ref[...].astype(f32))
-    level_at = substeps(*[jnp.concatenate([x, side_ref[i]], 1) for i, x in enumerate(own)], *scratch, 16)
-    out_ref[...] = level_at(0, 0, rows)[:, 0:cols]
-
-
-def flow_ends_kernel(inner_ref, level_ref, side_ref, slope_ref, dir_ref, rain_ref, first_swap_ref, second_swap_ref, out_ref, *scratch):
-    rows, cols = level_ref.shape
-    h = SUBSTEPS
-    above, below = from_turns(
-        lax.axis_index("tx"), lax.axis_size("tx"),
-        first_swap_ref[...].astype(f32), second_swap_ref[...].astype(f32),
-    )
-    fields = []
-    for i, ref in enumerate((level_ref, rain_ref, slope_ref, dir_ref)):
-        ends = []
-        for at in (slice(0, 2 * h), slice(rows - 2 * h, rows)):
-            own = ref[at, :].astype(f32)
-            if i == 2:
-                own = runoff_coef * jnp.sqrt(own)
-            ends.append(jnp.concatenate([own, side_ref[i, at, :]], 1))
-        fields.append(jnp.concatenate([above[i * h : (i + 1) * h], *ends, below[i * h : (i + 1) * h]], 0))
-    level_at = substeps(*fields, *scratch, 16)
-    out_ref[h : rows - h, :] = inner_ref[h : rows - h, :]
-    out_ref[0:h, :] = level_at(0, h, h)[:, 0:cols]
-    out_ref[rows - h :, :] = level_at(0, 4 * h, h)[:, 0:cols]
-
-
-def flow_scratch(rows, cols):
-    return [
-        pltpu.VMEM((rows, cols), f32),
-        pltpu.VMEM((rows, cols), f32),
-        pltpu.VMEM((8, rows, cols), f32),
-        pltpu.VMEM((2, rows, cols), f32),
-        pltpu.VMEM((2, rows + 2 * SUBSTEPS, cols), f32),
-        pltpu.VMEM((2, rows + 2 * SUBSTEPS, cols), f32),
-    ]
+    out_ref[...] = level_at(0, h, rows)[:, 0 : out_ref.shape[1]]
 
 
 def hbm_specs(n):
@@ -569,37 +553,51 @@
     tile_rows, tile_cols = depth.shape
     capacity = max(2, 2 * az_lines // devices)
 
-    def swaps(axis, first, second):
-        size = lax.axis_size(axis)
+    n_tx, n_ty = lax.axis_size("tx"), lax.axis_size("ty")
+
+    def swaps(first, second, stride):
+        size = devices // stride
         out = []
         for start, x in enumerate((first, second)):
-            pairs = [(i, (i + 1) % size) for i in range(start, size, 2)]
-            out.append(lax.ppermute(x, axis, pairs + [(j, i) for i, j in pairs]))
+            to = {}
+            for place in range(start, size, 2):
+                for k in range(stride):
+                    i, j = place * stride + k, (place + 1) % size * stride + k
+                    if place == size - 1 and stride > 1:
+                        ends = (i, i ^ 1), (j, j ^ 1)
+                    else:
+                        ends = (i, j), (j, i)
+                    to.update(ends)
+            out.append(lax.ppermute(x, both, sorted(to.items())))
         return out
 
     params = pltpu.CompilerParams(vmem_limit_bytes=VMEM_LIMIT)
     message = pltpu.VMEM((32, range_px), bf16)
-    small = (
+    handed = (
+        sar_image,
         jnp.transpose(kernel_first, (2, 3, 1, 0)),
+        jnp.transpose(kernel_second, (2, 3, 0, 1)).reshape(9 * CH, CH),
+        jnp.transpose(kernel_third, (2, 3, 0, 1)).reshape(9 * CH, CH),
         jnp.transpose(kernel_last[0], (1, 2, 0)),
         block_tile.reshape(1, az_lines),
         block_row.reshape(1, az_lines),
-    )
-    first, second, *small = pl.pallas_call(
+        geo_weight,
+        cell_index,
+    )
+    first, second, sar_image, *handed = pl.pallas_call(
         edge_kernel,
-        out_shape=(message, message, *[pltpu.VMEM(x.shape, x.dtype) for x in small]),
-        in_specs=hbm_specs(9),
-        out_specs=tuple(vmem_specs(6)),
+        out_shape=(message, message, *[pltpu.VMEM(x.shape, x.dtype) for x in handed]),
+        in_specs=hbm_specs(4 + len(handed)),
+        out_specs=tuple(vmem_specs(2 + len(handed))),
         scratch_shapes=[
-            pltpu.VMEM((2, 16, range_px), bf16),
-            pltpu.VMEM((2, 16, range_px), bf16),
             *[pltpu.VMEM(x.shape, x.dtype) for x in (depth, slope, rain, flow_dir)],
-            pltpu.SemaphoreType.DMA((10,)),
+            pltpu.SemaphoreType.DMA((4 + len(handed),)),
         ],
         compiler_params=pltpu.CompilerParams(vmem_limit_bytes=VMEM_MOST),
         name="edges",
-    )(sar_image, depth, slope, rain, flow_dir, *small)
-    halo = swaps(both, first, second)
+    )(depth, slope, rain, flow_dir, *handed)
+    geo_weight, cell_index = handed[-2:]
+    halo = swaps(first, second, 1)
 
     rows, cols = OUT_LINES * CH, IN_LINES * CH
     slots = devices * capacity * 4
@@ -640,11 +638,7 @@
         cost_estimate=cost(8_000_000_000),
         name="inner",
     )(
-        small[0],
-        jnp.transpose(kernel_second, (2, 3, 0, 1)).reshape(9 * CH, CH),
-        jnp.transpose(kernel_third, (2, 3, 0, 1)).reshape(9 * CH, CH),
-        *small[1:],
-        sar_image, geo_weight, cell_index,
+        *handed[:-2], sar_image, geo_weight, cell_index,
     )
     fraction, send = pl.pallas_call(
         functools.partial(ends_kernel, devices, capacity),
@@ -664,42 +658,44 @@
     ).reshape(devices * send_rows, LANES)
 
     wide_cols = tile_cols + LANES
+    wide = jax.ShapeDtypeStruct((tile_rows, wide_cols), f32)
     edge = jax.ShapeDtypeStruct((4 * SUBSTEPS, wide_cols), bf16)
     level, side, first, second = pl.pallas_call(
         functools.partial(level_kernel, devices),
-        out_shape=(
-            jax.ShapeDtypeStruct((tile_rows, tile_cols), f32),
-            jax.ShapeDtypeStruct((4, tile_rows, LANES), f32),
-            edge,
-            edge,
-        ),
+        out_shape=(wide, jax.ShapeDtypeStruct((3, tile_rows, LANES), f32), edge, edge),
         in_specs=vmem_specs(7),
         out_specs=tuple(vmem_specs(4)),
         compiler_params=params,
         name="level",
     )(got, *halo, depth, slope, rain, flow_dir)
 
-    row_halo = swaps("tx", first, second)
-
-    inner = pl.pallas_call(
-        flow_inner_kernel,
+    row_halo = swaps(first, second, n_ty)
+
+    rain_wide, conv_wide, shares = pl.pallas_call(
+        static_kernel,
+        out_shape=(wide, wide, jax.ShapeDtypeStruct((8, tile_rows, wide_cols), f32)),
+        in_specs=vmem_specs(4),
+        out_specs=tuple(vmem_specs(3)),
+        compiler_params=params,
+        cost_estimate=cost(2_000_000_000),
+        name="static",
+    )(side, slope, rain, flow_dir)
+    flow_rows = tile_rows + 2 * SUBSTEPS
+    level = pl.pallas_call(
+        flow_kernel,
         out_shape=jax.ShapeDtypeStruct((tile_rows, tile_cols), f32),
-        in_specs=vmem_specs(5),
+        in_specs=vmem_specs(6),
         out_specs=vmem_specs(1)[0],
-        scratch_shapes=flow_scratch(tile_rows, wide_cols),
+        scratch_shapes=[
+            pltpu.VMEM((2, 2 * SUBSTEPS, wide_cols), f32),
+            pltpu.VMEM((8, 2 * SUBSTEPS, wide_cols), f32),
+            pltpu.VMEM((2, flow_rows, wide_cols), f32),
+            pltpu.VMEM((2, flow_rows + 2 * SUBSTEPS, wide_cols), f32),
+            pltpu.VMEM((2, flow_rows + 2 * SUBSTEPS, wide_cols), f32),
+        ],
         compiler_params=params,
-        cost_estimate=cost(5_000_000_000),
-        name="flow_inner",
-    )(level, side, slope, flow_dir, rain)
-    level = pl.pallas_call(
-        flow_ends_kernel,
-        out_shape=jax.ShapeDtypeStruct((tile_rows, tile_cols), f32),
-        in_specs=vmem_specs(8),
-        out_specs=vmem_specs(1)[0],
-        scratch_shapes=flow_scratch(6 * SUBSTEPS, wide_cols),
-        compiler_params=params,
-        name="flow_ends",
-    )(inner, level, side, slope, flow_dir, rain, *row_halo)
+        name="flow",
+    )(level, rain_wide, conv_wide, shares, *row_halo)
     return (fraction, level)
 
 

time: 41.9 us -> 40.8 us (0.974)
  waiting for transfers between devices: 0.39 us -> 2.24 us
  starting transfers between devices: 9.76 us -> 8.02 us
  Pallas kernels: 17 us -> 15.9 us
    ppermute x4, waiting for transfers between devices: 0.39 us -> 2.24 us  [swaps(): out.append(lax.ppermute(x, both, sorted(to.items())))]
    ppermute x4, starting transfers between devices: 9.76 us -> 8.02 us  [swaps(): out.append(lax.ppermute(x, both, sorted(to.items())))]
    pallas_call x3, Pallas kernels: 7.34 us -> 6.3 us  [the longest x1 4.64 us: per_device(): pl.pallas_call(flow_kernel, out_shape=jax.ShapeDtypeStruct((tile_rows, ti...]
  transfers between devices with their start and end apart: 4 -> 4, of which waited for: 1 -> 1; matrix products, arithmetic and copies ran while one was open for 0% -> 0% of each run, Pallas kernels for 23% -> 15%
where the time goes in v11:
time: 40.8 us; the launch traced here: 40.7 us
  Pallas kernels  15.9 us (39%)
  blocking collectives  13.8 us (34%)
  starting transfers between devices  8.02 us (20%)
  waiting for transfers between devices  2.24 us (5%)
  between operations  0.72 us (2%)
    all_to_all x1, blocking collectives, per_device(): lax.all_to_all(send.reshape(devices, send_rows, LANES), both, split_axis=...  13.8 us
    ppermute x4, starting transfers between devices, swaps(): out.append(lax.ppermute(x, both, sorted(to.items())))  8.02 us
    pallas_call x1, Pallas kernels, per_device(): pl.pallas_call(functools.partial(inner_kernel, devices, capacity), out_sh...  5.23 us
    pallas_call x1, Pallas kernels, per_device(): pl.pallas_call(flow_kernel, out_shape=jax.ShapeDtypeStruct((tile_rows, ti...  4.64 us
    pallas_call x1, Pallas kernels, per_device(): pl.pallas_call(functools.partial(ends_kernel, devices, capacity), out_sha...  2.82 us
    ppermute x4, waiting for transfers between devices, swaps(): out.append(lax.ppermute(x, both, sorted(to.items())))  2.24 us
    pallas_call x1, Pallas kernels, per_device(): pl.pallas_call(edge_kernel, out_shape=(message, message, *[pltpu.VMEM(x.s...  1.55 us
    pallas_call x1, Pallas kernels, per_device(): pl.pallas_call(functools.partial(level_kernel, devices), out_shape=(wide,...  0.92 us
  transfers between devices with their start and end apart: 4, of which 1 were waited for; matrix products, arithmetic and copies ran while one was open for 0% of the time, Pallas kernels for 15%

profile of v11, /device:TPU:0, one launch (start us, length us, event | category | flops | bytes accessed | tf_op | source)
XLA Modules:
  0.0 40.7 jit_solution(12325819775779960509)
XLA Ops:
  0.6 1.5 %edges.1 = (bf16[32,512]{1,0:T(8,128)(2,1)S(1)}, bf16[32,512]{1,0:T(8,128)(2,1)S(1)}, bf16[2,64,512]{2,1,0:T(8,128)(2,1)S(1)}, bf16[3,3,2,16]{3,2,1,0:T(2,128)(2...) custom-call(f32[256,256]{1,0:T(8,128)} %depth_ref.1, ...), custom_call_target="tpu_custom_call" | custom-call | tf_op jit(solution)/shard_map/edges/pallas_call | solution.py:587
  2.2 0.5 %collective-permute-start = (bf16[32,512]{1,0:T(8,128)(2,1)S(1)}, bf16[32,512]{1,0:T(8,128)(2,1)S(1)}, u32[]{:S(2)}, u32[]{:S(2)}) collective-permute-start(bf16[32,512]{1,0:T(8,128)(2,1)S(1)} %get-tuple-element.33), channel_id=1, source_target_pairs={{0,1},{1,0},{2,3},{3,2},{4,5},{5,4},{6,7},{7,6},{8,9},{9,8},{10,11... | collective-permute-start | bytes 98312 | tf_op jit(solution)/shard_map/ppermute | solution.py:571
  2.7 6.6 %collective-permute-start.1 = (bf16[32,512]{1,0:T(8,128)(2,1)S(1)}, bf16[32,512]{1,0:T(8,128)(2,1)S(1)}, u32[]{:S(2)}, u32[]{:S(2)}) collective-permute-start(bf16[32,512]{1,0:T(8,128)(2,1)S(1)} %get-tuple-element.34), channel_id=1, source_target_pairs={{0,31},{1,2},{2,1},{3,4},{4,3},{5,6},{6,5},{7,8},{8,7},{9,10},{10,... | collective-permute-start | bytes 98312 | tf_op jit(solution)/shard_map/ppermute | solution.py:571
  9.3 5.2 %inner.1 = (bf16[224,128]{1,0:T(8,128)(2,1)S(1)}, bf16[224,768]{1,0:T(8,128)(2,1)S(1)}, bf16[224,768]{1,0:T(8,128)(2,1)S(1)}, bf16[48,256]{1,0:T(8,128)(2,1)S(1)...) custom-call(bf16[3,3,2,16]{3,2,1,0:T(2,128)(2,1)S(1)} %get-tuple-ele, ...), custom_call_target="tpu_custom_call" | custom-call | flops 8000000000 | bytes 4000000 | tf_op jit(solution)/shard_map/inner/pallas_call | solution.py:612
  14.5 0.0 copy-start
  14.5 0.0 copy-start.1
  14.6 0.0 copy-start.2
  14.6 0.0 copy-start.3
  14.6 0.0 collective-permute-done.first_swap_ref
  14.6 0.0 collective-permute-done.1.second_swap_ref
  14.6 2.8 %ends.1 = (bf16[64,512]{1,0:T(8,128)(2,1)}, bf16[1280,128]{1,0:T(8,128)(2,1)S(1)}) custom-call(bf16[32,512]{1,0:T(8,128)(2,1)S(1)} %collective-permute-done.first_swap_ref, bf16[32,512]{1,0:T(8,128)(2,1)S(1)} %collective-permute-done.1.second_swap_ref, bf16[224,128]{1,0:T(8,128)(2,1)S(1)} %get-tuple-element.44.w1_ref, ...), custom_call_target="tpu_custom_call" | custom-call | tf_op jit(solution)/shard_map/ends/pallas_call | solution.py:643
  17.4 13.8 %all_to_all.5 = bf16[32,40,128]{2,1,0:T(8,128)(2,1)S(1)} all-to-all(bf16[32,40,128]{2,1,0:T(8,128)(2,1)S(1)} %bitcast.15), channel_id=1, replica_groups=mesh['tx'=8,'ty'=4] {'tx','ty'}, dimensions={0} | all-to-all | bytes 655360 | tf_op jit(solution)/shard_map/all_to_all | solution.py:656
  31.2 0.0 copy-done
  31.2 0.0 copy-done.1
  31.2 0.0 copy-done.2
  31.2 0.0 copy-done.3
  31.2 0.9 %level.1 = (f32[256,384]{1,0:T(8,128)S(1)}, f32[3,256,128]{2,1,0:T(8,128)S(1)}, bf16[32,384]{1,0:T(8,128)(2,1)S(1)}, bf16[32,384]{1,0:T(8,128)(2,1)S(1)}) custom-call(bf16[1280,128]{1,0:T(8,128)(2,1)S(1)} %bitcast.14, bf16[32,512]{1,0:T(8,128)(2,1)S(1)} %collective-permute-done.first_swap_ref, bf16[32,512]{1,0:T(8,128)(2,1)S(1)} %collective-permute-done.1.second_swap_ref, ...), custom_call_target="tpu_custom_call" | custom-call | tf_op jit(solution)/shard_map/level/pallas_call | solution.py:663
  32.2 0.9 %collective-permute-start.2 = (bf16[32,384]{1,0:T(8,128)(2,1)S(1)}, bf16[32,384]{1,0:T(8,128)(2,1)S(1)}, u32[]{:S(2)}, u32[]{:S(2)}) collective-permute-start(bf16[32,384]{1,0:T(8,128)(2,1)S(1)} %get-tuple-element.62), channel_id=1, source_target_pairs={{0,4},{1,5},{2,6},{3,7},{4,0},{5,1},{6,2},{7,3},{8,12},{9,13},{10,... | collective-permute-start | bytes 73736 | tf_op jit(solution)/shard_map/ppermute | solution.py:571
  33.1 0.0 collective-permute-start.3
  33.1 0.7 %static.1 = (f32[256,384]{1,0:T(8,128)S(1)}, f32[256,384]{1,0:T(8,128)S(1)}, f32[8,256,384]{2,1,0:T(8,128)S(1)}) custom-call(f32[3,256,128]{2,1,0:T(8,128)S(1)} %get-tuple-element.58.side_ref, f32[256,256]{1,0:T(8,128)S(1)} %copy-done.1, f32[256,256]{1,0:T(8,128)S(1)} %copy-done.2, s32[256,256]{1,0:T(8,128)S(1)} %copy-done.3), custom_call_target="tpu_custom_call" | custom-call | flops 2000000000 | bytes 4000000 | tf_op jit(solution)/shard_map/static/pallas_call | solution.py:674
  33.8 2.2 %collective-permute-done.2.first_swap_ref = bf16[32,384]{1,0:T(8,128)(2,1)S(1)} collective-permute-done((bf16[32,384]{1,0:T(8,128)(2,1)S(1)}, bf16[32,384]{1,0:T(8,128)(2,1)S(1)}, u32[]{:S(2)}, u32[]{:S(2)}) %collective-permute-start.2) | collective-permute-done | bytes 24608 | tf_op jit(solution)/shard_map/ppermute | solution.py:571
  36.0 0.0 collective-permute-done.3.second_swap_ref
  36.0 4.6 %flow.1 = f32[256,256]{1,0:T(8,128)} custom-call(f32[256,384]{1,0:T(8,128)S(1)} %get-tuple-element.57.level_ref, f32[256,384]{1,0:T(8,128)S(1)} %get-tuple-element.59.rain_ref, f32[256,384]{1,0:T(8,128)S(1)} %get-tuple-element.60.conv_ref, f32[8,256,384]{2,1,0:T(8,128)S(1)} %get-tuple-element.61.m_ref, ...), custom_call_target="tpu_custom_call" | custom-call | tf_op jit(solution)/shard_map/flow/pallas_call | solution.py:684
Async XLA Ops:
  2.2 12.4 %collective-permute-start = (bf16[32,512]{1,0:T(8,128)(2,1)S(1)}, bf16[32,512]{1,0:T(8,128)(2,1)S(1)}, u32[]{:S(2)}, u32[]{:S(2)}) collective-permute-start(bf16[32,512]{1,0:T(8,128)(2,1)S(1)} %get-tuple-element.33), channel_id=1, source_target_pairs={{0,1},{1,0},{2,3},{3,2},{4,5},{5,4},{6,7},{7,6},{8,9},{9,8},{10,11... | collective-permute-start | bytes 98312 | tf_op jit(solution)/shard_map/ppermute | solution.py:571
  2.7 11.9 %collective-permute-start.1 = (bf16[32,512]{1,0:T(8,128)(2,1)S(1)}, bf16[32,512]{1,0:T(8,128)(2,1)S(1)}, u32[]{:S(2)}, u32[]{:S(2)}) collective-permute-start(bf16[32,512]{1,0:T(8,128)(2,1)S(1)} %get-tuple-element.34), channel_id=1, source_target_pairs={{0,31},{1,2},{2,1},{3,4},{4,3},{5,6},{6,5},{7,8},{8,7},{9,10},{10,... | collective-permute-start | bytes 98312 | tf_op jit(solution)/shard_map/ppermute | solution.py:571
  14.5 16.7 %copy-start = (f32[256,256]{1,0:T(8,128)S(1)}, f32[256,256]{1,0:T(8,128)}, u32[]{:S(2)}) copy-start(f32[256,256]{1,0:T(8,128)} %depth_ref.1) | copy-start | bytes 786436
  14.5 16.7 %copy-start.1 = (f32[256,256]{1,0:T(8,128)S(1)}, f32[256,256]{1,0:T(8,128)}, u32[]{:S(2)}) copy-start(f32[256,256]{1,0:T(8,128)} %slope_ref.3) | copy-start | bytes 786436
  14.6 16.7 %copy-start.2 = (f32[256,256]{1,0:T(8,128)S(1)}, f32[256,256]{1,0:T(8,128)}, u32[]{:S(2)}) copy-start(f32[256,256]{1,0:T(8,128)} %rain_ref.3) | copy-start | bytes 786436
  14.6 16.6 %copy-start.3 = (s32[256,256]{1,0:T(8,128)S(1)}, s32[256,256]{1,0:T(8,128)}, u32[]{:S(2)}) copy-start(s32[256,256]{1,0:T(8,128)} %dir_ref.3) | copy-start | bytes 786436
  32.2 3.9 %collective-permute-start.2 = (bf16[32,384]{1,0:T(8,128)(2,1)S(1)}, bf16[32,384]{1,0:T(8,128)(2,1)S(1)}, u32[]{:S(2)}, u32[]{:S(2)}) collective-permute-start(bf16[32,384]{1,0:T(8,128)(2,1)S(1)} %get-tuple-element.62), channel_id=1, source_target_pairs={{0,4},{1,5},{2,6},{3,7},{4,0},{5,1},{6,2},{7,3},{8,12},{9,13},{10,... | collective-permute-start | bytes 73736 | tf_op jit(solution)/shard_map/ppermute | solution.py:571
  33.1 3.0 %collective-permute-start.3 = (bf16[32,384]{1,0:T(8,128)(2,1)S(1)}, bf16[32,384]{1,0:T(8,128)(2,1)S(1)}, u32[]{:S(2)}, u32[]{:S(2)}) collective-permute-start(bf16[32,384]{1,0:T(8,128)(2,1)S(1)} %get-tuple-element.63), channel_id=1, source_target_pairs={{0,1},{1,0},{2,3},{3,2},{4,8},{5,9},{6,10},{7,11},{8,4},{9,5},{10,... | collective-permute-start | bytes 73736 | tf_op jit(solution)/shard_map/ppermute | solution.py:571

commit v12 on v9

--- a/solution.py
+++ b/solution.py
@@ -16,7 +16,7 @@
 END_LINES = 8
 LANES = 128
 VMEM_LIMIT = 48 * 1024 * 1024
-VMEM_MOST = 61880 * 1024
+VMEM_MOST = 60160 * 1024
 
 wet_depth = 0.5
 runoff_coef = 0.25
@@ -119,27 +119,24 @@
 
 
 def edge_kernel(
-    sar_hbm, depth_hbm, slope_hbm, rain_hbm, dir_hbm, k1_hbm, k4_hbm, tile_hbm, row_hbm,
-    first_swap_ref, second_swap_ref, k1_ref, k4_ref, tile_ref, row_ref,
-    last_ref, first_ref, depth_ref, slope_ref, rain_ref, dir_ref, sems,
+    depth_hbm, slope_hbm, rain_hbm, dir_hbm, sar_hbm, *refs
 ):
+    n_on = (len(refs) - 8) // 2
+    on_hbm = refs[:n_on]
+    first_swap_ref, second_swap_ref, sar_ref, *on_refs = refs[n_on : 2 * n_on + 3]
+    depth_ref, slope_ref, rain_ref, dir_ref, sems = refs[2 * n_on + 3 :]
     even = rem(lax.axis_index("tx") * lax.axis_size("ty") + lax.axis_index("ty"), 2) == 0
     lines, px = sar_hbm.shape[1:]
     cols = depth_hbm.shape[1]
     h = SUBSTEPS
-    copies = [
-        pltpu.make_async_copy(src, dst, sems.at[i])
-        for i, (src, dst) in enumerate(
-            (
-                (depth_hbm, depth_ref), (slope_hbm, slope_ref), (rain_hbm, rain_ref), (dir_hbm, dir_ref),
-                (sar_hbm.at[:, lines - 16 : lines, :], last_ref), (sar_hbm.at[:, 0:16, :], first_ref),
-                (k1_hbm, k1_ref), (k4_hbm, k4_ref), (tile_hbm, tile_ref), (row_hbm, row_ref),
-            )
-        )
-    ]
+    pairs = (
+        (depth_hbm, depth_ref), (slope_hbm, slope_ref), (rain_hbm, rain_ref), (dir_hbm, dir_ref),
+        (sar_hbm, sar_ref), *zip(on_hbm, on_refs),
+    )
+    copies = [pltpu.make_async_copy(src, dst, sems.at[i]) for i, (src, dst) in enumerate(pairs)]
     for copy in copies:
         copy.start()
-    for copy in copies:
+    for copy in copies[0:5]:
         copy.wait()
     fields = (
         depth_ref[...],
@@ -149,11 +146,11 @@
     )
     zeros = jnp.zeros((8, px), f32)
     messages = []
-    for image_ref, lo, strip in (
-        (last_ref, 16 - HALO_LINES, lambda x: jnp.transpose(x[:, cols - LANES :], (1, 0))[LANES - h :]),
-        (first_ref, 0, lambda x: jnp.transpose(x[:, 0:LANES], (1, 0))[0:h]),
+    for at, lo, strip in (
+        (lines - 16, 16 - HALO_LINES, lambda x: jnp.transpose(x[:, cols - LANES :], (1, 0))[LANES - h :]),
+        (0, 0, lambda x: jnp.transpose(x[:, 0:LANES], (1, 0))[0:h]),
     ):
-        image = [image_ref[ch].astype(f32)[lo : lo + HALO_LINES] for ch in range(2)]
+        image = [sar_ref[ch, at : at + 16, :].astype(f32)[lo : lo + HALO_LINES] for ch in range(2)]
         strips = [strip(x) for x in fields]
         messages.append(
             jnp.concatenate([jnp.concatenate(strips[0:2], 1), jnp.concatenate(strips[2:4], 1), *image, zeros], 0)
@@ -161,6 +158,8 @@
     first, second = in_turn(even, *messages)
     first_swap_ref[...] = first.astype(bf16)
     second_swap_ref[...] = second.astype(bf16)
+    for copy in copies[5:]:
+        copy.wait()
 
 
 def in_turn(even, to_next, to_previous):
@@ -569,37 +568,51 @@
     tile_rows, tile_cols = depth.shape
     capacity = max(2, 2 * az_lines // devices)
 
-    def swaps(axis, first, second):
-        size = lax.axis_size(axis)
+    n_tx, n_ty = lax.axis_size("tx"), lax.axis_size("ty")
+
+    def swaps(first, second, stride):
+        size = devices // stride
         out = []
         for start, x in enumerate((first, second)):
-            pairs = [(i, (i + 1) % size) for i in range(start, size, 2)]
-            out.append(lax.ppermute(x, axis, pairs + [(j, i) for i, j in pairs]))
+            to = {}
+            for place in range(start, size, 2):
+                for k in range(stride):
+                    i, j = place * stride + k, (place + 1) % size * stride + k
+                    if place == size - 1 and stride > 1:
+                        ends = (i, i ^ 1), (j, j ^ 1)
+                    else:
+                        ends = (i, j), (j, i)
+                    to.update(ends)
+            out.append(lax.ppermute(x, both, sorted(to.items())))
         return out
 
     params = pltpu.CompilerParams(vmem_limit_bytes=VMEM_LIMIT)
     message = pltpu.VMEM((32, range_px), bf16)
-    small = (
+    handed = (
+        sar_image,
         jnp.transpose(kernel_first, (2, 3, 1, 0)),
+        jnp.transpose(kernel_second, (2, 3, 0, 1)).reshape(9 * CH, CH),
+        jnp.transpose(kernel_third, (2, 3, 0, 1)).reshape(9 * CH, CH),
         jnp.transpose(kernel_last[0], (1, 2, 0)),
         block_tile.reshape(1, az_lines),
         block_row.reshape(1, az_lines),
-    )
-    first, second, *small = pl.pallas_call(
+        geo_weight,
+        cell_index,
+    )
+    first, second, sar_image, *handed = pl.pallas_call(
         edge_kernel,
-        out_shape=(message, message, *[pltpu.VMEM(x.shape, x.dtype) for x in small]),
-        in_specs=hbm_specs(9),
-        out_specs=tuple(vmem_specs(6)),
+        out_shape=(message, message, *[pltpu.VMEM(x.shape, x.dtype) for x in handed]),
+        in_specs=hbm_specs(4 + len(handed)),
+        out_specs=tuple(vmem_specs(2 + len(handed))),
         scratch_shapes=[
-            pltpu.VMEM((2, 16, range_px), bf16),
-            pltpu.VMEM((2, 16, range_px), bf16),
             *[pltpu.VMEM(x.shape, x.dtype) for x in (depth, slope, rain, flow_dir)],
-            pltpu.SemaphoreType.DMA((10,)),
+            pltpu.SemaphoreType.DMA((4 + len(handed),)),
         ],
         compiler_params=pltpu.CompilerParams(vmem_limit_bytes=VMEM_MOST),
         name="edges",
-    )(sar_image, depth, slope, rain, flow_dir, *small)
-    halo = swaps(both, first, second)
+    )(depth, slope, rain, flow_dir, *handed)
+    geo_weight, cell_index = handed[-2:]
+    halo = swaps(first, second, 1)
 
     rows, cols = OUT_LINES * CH, IN_LINES * CH
     slots = devices * capacity * 4
@@ -640,11 +653,7 @@
         cost_estimate=cost(8_000_000_000),
         name="inner",
     )(
-        small[0],
-        jnp.transpose(kernel_second, (2, 3, 0, 1)).reshape(9 * CH, CH),
-        jnp.transpose(kernel_third, (2, 3, 0, 1)).reshape(9 * CH, CH),
-        *small[1:],
-        sar_image, geo_weight, cell_index,
+        *handed[:-2], sar_image, geo_weight, cell_index,
     )
     fraction, send = pl.pallas_call(
         functools.partial(ends_kernel, devices, capacity),
@@ -679,7 +688,7 @@
         name="level",
     )(got, *halo, depth, slope, rain, flow_dir)
 
-    row_halo = swaps("tx", first, second)
+    row_halo = swaps(first, second, n_ty)
 
     inner = pl.pallas_call(
         flow_inner_kernel,

time: 41.9 us -> 39.8 us (0.950)
  starting transfers between devices: 9.76 us -> 8.02 us
    ppermute x4, starting transfers between devices: 9.76 us -> 8.02 us  [swaps(): out.append(lax.ppermute(x, both, sorted(to.items())))]
  transfers between devices with their start and end apart: 4 -> 4, of which waited for: 1 -> 0; matrix products, arithmetic and copies ran while one was open for 0% -> 0% of each run, Pallas kernels for 23% -> 24%
where the time goes in v12:
time: 39.8 us; the launch traced here: 39.5 us
  Pallas kernels  16.9 us (42%)
  blocking collectives  13.8 us (35%)
  starting transfers between devices  8.02 us (20%)
  between operations  0.72 us (2%)
    all_to_all x1, blocking collectives, per_device(): lax.all_to_all(send.reshape(devices, send_rows, LANES), both, split_axis=...  13.8 us
    ppermute x4, starting transfers between devices, swaps(): out.append(lax.ppermute(x, both, sorted(to.items())))  8.02 us
    pallas_call x1, Pallas kernels, per_device(): pl.pallas_call(functools.partial(inner_kernel, devices, capacity), out_sh...  5.23 us
    pallas_call x1, Pallas kernels, per_device(): pl.pallas_call(flow_inner_kernel, out_shape=jax.ShapeDtypeStruct((tile_ro...  4.38 us
    pallas_call x1, Pallas kernels, per_device(): pl.pallas_call(functools.partial(ends_kernel, devices, capacity), out_sha...  2.83 us
    pallas_call x1, Pallas kernels, per_device(): pl.pallas_call(flow_ends_kernel, out_shape=jax.ShapeDtypeStruct((tile_row...  2.04 us
    pallas_call x1, Pallas kernels, per_device(): pl.pallas_call(edge_kernel, out_shape=(message, message, *[pltpu.VMEM(x.s...  1.55 us
    pallas_call x1, Pallas kernels, per_device(): pl.pallas_call(functools.partial(level_kernel, devices), out_shape=(jax.S...  0.92 us
  transfers between devices with their start and end apart: 4, of which 0 were waited for; matrix products, arithmetic and copies ran while one was open for 0% of the time, Pallas kernels for 24%

profile of v12, /device:TPU:0, one launch (start us, length us, event | category | flops | bytes accessed | tf_op | source)
XLA Modules:
  0.0 39.5 jit_solution(14776483065032026501)
XLA Ops:
  0.6 1.5 %edges.1 = (bf16[32,512]{1,0:T(8,128)(2,1)S(1)}, bf16[32,512]{1,0:T(8,128)(2,1)S(1)}, bf16[2,64,512]{2,1,0:T(8,128)(2,1)S(1)}, bf16[3,3,2,16]{3,2,1,0:T(2,128)(2...) custom-call(f32[256,256]{1,0:T(8,128)} %depth_ref.1, ...), custom_call_target="tpu_custom_call" | custom-call | tf_op jit(solution)/shard_map/edges/pallas_call | solution.py:602
  2.2 0.5 %collective-permute-start = (bf16[32,512]{1,0:T(8,128)(2,1)S(1)}, bf16[32,512]{1,0:T(8,128)(2,1)S(1)}, u32[]{:S(2)}, u32[]{:S(2)}) collective-permute-start(bf16[32,512]{1,0:T(8,128)(2,1)S(1)} %get-tuple-element.30), channel_id=1, source_target_pairs={{0,1},{1,0},{2,3},{3,2},{4,5},{5,4},{6,7},{7,6},{8,9},{9,8},{10,11... | collective-permute-start | bytes 98312 | tf_op jit(solution)/shard_map/ppermute | solution.py:586
  2.7 6.6 %collective-permute-start.1 = (bf16[32,512]{1,0:T(8,128)(2,1)S(1)}, bf16[32,512]{1,0:T(8,128)(2,1)S(1)}, u32[]{:S(2)}, u32[]{:S(2)}) collective-permute-start(bf16[32,512]{1,0:T(8,128)(2,1)S(1)} %get-tuple-element.31), channel_id=1, source_target_pairs={{0,31},{1,2},{2,1},{3,4},{4,3},{5,6},{6,5},{7,8},{8,7},{9,10},{10,... | collective-permute-start | bytes 98312 | tf_op jit(solution)/shard_map/ppermute | solution.py:586
  9.3 5.2 %inner.1 = (bf16[224,128]{1,0:T(8,128)(2,1)S(1)}, bf16[224,768]{1,0:T(8,128)(2,1)S(1)}, bf16[224,768]{1,0:T(8,128)(2,1)S(1)}, bf16[48,256]{1,0:T(8,128)(2,1)S(1)...) custom-call(bf16[3,3,2,16]{3,2,1,0:T(2,128)(2,1)S(1)} %get-tuple-ele, ...), custom_call_target="tpu_custom_call" | custom-call | flops 8000000000 | bytes 4000000 | tf_op jit(solution)/shard_map/inner/pallas_call | solution.py:627
  14.5 0.0 collective-permute-done.first_swap_ref
  14.5 0.0 collective-permute-done.1.second_swap_ref
  14.5 0.0 copy-start.2
  14.6 0.0 copy-start.3
  14.6 2.8 %ends.1 = (bf16[64,512]{1,0:T(8,128)(2,1)}, bf16[1280,128]{1,0:T(8,128)(2,1)S(1)}) custom-call(bf16[32,512]{1,0:T(8,128)(2,1)S(1)} %collective-permute-done.first_swap_ref, bf16[32,512]{1,0:T(8,128)(2,1)S(1)} %collective-permute-done.1.second_swap_ref, bf16[224,128]{1,0:T(8,128)(2,1)S(1)} %get-tuple-element.41.w1_ref, ...), custom_call_target="tpu_custom_call" | custom-call | tf_op jit(solution)/shard_map/ends/pallas_call | solution.py:658
  17.4 0.0 copy-start
  17.4 0.0 copy-start.1
  17.4 13.8 %all_to_all.5 = bf16[32,40,128]{2,1,0:T(8,128)(2,1)S(1)} all-to-all(bf16[32,40,128]{2,1,0:T(8,128)(2,1)S(1)} %bitcast.15), channel_id=1, replica_groups=mesh['tx'=8,'ty'=4] {'tx','ty'}, dimensions={0} | all-to-all | bytes 655360 | tf_op jit(solution)/shard_map/all_to_all | solution.py:671
  31.2 0.0 copy-done.2
  31.2 0.0 copy-done.3
  31.2 0.0 copy-done
  31.2 0.0 copy-done.1
  31.2 0.9 %level.1 = (f32[256,256]{1,0:T(8,128)S(1)}, f32[4,256,128]{2,1,0:T(8,128)S(1)}, bf16[32,384]{1,0:T(8,128)(2,1)S(1)}, bf16[32,384]{1,0:T(8,128)(2,1)S(1)}) custom-call(bf16[1280,128]{1,0:T(8,128)(2,1)S(1)} %bitcast.14, bf16[32,512]{1,0:T(8,128)(2,1)S(1)} %collective-permute-done.first_swap_ref, bf16[32,512]{1,0:T(8,128)(2,1)S(1)} %collective-permute-done.1.second_swap_ref, ...), custom_call_target="tpu_custom_call" | custom-call | tf_op jit(solution)/shard_map/level/pallas_call | solution.py:677
  32.2 0.9 %collective-permute-start.2 = (bf16[32,384]{1,0:T(8,128)(2,1)S(1)}, bf16[32,384]{1,0:T(8,128)(2,1)S(1)}, u32[]{:S(2)}, u32[]{:S(2)}) collective-permute-start(bf16[32,384]{1,0:T(8,128)(2,1)S(1)} %get-tuple-element.56), channel_id=1, source_target_pairs={{0,4},{1,5},{2,6},{3,7},{4,0},{5,1},{6,2},{7,3},{8,12},{9,13},{10,... | collective-permute-start | bytes 73736 | tf_op jit(solution)/shard_map/ppermute | solution.py:586
  33.1 0.0 collective-permute-start.3
  33.1 4.4 %flow_inner.1.inner_ref = f32[256,256]{1,0:T(8,128)S(1)} custom-call(f32[256,256]{1,0:T(8,128)S(1)} %get-tuple-element.54.level_ref, f32[4,256,128]{2,1,0:T(8,128)S(1)} %get-tuple-element.55.side_ref, f32[256,256]{1,0:T(8,128)S(1)} %copy-done, s32[256,256]{1,0:T(8,128)S(1)} %copy-done.2, f32[256,256]{1,0:T(8,128)S(1)} %copy-done.1), custom_call_target="tpu_custom_call" | custom-call | flops 5000000000 | bytes 4000000 | tf_op jit(solution)/shard_map/flow_inner/pallas_call | solution.py:693
  37.5 0.0 collective-permute-done.2.first_swap_ref
  37.5 0.0 collective-permute-done.3.second_swap_ref
  37.5 2.0 %flow_ends.1 = f32[256,256]{1,0:T(8,128)} custom-call(f32[256,256]{1,0:T(8,128)S(1)} %flow_inner.1.inner_ref, f32[256,256]{1,0:T(8,128)S(1)} %get-tuple-element.54.level_ref, f32[4,256,128]{2,1,0:T(8,128)S(1)} %get-tuple-element.55.side_ref, f32[256,256]{1,0:T(8,128)S(1)} %copy-done, s32[256,256]{1,0:T(8,128)S(1)} %copy-done.2, f32[256,256]{1,0:T(8,128)S(1)} %copy-done.1, ...), custom_call_target="tpu_custom_call" | custom-call | tf_op jit(solution)/shard_map/flow_ends/pallas_call | solution.py:703
Async XLA Ops:
  2.2 12.3 %collective-permute-start = (bf16[32,512]{1,0:T(8,128)(2,1)S(1)}, bf16[32,512]{1,0:T(8,128)(2,1)S(1)}, u32[]{:S(2)}, u32[]{:S(2)}) collective-permute-start(bf16[32,512]{1,0:T(8,128)(2,1)S(1)} %get-tuple-element.30), channel_id=1, source_target_pairs={{0,1},{1,0},{2,3},{3,2},{4,5},{5,4},{6,7},{7,6},{8,9},{9,8},{10,11... | collective-permute-start | bytes 98312 | tf_op jit(solution)/shard_map/ppermute | solution.py:586
  2.7 11.8 %collective-permute-start.1 = (bf16[32,512]{1,0:T(8,128)(2,1)S(1)}, bf16[32,512]{1,0:T(8,128)(2,1)S(1)}, u32[]{:S(2)}, u32[]{:S(2)}) collective-permute-start(bf16[32,512]{1,0:T(8,128)(2,1)S(1)} %get-tuple-element.31), channel_id=1, source_target_pairs={{0,31},{1,2},{2,1},{3,4},{4,3},{5,6},{6,5},{7,8},{8,7},{9,10},{10,... | collective-permute-start | bytes 98312 | tf_op jit(solution)/shard_map/ppermute | solution.py:586
  14.5 16.7 %copy-start.2 = (s32[256,256]{1,0:T(8,128)S(1)}, s32[256,256]{1,0:T(8,128)}, u32[]{:S(2)}) copy-start(s32[256,256]{1,0:T(8,128)} %dir_ref.5) | copy-start | bytes 786436
  14.6 16.7 %copy-start.3 = (f32[256,256]{1,0:T(8,128)S(1)}, f32[256,256]{1,0:T(8,128)}, u32[]{:S(2)}) copy-start(f32[256,256]{1,0:T(8,128)} %depth_ref.1) | copy-start | bytes 786436
  17.4 13.8 %copy-start = (f32[256,256]{1,0:T(8,128)S(1)}, f32[256,256]{1,0:T(8,128)}, u32[]{:S(2)}) copy-start(f32[256,256]{1,0:T(8,128)} %slope_ref.5) | copy-start | bytes 786436
  17.4 13.8 %copy-start.1 = (f32[256,256]{1,0:T(8,128)S(1)}, f32[256,256]{1,0:T(8,128)}, u32[]{:S(2)}) copy-start(f32[256,256]{1,0:T(8,128)} %rain_ref.5) | copy-start | bytes 786436
  32.2 5.3 %collective-permute-start.2 = (bf16[32,384]{1,0:T(8,128)(2,1)S(1)}, bf16[32,384]{1,0:T(8,128)(2,1)S(1)}, u32[]{:S(2)}, u32[]{:S(2)}) collective-permute-start(bf16[32,384]{1,0:T(8,128)(2,1)S(1)} %get-tuple-element.56), channel_id=1, source_target_pairs={{0,4},{1,5},{2,6},{3,7},{4,0},{5,1},{6,2},{7,3},{8,12},{9,13},{10,... | collective-permute-start | bytes 73736 | tf_op jit(solution)/shard_map/ppermute | solution.py:586
  33.1 4.4 %collective-permute-start.3 = (bf16[32,384]{1,0:T(8,128)(2,1)S(1)}, bf16[32,384]{1,0:T(8,128)(2,1)S(1)}, u32[]{:S(2)}, u32[]{:S(2)}) collective-permute-start(bf16[32,384]{1,0:T(8,128)(2,1)S(1)} %get-tuple-element.57), channel_id=1, source_target_pairs={{0,1},{1,0},{2,3},{3,2},{4,8},{5,9},{6,10},{7,11},{8,4},{9,5},{10,... | collective-permute-start | bytes 73736 | tf_op jit(solution)/shard_map/ppermute | solution.py:586

commit v13 on v12

--- a/solution.py
+++ b/solution.py
@@ -209,7 +209,7 @@
         wide = sum(dot(k_ref[ky * 3 * CH : (ky + 1) * 3 * CH, :], spread[ky]) for ky in range(3))
         for kx in range(3):
             for i in range(OUT_LINES):
-                w_ref[i * CH : (i + 1) * CH, kx * cols : (kx + 1) * cols] = wide[
+                w_ref[kx * rows + i * CH : kx * rows + (i + 1) * CH, :] = wide[
                     kx * CH : (kx + 1) * CH, i * cols : (i + 1) * cols
                 ].astype(bf16)
     wide4 = dot(t4_ref[...].astype(bf16), tile4)
@@ -261,19 +261,11 @@
     for ch in range(2):
         s_ref[ch, 0:lines, :] = sar_ref[ch].astype(f32)
         s_ref[ch, lines:, :] = jnp.zeros((s_ref.shape[1] - lines, px), f32)
-    total = xa_ref.shape[1] // CH
-    xa_ref[:, (total - 2) * CH :, :] = jnp.zeros((3, 2 * CH, px), bf16)
+    total = xa_ref.shape[0] // CH
+    xa_ref[(total - 2) * CH :, :] = jnp.zeros((2 * CH, px), bf16)
 
     def put(ref, line, acc):
-        feat = jnp.maximum(acc, 0.0).astype(bf16)
-        at = slice(line * CH, line * CH + rows)
-        if len(ref.shape) == 2:
-            ref[at, :] = feat
-            return
-        before, after = pixel_shifts(feat)
-        ref[0, at, :] = before
-        ref[1, at, :] = feat
-        ref[2, at, :] = after
+        ref[line * CH : line * CH + rows, :] = jnp.maximum(acc, 0.0).astype(bf16)
 
     full = (lines + 4) // OUT_LINES + 1
     for b in range(full):
@@ -283,15 +275,15 @@
     for w_ref, src, dst, line, blocks in ((w2_ref, xa_ref, xb_ref, 2, full), (w3_ref, xb_ref, x3_ref, 3, full - 1)):
         for b in range(blocks):
             at = line + b * OUT_LINES
-            x = src[:, (at - 1) * CH : (at - 1) * CH + cols, :].reshape(3 * cols, px)
-            put(dst, at, dot(w_ref[...], x))
+            sums = dot(w_ref[...], src[(at - 1) * CH : (at - 1) * CH + cols, :])
+            put(dst, at, merged(sums, rows))
 
     def ends_of(lo, center):
         hi = lines - lo - 2
         return jnp.concatenate([center[at * CH : (at + 2) * CH, :] for at in (lo, hi)], 0)
 
-    e1_ref[...] = ends_of(3, xa_ref.at[1])
-    e2_ref[...] = ends_of(4, xb_ref.at[1])
+    e1_ref[...] = ends_of(3, xa_ref)
+    e2_ref[...] = ends_of(4, xb_ref)
     e3_ref[...] = ends_of(5, x3_ref)
     logit_ref[0:END_LINES, :] = jnp.zeros((END_LINES, px), f32)
     starts = [3 + b * OUT_LINES for b in range(full - 2)] + [lines - 5 - IN_LINES]
@@ -347,14 +339,13 @@
     low = jnp.where(me == 0, n, 0)
     high = jnp.where(me == devices - 1, OUT_LINES - n, 2 * OUT_LINES)
     for layer, (w_ref, e_ref) in enumerate(((w1_ref, e1_ref), (w2_ref, e2_ref), (w3_ref, e3_ref)), 1):
-        acc = jnp.maximum(dot(w_ref[...], x), 0.0)
+        acc = dot(w_ref[...], x)
+        acc = jnp.maximum(acc if layer == 1 else merged(acc, rows), 0.0)
         inside = (out_line >= low - layer) & (out_line < high + layer)
         feat = jnp.where(inside, acc, 0.0).astype(bf16)
         block = jnp.concatenate([feat[0 : 6 * CH], e_ref[...], feat[8 * CH :]], 0)
-        if layer < 3:
-            before, after = pixel_shifts(block)
-            x = jnp.concatenate([before, block, after], 0)
-    frac = sigmoid(merged(dot(w4_ref[...], block), CH)).astype(f32)
+        x = block
+    frac = sigmoid(merged(dot(w4_ref[...], x), CH)).astype(f32)
     f_ref[...] = frac_in[...].astype(f32)
     f_ref[0:6, :] = frac[0:6]
     f_ref[lines - 6 :, :] = frac[8:14]
@@ -628,8 +619,8 @@
         functools.partial(inner_kernel, devices, capacity),
         out_shape=(
             jax.ShapeDtypeStruct((rows, LANES), bf16),
-            jax.ShapeDtypeStruct((rows, 3 * cols), bf16),
-            jax.ShapeDtypeStruct((rows, 3 * cols), bf16),
+            jax.ShapeDtypeStruct((3 * rows, cols), bf16),
+            jax.ShapeDtypeStruct((3 * rows, cols), bf16),
             jax.ShapeDtypeStruct((3 * CH, cols), bf16),
             jax.ShapeDtypeStruct((slots, 2 * END_LINES * CH), bf16),
             jax.ShapeDtypeStruct((8 * devices, LANES), f32),
@@ -643,8 +634,8 @@
             pltpu.VMEM((24, CH), f32),
             pltpu.VMEM((16, CH), f32),
             pltpu.VMEM((2, *blocks_in), f32),
-            pltpu.VMEM((3, feats, range_px), bf16),
-            pltpu.VMEM((3, feats, range_px), bf16),
+            pltpu.VMEM((feats, range_px), bf16),
+            pltpu.VMEM((feats, range_px), bf16),
             pltpu.VMEM((feats, range_px), bf16),
             pltpu.VMEM(blocks_in, f32),
             pltpu.VMEM(((az_lines - 2 * END_LINES) * CH, tile_cols // 4), f32),

time: 39.8 us -> 40.6 us (1.020)
  Pallas kernels: 16.9 us -> 17.8 us
    pallas_call x1, Pallas kernels: 5.23 us -> 6.05 us  [per_device(): pl.pallas_call(functools.partial(inner_kernel, devices, capacity), out_sh...]
  transfers between devices with their start and end apart: 4 -> 4, of which waited for: 0 -> 0; matrix products, arithmetic and copies ran while one was open for 0% -> 0% of each run, Pallas kernels for 24% -> 26%
where the time goes in v13:
time: 40.6 us; the launch traced here: 40.4 us
  Pallas kernels  17.8 us (44%)
  blocking collectives  13.8 us (34%)
  starting transfers between devices  8.02 us (20%)
  between operations  0.72 us (2%)
    all_to_all x1, blocking collectives, per_device(): lax.all_to_all(send.reshape(devices, send_rows, LANES), both, split_axis=...  13.8 us
    ppermute x4, starting transfers between devices, swaps(): out.append(lax.ppermute(x, both, sorted(to.items())))  8.02 us
    pallas_call x1, Pallas kernels, per_device(): pl.pallas_call(functools.partial(inner_kernel, devices, capacity), out_sh...  6.05 us
    pallas_call x1, Pallas kernels, per_device(): pl.pallas_call(flow_inner_kernel, out_shape=jax.ShapeDtypeStruct((tile_ro...  4.38 us
    pallas_call x1, Pallas kernels, per_device(): pl.pallas_call(functools.partial(ends_kernel, devices, capacity), out_sha...  2.89 us
    pallas_call x1, Pallas kernels, per_device(): pl.pallas_call(flow_ends_kernel, out_shape=jax.ShapeDtypeStruct((tile_row...  2.04 us
    pallas_call x1, Pallas kernels, per_device(): pl.pallas_call(edge_kernel, out_shape=(message, message, *[pltpu.VMEM(x.s...  1.55 us
    pallas_call x1, Pallas kernels, per_device(): pl.pallas_call(functools.partial(level_kernel, devices), out_shape=(jax.S...  0.92 us
  transfers between devices with their start and end apart: 4, of which 0 were waited for; matrix products, arithmetic and copies ran while one was open for 0% of the time, Pallas kernels for 26%

profile of v13, /device:TPU:0, one launch (start us, length us, event | category | flops | bytes accessed | tf_op | source)
XLA Modules:
  0.0 40.4 jit_solution(45841406735276762)
XLA Ops:
  0.6 1.5 %edges.1 = (bf16[32,512]{1,0:T(8,128)(2,1)S(1)}, bf16[32,512]{1,0:T(8,128)(2,1)S(1)}, bf16[2,64,512]{2,1,0:T(8,128)(2,1)S(1)}, bf16[3,3,2,16]{3,2,1,0:T(2,128)(2...) custom-call(f32[256,256]{1,0:T(8,128)} %depth_ref.1, ...), custom_call_target="tpu_custom_call" | custom-call | tf_op jit(solution)/shard_map/edges/pallas_call | solution.py:593
  2.2 0.5 %collective-permute-start = (bf16[32,512]{1,0:T(8,128)(2,1)S(1)}, bf16[32,512]{1,0:T(8,128)(2,1)S(1)}, u32[]{:S(2)}, u32[]{:S(2)}) collective-permute-start(bf16[32,512]{1,0:T(8,128)(2,1)S(1)} %get-tuple-element.30), channel_id=1, source_target_pairs={{0,1},{1,0},{2,3},{3,2},{4,5},{5,4},{6,7},{7,6},{8,9},{9,8},{10,11... | collective-permute-start | bytes 98312 | tf_op jit(solution)/shard_map/ppermute | solution.py:577
  2.7 6.6 %collective-permute-start.1 = (bf16[32,512]{1,0:T(8,128)(2,1)S(1)}, bf16[32,512]{1,0:T(8,128)(2,1)S(1)}, u32[]{:S(2)}, u32[]{:S(2)}) collective-permute-start(bf16[32,512]{1,0:T(8,128)(2,1)S(1)} %get-tuple-element.31), channel_id=1, source_target_pairs={{0,31},{1,2},{2,1},{3,4},{4,3},{5,6},{6,5},{7,8},{8,7},{9,10},{10,... | collective-permute-start | bytes 98312 | tf_op jit(solution)/shard_map/ppermute | solution.py:577
  9.3 6.0 %inner.1 = (bf16[224,128]{1,0:T(8,128)(2,1)S(1)}, bf16[672,256]{1,0:T(8,128)(2,1)S(1)}, bf16[672,256]{1,0:T(8,128)(2,1)S(1)}, bf16[48,256]{1,0:T(8,128)(2,1)S(1)...) custom-call(bf16[3,3,2,16]{3,2,1,0:T(2,128)(2,1)S(1)} %get-tuple-ele, ...), custom_call_target="tpu_custom_call" | custom-call | flops 8000000000 | bytes 4000000 | tf_op jit(solution)/shard_map/inner/pallas_call | solution.py:618
  15.3 0.0 collective-permute-done.first_swap_ref
  15.4 0.0 collective-permute-done.1.second_swap_ref
  15.4 0.0 copy-start.2
  15.4 0.0 copy-start.3
  15.4 2.9 %ends.1 = (bf16[64,512]{1,0:T(8,128)(2,1)}, bf16[1280,128]{1,0:T(8,128)(2,1)S(1)}) custom-call(bf16[32,512]{1,0:T(8,128)(2,1)S(1)} %collective-permute-done.first_swap_ref, bf16[32,512]{1,0:T(8,128)(2,1)S(1)} %collective-permute-done.1.second_swap_ref, bf16[224,128]{1,0:T(8,128)(2,1)S(1)} %get-tuple-element.41.w1_ref, ...), custom_call_target="tpu_custom_call" | custom-call | tf_op jit(solution)/shard_map/ends/pallas_call | solution.py:649
  18.3 0.0 copy-start
  18.3 0.0 copy-start.1
  18.3 13.8 %all_to_all.5 = bf16[32,40,128]{2,1,0:T(8,128)(2,1)S(1)} all-to-all(bf16[32,40,128]{2,1,0:T(8,128)(2,1)S(1)} %bitcast.15), channel_id=1, replica_groups=mesh['tx'=8,'ty'=4] {'tx','ty'}, dimensions={0} | all-to-all | bytes 655360 | tf_op jit(solution)/shard_map/all_to_all | solution.py:662
  32.1 0.0 copy-done.2
  32.1 0.0 copy-done.3
  32.1 0.0 copy-done
  32.1 0.0 copy-done.1
  32.1 0.9 %level.1 = (f32[256,256]{1,0:T(8,128)S(1)}, f32[4,256,128]{2,1,0:T(8,128)S(1)}, bf16[32,384]{1,0:T(8,128)(2,1)S(1)}, bf16[32,384]{1,0:T(8,128)(2,1)S(1)}) custom-call(bf16[1280,128]{1,0:T(8,128)(2,1)S(1)} %bitcast.14, bf16[32,512]{1,0:T(8,128)(2,1)S(1)} %collective-permute-done.first_swap_ref, bf16[32,512]{1,0:T(8,128)(2,1)S(1)} %collective-permute-done.1.second_swap_ref, ...), custom_call_target="tpu_custom_call" | custom-call | tf_op jit(solution)/shard_map/level/pallas_call | solution.py:668
  33.1 0.9 %collective-permute-start.2 = (bf16[32,384]{1,0:T(8,128)(2,1)S(1)}, bf16[32,384]{1,0:T(8,128)(2,1)S(1)}, u32[]{:S(2)}, u32[]{:S(2)}) collective-permute-start(bf16[32,384]{1,0:T(8,128)(2,1)S(1)} %get-tuple-element.56), channel_id=1, source_target_pairs={{0,4},{1,5},{2,6},{3,7},{4,0},{5,1},{6,2},{7,3},{8,12},{9,13},{10,... | collective-permute-start | bytes 73736 | tf_op jit(solution)/shard_map/ppermute | solution.py:577
  34.0 0.0 collective-permute-start.3
  34.0 4.4 %flow_inner.1.inner_ref = f32[256,256]{1,0:T(8,128)S(1)} custom-call(f32[256,256]{1,0:T(8,128)S(1)} %get-tuple-element.54.level_ref, f32[4,256,128]{2,1,0:T(8,128)S(1)} %get-tuple-element.55.side_ref, f32[256,256]{1,0:T(8,128)S(1)} %copy-done, s32[256,256]{1,0:T(8,128)S(1)} %copy-done.2, f32[256,256]{1,0:T(8,128)S(1)} %copy-done.1), custom_call_target="tpu_custom_call" | custom-call | flops 5000000000 | bytes 4000000 | tf_op jit(solution)/shard_map/flow_inner/pallas_call | solution.py:684
  38.4 0.0 collective-permute-done.2.first_swap_ref
  38.4 0.0 collective-permute-done.3.second_swap_ref
  38.4 2.0 %flow_ends.1 = f32[256,256]{1,0:T(8,128)} custom-call(f32[256,256]{1,0:T(8,128)S(1)} %flow_inner.1.inner_ref, f32[256,256]{1,0:T(8,128)S(1)} %get-tuple-element.54.level_ref, f32[4,256,128]{2,1,0:T(8,128)S(1)} %get-tuple-element.55.side_ref, f32[256,256]{1,0:T(8,128)S(1)} %copy-done, s32[256,256]{1,0:T(8,128)S(1)} %copy-done.2, f32[256,256]{1,0:T(8,128)S(1)} %copy-done.1, ...), custom_call_target="tpu_custom_call" | custom-call | tf_op jit(solution)/shard_map/flow_ends/pallas_call | solution.py:694
Async XLA Ops:
  2.2 13.2 %collective-permute-start = (bf16[32,512]{1,0:T(8,128)(2,1)S(1)}, bf16[32,512]{1,0:T(8,128)(2,1)S(1)}, u32[]{:S(2)}, u32[]{:S(2)}) collective-permute-start(bf16[32,512]{1,0:T(8,128)(2,1)S(1)} %get-tuple-element.30), channel_id=1, source_target_pairs={{0,1},{1,0},{2,3},{3,2},{4,5},{5,4},{6,7},{7,6},{8,9},{9,8},{10,11... | collective-permute-start | bytes 98312 | tf_op jit(solution)/shard_map/ppermute | solution.py:577
  2.7 12.7 %collective-permute-start.1 = (bf16[32,512]{1,0:T(8,128)(2,1)S(1)}, bf16[32,512]{1,0:T(8,128)(2,1)S(1)}, u32[]{:S(2)}, u32[]{:S(2)}) collective-permute-start(bf16[32,512]{1,0:T(8,128)(2,1)S(1)} %get-tuple-element.31), channel_id=1, source_target_pairs={{0,31},{1,2},{2,1},{3,4},{4,3},{5,6},{6,5},{7,8},{8,7},{9,10},{10,... | collective-permute-start | bytes 98312 | tf_op jit(solution)/shard_map/ppermute | solution.py:577
  15.4 16.7 %copy-start.2 = (s32[256,256]{1,0:T(8,128)S(1)}, s32[256,256]{1,0:T(8,128)}, u32[]{:S(2)}) copy-start(s32[256,256]{1,0:T(8,128)} %dir_ref.5) | copy-start | bytes 786436
  15.4 16.7 %copy-start.3 = (f32[256,256]{1,0:T(8,128)S(1)}, f32[256,256]{1,0:T(8,128)}, u32[]{:S(2)}) copy-start(f32[256,256]{1,0:T(8,128)} %depth_ref.1) | copy-start | bytes 786436
  18.3 13.8 %copy-start = (f32[256,256]{1,0:T(8,128)S(1)}, f32[256,256]{1,0:T(8,128)}, u32[]{:S(2)}) copy-start(f32[256,256]{1,0:T(8,128)} %slope_ref.5) | copy-start | bytes 786436
  18.3 13.8 %copy-start.1 = (f32[256,256]{1,0:T(8,128)S(1)}, f32[256,256]{1,0:T(8,128)}, u32[]{:S(2)}) copy-start(f32[256,256]{1,0:T(8,128)} %rain_ref.5) | copy-start | bytes 786436
  33.1 5.3 %collective-permute-start.2 = (bf16[32,384]{1,0:T(8,128)(2,1)S(1)}, bf16[32,384]{1,0:T(8,128)(2,1)S(1)}, u32[]{:S(2)}, u32[]{:S(2)}) collective-permute-start(bf16[32,384]{1,0:T(8,128)(2,1)S(1)} %get-tuple-element.56), channel_id=1, source_target_pairs={{0,4},{1,5},{2,6},{3,7},{4,0},{5,1},{6,2},{7,3},{8,12},{9,13},{10,... | collective-permute-start | bytes 73736 | tf_op jit(solution)/shard_map/ppermute | solution.py:577
  34.0 4.4 %collective-permute-start.3 = (bf16[32,384]{1,0:T(8,128)(2,1)S(1)}, bf16[32,384]{1,0:T(8,128)(2,1)S(1)}, u32[]{:S(2)}, u32[]{:S(2)}) collective-permute-start(bf16[32,384]{1,0:T(8,128)(2,1)S(1)} %get-tuple-element.57), channel_id=1, source_target_pairs={{0,1},{1,0},{2,3},{3,2},{4,8},{5,9},{6,10},{7,11},{8,4},{9,5},{10,... | collective-permute-start | bytes 73736 | tf_op jit(solution)/shard_map/ppermute | solution.py:577

commit v14 on v12

--- a/solution.py
+++ b/solution.py
@@ -51,12 +51,15 @@
 
 
 def pixel_shifts(x):
-    width = x.shape[1]
-    pix = iota(x.shape, 1).astype(f32).astype(x.dtype)
-    end = (width - 1 - iota(x.shape, 1)).astype(f32).astype(x.dtype)
-    zero = jnp.zeros(x.shape, x.dtype)
-    before = jnp.where(pix == 0, zero, pltpu.roll(x, 1, 1))
-    after = jnp.where(end == 0, zero, pltpu.roll(x, width - 1, 1))
+    rows, width = x.shape
+    lane = iota((rows, LANES), 1)
+    zero = jnp.zeros((rows, LANES), x.dtype)
+    first = lane.astype(f32).astype(x.dtype) == 0
+    last = (LANES - 1 - lane).astype(f32).astype(x.dtype) == 0
+    before = pltpu.roll(x, 1, 1)
+    after = pltpu.roll(x, width - 1, 1)
+    before = jnp.concatenate([jnp.where(first, zero, before[:, 0:LANES]), before[:, LANES:]], 1)
+    after = jnp.concatenate([after[:, : width - LANES], jnp.where(last, zero, after[:, width - LANES :])], 1)
     return before, after
 
 
@@ -79,7 +82,6 @@
 def line_windows(cell, obs, cov, quarter):
     px = cell.shape[1]
     kind = iota((CH, px), 0)
-    is_obs = kind < CH // 2
     kind_part = rem(kind, CH // 2).astype(f32).astype(bf16)
     sub = kind.astype(f32).astype(bf16)
     one = jnp.ones((CH, px), bf16)
@@ -92,7 +94,8 @@
 
     out = []
     for i in range(cell.shape[0]):
-        value = jnp.where(is_obs, obs[i : i + 1], cov[i : i + 1]).astype(bf16)
+        pair = [jnp.broadcast_to(x[i : i + 1], (CH // 2, px)) for x in (obs, cov)]
+        value = jnp.concatenate(pair, 0).astype(bf16)
         left = jnp.where(kind_part == spread_row(part, i), value, nil)
         where_col = spread_row(col, i)
         hot = jnp.concatenate([jnp.where(sub + g * CH == where_col, one, nil) for g in range(quarter // CH)], 0)
@@ -265,7 +268,7 @@
     xa_ref[:, (total - 2) * CH :, :] = jnp.zeros((3, 2 * CH, px), bf16)
 
     def put(ref, line, acc):
-        feat = jnp.maximum(acc, 0.0).astype(bf16)
+        feat = jnp.maximum(acc.astype(bf16), jnp.zeros(acc.shape, bf16))
         at = slice(line * CH, line * CH + rows)
         if len(ref.shape) == 2:
             ref[at, :] = feat
@@ -343,13 +346,14 @@
         own = sar_ref[ch].astype(f32)
         pieces += [above[ch * n : (ch + 1) * n], own[0:n], own[lines - n :], below[ch * n : (ch + 1) * n]]
     x = image_columns(jnp.concatenate(pieces, 0))
-    out_line = quo(iota((rows, px), 0), CH)
+    out_line = quo(iota((rows, px), 0), CH).astype(f32).astype(bf16)
     low = jnp.where(me == 0, n, 0)
     high = jnp.where(me == devices - 1, OUT_LINES - n, 2 * OUT_LINES)
     for layer, (w_ref, e_ref) in enumerate(((w1_ref, e1_ref), (w2_ref, e2_ref), (w3_ref, e3_ref)), 1):
-        acc = jnp.maximum(dot(w_ref[...], x), 0.0)
-        inside = (out_line >= low - layer) & (out_line < high + layer)
-        feat = jnp.where(inside, acc, 0.0).astype(bf16)
+        acc = dot(w_ref[...], x).astype(bf16)
+        inside = (out_line >= (low - layer).astype(f32).astype(bf16)) & (out_line < (high + layer).astype(f32).astype(bf16))
+        nil = jnp.zeros(acc.shape, bf16)
+        feat = jnp.where(inside, jnp.maximum(acc, nil), nil)
         block = jnp.concatenate([feat[0 : 6 * CH], e_ref[...], feat[8 * CH :]], 0)
         if layer < 3:
             before, after = pixel_shifts(block)

time: 39.8 us -> 39.8 us (level)
  no operation moved by 1% of the time
where the time goes in v14:
time: 39.8 us; the launch traced here: 39.6 us
  Pallas kernels  17 us (43%)
  blocking collectives  13.8 us (35%)
  starting transfers between devices  8.02 us (20%)
  between operations  0.72 us (2%)
    all_to_all x1, blocking collectives, per_device(): lax.all_to_all(send.reshape(devices, send_rows, LANES), both, split_axis=...  13.8 us
    ppermute x4, starting transfers between devices, swaps(): out.append(lax.ppermute(x, both, sorted(to.items())))  8.02 us
    pallas_call x1, Pallas kernels, per_device(): pl.pallas_call(functools.partial(inner_kernel, devices, capacity), out_sh...  5.29 us
    pallas_call x1, Pallas kernels, per_device(): pl.pallas_call(flow_inner_kernel, out_shape=jax.ShapeDtypeStruct((tile_ro...  4.38 us
    pallas_call x1, Pallas kernels, per_device(): pl.pallas_call(functools.partial(ends_kernel, devices, capacity), out_sha...  2.81 us
    pallas_call x1, Pallas kernels, per_device(): pl.pallas_call(flow_ends_kernel, out_shape=jax.ShapeDtypeStruct((tile_row...  2.04 us
    pallas_call x1, Pallas kernels, per_device(): pl.pallas_call(edge_kernel, out_shape=(message, message, *[pltpu.VMEM(x.s...  1.55 us
    pallas_call x1, Pallas kernels, per_device(): pl.pallas_call(functools.partial(level_kernel, devices), out_shape=(jax.S...  0.92 us
  transfers between devices with their start and end apart: 4, of which 0 were waited for; matrix products, arithmetic and copies ran while one was open for 0% of the time, Pallas kernels for 24%

profile of v14, /device:TPU:0, one launch (start us, length us, event | category | flops | bytes accessed | tf_op | source)
XLA Modules:
  0.0 39.6 jit_solution(8312664030951748199)
XLA Ops:
  0.6 1.5 %edges.1 = (bf16[32,512]{1,0:T(8,128)(2,1)S(1)}, bf16[32,512]{1,0:T(8,128)(2,1)S(1)}, bf16[2,64,512]{2,1,0:T(8,128)(2,1)S(1)}, bf16[3,3,2,16]{3,2,1,0:T(2,128)(2...) custom-call(f32[256,256]{1,0:T(8,128)} %depth_ref.1, ...), custom_call_target="tpu_custom_call" | custom-call | tf_op jit(solution)/shard_map/edges/pallas_call | solution.py:606
  2.2 0.5 %collective-permute-start = (bf16[32,512]{1,0:T(8,128)(2,1)S(1)}, bf16[32,512]{1,0:T(8,128)(2,1)S(1)}, u32[]{:S(2)}, u32[]{:S(2)}) collective-permute-start(bf16[32,512]{1,0:T(8,128)(2,1)S(1)} %get-tuple-element.30), channel_id=1, source_target_pairs={{0,1},{1,0},{2,3},{3,2},{4,5},{5,4},{6,7},{7,6},{8,9},{9,8},{10,11... | collective-permute-start | bytes 98312 | tf_op jit(solution)/shard_map/ppermute | solution.py:590
  2.7 6.6 %collective-permute-start.1 = (bf16[32,512]{1,0:T(8,128)(2,1)S(1)}, bf16[32,512]{1,0:T(8,128)(2,1)S(1)}, u32[]{:S(2)}, u32[]{:S(2)}) collective-permute-start(bf16[32,512]{1,0:T(8,128)(2,1)S(1)} %get-tuple-element.31), channel_id=1, source_target_pairs={{0,31},{1,2},{2,1},{3,4},{4,3},{5,6},{6,5},{7,8},{8,7},{9,10},{10,... | collective-permute-start | bytes 98312 | tf_op jit(solution)/shard_map/ppermute | solution.py:590
  9.3 5.3 %inner.1 = (bf16[224,128]{1,0:T(8,128)(2,1)S(1)}, bf16[224,768]{1,0:T(8,128)(2,1)S(1)}, bf16[224,768]{1,0:T(8,128)(2,1)S(1)}, bf16[48,256]{1,0:T(8,128)(2,1)S(1)...) custom-call(bf16[3,3,2,16]{3,2,1,0:T(2,128)(2,1)S(1)} %get-tuple-ele, ...), custom_call_target="tpu_custom_call" | custom-call | flops 8000000000 | bytes 4000000 | tf_op jit(solution)/shard_map/inner/pallas_call | solution.py:631
  14.6 0.0 collective-permute-done.first_swap_ref
  14.6 0.0 collective-permute-done.1.second_swap_ref
  14.6 0.0 copy-start.2
  14.6 0.0 copy-start.3
  14.6 2.8 %ends.1 = (bf16[64,512]{1,0:T(8,128)(2,1)}, bf16[1280,128]{1,0:T(8,128)(2,1)S(1)}) custom-call(bf16[32,512]{1,0:T(8,128)(2,1)S(1)} %collective-permute-done.first_swap_ref, bf16[32,512]{1,0:T(8,128)(2,1)S(1)} %collective-permute-done.1.second_swap_ref, bf16[224,128]{1,0:T(8,128)(2,1)S(1)} %get-tuple-element.41.w1_ref, ...), custom_call_target="tpu_custom_call" | custom-call | tf_op jit(solution)/shard_map/ends/pallas_call | solution.py:662
  17.4 0.0 copy-start
  17.5 0.0 copy-start.1
  17.5 13.8 %all_to_all.5 = bf16[32,40,128]{2,1,0:T(8,128)(2,1)S(1)} all-to-all(bf16[32,40,128]{2,1,0:T(8,128)(2,1)S(1)} %bitcast.15), channel_id=1, replica_groups=mesh['tx'=8,'ty'=4] {'tx','ty'}, dimensions={0} | all-to-all | bytes 655360 | tf_op jit(solution)/shard_map/all_to_all | solution.py:675
  31.3 0.0 copy-done.2
  31.3 0.0 copy-done.3
  31.3 0.0 copy-done
  31.3 0.0 copy-done.1
  31.3 0.9 %level.1 = (f32[256,256]{1,0:T(8,128)S(1)}, f32[4,256,128]{2,1,0:T(8,128)S(1)}, bf16[32,384]{1,0:T(8,128)(2,1)S(1)}, bf16[32,384]{1,0:T(8,128)(2,1)S(1)}) custom-call(bf16[1280,128]{1,0:T(8,128)(2,1)S(1)} %bitcast.14, bf16[32,512]{1,0:T(8,128)(2,1)S(1)} %collective-permute-done.first_swap_ref, bf16[32,512]{1,0:T(8,128)(2,1)S(1)} %collective-permute-done.1.second_swap_ref, ...), custom_call_target="tpu_custom_call" | custom-call | tf_op jit(solution)/shard_map/level/pallas_call | solution.py:681
  32.2 0.9 %collective-permute-start.2 = (bf16[32,384]{1,0:T(8,128)(2,1)S(1)}, bf16[32,384]{1,0:T(8,128)(2,1)S(1)}, u32[]{:S(2)}, u32[]{:S(2)}) collective-permute-start(bf16[32,384]{1,0:T(8,128)(2,1)S(1)} %get-tuple-element.56), channel_id=1, source_target_pairs={{0,4},{1,5},{2,6},{3,7},{4,0},{5,1},{6,2},{7,3},{8,12},{9,13},{10,... | collective-permute-start | bytes 73736 | tf_op jit(solution)/shard_map/ppermute | solution.py:590
  33.1 0.0 collective-permute-start.3
  33.1 4.4 %flow_inner.1.inner_ref = f32[256,256]{1,0:T(8,128)S(1)} custom-call(f32[256,256]{1,0:T(8,128)S(1)} %get-tuple-element.54.level_ref, f32[4,256,128]{2,1,0:T(8,128)S(1)} %get-tuple-element.55.side_ref, f32[256,256]{1,0:T(8,128)S(1)} %copy-done, s32[256,256]{1,0:T(8,128)S(1)} %copy-done.2, f32[256,256]{1,0:T(8,128)S(1)} %copy-done.1), custom_call_target="tpu_custom_call" | custom-call | flops 5000000000 | bytes 4000000 | tf_op jit(solution)/shard_map/flow_inner/pallas_call | solution.py:697
  37.5 0.0 collective-permute-done.2.first_swap_ref
  37.5 0.0 collective-permute-done.3.second_swap_ref
  37.5 2.0 %flow_ends.1 = f32[256,256]{1,0:T(8,128)} custom-call(f32[256,256]{1,0:T(8,128)S(1)} %flow_inner.1.inner_ref, f32[256,256]{1,0:T(8,128)S(1)} %get-tuple-element.54.level_ref, f32[4,256,128]{2,1,0:T(8,128)S(1)} %get-tuple-element.55.side_ref, f32[256,256]{1,0:T(8,128)S(1)} %copy-done, s32[256,256]{1,0:T(8,128)S(1)} %copy-done.2, f32[256,256]{1,0:T(8,128)S(1)} %copy-done.1, ...), custom_call_target="tpu_custom_call" | custom-call | tf_op jit(solution)/shard_map/flow_ends/pallas_call | solution.py:707
Async XLA Ops:
  2.2 12.4 %collective-permute-start = (bf16[32,512]{1,0:T(8,128)(2,1)S(1)}, bf16[32,512]{1,0:T(8,128)(2,1)S(1)}, u32[]{:S(2)}, u32[]{:S(2)}) collective-permute-start(bf16[32,512]{1,0:T(8,128)(2,1)S(1)} %get-tuple-element.30), channel_id=1, source_target_pairs={{0,1},{1,0},{2,3},{3,2},{4,5},{5,4},{6,7},{7,6},{8,9},{9,8},{10,11... | collective-permute-start | bytes 98312 | tf_op jit(solution)/shard_map/ppermute | solution.py:590
  2.7 11.9 %collective-permute-start.1 = (bf16[32,512]{1,0:T(8,128)(2,1)S(1)}, bf16[32,512]{1,0:T(8,128)(2,1)S(1)}, u32[]{:S(2)}, u32[]{:S(2)}) collective-permute-start(bf16[32,512]{1,0:T(8,128)(2,1)S(1)} %get-tuple-element.31), channel_id=1, source_target_pairs={{0,31},{1,2},{2,1},{3,4},{4,3},{5,6},{6,5},{7,8},{8,7},{9,10},{10,... | collective-permute-start | bytes 98312 | tf_op jit(solution)/shard_map/ppermute | solution.py:590
  14.6 16.7 %copy-start.2 = (s32[256,256]{1,0:T(8,128)S(1)}, s32[256,256]{1,0:T(8,128)}, u32[]{:S(2)}) copy-start(s32[256,256]{1,0:T(8,128)} %dir_ref.5) | copy-start | bytes 786436
  14.6 16.7 %copy-start.3 = (f32[256,256]{1,0:T(8,128)S(1)}, f32[256,256]{1,0:T(8,128)}, u32[]{:S(2)}) copy-start(f32[256,256]{1,0:T(8,128)} %depth_ref.1) | copy-start | bytes 786436
  17.4 13.8 %copy-start = (f32[256,256]{1,0:T(8,128)S(1)}, f32[256,256]{1,0:T(8,128)}, u32[]{:S(2)}) copy-start(f32[256,256]{1,0:T(8,128)} %slope_ref.5) | copy-start | bytes 786436
  17.5 13.8 %copy-start.1 = (f32[256,256]{1,0:T(8,128)S(1)}, f32[256,256]{1,0:T(8,128)}, u32[]{:S(2)}) copy-start(f32[256,256]{1,0:T(8,128)} %rain_ref.5) | copy-start | bytes 786436
  32.2 5.3 %collective-permute-start.2 = (bf16[32,384]{1,0:T(8,128)(2,1)S(1)}, bf16[32,384]{1,0:T(8,128)(2,1)S(1)}, u32[]{:S(2)}, u32[]{:S(2)}) collective-permute-start(bf16[32,384]{1,0:T(8,128)(2,1)S(1)} %get-tuple-element.56), channel_id=1, source_target_pairs={{0,4},{1,5},{2,6},{3,7},{4,0},{5,1},{6,2},{7,3},{8,12},{9,13},{10,... | collective-permute-start | bytes 73736 | tf_op jit(solution)/shard_map/ppermute | solution.py:590
  33.1 4.4 %collective-permute-start.3 = (bf16[32,384]{1,0:T(8,128)(2,1)S(1)}, bf16[32,384]{1,0:T(8,128)(2,1)S(1)}, u32[]{:S(2)}, u32[]{:S(2)}) collective-permute-start(bf16[32,384]{1,0:T(8,128)(2,1)S(1)} %get-tuple-element.57), channel_id=1, source_target_pairs={{0,1},{1,0},{2,3},{3,2},{4,8},{5,9},{6,10},{7,11},{8,4},{9,5},{10,... | collective-permute-start | bytes 73736 | tf_op jit(solution)/shard_map/ppermute | solution.py:590

commit v15 on v14

--- a/solution.py
+++ b/solution.py
@@ -12,6 +12,8 @@
 CH = 16
 OUT_LINES = 14
 IN_LINES = OUT_LINES + 2
+MID_LINES = 3
+MID_IN = MID_LINES + 2
 HALO_LINES = 4
 END_LINES = 8
 LANES = 128
@@ -73,6 +75,10 @@
     before, after = pixel_shifts(x)
     pad = jnp.zeros((LANES - 3 * x.shape[0], x.shape[1]), f32)
     return jnp.concatenate([before, x, after, pad], 0).astype(bf16)
+
+
+def mid_columns(before, x, after):
+    return jnp.concatenate([before, x, after, x[0:CH]], 0)
 
 
 def sigmoid(x):
@@ -191,9 +197,9 @@
     rows = OUT_LINES * CH
     cols = IN_LINES * CH
 
-    out_of = quo(iota((CH, OUT_LINES * cols), 1), cols)
-    in_of = rem(iota((CH, OUT_LINES * cols), 1), cols) - iota((CH, OUT_LINES * cols), 0)
-    spread = [(in_of == CH * (out_of + ky)).astype(bf16) for ky in range(3)]
+    n2 = MID_LINES * cols
+    spot2 = rem(iota((CH, n2), 1), cols) - iota((CH, n2), 0)
+    line2 = quo(iota((CH, n2), 1), cols)
     n1 = OUT_LINES * LANES
     group1 = quo(rem(iota((8, n1), 1), LANES), IN_LINES) == iota((8, n1), 0)
     line1 = rem(iota((8, n1), 1), IN_LINES) - quo(iota((8, n1), 1), LANES)
@@ -208,13 +214,13 @@
     wide1 = sum(dot_0(t1_ref[ky * 8 : ky * 8 + 8, :].astype(bf16), spread1[ky]) for ky in range(3))
     for i in range(OUT_LINES):
         w1_ref[i * CH : (i + 1) * CH, :] = wide1[:, i * LANES : (i + 1) * LANES].astype(bf16)
+    spread2 = [
+        (spot2 == (kx * MID_IN + ky + line2) * CH).astype(bf16) for ky in range(3) for kx in range(3)
+    ]
     for k_ref, w_ref in ((k2_ref, w2_ref), (k3_ref, w3_ref)):
-        wide = sum(dot(k_ref[ky * 3 * CH : (ky + 1) * 3 * CH, :], spread[ky]) for ky in range(3))
-        for kx in range(3):
-            for i in range(OUT_LINES):
-                w_ref[i * CH : (i + 1) * CH, kx * cols : (kx + 1) * cols] = wide[
-                    kx * CH : (kx + 1) * CH, i * cols : (i + 1) * cols
-                ].astype(bf16)
+        wide = sum(dot(k_ref[n * CH : (n + 1) * CH, :], spread2[n]) for n in range(9))
+        for i in range(MID_LINES):
+            w_ref[i * CH : (i + 1) * CH, :] = wide[:, i * cols : (i + 1) * cols].astype(bf16)
     wide4 = dot(t4_ref[...].astype(bf16), tile4)
     w4_ref[...] = jnp.concatenate(
         [
@@ -268,6 +274,7 @@
     xa_ref[:, (total - 2) * CH :, :] = jnp.zeros((3, 2 * CH, px), bf16)
 
     def put(ref, line, acc):
+        rows = acc.shape[0]
         feat = jnp.maximum(acc.astype(bf16), jnp.zeros(acc.shape, bf16))
         at = slice(line * CH, line * CH + rows)
         if len(ref.shape) == 2:
@@ -283,11 +290,11 @@
         at = b * OUT_LINES
         x = jnp.concatenate([s_ref[0, at : at + IN_LINES, :], s_ref[1, at : at + IN_LINES, :]], 0)
         put(xa_ref, 1 + at, dot(w1_ref[...], image_columns(x)))
-    for w_ref, src, dst, line, blocks in ((w2_ref, xa_ref, xb_ref, 2, full), (w3_ref, xb_ref, x3_ref, 3, full - 1)):
-        for b in range(blocks):
-            at = line + b * OUT_LINES
-            x = src[:, (at - 1) * CH : (at - 1) * CH + cols, :].reshape(3 * cols, px)
-            put(dst, at, dot(w_ref[...], x))
+    stop = lines - 4
+    for w_ref, src, dst, line, end_line in ((w2_ref, xa_ref, xb_ref, 2, stop), (w3_ref, xb_ref, x3_ref, 3, stop - 1)):
+        for at in range(line, end_line, MID_LINES):
+            x = src[:, (at - 1) * CH : (at - 1 + MID_IN) * CH, :]
+            put(dst, at, dot(w_ref[...], mid_columns(*[x[i] for i in range(3)])))
 
     def ends_of(lo, center):
         hi = lines - lo - 2
@@ -346,18 +353,30 @@
         own = sar_ref[ch].astype(f32)
         pieces += [above[ch * n : (ch + 1) * n], own[0:n], own[lines - n :], below[ch * n : (ch + 1) * n]]
     x = image_columns(jnp.concatenate(pieces, 0))
-    out_line = quo(iota((rows, px), 0), CH).astype(f32).astype(bf16)
+    half = 6 * CH
+    out_line = quo(iota((half, px), 0), CH).astype(f32).astype(bf16)
+    nil = jnp.zeros((half, px), bf16)
     low = jnp.where(me == 0, n, 0)
-    high = jnp.where(me == devices - 1, OUT_LINES - n, 2 * OUT_LINES)
+    high = jnp.where(me == devices - 1, OUT_LINES - 8 - n, OUT_LINES)
     for layer, (w_ref, e_ref) in enumerate(((w1_ref, e1_ref), (w2_ref, e2_ref), (w3_ref, e3_ref)), 1):
-        acc = dot(w_ref[...], x).astype(bf16)
-        inside = (out_line >= (low - layer).astype(f32).astype(bf16)) & (out_line < (high + layer).astype(f32).astype(bf16))
-        nil = jnp.zeros(acc.shape, bf16)
-        feat = jnp.where(inside, jnp.maximum(acc, nil), nil)
-        block = jnp.concatenate([feat[0 : 6 * CH], e_ref[...], feat[8 * CH :]], 0)
-        if layer < 3:
+        if layer == 1:
+            acc = dot(w_ref[...], x).astype(bf16)
+            top, bottom = acc[0:half], acc[8 * CH :]
+        else:
             before, after = pixel_shifts(block)
-            x = jnp.concatenate([before, block, after], 0)
+            top, bottom = [
+                jnp.concatenate(
+                    [
+                        dot(w_ref[...], mid_columns(*[y[at * CH : (at + MID_IN) * CH] for y in (before, block, after)]))
+                        for at in (first, first + MID_LINES)
+                    ],
+                    0,
+                ).astype(bf16)
+                for first in (0, 8)
+            ]
+        top = jnp.where(out_line >= (low - layer).astype(f32).astype(bf16), jnp.maximum(top, nil), nil)
+        bottom = jnp.where(out_line < (high + layer).astype(f32).astype(bf16), jnp.maximum(bottom, nil), nil)
+        block = jnp.concatenate([top, e_ref[...], bottom], 0)
     frac = sigmoid(merged(dot(w4_ref[...], block), CH)).astype(f32)
     f_ref[...] = frac_in[...].astype(f32)
     f_ref[0:6, :] = frac[0:6]
@@ -632,8 +651,8 @@
         functools.partial(inner_kernel, devices, capacity),
         out_shape=(
             jax.ShapeDtypeStruct((rows, LANES), bf16),
-            jax.ShapeDtypeStruct((rows, 3 * cols), bf16),
-            jax.ShapeDtypeStruct((rows, 3 * cols), bf16),
+            jax.ShapeDtypeStruct((MID_LINES * CH, cols), bf16),
+            jax.ShapeDtypeStruct((MID_LINES * CH, cols), bf16),
             jax.ShapeDtypeStruct((3 * CH, cols), bf16),
             jax.ShapeDtypeStruct((slots, 2 * END_LINES * CH), bf16),
             jax.ShapeDtypeStruct((8 * devices, LANES), f32),

time: 39.8 us -> 39.6 us (level)
  Pallas kernels: 17 us -> 16.5 us
where the time goes in v15:
time: 39.6 us; the launch traced here: 39.3 us
  Pallas kernels  16.5 us (42%)
  blocking collectives  14.1 us (36%)
  starting transfers between devices  8.02 us (20%)
  between operations  0.72 us (2%)
    all_to_all x1, blocking collectives, per_device(): lax.all_to_all(send.reshape(devices, send_rows, LANES), both, split_axis=...  14.1 us
    ppermute x4, starting transfers between devices, swaps(): out.append(lax.ppermute(x, both, sorted(to.items())))  8.02 us
    pallas_call x1, Pallas kernels, per_device(): pl.pallas_call(functools.partial(inner_kernel, devices, capacity), out_sh...  4.96 us
    pallas_call x1, Pallas kernels, per_device(): pl.pallas_call(flow_inner_kernel, out_shape=jax.ShapeDtypeStruct((tile_ro...  4.38 us
    pallas_call x1, Pallas kernels, per_device(): pl.pallas_call(functools.partial(ends_kernel, devices, capacity), out_sha...  2.65 us
    pallas_call x1, Pallas kernels, per_device(): pl.pallas_call(flow_ends_kernel, out_shape=jax.ShapeDtypeStruct((tile_row...  2.04 us
    pallas_call x1, Pallas kernels, per_device(): pl.pallas_call(edge_kernel, out_shape=(message, message, *[pltpu.VMEM(x.s...  1.55 us
    pallas_call x1, Pallas kernels, per_device(): pl.pallas_call(functools.partial(level_kernel, devices), out_shape=(jax.S...  0.92 us
  transfers between devices with their start and end apart: 4, of which 0 were waited for; matrix products, arithmetic and copies ran while one was open for 0% of the time, Pallas kernels for 24%

profile of v15, /device:TPU:0, one launch (start us, length us, event | category | flops | bytes accessed | tf_op | source)
XLA Modules:
  0.0 39.3 jit_solution(1908822187488502564)
XLA Ops:
  0.6 1.5 %edges.1 = (bf16[32,512]{1,0:T(8,128)(2,1)S(1)}, bf16[32,512]{1,0:T(8,128)(2,1)S(1)}, bf16[2,64,512]{2,1,0:T(8,128)(2,1)S(1)}, bf16[3,3,2,16]{3,2,1,0:T(2,128)(2...) custom-call(f32[256,256]{1,0:T(8,128)} %depth_ref.1, ...), custom_call_target="tpu_custom_call" | custom-call | tf_op jit(solution)/shard_map/edges/pallas_call | solution.py:625
  2.2 0.5 %collective-permute-start = (bf16[32,512]{1,0:T(8,128)(2,1)S(1)}, bf16[32,512]{1,0:T(8,128)(2,1)S(1)}, u32[]{:S(2)}, u32[]{:S(2)}) collective-permute-start(bf16[32,512]{1,0:T(8,128)(2,1)S(1)} %get-tuple-element.30), channel_id=1, source_target_pairs={{0,1},{1,0},{2,3},{3,2},{4,5},{5,4},{6,7},{7,6},{8,9},{9,8},{10,11... | collective-permute-start | bytes 98312 | tf_op jit(solution)/shard_map/ppermute | solution.py:609
  2.7 6.6 %collective-permute-start.1 = (bf16[32,512]{1,0:T(8,128)(2,1)S(1)}, bf16[32,512]{1,0:T(8,128)(2,1)S(1)}, u32[]{:S(2)}, u32[]{:S(2)}) collective-permute-start(bf16[32,512]{1,0:T(8,128)(2,1)S(1)} %get-tuple-element.31), channel_id=1, source_target_pairs={{0,31},{1,2},{2,1},{3,4},{4,3},{5,6},{6,5},{7,8},{8,7},{9,10},{10,... | collective-permute-start | bytes 98312 | tf_op jit(solution)/shard_map/ppermute | solution.py:609
  9.3 5.0 %inner.1 = (bf16[224,128]{1,0:T(8,128)(2,1)S(1)}, bf16[48,256]{1,0:T(8,128)(2,1)S(1)}, bf16[48,256]{1,0:T(8,128)(2,1)S(1)}, bf16[48,256]{1,0:T(8,128)(2,1)S(1)},...) custom-call(bf16[3,3,2,16]{3,2,1,0:T(2,128)(2,1)S(1)} %get-tuple-ele, ...), custom_call_target="tpu_custom_call" | custom-call | flops 8000000000 | bytes 4000000 | tf_op jit(solution)/shard_map/inner/pallas_call | solution.py:650
  14.3 0.0 collective-permute-done.first_swap_ref
  14.3 0.0 collective-permute-done.1.second_swap_ref
  14.3 0.0 copy-start.2
  14.3 0.0 copy-start.3
  14.3 2.6 %ends.1 = (bf16[64,512]{1,0:T(8,128)(2,1)}, bf16[1280,128]{1,0:T(8,128)(2,1)S(1)}) custom-call(bf16[32,512]{1,0:T(8,128)(2,1)S(1)} %collective-permute-done.first_swap_ref, bf16[32,512]{1,0:T(8,128)(2,1)S(1)} %collective-permute-done.1.second_swap_ref, bf16[224,128]{1,0:T(8,128)(2,1)S(1)} %get-tuple-element.41.w1_ref, ...), custom_call_target="tpu_custom_call" | custom-call | tf_op jit(solution)/shard_map/ends/pallas_call | solution.py:681
  17.0 0.0 copy-start
  17.0 0.0 copy-start.1
  17.0 14.1 %all_to_all.5 = bf16[32,40,128]{2,1,0:T(8,128)(2,1)S(1)} all-to-all(bf16[32,40,128]{2,1,0:T(8,128)(2,1)S(1)} %bitcast.15), channel_id=1, replica_groups=mesh['tx'=8,'ty'=4] {'tx','ty'}, dimensions={0} | all-to-all | bytes 655360 | tf_op jit(solution)/shard_map/all_to_all | solution.py:694
  31.0 0.0 copy-done.2
  31.0 0.0 copy-done.3
  31.0 0.0 copy-done
  31.0 0.0 copy-done.1
  31.1 0.9 %level.1 = (f32[256,256]{1,0:T(8,128)S(1)}, f32[4,256,128]{2,1,0:T(8,128)S(1)}, bf16[32,384]{1,0:T(8,128)(2,1)S(1)}, bf16[32,384]{1,0:T(8,128)(2,1)S(1)}) custom-call(bf16[1280,128]{1,0:T(8,128)(2,1)S(1)} %bitcast.14, bf16[32,512]{1,0:T(8,128)(2,1)S(1)} %collective-permute-done.first_swap_ref, bf16[32,512]{1,0:T(8,128)(2,1)S(1)} %collective-permute-done.1.second_swap_ref, ...), custom_call_target="tpu_custom_call" | custom-call | tf_op jit(solution)/shard_map/level/pallas_call | solution.py:700
  32.0 0.9 %collective-permute-start.2 = (bf16[32,384]{1,0:T(8,128)(2,1)S(1)}, bf16[32,384]{1,0:T(8,128)(2,1)S(1)}, u32[]{:S(2)}, u32[]{:S(2)}) collective-permute-start(bf16[32,384]{1,0:T(8,128)(2,1)S(1)} %get-tuple-element.56), channel_id=1, source_target_pairs={{0,4},{1,5},{2,6},{3,7},{4,0},{5,1},{6,2},{7,3},{8,12},{9,13},{10,... | collective-permute-start | bytes 73736 | tf_op jit(solution)/shard_map/ppermute | solution.py:609
  32.9 0.0 collective-permute-start.3
  32.9 4.4 %flow_inner.1.inner_ref = f32[256,256]{1,0:T(8,128)S(1)} custom-call(f32[256,256]{1,0:T(8,128)S(1)} %get-tuple-element.54.level_ref, f32[4,256,128]{2,1,0:T(8,128)S(1)} %get-tuple-element.55.side_ref, f32[256,256]{1,0:T(8,128)S(1)} %copy-done, s32[256,256]{1,0:T(8,128)S(1)} %copy-done.2, f32[256,256]{1,0:T(8,128)S(1)} %copy-done.1), custom_call_target="tpu_custom_call" | custom-call | flops 5000000000 | bytes 4000000 | tf_op jit(solution)/shard_map/flow_inner/pallas_call | solution.py:716
  37.3 0.0 collective-permute-done.2.first_swap_ref
  37.3 0.0 collective-permute-done.3.second_swap_ref
  37.3 2.0 %flow_ends.1 = f32[256,256]{1,0:T(8,128)} custom-call(f32[256,256]{1,0:T(8,128)S(1)} %flow_inner.1.inner_ref, f32[256,256]{1,0:T(8,128)S(1)} %get-tuple-element.54.level_ref, f32[4,256,128]{2,1,0:T(8,128)S(1)} %get-tuple-element.55.side_ref, f32[256,256]{1,0:T(8,128)S(1)} %copy-done, s32[256,256]{1,0:T(8,128)S(1)} %copy-done.2, f32[256,256]{1,0:T(8,128)S(1)} %copy-done.1, ...), custom_call_target="tpu_custom_call" | custom-call | tf_op jit(solution)/shard_map/flow_ends/pallas_call | solution.py:726
Async XLA Ops:
  2.2 12.1 %collective-permute-start = (bf16[32,512]{1,0:T(8,128)(2,1)S(1)}, bf16[32,512]{1,0:T(8,128)(2,1)S(1)}, u32[]{:S(2)}, u32[]{:S(2)}) collective-permute-start(bf16[32,512]{1,0:T(8,128)(2,1)S(1)} %get-tuple-element.30), channel_id=1, source_target_pairs={{0,1},{1,0},{2,3},{3,2},{4,5},{5,4},{6,7},{7,6},{8,9},{9,8},{10,11... | collective-permute-start | bytes 98312 | tf_op jit(solution)/shard_map/ppermute | solution.py:609
  2.7 11.6 %collective-permute-start.1 = (bf16[32,512]{1,0:T(8,128)(2,1)S(1)}, bf16[32,512]{1,0:T(8,128)(2,1)S(1)}, u32[]{:S(2)}, u32[]{:S(2)}) collective-permute-start(bf16[32,512]{1,0:T(8,128)(2,1)S(1)} %get-tuple-element.31), channel_id=1, source_target_pairs={{0,31},{1,2},{2,1},{3,4},{4,3},{5,6},{6,5},{7,8},{8,7},{9,10},{10,... | collective-permute-start | bytes 98312 | tf_op jit(solution)/shard_map/ppermute | solution.py:609
  14.3 16.7 %copy-start.2 = (s32[256,256]{1,0:T(8,128)S(1)}, s32[256,256]{1,0:T(8,128)}, u32[]{:S(2)}) copy-start(s32[256,256]{1,0:T(8,128)} %dir_ref.5) | copy-start | bytes 786436
  14.3 16.7 %copy-start.3 = (f32[256,256]{1,0:T(8,128)S(1)}, f32[256,256]{1,0:T(8,128)}, u32[]{:S(2)}) copy-start(f32[256,256]{1,0:T(8,128)} %depth_ref.1) | copy-start | bytes 786436
  17.0 14.1 %copy-start = (f32[256,256]{1,0:T(8,128)S(1)}, f32[256,256]{1,0:T(8,128)}, u32[]{:S(2)}) copy-start(f32[256,256]{1,0:T(8,128)} %slope_ref.5) | copy-start | bytes 786436
  17.0 14.1 %copy-start.1 = (f32[256,256]{1,0:T(8,128)S(1)}, f32[256,256]{1,0:T(8,128)}, u32[]{:S(2)}) copy-start(f32[256,256]{1,0:T(8,128)} %rain_ref.5) | copy-start | bytes 786436
  32.0 5.3 %collective-permute-start.2 = (bf16[32,384]{1,0:T(8,128)(2,1)S(1)}, bf16[32,384]{1,0:T(8,128)(2,1)S(1)}, u32[]{:S(2)}, u32[]{:S(2)}) collective-permute-start(bf16[32,384]{1,0:T(8,128)(2,1)S(1)} %get-tuple-element.56), channel_id=1, source_target_pairs={{0,4},{1,5},{2,6},{3,7},{4,0},{5,1},{6,2},{7,3},{8,12},{9,13},{10,... | collective-permute-start | bytes 73736 | tf_op jit(solution)/shard_map/ppermute | solution.py:609
  32.9 4.4 %collective-permute-start.3 = (bf16[32,384]{1,0:T(8,128)(2,1)S(1)}, bf16[32,384]{1,0:T(8,128)(2,1)S(1)}, u32[]{:S(2)}, u32[]{:S(2)}) collective-permute-start(bf16[32,384]{1,0:T(8,128)(2,1)S(1)} %get-tuple-element.57), channel_id=1, source_target_pairs={{0,1},{1,0},{2,3},{3,2},{4,8},{5,9},{6,10},{7,11},{8,4},{9,5},{10,... | collective-permute-start | bytes 73736 | tf_op jit(solution)/shard_map/ppermute | solution.py:609

commit v16 on v15

--- a/solution.py
+++ b/solution.py
@@ -312,15 +312,13 @@
     quarter = wnd_ref.shape[1]
     group = 16
 
-    def window_group(g, carry):
-        at = pl.ds(pl.multiple_of(g * group + END_LINES, END_LINES), group)
+    for g in range((lines - 2 * END_LINES) // group):
+        at = slice(g * group + END_LINES, (g + 1) * group + END_LINES)
         cov = gw_ref[at, :]
         obs = sigmoid(logit_ref[at, :]).astype(f32) * cov
         for i, sums in enumerate(line_windows(cell_ref[at, :], obs, cov, quarter)):
-            wnd_ref[pl.ds(pl.multiple_of(g * (CH * group) + CH * i, CH), CH), :] = sums
-        return carry
-
-    lax.fori_loop(0, (lines - 2 * END_LINES) // group, window_group, 0)
+            to = CH * (group * g + i)
+            wnd_ref[to : to + CH, :] = sums
     slots_ref[...] = dot(perm[:, end : wnd_rows - end], window_goods(wnd_ref[...]))
 
 
@@ -596,7 +594,7 @@
     def swaps(first, second, stride):
         size = devices // stride
         out = []
-        for start, x in enumerate((first, second)):
+        for start, x in ((1, second), (0, first)):
             to = {}
             for place in range(start, size, 2):
                 for k in range(stride):
@@ -607,7 +605,7 @@
                         ends = (i, j), (j, i)
                     to.update(ends)
             out.append(lax.ppermute(x, both, sorted(to.items())))
-        return out
+        return out[::-1]
 
     params = pltpu.CompilerParams(vmem_limit_bytes=VMEM_LIMIT)
     message = pltpu.VMEM((32, range_px), bf16)

time: 39.6 us -> 39.6 us (level)
  Pallas kernels: 16.5 us -> 15.8 us
  blocking collectives: 14.1 us -> 14.7 us
    pallas_call x1, Pallas kernels: 4.96 us -> 4.3 us  [per_device(): pl.pallas_call(functools.partial(inner_kernel, devices, capacity), out_sh...]
    all_to_all x1, blocking collectives: 14.1 us -> 14.7 us  [per_device(): lax.all_to_all(send.reshape(devices, send_rows, LANES), both, split_axis=...]
  transfers between devices with their start and end apart: 4 -> 4, of which waited for: 0 -> 0; matrix products, arithmetic and copies ran while one was open for 0% -> 0% of each run, Pallas kernels for 24% -> 22%
where the time goes in v16:
time: 39.6 us; the launch traced here: 39.3 us
  Pallas kernels  15.8 us (40%)
  blocking collectives  14.7 us (37%)
  starting transfers between devices  8.02 us (20%)
  between operations  0.72 us (2%)
    all_to_all x1, blocking collectives, per_device(): lax.all_to_all(send.reshape(devices, send_rows, LANES), both, split_axis=...  14.7 us
    ppermute x4, starting transfers between devices, swaps(): out.append(lax.ppermute(x, both, sorted(to.items())))  8.02 us
    pallas_call x1, Pallas kernels, per_device(): pl.pallas_call(flow_inner_kernel, out_shape=jax.ShapeDtypeStruct((tile_ro...  4.38 us
    pallas_call x1, Pallas kernels, per_device(): pl.pallas_call(functools.partial(inner_kernel, devices, capacity), out_sh...  4.3 us
    pallas_call x1, Pallas kernels, per_device(): pl.pallas_call(functools.partial(ends_kernel, devices, capacity), out_sha...  2.65 us
    pallas_call x1, Pallas kernels, per_device(): pl.pallas_call(flow_ends_kernel, out_shape=jax.ShapeDtypeStruct((tile_row...  2.04 us
    pallas_call x1, Pallas kernels, per_device(): pl.pallas_call(edge_kernel, out_shape=(message, message, *[pltpu.VMEM(x.s...  1.55 us
    pallas_call x1, Pallas kernels, per_device(): pl.pallas_call(functools.partial(level_kernel, devices), out_shape=(jax.S...  0.92 us
  transfers between devices with their start and end apart: 4, of which 0 were waited for; matrix products, arithmetic and copies ran while one was open for 0% of the time, Pallas kernels for 22%

profile of v16, /device:TPU:0, one launch (start us, length us, event | category | flops | bytes accessed | tf_op | source)
XLA Modules:
  0.0 39.3 jit_solution(15314806205430805323)
XLA Ops:
  0.6 1.5 %edges.1 = (bf16[32,512]{1,0:T(8,128)(2,1)S(1)}, bf16[32,512]{1,0:T(8,128)(2,1)S(1)}, bf16[2,64,512]{2,1,0:T(8,128)(2,1)S(1)}, bf16[3,3,2,16]{3,2,1,0:T(2,128)(2...) custom-call(f32[256,256]{1,0:T(8,128)} %depth_ref.1, ...), custom_call_target="tpu_custom_call" | custom-call | tf_op jit(solution)/shard_map/edges/pallas_call | solution.py:623
  2.2 0.5 %collective-permute-start = (bf16[32,512]{1,0:T(8,128)(2,1)S(1)}, bf16[32,512]{1,0:T(8,128)(2,1)S(1)}, u32[]{:S(2)}, u32[]{:S(2)}) collective-permute-start(bf16[32,512]{1,0:T(8,128)(2,1)S(1)} %get-tuple-element.30), channel_id=1, source_target_pairs={{0,1},{1,0},{2,3},{3,2},{4,5},{5,4},{6,7},{7,6},{8,9},{9,8},{10,11... | collective-permute-start | bytes 98312 | tf_op jit(solution)/shard_map/ppermute | solution.py:607
  2.7 6.6 %collective-permute-start.1 = (bf16[32,512]{1,0:T(8,128)(2,1)S(1)}, bf16[32,512]{1,0:T(8,128)(2,1)S(1)}, u32[]{:S(2)}, u32[]{:S(2)}) collective-permute-start(bf16[32,512]{1,0:T(8,128)(2,1)S(1)} %get-tuple-element.31), channel_id=1, source_target_pairs={{0,31},{1,2},{2,1},{3,4},{4,3},{5,6},{6,5},{7,8},{8,7},{9,10},{10,... | collective-permute-start | bytes 98312 | tf_op jit(solution)/shard_map/ppermute | solution.py:607
  9.3 4.3 %inner.1 = (bf16[224,128]{1,0:T(8,128)(2,1)S(1)}, bf16[48,256]{1,0:T(8,128)(2,1)S(1)}, bf16[48,256]{1,0:T(8,128)(2,1)S(1)}, bf16[48,256]{1,0:T(8,128)(2,1)S(1)},...) custom-call(bf16[3,3,2,16]{3,2,1,0:T(2,128)(2,1)S(1)} %get-tuple-ele, ...), custom_call_target="tpu_custom_call" | custom-call | flops 8000000000 | bytes 4000000 | tf_op jit(solution)/shard_map/inner/pallas_call | solution.py:648
  13.6 0.0 collective-permute-done.first_swap_ref
  13.6 0.0 collective-permute-done.1.second_swap_ref
  13.6 0.0 copy-start.2
  13.6 0.0 copy-start.3
  13.7 2.6 %ends.1 = (bf16[64,512]{1,0:T(8,128)(2,1)}, bf16[1280,128]{1,0:T(8,128)(2,1)S(1)}) custom-call(bf16[32,512]{1,0:T(8,128)(2,1)S(1)} %collective-permute-done.first_swap_ref, bf16[32,512]{1,0:T(8,128)(2,1)S(1)} %collective-permute-done.1.second_swap_ref, bf16[224,128]{1,0:T(8,128)(2,1)S(1)} %get-tuple-element.41.w1_ref, ...), custom_call_target="tpu_custom_call" | custom-call | tf_op jit(solution)/shard_map/ends/pallas_call | solution.py:679
  16.3 0.0 copy-start
  16.3 0.0 copy-start.1
  16.3 14.7 %all_to_all.5 = bf16[32,40,128]{2,1,0:T(8,128)(2,1)S(1)} all-to-all(bf16[32,40,128]{2,1,0:T(8,128)(2,1)S(1)} %bitcast.15), channel_id=1, replica_groups=mesh['tx'=8,'ty'=4] {'tx','ty'}, dimensions={0} | all-to-all | bytes 655360 | tf_op jit(solution)/shard_map/all_to_all | solution.py:692
  31.0 0.0 copy-done.2
  31.0 0.0 copy-done.3
  31.0 0.0 copy-done
  31.0 0.0 copy-done.1
  31.1 0.9 %level.1 = (f32[256,256]{1,0:T(8,128)S(1)}, f32[4,256,128]{2,1,0:T(8,128)S(1)}, bf16[32,384]{1,0:T(8,128)(2,1)S(1)}, bf16[32,384]{1,0:T(8,128)(2,1)S(1)}) custom-call(bf16[1280,128]{1,0:T(8,128)(2,1)S(1)} %bitcast.14, bf16[32,512]{1,0:T(8,128)(2,1)S(1)} %collective-permute-done.first_swap_ref, bf16[32,512]{1,0:T(8,128)(2,1)S(1)} %collective-permute-done.1.second_swap_ref, ...), custom_call_target="tpu_custom_call" | custom-call | tf_op jit(solution)/shard_map/level/pallas_call | solution.py:698
  32.0 0.9 %collective-permute-start.2 = (bf16[32,384]{1,0:T(8,128)(2,1)S(1)}, bf16[32,384]{1,0:T(8,128)(2,1)S(1)}, u32[]{:S(2)}, u32[]{:S(2)}) collective-permute-start(bf16[32,384]{1,0:T(8,128)(2,1)S(1)} %get-tuple-element.56), channel_id=1, source_target_pairs={{0,4},{1,5},{2,6},{3,7},{4,0},{5,1},{6,2},{7,3},{8,12},{9,13},{10,... | collective-permute-start | bytes 73736 | tf_op jit(solution)/shard_map/ppermute | solution.py:607
  32.9 0.0 collective-permute-start.3
  32.9 4.4 %flow_inner.1.inner_ref = f32[256,256]{1,0:T(8,128)S(1)} custom-call(f32[256,256]{1,0:T(8,128)S(1)} %get-tuple-element.54.level_ref, f32[4,256,128]{2,1,0:T(8,128)S(1)} %get-tuple-element.55.side_ref, f32[256,256]{1,0:T(8,128)S(1)} %copy-done, s32[256,256]{1,0:T(8,128)S(1)} %copy-done.2, f32[256,256]{1,0:T(8,128)S(1)} %copy-done.1), custom_call_target="tpu_custom_call" | custom-call | flops 5000000000 | bytes 4000000 | tf_op jit(solution)/shard_map/flow_inner/pallas_call | solution.py:714
  37.3 0.0 collective-permute-done.2.first_swap_ref
  37.3 0.0 collective-permute-done.3.second_swap_ref
  37.3 2.0 %flow_ends.1 = f32[256,256]{1,0:T(8,128)} custom-call(f32[256,256]{1,0:T(8,128)S(1)} %flow_inner.1.inner_ref, f32[256,256]{1,0:T(8,128)S(1)} %get-tuple-element.54.level_ref, f32[4,256,128]{2,1,0:T(8,128)S(1)} %get-tuple-element.55.side_ref, f32[256,256]{1,0:T(8,128)S(1)} %copy-done, s32[256,256]{1,0:T(8,128)S(1)} %copy-done.2, f32[256,256]{1,0:T(8,128)S(1)} %copy-done.1, ...), custom_call_target="tpu_custom_call" | custom-call | tf_op jit(solution)/shard_map/flow_ends/pallas_call | solution.py:724
Async XLA Ops:
  2.2 11.4 %collective-permute-start = (bf16[32,512]{1,0:T(8,128)(2,1)S(1)}, bf16[32,512]{1,0:T(8,128)(2,1)S(1)}, u32[]{:S(2)}, u32[]{:S(2)}) collective-permute-start(bf16[32,512]{1,0:T(8,128)(2,1)S(1)} %get-tuple-element.30), channel_id=1, source_target_pairs={{0,1},{1,0},{2,3},{3,2},{4,5},{5,4},{6,7},{7,6},{8,9},{9,8},{10,11... | collective-permute-start | bytes 98312 | tf_op jit(solution)/shard_map/ppermute | solution.py:607
  2.7 10.9 %collective-permute-start.1 = (bf16[32,512]{1,0:T(8,128)(2,1)S(1)}, bf16[32,512]{1,0:T(8,128)(2,1)S(1)}, u32[]{:S(2)}, u32[]{:S(2)}) collective-permute-start(bf16[32,512]{1,0:T(8,128)(2,1)S(1)} %get-tuple-element.31), channel_id=1, source_target_pairs={{0,31},{1,2},{2,1},{3,4},{4,3},{5,6},{6,5},{7,8},{8,7},{9,10},{10,... | collective-permute-start | bytes 98312 | tf_op jit(solution)/shard_map/ppermute | solution.py:607
  13.6 17.4 %copy-start.2 = (s32[256,256]{1,0:T(8,128)S(1)}, s32[256,256]{1,0:T(8,128)}, u32[]{:S(2)}) copy-start(s32[256,256]{1,0:T(8,128)} %dir_ref.5) | copy-start | bytes 786436
  13.6 17.4 %copy-start.3 = (f32[256,256]{1,0:T(8,128)S(1)}, f32[256,256]{1,0:T(8,128)}, u32[]{:S(2)}) copy-start(f32[256,256]{1,0:T(8,128)} %depth_ref.1) | copy-start | bytes 786436
  16.3 14.7 %copy-start = (f32[256,256]{1,0:T(8,128)S(1)}, f32[256,256]{1,0:T(8,128)}, u32[]{:S(2)}) copy-start(f32[256,256]{1,0:T(8,128)} %slope_ref.5) | copy-start | bytes 786436
  16.3 14.7 %copy-start.1 = (f32[256,256]{1,0:T(8,128)S(1)}, f32[256,256]{1,0:T(8,128)}, u32[]{:S(2)}) copy-start(f32[256,256]{1,0:T(8,128)} %rain_ref.5) | copy-start | bytes 786436
  32.0 5.3 %collective-permute-start.2 = (bf16[32,384]{1,0:T(8,128)(2,1)S(1)}, bf16[32,384]{1,0:T(8,128)(2,1)S(1)}, u32[]{:S(2)}, u32[]{:S(2)}) collective-permute-start(bf16[32,384]{1,0:T(8,128)(2,1)S(1)} %get-tuple-element.56), channel_id=1, source_target_pairs={{0,4},{1,5},{2,6},{3,7},{4,0},{5,1},{6,2},{7,3},{8,12},{9,13},{10,... | collective-permute-start | bytes 73736 | tf_op jit(solution)/shard_map/ppermute | solution.py:607
  32.9 4.4 %collective-permute-start.3 = (bf16[32,384]{1,0:T(8,128)(2,1)S(1)}, bf16[32,384]{1,0:T(8,128)(2,1)S(1)}, u32[]{:S(2)}, u32[]{:S(2)}) collective-permute-start(bf16[32,384]{1,0:T(8,128)(2,1)S(1)} %get-tuple-element.57), channel_id=1, source_target_pairs={{0,1},{1,0},{2,3},{3,2},{4,8},{5,9},{6,10},{7,11},{8,4},{9,5},{10,... | collective-permute-start | bytes 73736 | tf_op jit(solution)/shard_map/ppermute | solution.py:607

commit v17 on v16

--- a/solution.py
+++ b/solution.py
@@ -332,7 +332,7 @@
 
 def ends_kernel(
     devices, capacity,
-    first_swap_ref, second_swap_ref, w1_ref, w2_ref, w3_ref, w4_ref, perm_ref, extra_ref, frac_in, slots_in, e1_ref, e2_ref, e3_ref,
+    second_swap_ref, first_swap_ref, w1_ref, w2_ref, w3_ref, w4_ref, perm_ref, extra_ref, frac_in, slots_in, e1_ref, e2_ref, e3_ref,
     sar_ref, gw_ref, cell_ref,
     frac_ref, send_ref,
     f_ref,
@@ -417,7 +417,7 @@
 
 def level_kernel(
     devices,
-    got_ref, first_swap_ref, second_swap_ref, depth_ref, slope_ref, rain_ref, dir_ref,
+    got_ref, second_swap_ref, first_swap_ref, depth_ref, slope_ref, rain_ref, dir_ref,
     level_ref, side_ref, first_ref, second_ref,
 ):
     tile_rows, tile_cols = depth_ref.shape
@@ -527,7 +527,11 @@
         substep(1, 0)
         return carry
 
-    lax.fori_loop(0, SUBSTEPS // 2, substep_pair, 0)
+    if rows > LANES:
+        lax.fori_loop(0, SUBSTEPS // 2, substep_pair, 0)
+    else:
+        for i in range(SUBSTEPS // 2):
+            substep_pair(i, 0)
     return level_at
 
 
@@ -687,7 +691,7 @@
         scratch_shapes=[pltpu.VMEM((az_lines, range_px), f32)],
         compiler_params=params,
         name="ends",
-    )(*halo, *prepared, sar_image, geo_weight, cell_index)
+    )(*halo[::-1], *prepared, sar_image, geo_weight, cell_index)
 
     got = lax.all_to_all(
         send.reshape(devices, send_rows, LANES), both, split_axis=0, concat_axis=0, tiled=True
@@ -707,7 +711,7 @@
         out_specs=tuple(vmem_specs(4)),
         compiler_params=params,
         name="level",
-    )(got, *halo, depth, slope, rain, flow_dir)
+    )(got, *halo[::-1], depth, slope, rain, flow_dir)
 
     row_halo = swaps(first, second, n_ty)
 

time: 39.6 us -> 38.8 us (0.980)
  starting transfers between devices: 8.02 us -> 7.35 us
    ppermute x4, starting transfers between devices: 8.02 us -> 7.35 us  [swaps(): out.append(lax.ppermute(x, both, sorted(to.items())))]
where the time goes in v17:
time: 38.8 us; the launch traced here: 38.6 us
  Pallas kernels  15.8 us (41%)
  blocking collectives  14.8 us (38%)
  starting transfers between devices  7.35 us (19%)
  between operations  0.72 us (2%)
    all_to_all x1, blocking collectives, per_device(): lax.all_to_all(send.reshape(devices, send_rows, LANES), both, split_axis=...  14.8 us
    ppermute x4, starting transfers between devices, swaps(): out.append(lax.ppermute(x, both, sorted(to.items())))  7.35 us
    pallas_call x1, Pallas kernels, per_device(): pl.pallas_call(flow_inner_kernel, out_shape=jax.ShapeDtypeStruct((tile_ro...  4.38 us
    pallas_call x1, Pallas kernels, per_device(): pl.pallas_call(functools.partial(inner_kernel, devices, capacity), out_sh...  4.28 us
    pallas_call x1, Pallas kernels, per_device(): pl.pallas_call(functools.partial(ends_kernel, devices, capacity), out_sha...  2.65 us
    pallas_call x1, Pallas kernels, per_device(): pl.pallas_call(flow_ends_kernel, out_shape=jax.ShapeDtypeStruct((tile_row...  2 us
    pallas_call x1, Pallas kernels, per_device(): pl.pallas_call(edge_kernel, out_shape=(message, message, *[pltpu.VMEM(x.s...  1.55 us
    pallas_call x1, Pallas kernels, per_device(): pl.pallas_call(functools.partial(level_kernel, devices), out_shape=(jax.S...  0.92 us
  transfers between devices with their start and end apart: 4, of which 0 were waited for; matrix products, arithmetic and copies ran while one was open for 0% of the time, Pallas kernels for 22%

profile of v17, /device:TPU:0, one launch (start us, length us, event | category | flops | bytes accessed | tf_op | source)
XLA Modules:
  0.0 38.6 jit_solution(10623028441588069509)
XLA Ops:
  0.6 1.5 %edges.1 = (bf16[32,512]{1,0:T(8,128)(2,1)S(1)}, bf16[32,512]{1,0:T(8,128)(2,1)S(1)}, bf16[2,64,512]{2,1,0:T(8,128)(2,1)S(1)}, bf16[3,3,2,16]{3,2,1,0:T(2,128)(2...) custom-call(f32[256,256]{1,0:T(8,128)} %depth_ref.1, ...), custom_call_target="tpu_custom_call" | custom-call | tf_op jit(solution)/shard_map/edges/pallas_call | solution.py:627
  2.2 6.4 %collective-permute-start = (bf16[32,512]{1,0:T(8,128)(2,1)S(1)}, bf16[32,512]{1,0:T(8,128)(2,1)S(1)}, u32[]{:S(2)}, u32[]{:S(2)}) collective-permute-start(bf16[32,512]{1,0:T(8,128)(2,1)S(1)} %get-tuple-element.30), channel_id=1, source_target_pairs={{0,31},{1,2},{2,1},{3,4},{4,3},{5,6},{6,5},{7,8},{8,7},{9,10},{10,... | collective-permute-start | bytes 98312 | tf_op jit(solution)/shard_map/ppermute | solution.py:611
  8.6 0.0 collective-permute-start.1
  8.6 4.3 %inner.1 = (bf16[224,128]{1,0:T(8,128)(2,1)S(1)}, bf16[48,256]{1,0:T(8,128)(2,1)S(1)}, bf16[48,256]{1,0:T(8,128)(2,1)S(1)}, bf16[48,256]{1,0:T(8,128)(2,1)S(1)},...) custom-call(bf16[3,3,2,16]{3,2,1,0:T(2,128)(2,1)S(1)} %get-tuple-ele, ...), custom_call_target="tpu_custom_call" | custom-call | flops 8000000000 | bytes 4000000 | tf_op jit(solution)/shard_map/inner/pallas_call | solution.py:652
  12.9 0.0 collective-permute-done.second_swap_ref
  12.9 0.0 collective-permute-done.1.first_swap_ref
  12.9 0.0 copy-start.2
  12.9 0.0 copy-start.3
  13.0 2.6 %ends.1 = (bf16[64,512]{1,0:T(8,128)(2,1)}, bf16[1280,128]{1,0:T(8,128)(2,1)S(1)}) custom-call(bf16[32,512]{1,0:T(8,128)(2,1)S(1)} %collective-permute-done.second_swap_ref, bf16[32,512]{1,0:T(8,128)(2,1)S(1)} %collective-permute-done.1.first_swap_ref, bf16[224,128]{1,0:T(8,128)(2,1)S(1)} %get-tuple-element.41.w1_ref, ...), custom_call_target="tpu_custom_call" | custom-call | tf_op jit(solution)/shard_map/ends/pallas_call | solution.py:683
  15.6 0.0 copy-start
  15.6 0.0 copy-start.1
  15.6 14.8 %all_to_all.5 = bf16[32,40,128]{2,1,0:T(8,128)(2,1)S(1)} all-to-all(bf16[32,40,128]{2,1,0:T(8,128)(2,1)S(1)} %bitcast.15), channel_id=1, replica_groups=mesh['tx'=8,'ty'=4] {'tx','ty'}, dimensions={0} | all-to-all | bytes 655360 | tf_op jit(solution)/shard_map/all_to_all | solution.py:696
  30.4 0.0 copy-done.2
  30.4 0.0 copy-done.3
  30.4 0.0 copy-done
  30.4 0.0 copy-done.1
  30.4 0.9 %level.1 = (f32[256,256]{1,0:T(8,128)S(1)}, f32[4,256,128]{2,1,0:T(8,128)S(1)}, bf16[32,384]{1,0:T(8,128)(2,1)S(1)}, bf16[32,384]{1,0:T(8,128)(2,1)S(1)}) custom-call(bf16[1280,128]{1,0:T(8,128)(2,1)S(1)} %bitcast.14, bf16[32,512]{1,0:T(8,128)(2,1)S(1)} %collective-permute-done.second_swap_ref, bf16[32,512]{1,0:T(8,128)(2,1)S(1)} %collective-permute-done.1.first_swap_ref, ...), custom_call_target="tpu_custom_call" | custom-call | tf_op jit(solution)/shard_map/level/pallas_call | solution.py:702
  31.3 0.9 %collective-permute-start.2 = (bf16[32,384]{1,0:T(8,128)(2,1)S(1)}, bf16[32,384]{1,0:T(8,128)(2,1)S(1)}, u32[]{:S(2)}, u32[]{:S(2)}) collective-permute-start(bf16[32,384]{1,0:T(8,128)(2,1)S(1)} %get-tuple-element.56), channel_id=1, source_target_pairs={{0,4},{1,5},{2,6},{3,7},{4,0},{5,1},{6,2},{7,3},{8,12},{9,13},{10,... | collective-permute-start | bytes 73736 | tf_op jit(solution)/shard_map/ppermute | solution.py:611
  32.2 0.0 collective-permute-start.3
  32.2 4.4 %flow_inner.1.inner_ref = f32[256,256]{1,0:T(8,128)S(1)} custom-call(f32[256,256]{1,0:T(8,128)S(1)} %get-tuple-element.54.level_ref, f32[4,256,128]{2,1,0:T(8,128)S(1)} %get-tuple-element.55.side_ref, f32[256,256]{1,0:T(8,128)S(1)} %copy-done, s32[256,256]{1,0:T(8,128)S(1)} %copy-done.2, f32[256,256]{1,0:T(8,128)S(1)} %copy-done.1), custom_call_target="tpu_custom_call" | custom-call | flops 5000000000 | bytes 4000000 | tf_op jit(solution)/shard_map/flow_inner/pallas_call | solution.py:718
  36.6 0.0 collective-permute-done.2.first_swap_ref
  36.6 0.0 collective-permute-done.3.second_swap_ref
  36.6 2.0 %flow_ends.1 = f32[256,256]{1,0:T(8,128)} custom-call(f32[256,256]{1,0:T(8,128)S(1)} %flow_inner.1.inner_ref, f32[256,256]{1,0:T(8,128)S(1)} %get-tuple-element.54.level_ref, f32[4,256,128]{2,1,0:T(8,128)S(1)} %get-tuple-element.55.side_ref, f32[256,256]{1,0:T(8,128)S(1)} %copy-done, s32[256,256]{1,0:T(8,128)S(1)} %copy-done.2, f32[256,256]{1,0:T(8,128)S(1)} %copy-done.1, ...), custom_call_target="tpu_custom_call" | custom-call | tf_op jit(solution)/shard_map/flow_ends/pallas_call | solution.py:728
Async XLA Ops:
  2.2 10.7 %collective-permute-start = (bf16[32,512]{1,0:T(8,128)(2,1)S(1)}, bf16[32,512]{1,0:T(8,128)(2,1)S(1)}, u32[]{:S(2)}, u32[]{:S(2)}) collective-permute-start(bf16[32,512]{1,0:T(8,128)(2,1)S(1)} %get-tuple-element.30), channel_id=1, source_target_pairs={{0,31},{1,2},{2,1},{3,4},{4,3},{5,6},{6,5},{7,8},{8,7},{9,10},{10,... | collective-permute-start | bytes 98312 | tf_op jit(solution)/shard_map/ppermute | solution.py:611
  8.6 4.3 %collective-permute-start.1 = (bf16[32,512]{1,0:T(8,128)(2,1)S(1)}, bf16[32,512]{1,0:T(8,128)(2,1)S(1)}, u32[]{:S(2)}, u32[]{:S(2)}) collective-permute-start(bf16[32,512]{1,0:T(8,128)(2,1)S(1)} %get-tuple-element.31), channel_id=1, source_target_pairs={{0,1},{1,0},{2,3},{3,2},{4,5},{5,4},{6,7},{7,6},{8,9},{9,8},{10,11... | collective-permute-start | bytes 98312 | tf_op jit(solution)/shard_map/ppermute | solution.py:611
  12.9 17.4 %copy-start.2 = (s32[256,256]{1,0:T(8,128)S(1)}, s32[256,256]{1,0:T(8,128)}, u32[]{:S(2)}) copy-start(s32[256,256]{1,0:T(8,128)} %dir_ref.5) | copy-start | bytes 786436
  12.9 17.4 %copy-start.3 = (f32[256,256]{1,0:T(8,128)S(1)}, f32[256,256]{1,0:T(8,128)}, u32[]{:S(2)}) copy-start(f32[256,256]{1,0:T(8,128)} %depth_ref.1) | copy-start | bytes 786436
  15.6 14.8 %copy-start = (f32[256,256]{1,0:T(8,128)S(1)}, f32[256,256]{1,0:T(8,128)}, u32[]{:S(2)}) copy-start(f32[256,256]{1,0:T(8,128)} %slope_ref.5) | copy-start | bytes 786436
  15.6 14.8 %copy-start.1 = (f32[256,256]{1,0:T(8,128)S(1)}, f32[256,256]{1,0:T(8,128)}, u32[]{:S(2)}) copy-start(f32[256,256]{1,0:T(8,128)} %rain_ref.5) | copy-start | bytes 786436
  31.3 5.3 %collective-permute-start.2 = (bf16[32,384]{1,0:T(8,128)(2,1)S(1)}, bf16[32,384]{1,0:T(8,128)(2,1)S(1)}, u32[]{:S(2)}, u32[]{:S(2)}) collective-permute-start(bf16[32,384]{1,0:T(8,128)(2,1)S(1)} %get-tuple-element.56), channel_id=1, source_target_pairs={{0,4},{1,5},{2,6},{3,7},{4,0},{5,1},{6,2},{7,3},{8,12},{9,13},{10,... | collective-permute-start | bytes 73736 | tf_op jit(solution)/shard_map/ppermute | solution.py:611
  32.2 4.4 %collective-permute-start.3 = (bf16[32,384]{1,0:T(8,128)(2,1)S(1)}, bf16[32,384]{1,0:T(8,128)(2,1)S(1)}, u32[]{:S(2)}, u32[]{:S(2)}) collective-permute-start(bf16[32,384]{1,0:T(8,128)(2,1)S(1)} %get-tuple-element.57), channel_id=1, source_target_pairs={{0,1},{1,0},{2,3},{3,2},{4,8},{5,9},{6,10},{7,11},{8,4},{9,5},{10,... | collective-permute-start | bytes 73736 | tf_op jit(solution)/shard_map/ppermute | solution.py:611

commit v18 on v17

--- a/solution.py
+++ b/solution.py
@@ -538,11 +538,11 @@
 def flow_inner_kernel(level_ref, side_ref, slope_ref, dir_ref, rain_ref, out_ref, *scratch):
     rows, cols = level_ref.shape
     own = (level_ref[...], rain_ref[...], runoff_coef * jnp.sqrt(slope_ref[...]), dir_ref[...].astype(f32))
-    level_at = substeps(*[jnp.concatenate([x, side_ref[i]], 1) for i, x in enumerate(own)], *scratch, 16)
+    level_at = substeps(*[jnp.concatenate([x, side_ref[i]], 1) for i, x in enumerate(own)], *scratch, 8)
     out_ref[...] = level_at(0, 0, rows)[:, 0:cols]
 
 
-def flow_ends_kernel(inner_ref, level_ref, side_ref, slope_ref, dir_ref, rain_ref, first_swap_ref, second_swap_ref, out_ref, *scratch):
+def flow_ends_kernel(inner_ref, level_ref, side_ref, slope_ref, dir_ref, rain_ref, second_swap_ref, first_swap_ref, out_ref, *scratch):
     rows, cols = level_ref.shape
     h = SUBSTEPS
     above, below = from_turns(
@@ -733,7 +733,7 @@
         scratch_shapes=flow_scratch(6 * SUBSTEPS, wide_cols),
         compiler_params=params,
         name="flow_ends",
-    )(inner, level, side, slope, flow_dir, rain, *row_halo)
+    )(inner, level, side, slope, flow_dir, rain, *row_halo[::-1])
     return (fraction, level)
 
 

time: 38.8 us -> 40.4 us (1.041)
  starting transfers between devices: 7.35 us -> 8.82 us
    ppermute x4, starting transfers between devices: 7.35 us -> 8.82 us  [swaps(): out.append(lax.ppermute(x, both, sorted(to.items())))]
where the time goes in v18:
time: 40.4 us; the launch traced here: 40.2 us
  Pallas kernels  15.9 us (39%)
  blocking collectives  14.8 us (37%)
  starting transfers between devices  8.82 us (22%)
  between operations  0.72 us (2%)
    all_to_all x1, blocking collectives, per_device(): lax.all_to_all(send.reshape(devices, send_rows, LANES), both, split_axis=...  14.8 us
    ppermute x4, starting transfers between devices, swaps(): out.append(lax.ppermute(x, both, sorted(to.items())))  8.82 us
    pallas_call x1, Pallas kernels, per_device(): pl.pallas_call(flow_inner_kernel, out_shape=jax.ShapeDtypeStruct((tile_ro...  4.48 us
    pallas_call x1, Pallas kernels, per_device(): pl.pallas_call(functools.partial(inner_kernel, devices, capacity), out_sh...  4.28 us
    pallas_call x1, Pallas kernels, per_device(): pl.pallas_call(functools.partial(ends_kernel, devices, capacity), out_sha...  2.65 us
    pallas_call x1, Pallas kernels, per_device(): pl.pallas_call(flow_ends_kernel, out_shape=jax.ShapeDtypeStruct((tile_row...  2 us
    pallas_call x1, Pallas kernels, per_device(): pl.pallas_call(edge_kernel, out_shape=(message, message, *[pltpu.VMEM(x.s...  1.55 us
    pallas_call x1, Pallas kernels, per_device(): pl.pallas_call(functools.partial(level_kernel, devices), out_shape=(jax.S...  0.92 us
  transfers between devices with their start and end apart: 4, of which 0 were waited for; matrix products, arithmetic and copies ran while one was open for 0% of the time, Pallas kernels for 22%

profile of v18, /device:TPU:0, one launch (start us, length us, event | category | flops | bytes accessed | tf_op | source)
XLA Modules:
  0.0 40.2 jit_solution(5974703757744192684)
XLA Ops:
  0.6 1.5 %edges.1 = (bf16[32,512]{1,0:T(8,128)(2,1)S(1)}, bf16[32,512]{1,0:T(8,128)(2,1)S(1)}, bf16[2,64,512]{2,1,0:T(8,128)(2,1)S(1)}, bf16[3,3,2,16]{3,2,1,0:T(2,128)(2...) custom-call(f32[256,256]{1,0:T(8,128)} %depth_ref.1, ...), custom_call_target="tpu_custom_call" | custom-call | tf_op jit(solution)/shard_map/edges/pallas_call | solution.py:627
  2.2 6.4 %collective-permute-start = (bf16[32,512]{1,0:T(8,128)(2,1)S(1)}, bf16[32,512]{1,0:T(8,128)(2,1)S(1)}, u32[]{:S(2)}, u32[]{:S(2)}) collective-permute-start(bf16[32,512]{1,0:T(8,128)(2,1)S(1)} %get-tuple-element.30), channel_id=1, source_target_pairs={{0,31},{1,2},{2,1},{3,4},{4,3},{5,6},{6,5},{7,8},{8,7},{9,10},{10,... | collective-permute-start | bytes 98312 | tf_op jit(solution)/shard_map/ppermute | solution.py:611
  8.6 0.0 collective-permute-start.1
  8.6 4.3 %inner.1 = (bf16[224,128]{1,0:T(8,128)(2,1)S(1)}, bf16[48,256]{1,0:T(8,128)(2,1)S(1)}, bf16[48,256]{1,0:T(8,128)(2,1)S(1)}, bf16[48,256]{1,0:T(8,128)(2,1)S(1)},...) custom-call(bf16[3,3,2,16]{3,2,1,0:T(2,128)(2,1)S(1)} %get-tuple-ele, ...), custom_call_target="tpu_custom_call" | custom-call | flops 8000000000 | bytes 4000000 | tf_op jit(solution)/shard_map/inner/pallas_call | solution.py:652
  12.9 0.0 collective-permute-done.second_swap_ref
  12.9 0.0 collective-permute-done.1.first_swap_ref
  12.9 0.0 copy-start.2
  12.9 0.0 copy-start.3
  13.0 2.6 %ends.1 = (bf16[64,512]{1,0:T(8,128)(2,1)}, bf16[1280,128]{1,0:T(8,128)(2,1)S(1)}) custom-call(bf16[32,512]{1,0:T(8,128)(2,1)S(1)} %collective-permute-done.second_swap_ref, bf16[32,512]{1,0:T(8,128)(2,1)S(1)} %collective-permute-done.1.first_swap_ref, bf16[224,128]{1,0:T(8,128)(2,1)S(1)} %get-tuple-element.41.w1_ref, ...), custom_call_target="tpu_custom_call" | custom-call | tf_op jit(solution)/shard_map/ends/pallas_call | solution.py:683
  15.6 0.0 copy-start
  15.6 0.0 copy-start.1
  15.6 14.8 %all_to_all.5 = bf16[32,40,128]{2,1,0:T(8,128)(2,1)S(1)} all-to-all(bf16[32,40,128]{2,1,0:T(8,128)(2,1)S(1)} %bitcast.15), channel_id=1, replica_groups=mesh['tx'=8,'ty'=4] {'tx','ty'}, dimensions={0} | all-to-all | bytes 655360 | tf_op jit(solution)/shard_map/all_to_all | solution.py:696
  30.4 0.0 copy-done.2
  30.4 0.0 copy-done.3
  30.4 0.0 copy-done
  30.4 0.0 copy-done.1
  30.4 0.9 %level.1 = (f32[256,256]{1,0:T(8,128)S(1)}, f32[4,256,128]{2,1,0:T(8,128)S(1)}, bf16[32,384]{1,0:T(8,128)(2,1)S(1)}, bf16[32,384]{1,0:T(8,128)(2,1)S(1)}) custom-call(bf16[1280,128]{1,0:T(8,128)(2,1)S(1)} %bitcast.14, bf16[32,512]{1,0:T(8,128)(2,1)S(1)} %collective-permute-done.second_swap_ref, bf16[32,512]{1,0:T(8,128)(2,1)S(1)} %collective-permute-done.1.first_swap_ref, ...), custom_call_target="tpu_custom_call" | custom-call | tf_op jit(solution)/shard_map/level/pallas_call | solution.py:702
  31.3 0.1 collective-permute-start.2
  31.4 2.3 %collective-permute-start.3 = (bf16[32,384]{1,0:T(8,128)(2,1)S(1)}, bf16[32,384]{1,0:T(8,128)(2,1)S(1)}, u32[]{:S(2)}, u32[]{:S(2)}) collective-permute-start(bf16[32,384]{1,0:T(8,128)(2,1)S(1)} %get-tuple-element.57), channel_id=1, source_target_pairs={{0,4},{1,5},{2,6},{3,7},{4,0},{5,1},{6,2},{7,3},{8,12},{9,13},{10,... | collective-permute-start | bytes 73736 | tf_op jit(solution)/shard_map/ppermute | solution.py:611
  33.7 4.5 %flow_inner.1.inner_ref = f32[256,256]{1,0:T(8,128)S(1)} custom-call(f32[256,256]{1,0:T(8,128)S(1)} %get-tuple-element.54.level_ref, f32[4,256,128]{2,1,0:T(8,128)S(1)} %get-tuple-element.55.side_ref, f32[256,256]{1,0:T(8,128)S(1)} %copy-done, s32[256,256]{1,0:T(8,128)S(1)} %copy-done.2, f32[256,256]{1,0:T(8,128)S(1)} %copy-done.1), custom_call_target="tpu_custom_call" | custom-call | flops 5000000000 | bytes 4000000 | tf_op jit(solution)/shard_map/flow_inner/pallas_call | solution.py:718
  38.2 0.0 collective-permute-done.2.second_swap_ref
  38.2 0.0 collective-permute-done.3.first_swap_ref
  38.2 2.0 %flow_ends.1 = f32[256,256]{1,0:T(8,128)} custom-call(f32[256,256]{1,0:T(8,128)S(1)} %flow_inner.1.inner_ref, f32[256,256]{1,0:T(8,128)S(1)} %get-tuple-element.54.level_ref, f32[4,256,128]{2,1,0:T(8,128)S(1)} %get-tuple-element.55.side_ref, f32[256,256]{1,0:T(8,128)S(1)} %copy-done, s32[256,256]{1,0:T(8,128)S(1)} %copy-done.2, f32[256,256]{1,0:T(8,128)S(1)} %copy-done.1, ...), custom_call_target="tpu_custom_call" | custom-call | tf_op jit(solution)/shard_map/flow_ends/pallas_call | solution.py:728
Async XLA Ops:
  2.2 10.7 %collective-permute-start = (bf16[32,512]{1,0:T(8,128)(2,1)S(1)}, bf16[32,512]{1,0:T(8,128)(2,1)S(1)}, u32[]{:S(2)}, u32[]{:S(2)}) collective-permute-start(bf16[32,512]{1,0:T(8,128)(2,1)S(1)} %get-tuple-element.30), channel_id=1, source_target_pairs={{0,31},{1,2},{2,1},{3,4},{4,3},{5,6},{6,5},{7,8},{8,7},{9,10},{10,... | collective-permute-start | bytes 98312 | tf_op jit(solution)/shard_map/ppermute | solution.py:611
  8.6 4.3 %collective-permute-start.1 = (bf16[32,512]{1,0:T(8,128)(2,1)S(1)}, bf16[32,512]{1,0:T(8,128)(2,1)S(1)}, u32[]{:S(2)}, u32[]{:S(2)}) collective-permute-start(bf16[32,512]{1,0:T(8,128)(2,1)S(1)} %get-tuple-element.31), channel_id=1, source_target_pairs={{0,1},{1,0},{2,3},{3,2},{4,5},{5,4},{6,7},{7,6},{8,9},{9,8},{10,11... | collective-permute-start | bytes 98312 | tf_op jit(solution)/shard_map/ppermute | solution.py:611
  12.9 17.4 %copy-start.2 = (s32[256,256]{1,0:T(8,128)S(1)}, s32[256,256]{1,0:T(8,128)}, u32[]{:S(2)}) copy-start(s32[256,256]{1,0:T(8,128)} %dir_ref.5) | copy-start | bytes 786436
  12.9 17.4 %copy-start.3 = (f32[256,256]{1,0:T(8,128)S(1)}, f32[256,256]{1,0:T(8,128)}, u32[]{:S(2)}) copy-start(f32[256,256]{1,0:T(8,128)} %depth_ref.1) | copy-start | bytes 786436
  15.6 14.8 %copy-start = (f32[256,256]{1,0:T(8,128)S(1)}, f32[256,256]{1,0:T(8,128)}, u32[]{:S(2)}) copy-start(f32[256,256]{1,0:T(8,128)} %slope_ref.5) | copy-start | bytes 786436
  15.6 14.8 %copy-start.1 = (f32[256,256]{1,0:T(8,128)S(1)}, f32[256,256]{1,0:T(8,128)}, u32[]{:S(2)}) copy-start(f32[256,256]{1,0:T(8,128)} %rain_ref.5) | copy-start | bytes 786436
  31.3 6.9 %collective-permute-start.2 = (bf16[32,384]{1,0:T(8,128)(2,1)S(1)}, bf16[32,384]{1,0:T(8,128)(2,1)S(1)}, u32[]{:S(2)}, u32[]{:S(2)}) collective-permute-start(bf16[32,384]{1,0:T(8,128)(2,1)S(1)} %get-tuple-element.56), channel_id=1, source_target_pairs={{0,1},{1,0},{2,3},{3,2},{4,8},{5,9},{6,10},{7,11},{8,4},{9,5},{10,... | collective-permute-start | bytes 73736 | tf_op jit(solution)/shard_map/ppermute | solution.py:611
  31.4 6.8 %collective-permute-start.3 = (bf16[32,384]{1,0:T(8,128)(2,1)S(1)}, bf16[32,384]{1,0:T(8,128)(2,1)S(1)}, u32[]{:S(2)}, u32[]{:S(2)}) collective-permute-start(bf16[32,384]{1,0:T(8,128)(2,1)S(1)} %get-tuple-element.57), channel_id=1, source_target_pairs={{0,4},{1,5},{2,6},{3,7},{4,0},{5,1},{6,2},{7,3},{8,12},{9,13},{10,... | collective-permute-start | bytes 73736 | tf_op jit(solution)/shard_map/ppermute | solution.py:611

commit v19 on v17

--- a/solution.py
+++ b/solution.py
@@ -1,4 +1,5 @@
 import functools
+import math
 
 import jax
 import jax.numpy as jnp
@@ -511,7 +512,7 @@
     def substep(buf, new):
         for r in range(0, rows, chunk):
             level = level_at(buf, r, chunk)
-            power = level * jnp.exp((2.0 / 3.0) * jnp.log(jnp.maximum(jnp.abs(level), 1e-30)))
+            power = level * jnp.exp2((2.0 / 3.0 / math.log(2.0)) * jnp.log(jnp.maximum(jnp.abs(level), 1e-30)))
             from_right = pltpu.roll(power, cols - 1, 1)
             from_left = pltpu.roll(power, 1, 1)
             m = [m_ref[d, r : r + chunk, :] for d in range(8)]
@@ -538,7 +539,7 @@
 def flow_inner_kernel(level_ref, side_ref, slope_ref, dir_ref, rain_ref, out_ref, *scratch):
     rows, cols = level_ref.shape
     own = (level_ref[...], rain_ref[...], runoff_coef * jnp.sqrt(slope_ref[...]), dir_ref[...].astype(f32))
-    level_at = substeps(*[jnp.concatenate([x, side_ref[i]], 1) for i, x in enumerate(own)], *scratch, 16)
+    level_at = substeps(*[jnp.concatenate([x, side_ref[i]], 1) for i, x in enumerate(own)], *scratch, 32)
     out_ref[...] = level_at(0, 0, rows)[:, 0:cols]
 
 

time: 38.8 us -> 38.8 us (level)
  no operation moved by 1% of the time
where the time goes in v19:
time: 38.8 us; the launch traced here: 38.6 us
  Pallas kernels  15.7 us (40%)
  blocking collectives  14.8 us (38%)
  starting transfers between devices  7.35 us (19%)
  between operations  0.72 us (2%)
    all_to_all x1, blocking collectives, per_device(): lax.all_to_all(send.reshape(devices, send_rows, LANES), both, split_axis=...  14.8 us
    ppermute x4, starting transfers between devices, swaps(): out.append(lax.ppermute(x, both, sorted(to.items())))  7.35 us
    pallas_call x1, Pallas kernels, per_device(): pl.pallas_call(flow_inner_kernel, out_shape=jax.ShapeDtypeStruct((tile_ro...  4.35 us
    pallas_call x1, Pallas kernels, per_device(): pl.pallas_call(functools.partial(inner_kernel, devices, capacity), out_sh...  4.28 us
    pallas_call x1, Pallas kernels, per_device(): pl.pallas_call(functools.partial(ends_kernel, devices, capacity), out_sha...  2.65 us
    pallas_call x1, Pallas kernels, per_device(): pl.pallas_call(flow_ends_kernel, out_shape=jax.ShapeDtypeStruct((tile_row...  1.98 us
    pallas_call x1, Pallas kernels, per_device(): pl.pallas_call(edge_kernel, out_shape=(message, message, *[pltpu.VMEM(x.s...  1.55 us
    pallas_call x1, Pallas kernels, per_device(): pl.pallas_call(functools.partial(level_kernel, devices), out_shape=(jax.S...  0.92 us
  transfers between devices with their start and end apart: 4, of which 0 were waited for; matrix products, arithmetic and copies ran while one was open for 0% of the time, Pallas kernels for 22%

profile of v19, /device:TPU:0, one launch (start us, length us, event | category | flops | bytes accessed | tf_op | source)
XLA Modules:
  0.0 38.6 jit_solution(15371216848746036009)
XLA Ops:
  0.6 1.5 %edges.1 = (bf16[32,512]{1,0:T(8,128)(2,1)S(1)}, bf16[32,512]{1,0:T(8,128)(2,1)S(1)}, bf16[2,64,512]{2,1,0:T(8,128)(2,1)S(1)}, bf16[3,3,2,16]{3,2,1,0:T(2,128)(2...) custom-call(f32[256,256]{1,0:T(8,128)} %depth_ref.1, ...), custom_call_target="tpu_custom_call" | custom-call | tf_op jit(solution)/shard_map/edges/pallas_call | solution.py:628
  2.2 6.4 %collective-permute-start = (bf16[32,512]{1,0:T(8,128)(2,1)S(1)}, bf16[32,512]{1,0:T(8,128)(2,1)S(1)}, u32[]{:S(2)}, u32[]{:S(2)}) collective-permute-start(bf16[32,512]{1,0:T(8,128)(2,1)S(1)} %get-tuple-element.30), channel_id=1, source_target_pairs={{0,31},{1,2},{2,1},{3,4},{4,3},{5,6},{6,5},{7,8},{8,7},{9,10},{10,... | collective-permute-start | bytes 98312 | tf_op jit(solution)/shard_map/ppermute | solution.py:612
  8.6 0.0 collective-permute-start.1
  8.6 4.3 %inner.1 = (bf16[224,128]{1,0:T(8,128)(2,1)S(1)}, bf16[48,256]{1,0:T(8,128)(2,1)S(1)}, bf16[48,256]{1,0:T(8,128)(2,1)S(1)}, bf16[48,256]{1,0:T(8,128)(2,1)S(1)},...) custom-call(bf16[3,3,2,16]{3,2,1,0:T(2,128)(2,1)S(1)} %get-tuple-ele, ...), custom_call_target="tpu_custom_call" | custom-call | flops 8000000000 | bytes 4000000 | tf_op jit(solution)/shard_map/inner/pallas_call | solution.py:653
  12.9 0.0 collective-permute-done.second_swap_ref
  12.9 0.0 collective-permute-done.1.first_swap_ref
  12.9 0.0 copy-start.2
  12.9 0.0 copy-start.3
  13.0 2.6 %ends.1 = (bf16[64,512]{1,0:T(8,128)(2,1)}, bf16[1280,128]{1,0:T(8,128)(2,1)S(1)}) custom-call(bf16[32,512]{1,0:T(8,128)(2,1)S(1)} %collective-permute-done.second_swap_ref, bf16[32,512]{1,0:T(8,128)(2,1)S(1)} %collective-permute-done.1.first_swap_ref, bf16[224,128]{1,0:T(8,128)(2,1)S(1)} %get-tuple-element.41.w1_ref, ...), custom_call_target="tpu_custom_call" | custom-call | tf_op jit(solution)/shard_map/ends/pallas_call | solution.py:684
  15.6 0.0 copy-start
  15.6 0.0 copy-start.1
  15.6 14.8 %all_to_all.5 = bf16[32,40,128]{2,1,0:T(8,128)(2,1)S(1)} all-to-all(bf16[32,40,128]{2,1,0:T(8,128)(2,1)S(1)} %bitcast.15), channel_id=1, replica_groups=mesh['tx'=8,'ty'=4] {'tx','ty'}, dimensions={0} | all-to-all | bytes 655360 | tf_op jit(solution)/shard_map/all_to_all | solution.py:697
  30.4 0.0 copy-done.2
  30.4 0.0 copy-done.3
  30.4 0.0 copy-done
  30.4 0.0 copy-done.1
  30.4 0.9 %level.1 = (f32[256,256]{1,0:T(8,128)S(1)}, f32[4,256,128]{2,1,0:T(8,128)S(1)}, bf16[32,384]{1,0:T(8,128)(2,1)S(1)}, bf16[32,384]{1,0:T(8,128)(2,1)S(1)}) custom-call(bf16[1280,128]{1,0:T(8,128)(2,1)S(1)} %bitcast.14, bf16[32,512]{1,0:T(8,128)(2,1)S(1)} %collective-permute-done.second_swap_ref, bf16[32,512]{1,0:T(8,128)(2,1)S(1)} %collective-permute-done.1.first_swap_ref, ...), custom_call_target="tpu_custom_call" | custom-call | tf_op jit(solution)/shard_map/level/pallas_call | solution.py:703
  31.3 0.9 %collective-permute-start.2 = (bf16[32,384]{1,0:T(8,128)(2,1)S(1)}, bf16[32,384]{1,0:T(8,128)(2,1)S(1)}, u32[]{:S(2)}, u32[]{:S(2)}) collective-permute-start(bf16[32,384]{1,0:T(8,128)(2,1)S(1)} %get-tuple-element.56), channel_id=1, source_target_pairs={{0,4},{1,5},{2,6},{3,7},{4,0},{5,1},{6,2},{7,3},{8,12},{9,13},{10,... | collective-permute-start | bytes 73736 | tf_op jit(solution)/shard_map/ppermute | solution.py:612
  32.2 0.0 collective-permute-start.3
  32.2 4.4 %flow_inner.1.inner_ref = f32[256,256]{1,0:T(8,128)S(1)} custom-call(f32[256,256]{1,0:T(8,128)S(1)} %get-tuple-element.54.level_ref, f32[4,256,128]{2,1,0:T(8,128)S(1)} %get-tuple-element.55.side_ref, f32[256,256]{1,0:T(8,128)S(1)} %copy-done, s32[256,256]{1,0:T(8,128)S(1)} %copy-done.2, f32[256,256]{1,0:T(8,128)S(1)} %copy-done.1), custom_call_target="tpu_custom_call" | custom-call | flops 5000000000 | bytes 4000000 | tf_op jit(solution)/shard_map/flow_inner/pallas_call | solution.py:719
  36.6 0.0 collective-permute-done.2.first_swap_ref
  36.6 0.0 collective-permute-done.3.second_swap_ref
  36.6 2.0 %flow_ends.1 = f32[256,256]{1,0:T(8,128)} custom-call(f32[256,256]{1,0:T(8,128)S(1)} %flow_inner.1.inner_ref, f32[256,256]{1,0:T(8,128)S(1)} %get-tuple-element.54.level_ref, f32[4,256,128]{2,1,0:T(8,128)S(1)} %get-tuple-element.55.side_ref, f32[256,256]{1,0:T(8,128)S(1)} %copy-done, s32[256,256]{1,0:T(8,128)S(1)} %copy-done.2, f32[256,256]{1,0:T(8,128)S(1)} %copy-done.1, ...), custom_call_target="tpu_custom_call" | custom-call | tf_op jit(solution)/shard_map/flow_ends/pallas_call | solution.py:729
Async XLA Ops:
  2.2 10.7 %collective-permute-start = (bf16[32,512]{1,0:T(8,128)(2,1)S(1)}, bf16[32,512]{1,0:T(8,128)(2,1)S(1)}, u32[]{:S(2)}, u32[]{:S(2)}) collective-permute-start(bf16[32,512]{1,0:T(8,128)(2,1)S(1)} %get-tuple-element.30), channel_id=1, source_target_pairs={{0,31},{1,2},{2,1},{3,4},{4,3},{5,6},{6,5},{7,8},{8,7},{9,10},{10,... | collective-permute-start | bytes 98312 | tf_op jit(solution)/shard_map/ppermute | solution.py:612
  8.6 4.3 %collective-permute-start.1 = (bf16[32,512]{1,0:T(8,128)(2,1)S(1)}, bf16[32,512]{1,0:T(8,128)(2,1)S(1)}, u32[]{:S(2)}, u32[]{:S(2)}) collective-permute-start(bf16[32,512]{1,0:T(8,128)(2,1)S(1)} %get-tuple-element.31), channel_id=1, source_target_pairs={{0,1},{1,0},{2,3},{3,2},{4,5},{5,4},{6,7},{7,6},{8,9},{9,8},{10,11... | collective-permute-start | bytes 98312 | tf_op jit(solution)/shard_map/ppermute | solution.py:612
  12.9 17.4 %copy-start.2 = (s32[256,256]{1,0:T(8,128)S(1)}, s32[256,256]{1,0:T(8,128)}, u32[]{:S(2)}) copy-start(s32[256,256]{1,0:T(8,128)} %dir_ref.5) | copy-start | bytes 786436
  12.9 17.4 %copy-start.3 = (f32[256,256]{1,0:T(8,128)S(1)}, f32[256,256]{1,0:T(8,128)}, u32[]{:S(2)}) copy-start(f32[256,256]{1,0:T(8,128)} %depth_ref.1) | copy-start | bytes 786436
  15.6 14.8 %copy-start = (f32[256,256]{1,0:T(8,128)S(1)}, f32[256,256]{1,0:T(8,128)}, u32[]{:S(2)}) copy-start(f32[256,256]{1,0:T(8,128)} %slope_ref.5) | copy-start | bytes 786436
  15.6 14.8 %copy-start.1 = (f32[256,256]{1,0:T(8,128)S(1)}, f32[256,256]{1,0:T(8,128)}, u32[]{:S(2)}) copy-start(f32[256,256]{1,0:T(8,128)} %rain_ref.5) | copy-start | bytes 786436
  31.3 5.3 %collective-permute-start.2 = (bf16[32,384]{1,0:T(8,128)(2,1)S(1)}, bf16[32,384]{1,0:T(8,128)(2,1)S(1)}, u32[]{:S(2)}, u32[]{:S(2)}) collective-permute-start(bf16[32,384]{1,0:T(8,128)(2,1)S(1)} %get-tuple-element.56), channel_id=1, source_target_pairs={{0,4},{1,5},{2,6},{3,7},{4,0},{5,1},{6,2},{7,3},{8,12},{9,13},{10,... | collective-permute-start | bytes 73736 | tf_op jit(solution)/shard_map/ppermute | solution.py:612
  32.2 4.4 %collective-permute-start.3 = (bf16[32,384]{1,0:T(8,128)(2,1)S(1)}, bf16[32,384]{1,0:T(8,128)(2,1)S(1)}, u32[]{:S(2)}, u32[]{:S(2)}) collective-permute-start(bf16[32,384]{1,0:T(8,128)(2,1)S(1)} %get-tuple-element.57), channel_id=1, source_target_pairs={{0,1},{1,0},{2,3},{3,2},{4,8},{5,9},{6,10},{7,11},{8,4},{9,5},{10,... | collective-permute-start | bytes 73736 | tf_op jit(solution)/shard_map/ppermute | solution.py:612

commit v20 on v19

--- a/solution.py
+++ b/solution.py
@@ -146,24 +146,21 @@
     copies = [pltpu.make_async_copy(src, dst, sems.at[i]) for i, (src, dst) in enumerate(pairs)]
     for copy in copies:
         copy.start()
-    for copy in copies[0:5]:
-        copy.wait()
-    fields = (
-        depth_ref[...],
-        runoff_coef * jnp.sqrt(slope_ref[...]),
-        rain_ref[...],
-        dir_ref[...].astype(f32),
-    )
     zeros = jnp.zeros((8, px), f32)
+    strips = ([], [])
+    for i, ref in enumerate((depth_ref, slope_ref, rain_ref, dir_ref)):
+        copies[i].wait()
+        own = [ref[:, cols - LANES :].astype(f32), ref[:, 0:LANES].astype(f32)]
+        if i == 1:
+            own = [runoff_coef * jnp.sqrt(x) for x in own]
+        strips[0].append(jnp.transpose(own[0], (1, 0))[LANES - h :])
+        strips[1].append(jnp.transpose(own[1], (1, 0))[0:h])
+    copies[4].wait()
     messages = []
-    for at, lo, strip in (
-        (lines - 16, 16 - HALO_LINES, lambda x: jnp.transpose(x[:, cols - LANES :], (1, 0))[LANES - h :]),
-        (0, 0, lambda x: jnp.transpose(x[:, 0:LANES], (1, 0))[0:h]),
-    ):
+    for strip, at, lo in ((strips[0], lines - 16, 16 - HALO_LINES), (strips[1], 0, 0)):
         image = [sar_ref[ch, at : at + 16, :].astype(f32)[lo : lo + HALO_LINES] for ch in range(2)]
-        strips = [strip(x) for x in fields]
         messages.append(
-            jnp.concatenate([jnp.concatenate(strips[0:2], 1), jnp.concatenate(strips[2:4], 1), *image, zeros], 0)
+            jnp.concatenate([jnp.concatenate(strip[0:2], 1), jnp.concatenate(strip[2:4], 1), *image, zeros], 0)
         )
     first, second = in_turn(even, *messages)
     first_swap_ref[...] = first.astype(bf16)
@@ -539,7 +536,7 @@
 def flow_inner_kernel(level_ref, side_ref, slope_ref, dir_ref, rain_ref, out_ref, *scratch):
     rows, cols = level_ref.shape
     own = (level_ref[...], rain_ref[...], runoff_coef * jnp.sqrt(slope_ref[...]), dir_ref[...].astype(f32))
-    level_at = substeps(*[jnp.concatenate([x, side_ref[i]], 1) for i, x in enumerate(own)], *scratch, 32)
+    level_at = substeps(*[jnp.concatenate([x, side_ref[i]], 1) for i, x in enumerate(own)], *scratch, 64)
     out_ref[...] = level_at(0, 0, rows)[:, 0:cols]
 
 
@@ -559,7 +556,7 @@
                 own = runoff_coef * jnp.sqrt(own)
             ends.append(jnp.concatenate([own, side_ref[i, at, :]], 1))
         fields.append(jnp.concatenate([above[i * h : (i + 1) * h], *ends, below[i * h : (i + 1) * h]], 0))
-    level_at = substeps(*fields, *scratch, 16)
+    level_at = substeps(*fields, *scratch, 6 * h)
     out_ref[h : rows - h, :] = inner_ref[h : rows - h, :]
     out_ref[0:h, :] = level_at(0, h, h)[:, 0:cols]
     out_ref[rows - h :, :] = level_at(0, 4 * h, h)[:, 0:cols]

time: 38.8 us -> 38.9 us (level)
  transfers between devices with their start and end apart: 4 -> 4, of which waited for: 0 -> 0; matrix products, arithmetic and copies ran while one was open for 0% -> 0% of each run, Pallas kernels for 22% -> 23%
where the time goes in v20:
time: 38.9 us; the launch traced here: 38.6 us
  Pallas kernels  15.8 us (41%)
  blocking collectives  14.8 us (38%)
  starting transfers between devices  7.35 us (19%)
  between operations  0.72 us (2%)
    all_to_all x1, blocking collectives, per_device(): lax.all_to_all(send.reshape(devices, send_rows, LANES), both, split_axis=...  14.8 us
    ppermute x4, starting transfers between devices, swaps(): out.append(lax.ppermute(x, both, sorted(to.items())))  7.35 us
    pallas_call x1, Pallas kernels, per_device(): pl.pallas_call(flow_inner_kernel, out_shape=jax.ShapeDtypeStruct((tile_ro...  4.44 us
    pallas_call x1, Pallas kernels, per_device(): pl.pallas_call(functools.partial(inner_kernel, devices, capacity), out_sh...  4.28 us
    pallas_call x1, Pallas kernels, per_device(): pl.pallas_call(functools.partial(ends_kernel, devices, capacity), out_sha...  2.65 us
    pallas_call x1, Pallas kernels, per_device(): pl.pallas_call(flow_ends_kernel, out_shape=jax.ShapeDtypeStruct((tile_row...  1.98 us
    pallas_call x1, Pallas kernels, per_device(): pl.pallas_call(edge_kernel, out_shape=(message, message, *[pltpu.VMEM(x.s...  1.53 us
    pallas_call x1, Pallas kernels, per_device(): pl.pallas_call(functools.partial(level_kernel, devices), out_shape=(jax.S...  0.92 us
  transfers between devices with their start and end apart: 4, of which 0 were waited for; matrix products, arithmetic and copies ran while one was open for 0% of the time, Pallas kernels for 23%

profile of v20, /device:TPU:0, one launch (start us, length us, event | category | flops | bytes accessed | tf_op | source)
XLA Modules:
  0.0 38.6 jit_solution(7286959276849056038)
XLA Ops:
  0.6 1.5 %edges.1 = (bf16[32,512]{1,0:T(8,128)(2,1)S(1)}, bf16[32,512]{1,0:T(8,128)(2,1)S(1)}, bf16[2,64,512]{2,1,0:T(8,128)(2,1)S(1)}, bf16[3,3,2,16]{3,2,1,0:T(2,128)(2...) custom-call(f32[256,256]{1,0:T(8,128)} %depth_ref.1, ...), custom_call_target="tpu_custom_call" | custom-call | tf_op jit(solution)/shard_map/edges/pallas_call | solution.py:625
  2.2 6.4 %collective-permute-start = (bf16[32,512]{1,0:T(8,128)(2,1)S(1)}, bf16[32,512]{1,0:T(8,128)(2,1)S(1)}, u32[]{:S(2)}, u32[]{:S(2)}) collective-permute-start(bf16[32,512]{1,0:T(8,128)(2,1)S(1)} %get-tuple-element.30), channel_id=1, source_target_pairs={{0,31},{1,2},{2,1},{3,4},{4,3},{5,6},{6,5},{7,8},{8,7},{9,10},{10,... | collective-permute-start | bytes 98312 | tf_op jit(solution)/shard_map/ppermute | solution.py:609
  8.6 0.0 collective-permute-start.1
  8.6 4.3 %inner.1 = (bf16[224,128]{1,0:T(8,128)(2,1)S(1)}, bf16[48,256]{1,0:T(8,128)(2,1)S(1)}, bf16[48,256]{1,0:T(8,128)(2,1)S(1)}, bf16[48,256]{1,0:T(8,128)(2,1)S(1)},...) custom-call(bf16[3,3,2,16]{3,2,1,0:T(2,128)(2,1)S(1)} %get-tuple-ele, ...), custom_call_target="tpu_custom_call" | custom-call | flops 8000000000 | bytes 4000000 | tf_op jit(solution)/shard_map/inner/pallas_call | solution.py:650
  12.9 0.0 collective-permute-done.second_swap_ref
  12.9 0.0 collective-permute-done.1.first_swap_ref
  12.9 0.0 copy-start.2
  12.9 0.0 copy-start.3
  12.9 2.6 %ends.1 = (bf16[64,512]{1,0:T(8,128)(2,1)}, bf16[1280,128]{1,0:T(8,128)(2,1)S(1)}) custom-call(bf16[32,512]{1,0:T(8,128)(2,1)S(1)} %collective-permute-done.second_swap_ref, bf16[32,512]{1,0:T(8,128)(2,1)S(1)} %collective-permute-done.1.first_swap_ref, bf16[224,128]{1,0:T(8,128)(2,1)S(1)} %get-tuple-element.41.w1_ref, ...), custom_call_target="tpu_custom_call" | custom-call | tf_op jit(solution)/shard_map/ends/pallas_call | solution.py:681
  15.6 0.0 copy-start
  15.6 0.0 copy-start.1
  15.6 14.8 %all_to_all.5 = bf16[32,40,128]{2,1,0:T(8,128)(2,1)S(1)} all-to-all(bf16[32,40,128]{2,1,0:T(8,128)(2,1)S(1)} %bitcast.15), channel_id=1, replica_groups=mesh['tx'=8,'ty'=4] {'tx','ty'}, dimensions={0} | all-to-all | bytes 655360 | tf_op jit(solution)/shard_map/all_to_all | solution.py:694
  30.3 0.0 copy-done.2
  30.4 0.0 copy-done.3
  30.4 0.0 copy-done
  30.4 0.0 copy-done.1
  30.4 0.9 %level.1 = (f32[256,256]{1,0:T(8,128)S(1)}, f32[4,256,128]{2,1,0:T(8,128)S(1)}, bf16[32,384]{1,0:T(8,128)(2,1)S(1)}, bf16[32,384]{1,0:T(8,128)(2,1)S(1)}) custom-call(bf16[1280,128]{1,0:T(8,128)(2,1)S(1)} %bitcast.14, bf16[32,512]{1,0:T(8,128)(2,1)S(1)} %collective-permute-done.second_swap_ref, bf16[32,512]{1,0:T(8,128)(2,1)S(1)} %collective-permute-done.1.first_swap_ref, ...), custom_call_target="tpu_custom_call" | custom-call | tf_op jit(solution)/shard_map/level/pallas_call | solution.py:700
  31.3 0.9 %collective-permute-start.2 = (bf16[32,384]{1,0:T(8,128)(2,1)S(1)}, bf16[32,384]{1,0:T(8,128)(2,1)S(1)}, u32[]{:S(2)}, u32[]{:S(2)}) collective-permute-start(bf16[32,384]{1,0:T(8,128)(2,1)S(1)} %get-tuple-element.56), channel_id=1, source_target_pairs={{0,4},{1,5},{2,6},{3,7},{4,0},{5,1},{6,2},{7,3},{8,12},{9,13},{10,... | collective-permute-start | bytes 73736 | tf_op jit(solution)/shard_map/ppermute | solution.py:609
  32.2 0.0 collective-permute-start.3
  32.2 4.4 %flow_inner.1.inner_ref = f32[256,256]{1,0:T(8,128)S(1)} custom-call(f32[256,256]{1,0:T(8,128)S(1)} %get-tuple-element.54.level_ref, f32[4,256,128]{2,1,0:T(8,128)S(1)} %get-tuple-element.55.side_ref, f32[256,256]{1,0:T(8,128)S(1)} %copy-done, s32[256,256]{1,0:T(8,128)S(1)} %copy-done.2, f32[256,256]{1,0:T(8,128)S(1)} %copy-done.1), custom_call_target="tpu_custom_call" | custom-call | flops 5000000000 | bytes 4000000 | tf_op jit(solution)/shard_map/flow_inner/pallas_call | solution.py:716
  36.6 0.0 collective-permute-done.2.first_swap_ref
  36.7 0.0 collective-permute-done.3.second_swap_ref
  36.7 2.0 %flow_ends.1 = f32[256,256]{1,0:T(8,128)} custom-call(f32[256,256]{1,0:T(8,128)S(1)} %flow_inner.1.inner_ref, f32[256,256]{1,0:T(8,128)S(1)} %get-tuple-element.54.level_ref, f32[4,256,128]{2,1,0:T(8,128)S(1)} %get-tuple-element.55.side_ref, f32[256,256]{1,0:T(8,128)S(1)} %copy-done, s32[256,256]{1,0:T(8,128)S(1)} %copy-done.2, f32[256,256]{1,0:T(8,128)S(1)} %copy-done.1, ...), custom_call_target="tpu_custom_call" | custom-call | tf_op jit(solution)/shard_map/flow_ends/pallas_call | solution.py:726
Async XLA Ops:
  2.2 10.7 %collective-permute-start = (bf16[32,512]{1,0:T(8,128)(2,1)S(1)}, bf16[32,512]{1,0:T(8,128)(2,1)S(1)}, u32[]{:S(2)}, u32[]{:S(2)}) collective-permute-start(bf16[32,512]{1,0:T(8,128)(2,1)S(1)} %get-tuple-element.30), channel_id=1, source_target_pairs={{0,31},{1,2},{2,1},{3,4},{4,3},{5,6},{6,5},{7,8},{8,7},{9,10},{10,... | collective-permute-start | bytes 98312 | tf_op jit(solution)/shard_map/ppermute | solution.py:609
  8.6 4.3 %collective-permute-start.1 = (bf16[32,512]{1,0:T(8,128)(2,1)S(1)}, bf16[32,512]{1,0:T(8,128)(2,1)S(1)}, u32[]{:S(2)}, u32[]{:S(2)}) collective-permute-start(bf16[32,512]{1,0:T(8,128)(2,1)S(1)} %get-tuple-element.31), channel_id=1, source_target_pairs={{0,1},{1,0},{2,3},{3,2},{4,5},{5,4},{6,7},{7,6},{8,9},{9,8},{10,11... | collective-permute-start | bytes 98312 | tf_op jit(solution)/shard_map/ppermute | solution.py:609
  12.9 17.4 %copy-start.2 = (s32[256,256]{1,0:T(8,128)S(1)}, s32[256,256]{1,0:T(8,128)}, u32[]{:S(2)}) copy-start(s32[256,256]{1,0:T(8,128)} %dir_ref.5) | copy-start | bytes 786436
  12.9 17.4 %copy-start.3 = (f32[256,256]{1,0:T(8,128)S(1)}, f32[256,256]{1,0:T(8,128)}, u32[]{:S(2)}) copy-start(f32[256,256]{1,0:T(8,128)} %depth_ref.1) | copy-start | bytes 786436
  15.6 14.8 %copy-start = (f32[256,256]{1,0:T(8,128)S(1)}, f32[256,256]{1,0:T(8,128)}, u32[]{:S(2)}) copy-start(f32[256,256]{1,0:T(8,128)} %slope_ref.5) | copy-start | bytes 786436
  15.6 14.8 %copy-start.1 = (f32[256,256]{1,0:T(8,128)S(1)}, f32[256,256]{1,0:T(8,128)}, u32[]{:S(2)}) copy-start(f32[256,256]{1,0:T(8,128)} %rain_ref.5) | copy-start | bytes 786436
  31.3 5.4 %collective-permute-start.2 = (bf16[32,384]{1,0:T(8,128)(2,1)S(1)}, bf16[32,384]{1,0:T(8,128)(2,1)S(1)}, u32[]{:S(2)}, u32[]{:S(2)}) collective-permute-start(bf16[32,384]{1,0:T(8,128)(2,1)S(1)} %get-tuple-element.56), channel_id=1, source_target_pairs={{0,4},{1,5},{2,6},{3,7},{4,0},{5,1},{6,2},{7,3},{8,12},{9,13},{10,... | collective-permute-start | bytes 73736 | tf_op jit(solution)/shard_map/ppermute | solution.py:609
  32.2 4.5 %collective-permute-start.3 = (bf16[32,384]{1,0:T(8,128)(2,1)S(1)}, bf16[32,384]{1,0:T(8,128)(2,1)S(1)}, u32[]{:S(2)}, u32[]{:S(2)}) collective-permute-start(bf16[32,384]{1,0:T(8,128)(2,1)S(1)} %get-tuple-element.57), channel_id=1, source_target_pairs={{0,1},{1,0},{2,3},{3,2},{4,8},{5,9},{6,10},{7,11},{8,4},{9,5},{10,... | collective-permute-start | bytes 73736 | tf_op jit(solution)/shard_map/ppermute | solution.py:609

commit v21 on v20

--- a/solution.py
+++ b/solution.py
@@ -436,15 +436,27 @@
         return dot(jnp.where(spread, rows, 0.0).astype(bf16), take.astype(bf16)).astype(bf16)
 
     lane = iota((1, k), 1)
-    offset = rem(lane, 2) + tile_rows * rem(quo(lane, 2), 2)
     info = jnp.broadcast_to(extra[:, 2:3], (devices, n, LANES)).reshape(k, LANES)
     info = jnp.where(rem(iota((k, LANES), 1), n) == entry, info, 0.0).astype(bf16)
     turns = (quo(iota((LANES, LANES), 0), n) == iota((LANES, LANES), 1)).astype(bf16)
     lines = transposed(dot(info, turns))
 
+    row = iota((tile_rows, LANES), 0).astype(f32).astype(bf16)
+    one = jnp.ones((tile_rows, LANES), bf16)
+    nil = jnp.zeros((tile_rows, LANES), bf16)
+
     def placer(turn):
-        target = lines[turn : turn + 1].astype(jnp.int32) + offset
-        return jnp.where(iota((2 * tile_rows, k), 0) == target, 1.0, 0.0).astype(bf16)
+        line = lines[turn : turn + 1] + rem(lane, 2).astype(f32)
+        parts = []
+        for quantity in range(2):
+            target = jnp.where(rem(quo(lane, 2), 2) == quantity, line, -1.0)
+            pieces = []
+            for at in range(0, k, LANES):
+                tile = jnp.broadcast_to(target[:, at : at + LANES], (CH, LANES)).astype(bf16)
+                tile = jnp.broadcast_to(tile[None], (tile_rows // CH, CH, LANES)).reshape(tile_rows, LANES)
+                pieces.append(jnp.where(row == tile, one, nil))
+            parts.append(jnp.concatenate(pieces, 1))
+        return jnp.concatenate(parts, 0)
 
     summed = dot(placer(0), main.astype(bf16))
     summed_side = dot(placer(1), strip(0, 0)) + dot(placer(2), strip(1, LANES - h))
@@ -536,7 +548,7 @@
 def flow_inner_kernel(level_ref, side_ref, slope_ref, dir_ref, rain_ref, out_ref, *scratch):
     rows, cols = level_ref.shape
     own = (level_ref[...], rain_ref[...], runoff_coef * jnp.sqrt(slope_ref[...]), dir_ref[...].astype(f32))
-    level_at = substeps(*[jnp.concatenate([x, side_ref[i]], 1) for i, x in enumerate(own)], *scratch, 64)
+    level_at = substeps(*[jnp.concatenate([x, side_ref[i]], 1) for i, x in enumerate(own)], *scratch, 32)
     out_ref[...] = level_at(0, 0, rows)[:, 0:cols]
 
 

time: 38.9 us -> 38.7 us (level)
  transfers between devices with their start and end apart: 4 -> 4, of which waited for: 0 -> 0; matrix products, arithmetic and copies ran while one was open for 0% -> 0% of each run, Pallas kernels for 23% -> 22%
where the time goes in v21:
time: 38.7 us; the launch traced here: 38.5 us
  Pallas kernels  15.6 us (40%)
  blocking collectives  14.8 us (38%)
  starting transfers between devices  7.35 us (19%)
  between operations  0.72 us (2%)
    all_to_all x1, blocking collectives, per_device(): lax.all_to_all(send.reshape(devices, send_rows, LANES), both, split_axis=...  14.8 us
    ppermute x4, starting transfers between devices, swaps(): out.append(lax.ppermute(x, both, sorted(to.items())))  7.35 us
    pallas_call x1, Pallas kernels, per_device(): pl.pallas_call(flow_inner_kernel, out_shape=jax.ShapeDtypeStruct((tile_ro...  4.35 us
    pallas_call x1, Pallas kernels, per_device(): pl.pallas_call(functools.partial(inner_kernel, devices, capacity), out_sh...  4.28 us
    pallas_call x1, Pallas kernels, per_device(): pl.pallas_call(functools.partial(ends_kernel, devices, capacity), out_sha...  2.65 us
    pallas_call x1, Pallas kernels, per_device(): pl.pallas_call(flow_ends_kernel, out_shape=jax.ShapeDtypeStruct((tile_row...  1.98 us
    pallas_call x1, Pallas kernels, per_device(): pl.pallas_call(edge_kernel, out_shape=(message, message, *[pltpu.VMEM(x.s...  1.53 us
    pallas_call x1, Pallas kernels, per_device(): pl.pallas_call(functools.partial(level_kernel, devices), out_shape=(jax.S...  0.87 us
  transfers between devices with their start and end apart: 4, of which 0 were waited for; matrix products, arithmetic and copies ran while one was open for 0% of the time, Pallas kernels for 22%

profile of v21, /device:TPU:0, one launch (start us, length us, event | category | flops | bytes accessed | tf_op | source)
XLA Modules:
  0.0 38.5 jit_solution(15056729138981599579)
XLA Ops:
  0.6 1.5 %edges.1 = (bf16[32,512]{1,0:T(8,128)(2,1)S(1)}, bf16[32,512]{1,0:T(8,128)(2,1)S(1)}, bf16[2,64,512]{2,1,0:T(8,128)(2,1)S(1)}, bf16[3,3,2,16]{3,2,1,0:T(2,128)(2...) custom-call(f32[256,256]{1,0:T(8,128)} %depth_ref.1, ...), custom_call_target="tpu_custom_call" | custom-call | tf_op jit(solution)/shard_map/edges/pallas_call | solution.py:637
  2.2 6.4 %collective-permute-start = (bf16[32,512]{1,0:T(8,128)(2,1)S(1)}, bf16[32,512]{1,0:T(8,128)(2,1)S(1)}, u32[]{:S(2)}, u32[]{:S(2)}) collective-permute-start(bf16[32,512]{1,0:T(8,128)(2,1)S(1)} %get-tuple-element.30), channel_id=1, source_target_pairs={{0,31},{1,2},{2,1},{3,4},{4,3},{5,6},{6,5},{7,8},{8,7},{9,10},{10,... | collective-permute-start | bytes 98312 | tf_op jit(solution)/shard_map/ppermute | solution.py:621
  8.6 0.0 collective-permute-start.1
  8.6 4.3 %inner.1 = (bf16[224,128]{1,0:T(8,128)(2,1)S(1)}, bf16[48,256]{1,0:T(8,128)(2,1)S(1)}, bf16[48,256]{1,0:T(8,128)(2,1)S(1)}, bf16[48,256]{1,0:T(8,128)(2,1)S(1)},...) custom-call(bf16[3,3,2,16]{3,2,1,0:T(2,128)(2,1)S(1)} %get-tuple-ele, ...), custom_call_target="tpu_custom_call" | custom-call | flops 8000000000 | bytes 4000000 | tf_op jit(solution)/shard_map/inner/pallas_call | solution.py:662
  12.9 0.0 collective-permute-done.second_swap_ref
  12.9 0.0 collective-permute-done.1.first_swap_ref
  12.9 0.0 copy-start.2
  12.9 0.0 copy-start.3
  12.9 2.6 %ends.1 = (bf16[64,512]{1,0:T(8,128)(2,1)}, bf16[1280,128]{1,0:T(8,128)(2,1)S(1)}) custom-call(bf16[32,512]{1,0:T(8,128)(2,1)S(1)} %collective-permute-done.second_swap_ref, bf16[32,512]{1,0:T(8,128)(2,1)S(1)} %collective-permute-done.1.first_swap_ref, bf16[224,128]{1,0:T(8,128)(2,1)S(1)} %get-tuple-element.41.w1_ref, ...), custom_call_target="tpu_custom_call" | custom-call | tf_op jit(solution)/shard_map/ends/pallas_call | solution.py:693
  15.6 0.0 copy-start
  15.6 0.0 copy-start.1
  15.6 14.8 %all_to_all.5 = bf16[32,40,128]{2,1,0:T(8,128)(2,1)S(1)} all-to-all(bf16[32,40,128]{2,1,0:T(8,128)(2,1)S(1)} %bitcast.15), channel_id=1, replica_groups=mesh['tx'=8,'ty'=4] {'tx','ty'}, dimensions={0} | all-to-all | bytes 655360 | tf_op jit(solution)/shard_map/all_to_all | solution.py:706
  30.3 0.0 copy-done.2
  30.4 0.0 copy-done.3
  30.4 0.0 copy-done
  30.4 0.0 copy-done.1
  30.4 0.9 %level.1 = (f32[256,256]{1,0:T(8,128)S(1)}, f32[4,256,128]{2,1,0:T(8,128)S(1)}, bf16[32,384]{1,0:T(8,128)(2,1)S(1)}, bf16[32,384]{1,0:T(8,128)(2,1)S(1)}) custom-call(bf16[1280,128]{1,0:T(8,128)(2,1)S(1)} %bitcast.14, bf16[32,512]{1,0:T(8,128)(2,1)S(1)} %collective-permute-done.second_swap_ref, bf16[32,512]{1,0:T(8,128)(2,1)S(1)} %collective-permute-done.1.first_swap_ref, ...), custom_call_target="tpu_custom_call" | custom-call | tf_op jit(solution)/shard_map/level/pallas_call | solution.py:712
  31.2 0.9 %collective-permute-start.2 = (bf16[32,384]{1,0:T(8,128)(2,1)S(1)}, bf16[32,384]{1,0:T(8,128)(2,1)S(1)}, u32[]{:S(2)}, u32[]{:S(2)}) collective-permute-start(bf16[32,384]{1,0:T(8,128)(2,1)S(1)} %get-tuple-element.56), channel_id=1, source_target_pairs={{0,4},{1,5},{2,6},{3,7},{4,0},{5,1},{6,2},{7,3},{8,12},{9,13},{10,... | collective-permute-start | bytes 73736 | tf_op jit(solution)/shard_map/ppermute | solution.py:621
  32.2 0.0 collective-permute-start.3
  32.2 4.4 %flow_inner.1.inner_ref = f32[256,256]{1,0:T(8,128)S(1)} custom-call(f32[256,256]{1,0:T(8,128)S(1)} %get-tuple-element.54.level_ref, f32[4,256,128]{2,1,0:T(8,128)S(1)} %get-tuple-element.55.side_ref, f32[256,256]{1,0:T(8,128)S(1)} %copy-done, s32[256,256]{1,0:T(8,128)S(1)} %copy-done.2, f32[256,256]{1,0:T(8,128)S(1)} %copy-done.1), custom_call_target="tpu_custom_call" | custom-call | flops 5000000000 | bytes 4000000 | tf_op jit(solution)/shard_map/flow_inner/pallas_call | solution.py:728
  36.5 0.0 collective-permute-done.2.first_swap_ref
  36.5 0.0 collective-permute-done.3.second_swap_ref
  36.5 2.0 %flow_ends.1 = f32[256,256]{1,0:T(8,128)} custom-call(f32[256,256]{1,0:T(8,128)S(1)} %flow_inner.1.inner_ref, f32[256,256]{1,0:T(8,128)S(1)} %get-tuple-element.54.level_ref, f32[4,256,128]{2,1,0:T(8,128)S(1)} %get-tuple-element.55.side_ref, f32[256,256]{1,0:T(8,128)S(1)} %copy-done, s32[256,256]{1,0:T(8,128)S(1)} %copy-done.2, f32[256,256]{1,0:T(8,128)S(1)} %copy-done.1, ...), custom_call_target="tpu_custom_call" | custom-call | tf_op jit(solution)/shard_map/flow_ends/pallas_call | solution.py:738
Async XLA Ops:
  2.2 10.7 %collective-permute-start = (bf16[32,512]{1,0:T(8,128)(2,1)S(1)}, bf16[32,512]{1,0:T(8,128)(2,1)S(1)}, u32[]{:S(2)}, u32[]{:S(2)}) collective-permute-start(bf16[32,512]{1,0:T(8,128)(2,1)S(1)} %get-tuple-element.30), channel_id=1, source_target_pairs={{0,31},{1,2},{2,1},{3,4},{4,3},{5,6},{6,5},{7,8},{8,7},{9,10},{10,... | collective-permute-start | bytes 98312 | tf_op jit(solution)/shard_map/ppermute | solution.py:621
  8.6 4.3 %collective-permute-start.1 = (bf16[32,512]{1,0:T(8,128)(2,1)S(1)}, bf16[32,512]{1,0:T(8,128)(2,1)S(1)}, u32[]{:S(2)}, u32[]{:S(2)}) collective-permute-start(bf16[32,512]{1,0:T(8,128)(2,1)S(1)} %get-tuple-element.31), channel_id=1, source_target_pairs={{0,1},{1,0},{2,3},{3,2},{4,5},{5,4},{6,7},{7,6},{8,9},{9,8},{10,11... | collective-permute-start | bytes 98312 | tf_op jit(solution)/shard_map/ppermute | solution.py:621
  12.9 17.4 %copy-start.2 = (s32[256,256]{1,0:T(8,128)S(1)}, s32[256,256]{1,0:T(8,128)}, u32[]{:S(2)}) copy-start(s32[256,256]{1,0:T(8,128)} %dir_ref.5) | copy-start | bytes 786436
  12.9 17.4 %copy-start.3 = (f32[256,256]{1,0:T(8,128)S(1)}, f32[256,256]{1,0:T(8,128)}, u32[]{:S(2)}) copy-start(f32[256,256]{1,0:T(8,128)} %depth_ref.1) | copy-start | bytes 786436
  15.6 14.8 %copy-start = (f32[256,256]{1,0:T(8,128)S(1)}, f32[256,256]{1,0:T(8,128)}, u32[]{:S(2)}) copy-start(f32[256,256]{1,0:T(8,128)} %slope_ref.5) | copy-start | bytes 786436
  15.6 14.8 %copy-start.1 = (f32[256,256]{1,0:T(8,128)S(1)}, f32[256,256]{1,0:T(8,128)}, u32[]{:S(2)}) copy-start(f32[256,256]{1,0:T(8,128)} %rain_ref.5) | copy-start | bytes 786436
  31.2 5.3 %collective-permute-start.2 = (bf16[32,384]{1,0:T(8,128)(2,1)S(1)}, bf16[32,384]{1,0:T(8,128)(2,1)S(1)}, u32[]{:S(2)}, u32[]{:S(2)}) collective-permute-start(bf16[32,384]{1,0:T(8,128)(2,1)S(1)} %get-tuple-element.56), channel_id=1, source_target_pairs={{0,4},{1,5},{2,6},{3,7},{4,0},{5,1},{6,2},{7,3},{8,12},{9,13},{10,... | collective-permute-start | bytes 73736 | tf_op jit(solution)/shard_map/ppermute | solution.py:621
  32.2 4.4 %collective-permute-start.3 = (bf16[32,384]{1,0:T(8,128)(2,1)S(1)}, bf16[32,384]{1,0:T(8,128)(2,1)S(1)}, u32[]{:S(2)}, u32[]{:S(2)}) collective-permute-start(bf16[32,384]{1,0:T(8,128)(2,1)S(1)} %get-tuple-element.57), channel_id=1, source_target_pairs={{0,1},{1,0},{2,3},{3,2},{4,8},{5,9},{6,10},{7,11},{8,4},{9,5},{10,... | collective-permute-start | bytes 73736 | tf_op jit(solution)/shard_map/ppermute | solution.py:621

commit v22 on v21

--- a/solution.py
+++ b/solution.py
@@ -537,7 +537,7 @@
         substep(1, 0)
         return carry
 
-    if rows > LANES:
+    if rows > 8 * LANES:
         lax.fori_loop(0, SUBSTEPS // 2, substep_pair, 0)
     else:
         for i in range(SUBSTEPS // 2):

time: 38.7 us -> 39 us (level)
  transfers between devices with their start and end apart: 4 -> 4, of which waited for: 0 -> 0; matrix products, arithmetic and copies ran while one was open for 0% -> 0% of each run, Pallas kernels for 22% -> 23%
where the time goes in v22:
time: 39 us; the launch traced here: 38.8 us
  Pallas kernels  15.9 us (41%)
  blocking collectives  14.8 us (38%)
  starting transfers between devices  7.35 us (19%)
  between operations  0.72 us (2%)
    all_to_all x1, blocking collectives, per_device(): lax.all_to_all(send.reshape(devices, send_rows, LANES), both, split_axis=...  14.8 us
    ppermute x4, starting transfers between devices, swaps(): out.append(lax.ppermute(x, both, sorted(to.items())))  7.35 us
    pallas_call x1, Pallas kernels, per_device(): pl.pallas_call(flow_inner_kernel, out_shape=jax.ShapeDtypeStruct((tile_ro...  4.59 us
    pallas_call x1, Pallas kernels, per_device(): pl.pallas_call(functools.partial(inner_kernel, devices, capacity), out_sh...  4.29 us
    pallas_call x1, Pallas kernels, per_device(): pl.pallas_call(functools.partial(ends_kernel, devices, capacity), out_sha...  2.64 us
    pallas_call x1, Pallas kernels, per_device(): pl.pallas_call(flow_ends_kernel, out_shape=jax.ShapeDtypeStruct((tile_row...  1.98 us
    pallas_call x1, Pallas kernels, per_device(): pl.pallas_call(edge_kernel, out_shape=(message, message, *[pltpu.VMEM(x.s...  1.53 us
    pallas_call x1, Pallas kernels, per_device(): pl.pallas_call(functools.partial(level_kernel, devices), out_shape=(jax.S...  0.87 us
  transfers between devices with their start and end apart: 4, of which 0 were waited for; matrix products, arithmetic and copies ran while one was open for 0% of the time, Pallas kernels for 23%

profile of v22, /device:TPU:0, one launch (start us, length us, event | category | flops | bytes accessed | tf_op | source)
XLA Modules:
  0.0 38.8 jit_solution(961080952230521283)
XLA Ops:
  0.6 1.5 %edges.1 = (bf16[32,512]{1,0:T(8,128)(2,1)S(1)}, bf16[32,512]{1,0:T(8,128)(2,1)S(1)}, bf16[2,64,512]{2,1,0:T(8,128)(2,1)S(1)}, bf16[3,3,2,16]{3,2,1,0:T(2,128)(2...) custom-call(f32[256,256]{1,0:T(8,128)} %depth_ref.1, ...), custom_call_target="tpu_custom_call" | custom-call | tf_op jit(solution)/shard_map/edges/pallas_call | solution.py:637
  2.2 6.4 %collective-permute-start = (bf16[32,512]{1,0:T(8,128)(2,1)S(1)}, bf16[32,512]{1,0:T(8,128)(2,1)S(1)}, u32[]{:S(2)}, u32[]{:S(2)}) collective-permute-start(bf16[32,512]{1,0:T(8,128)(2,1)S(1)} %get-tuple-element.30), channel_id=1, source_target_pairs={{0,31},{1,2},{2,1},{3,4},{4,3},{5,6},{6,5},{7,8},{8,7},{9,10},{10,... | collective-permute-start | bytes 98312 | tf_op jit(solution)/shard_map/ppermute | solution.py:621
  8.6 0.0 collective-permute-start.1
  8.6 4.3 %inner.1 = (bf16[224,128]{1,0:T(8,128)(2,1)S(1)}, bf16[48,256]{1,0:T(8,128)(2,1)S(1)}, bf16[48,256]{1,0:T(8,128)(2,1)S(1)}, bf16[48,256]{1,0:T(8,128)(2,1)S(1)},...) custom-call(bf16[3,3,2,16]{3,2,1,0:T(2,128)(2,1)S(1)} %get-tuple-ele, ...), custom_call_target="tpu_custom_call" | custom-call | flops 8000000000 | bytes 4000000 | tf_op jit(solution)/shard_map/inner/pallas_call | solution.py:662
  12.9 0.0 collective-permute-done.second_swap_ref
  12.9 0.0 collective-permute-done.1.first_swap_ref
  12.9 0.0 copy-start.2
  12.9 0.0 copy-start.3
  12.9 2.6 %ends.1 = (bf16[64,512]{1,0:T(8,128)(2,1)}, bf16[1280,128]{1,0:T(8,128)(2,1)S(1)}) custom-call(bf16[32,512]{1,0:T(8,128)(2,1)S(1)} %collective-permute-done.second_swap_ref, bf16[32,512]{1,0:T(8,128)(2,1)S(1)} %collective-permute-done.1.first_swap_ref, bf16[224,128]{1,0:T(8,128)(2,1)S(1)} %get-tuple-element.41.w1_ref, ...), custom_call_target="tpu_custom_call" | custom-call | tf_op jit(solution)/shard_map/ends/pallas_call | solution.py:693
  15.6 0.0 copy-start
  15.6 0.0 copy-start.1
  15.6 14.8 %all_to_all.5 = bf16[32,40,128]{2,1,0:T(8,128)(2,1)S(1)} all-to-all(bf16[32,40,128]{2,1,0:T(8,128)(2,1)S(1)} %bitcast.15), channel_id=1, replica_groups=mesh['tx'=8,'ty'=4] {'tx','ty'}, dimensions={0} | all-to-all | bytes 655360 | tf_op jit(solution)/shard_map/all_to_all | solution.py:706
  30.3 0.0 copy-done.2
  30.4 0.0 copy-done.3
  30.4 0.0 copy-done
  30.4 0.0 copy-done.1
  30.4 0.9 %level.1 = (f32[256,256]{1,0:T(8,128)S(1)}, f32[4,256,128]{2,1,0:T(8,128)S(1)}, bf16[32,384]{1,0:T(8,128)(2,1)S(1)}, bf16[32,384]{1,0:T(8,128)(2,1)S(1)}) custom-call(bf16[1280,128]{1,0:T(8,128)(2,1)S(1)} %bitcast.14, bf16[32,512]{1,0:T(8,128)(2,1)S(1)} %collective-permute-done.second_swap_ref, bf16[32,512]{1,0:T(8,128)(2,1)S(1)} %collective-permute-done.1.first_swap_ref, ...), custom_call_target="tpu_custom_call" | custom-call | tf_op jit(solution)/shard_map/level/pallas_call | solution.py:712
  31.2 0.9 %collective-permute-start.2 = (bf16[32,384]{1,0:T(8,128)(2,1)S(1)}, bf16[32,384]{1,0:T(8,128)(2,1)S(1)}, u32[]{:S(2)}, u32[]{:S(2)}) collective-permute-start(bf16[32,384]{1,0:T(8,128)(2,1)S(1)} %get-tuple-element.56), channel_id=1, source_target_pairs={{0,4},{1,5},{2,6},{3,7},{4,0},{5,1},{6,2},{7,3},{8,12},{9,13},{10,... | collective-permute-start | bytes 73736 | tf_op jit(solution)/shard_map/ppermute | solution.py:621
  32.2 0.0 collective-permute-start.3
  32.2 4.6 %flow_inner.1.inner_ref = f32[256,256]{1,0:T(8,128)S(1)} custom-call(f32[256,256]{1,0:T(8,128)S(1)} %get-tuple-element.54.level_ref, f32[4,256,128]{2,1,0:T(8,128)S(1)} %get-tuple-element.55.side_ref, f32[256,256]{1,0:T(8,128)S(1)} %copy-done, s32[256,256]{1,0:T(8,128)S(1)} %copy-done.2, f32[256,256]{1,0:T(8,128)S(1)} %copy-done.1), custom_call_target="tpu_custom_call" | custom-call | flops 5000000000 | bytes 4000000 | tf_op jit(solution)/shard_map/flow_inner/pallas_call | solution.py:728
  36.8 0.0 collective-permute-done.2.first_swap_ref
  36.8 0.0 collective-permute-done.3.second_swap_ref
  36.8 2.0 %flow_ends.1 = f32[256,256]{1,0:T(8,128)} custom-call(f32[256,256]{1,0:T(8,128)S(1)} %flow_inner.1.inner_ref, f32[256,256]{1,0:T(8,128)S(1)} %get-tuple-element.54.level_ref, f32[4,256,128]{2,1,0:T(8,128)S(1)} %get-tuple-element.55.side_ref, f32[256,256]{1,0:T(8,128)S(1)} %copy-done, s32[256,256]{1,0:T(8,128)S(1)} %copy-done.2, f32[256,256]{1,0:T(8,128)S(1)} %copy-done.1, ...), custom_call_target="tpu_custom_call" | custom-call | tf_op jit(solution)/shard_map/flow_ends/pallas_call | solution.py:738
Async XLA Ops:
  2.2 10.7 %collective-permute-start = (bf16[32,512]{1,0:T(8,128)(2,1)S(1)}, bf16[32,512]{1,0:T(8,128)(2,1)S(1)}, u32[]{:S(2)}, u32[]{:S(2)}) collective-permute-start(bf16[32,512]{1,0:T(8,128)(2,1)S(1)} %get-tuple-element.30), channel_id=1, source_target_pairs={{0,31},{1,2},{2,1},{3,4},{4,3},{5,6},{6,5},{7,8},{8,7},{9,10},{10,... | collective-permute-start | bytes 98312 | tf_op jit(solution)/shard_map/ppermute | solution.py:621
  8.6 4.3 %collective-permute-start.1 = (bf16[32,512]{1,0:T(8,128)(2,1)S(1)}, bf16[32,512]{1,0:T(8,128)(2,1)S(1)}, u32[]{:S(2)}, u32[]{:S(2)}) collective-permute-start(bf16[32,512]{1,0:T(8,128)(2,1)S(1)} %get-tuple-element.31), channel_id=1, source_target_pairs={{0,1},{1,0},{2,3},{3,2},{4,5},{5,4},{6,7},{7,6},{8,9},{9,8},{10,11... | collective-permute-start | bytes 98312 | tf_op jit(solution)/shard_map/ppermute | solution.py:621
  12.9 17.4 %copy-start.2 = (s32[256,256]{1,0:T(8,128)S(1)}, s32[256,256]{1,0:T(8,128)}, u32[]{:S(2)}) copy-start(s32[256,256]{1,0:T(8,128)} %dir_ref.5) | copy-start | bytes 786436
  12.9 17.4 %copy-start.3 = (f32[256,256]{1,0:T(8,128)S(1)}, f32[256,256]{1,0:T(8,128)}, u32[]{:S(2)}) copy-start(f32[256,256]{1,0:T(8,128)} %depth_ref.1) | copy-start | bytes 786436
  15.6 14.8 %copy-start = (f32[256,256]{1,0:T(8,128)S(1)}, f32[256,256]{1,0:T(8,128)}, u32[]{:S(2)}) copy-start(f32[256,256]{1,0:T(8,128)} %slope_ref.5) | copy-start | bytes 786436
  15.6 14.8 %copy-start.1 = (f32[256,256]{1,0:T(8,128)S(1)}, f32[256,256]{1,0:T(8,128)}, u32[]{:S(2)}) copy-start(f32[256,256]{1,0:T(8,128)} %rain_ref.5) | copy-start | bytes 786436
  31.2 5.5 %collective-permute-start.2 = (bf16[32,384]{1,0:T(8,128)(2,1)S(1)}, bf16[32,384]{1,0:T(8,128)(2,1)S(1)}, u32[]{:S(2)}, u32[]{:S(2)}) collective-permute-start(bf16[32,384]{1,0:T(8,128)(2,1)S(1)} %get-tuple-element.56), channel_id=1, source_target_pairs={{0,4},{1,5},{2,6},{3,7},{4,0},{5,1},{6,2},{7,3},{8,12},{9,13},{10,... | collective-permute-start | bytes 73736 | tf_op jit(solution)/shard_map/ppermute | solution.py:621
  32.2 4.6 %collective-permute-start.3 = (bf16[32,384]{1,0:T(8,128)(2,1)S(1)}, bf16[32,384]{1,0:T(8,128)(2,1)S(1)}, u32[]{:S(2)}, u32[]{:S(2)}) collective-permute-start(bf16[32,384]{1,0:T(8,128)(2,1)S(1)} %get-tuple-element.57), channel_id=1, source_target_pairs={{0,1},{1,0},{2,3},{3,2},{4,8},{5,9},{6,10},{7,11},{8,4},{9,5},{10,... | collective-permute-start | bytes 73736 | tf_op jit(solution)/shard_map/ppermute | solution.py:621
